TPU v7x, 32 devices: a whole 2x2x4 slice. The times are simulated.
32 devices in a mesh: dp: 8 (over y, x, core), tensor: 4 (over z).
Axes of the slice: x: 2, y: 2, z: 4, core: 2. Of those that a mesh axis runs over, the one named last changes fastest.
Arguments:
- tokens: bfloat16 [18432, 1536], P(('dp', 'tensor')), may hold values from -6 to 6
- teacher: bfloat16 [18432, 1536], P(('dp', 'tensor')), may hold values from -13 to 13
- valid_mask: int32 [18432], P('dp'), may hold values from 0 to 1, as said below
- norm1_gain: float32 [1536], replicated, may hold values from 0.5 to 1.5
- w_query: bfloat16 [1536, 1536], P(None, 'tensor'), may hold values from -0.15625 to 0.15625
- w_key: bfloat16 [1536, 1536], P(None, 'tensor'), may hold values from -0.15625 to 0.15625
- w_value: bfloat16 [1536, 1536], P(None, 'tensor'), may hold values from -0.15625 to 0.15625
- conv_weight: float32 [16, 6, 11], P('tensor'), may hold values from -0.6 to 2.1
- head_mix: float32 [8, 2, 2], P('tensor'), may hold values from -1.2 to 2
- gn_gain: float32 [16, 96], P('tensor'), may hold values from 0.5 to 1.5
- w_out: bfloat16 [1536, 1536], P(None, 'tensor'), may hold values from -0.15625 to 0.15625
- norm2_gain: float32 [1536], replicated, may hold values from 0.5 to 1.5
- w_gate: bfloat16 [1536, 4096], P(None, 'tensor'), may hold values from -0.15625 to 0.15625
- w_up: bfloat16 [1536, 4096], P(None, 'tensor'), may hold values from -0.15625 to 0.15625
- w_down: bfloat16 [1536, 4096], P(None, 'tensor'), may hold values from -0.09375 to 0.09375
Outputs:
- output: bfloat16 [18432, 1536], P(('dp', 'tensor'))
- loss: float32 [], replicated
- grad_input: float32 [18432, 1536], P(('dp', 'tensor'))
- grad_norm1_gain: float32 [1536], P('tensor')
- grad_w_query: float32 [1536, 1536], P(None, 'tensor')
- grad_w_key: float32 [1536, 1536], P(None, 'tensor')
- grad_w_value: float32 [1536, 1536], P(None, 'tensor')
- grad_conv_weight: float32 [16, 6, 11], P('tensor')
- grad_head_mix: float32 [8, 2, 2], P('tensor')
- grad_gn_gain: float32 [16, 96], P('tensor')
- grad_w_out: float32 [1536, 1536], P(None, 'tensor')
- grad_norm2_gain: float32 [1536], P('tensor')
- grad_w_gate: float32 [1536, 4096], P(None, 'tensor')
- grad_w_up: float32 [1536, 4096], P(None, 'tensor')
- grad_w_down: float32 [1536, 4096], P(None, 'tensor')
Inputs may be any that keep to these rules, and one draw needn't show every extreme that they name: `valid_mask`: in every tree the valid slots of the trunk and of each branch and leaf form a prefix of it of one slot or more.
All inputs are finite; a program needn't handle non-finite values.
Results may differ from a plain program's by a relative error of at most 0.018.
Values may be sent and summed in bfloat16 or wider, within the bound.
A program may use at most 448 MiB of HBM per device.

v0:
```python
import math

import jax
import jax.numpy as jnp
from jax import lax
from jax.sharding import PartitionSpec as P

H = 16
HD = 96
CQ = 6
CK = 11
TRUNK = 192
SEG = 32
TPG = 4
TREE = 576


def along_paths(array_in):
    tail_shape = array_in.shape[1:]
    trunk_part = array_in[:TRUNK]
    branch_part = array_in[TRUNK : TRUNK + 4 * SEG].reshape((4, SEG) + tail_shape)
    leaf_part = array_in[TRUNK + 4 * SEG :].reshape((8, SEG) + tail_shape)
    trunk_wide = jnp.broadcast_to(trunk_part[None], (8,) + trunk_part.shape)
    branch_wide = jnp.repeat(branch_part, 2, axis=0)
    return jnp.concatenate([trunk_wide, branch_wide, leaf_part], axis=1)


def from_paths(path_grads):
    tail_shape = path_grads.shape[2:]
    trunk_sum = jnp.sum(path_grads[:, :TRUNK], axis=0)
    branch_sum = jnp.sum(
        path_grads[:, TRUNK : TRUNK + SEG].reshape((4, 2, SEG) + tail_shape), axis=1
    )
    leaf_rows = path_grads[:, TRUNK + SEG :].reshape((8 * SEG,) + tail_shape)
    return jnp.concatenate(
        [trunk_sum, branch_sum.reshape((4 * SEG,) + tail_shape), leaf_rows], axis=0
    )


def owned_rows(trunk_out, path_out):
    tail_shape = path_out.shape[2:]
    branch_rows = path_out[0::2, :SEG].reshape((4 * SEG,) + tail_shape)
    leaf_rows = path_out[:, SEG:].reshape((8 * SEG,) + tail_shape)
    return jnp.concatenate([trunk_out, branch_rows, leaf_rows], axis=0)


def owned_split(full_rows):
    tail_shape = full_rows.shape[1:]
    branch_rows = full_rows[TRUNK : TRUNK + 4 * SEG].reshape((4, 1, SEG) + tail_shape)
    branch_wide = jnp.concatenate([branch_rows, jnp.zeros_like(branch_rows)], axis=1).reshape(
        (8, SEG) + tail_shape
    )
    leaf_rows = full_rows[TRUNK + 4 * SEG :].reshape((8, SEG) + tail_shape)
    return (full_rows[:TRUNK], jnp.concatenate([branch_wide, leaf_rows], axis=1))


def masked_scores(q_rows, k_rows, q_pos, k_valid):
    raw_scores = jnp.einsum("rhd,khd->hrk", q_rows, k_rows, preferred_element_type=jnp.float32) * (
        1.0 / math.sqrt(HD)
    )
    key_index = jnp.arange(k_rows.shape[0], dtype=jnp.int32)
    allowed = (key_index[None, :] <= q_pos[:, None]) & k_valid[None, :] & (q_pos[:, None] >= 0)
    return (jnp.where(allowed[None], raw_scores, 0.0), allowed)


def convolve(pre_scores, conv_w):
    out_rows = pre_scores.shape[1] - (CQ - 1)
    key_width = pre_scores.shape[2]
    half_width = CK // 2
    padded = jnp.pad(pre_scores, ((0, 0), (0, 0), (half_width, half_width)))
    conv_total = jnp.zeros((pre_scores.shape[0], out_rows, key_width), jnp.float32)
    for shift_q in range(CQ):
        for shift_k in range(CK):
            window = padded[
                :,
                CQ - 1 - shift_q : CQ - 1 - shift_q + out_rows,
                2 * half_width - shift_k : 2 * half_width - shift_k + key_width,
            ]
            conv_total = conv_total + conv_w[:, shift_q, shift_k][:, None, None] * window
    return (conv_total, padded)


def attend_forward(q_rows, k_rows, v_rows, q_pos, k_valid, conv_w, mix_w):
    pre_scores, allowed = masked_scores(q_rows, k_rows, q_pos, k_valid)
    conv_out, padded = convolve(pre_scores, conv_w)
    logits = jnp.where(allowed[CQ - 1 :][None], conv_out, -1e30)
    row_top = jnp.max(logits, axis=-1, keepdims=True)
    shifted = jnp.exp(logits - row_top)
    totals = jnp.sum(shifted, axis=-1, keepdims=True)
    probabilities = shifted / totals
    mixed_probs = jnp.sum(mix_w[:, :, None, None] * probabilities[None], axis=1).astype(
        jnp.bfloat16
    )
    head_out = jnp.einsum("hrk,khd->rhd", mixed_probs, v_rows, preferred_element_type=jnp.float32)
    return (head_out, (row_top + jnp.log(totals))[..., 0])


def attend_backward(q_rows, k_rows, v_rows, q_pos, k_valid, conv_w, mix_w, log_total, d_out):
    pre_scores, allowed = masked_scores(q_rows, k_rows, q_pos, k_valid)
    conv_out, padded = convolve(pre_scores, conv_w)
    kept_rows = allowed[CQ - 1 :]
    logits = jnp.where(kept_rows[None], conv_out, -1e30)
    probabilities = jnp.exp(logits - log_total[..., None])
    mixed_probs = jnp.sum(mix_w[:, :, None, None] * probabilities[None], axis=1).astype(
        jnp.bfloat16
    )
    d_values = jnp.einsum("hrk,rhd->khd", mixed_probs, d_out, preferred_element_type=jnp.float32)
    d_mixed = jnp.einsum("rhd,khd->hrk", d_out, v_rows, preferred_element_type=jnp.float32)
    d_mix = jnp.sum(d_mixed[:, None] * probabilities[None], axis=(2, 3))
    d_probs = jnp.sum(mix_w[:, :, None, None] * d_mixed[:, None], axis=0)
    d_logits = probabilities * (d_probs - jnp.sum(d_probs * probabilities, axis=-1, keepdims=True))
    d_conv_out = jnp.where(kept_rows[None], d_logits, 0.0)
    half_width = CK // 2
    out_rows = d_conv_out.shape[1]
    all_rows = pre_scores.shape[1]
    key_width = pre_scores.shape[2]
    d_padded = jnp.pad(d_conv_out, ((0, 0), (CQ - 1, CQ - 1), (half_width, half_width)))
    d_pre = jnp.zeros_like(pre_scores)
    kernel_grads = []
    for shift_q in range(CQ):
        for shift_k in range(CK):
            window = padded[
                :,
                CQ - 1 - shift_q : CQ - 1 - shift_q + out_rows,
                2 * half_width - shift_k : 2 * half_width - shift_k + key_width,
            ]
            kernel_grads.append(jnp.sum(d_conv_out * window, axis=(1, 2)))
            d_pre = (
                d_pre
                + conv_w[:, shift_q, shift_k][:, None, None]
                * d_padded[:, shift_q : shift_q + all_rows, shift_k : shift_k + key_width]
            )
    d_kernel = jnp.stack(kernel_grads, axis=-1).reshape(conv_w.shape)
    d_scores = jnp.where(allowed[None], d_pre, 0.0).astype(jnp.bfloat16)
    d_query = jnp.einsum("hrk,khd->rhd", d_scores, k_rows, preferred_element_type=jnp.float32) * (
        1.0 / math.sqrt(HD)
    )
    d_key = jnp.einsum("hrk,rhd->khd", d_scores, q_rows, preferred_element_type=jnp.float32) * (
        1.0 / math.sqrt(HD)
    )
    return (d_query, d_key, d_values, d_kernel, d_mix)


def block_inputs(queries3, keys3, values3, head_pick):
    q_grp = queries3[:, head_pick]
    k_grp = keys3[:, head_pick]
    v_grp = values3[:, head_pick]
    trunk_q = jnp.concatenate(
        [jnp.zeros((CQ - 1,) + q_grp.shape[1:], q_grp.dtype), q_grp[:TRUNK]], axis=0
    )
    path_q = along_paths(q_grp)[:, TRUNK - (CQ - 1) :]
    return (
        (trunk_q, k_grp[:TRUNK], v_grp[:TRUNK]),
        (path_q, along_paths(k_grp), along_paths(v_grp)),
    )


def local(
    tokens,
    teacher,
    valid_mask,
    norm1_gain,
    w_query,
    w_key,
    w_value,
    conv_weight,
    head_mix,
    gn_gain,
    w_out,
    norm2_gain,
    w_gate,
    w_up,
    w_down,
):
    local_rows = tokens.shape[0]
    model_width = tokens.shape[1]
    tensor_size = lax.axis_size("tensor")
    tensor_index = lax.axis_index("tensor")
    group_rows = local_rows * tensor_size
    width_local = w_query.shape[1]
    heads_local = width_local // HD
    mix_count = heads_local // 2
    inputs = tokens.astype(jnp.float32)
    inv_one = lax.rsqrt(jnp.mean(inputs * inputs, axis=-1, keepdims=True) + 1e-06)
    normed_one = (inputs * inv_one * norm1_gain).astype(jnp.bfloat16)
    normed_all = lax.all_gather(normed_one, "tensor", axis=0, tiled=True)
    queries = jnp.dot(normed_all, w_query, preferred_element_type=jnp.float32).astype(jnp.bfloat16)
    keys_all = jnp.dot(normed_all, w_key, preferred_element_type=jnp.float32).astype(jnp.bfloat16)
    values_all = jnp.dot(normed_all, w_value, preferred_element_type=jnp.float32).astype(
        jnp.bfloat16
    )
    queries3 = queries.reshape(group_rows, heads_local, HD)
    keys3 = keys_all.reshape(group_rows, heads_local, HD)
    values3 = values_all.reshape(group_rows, heads_local, HD)
    valid_all = valid_mask > 0
    trunk_pos = jnp.arange(-(CQ - 1), TRUNK, dtype=jnp.int32)
    path_pos = jnp.arange(TRUNK - (CQ - 1), TRUNK + 2 * SEG, dtype=jnp.int32)
    path_forward = jax.vmap(attend_forward, in_axes=(0, 0, 0, None, 0, None, None))
    path_backward = jax.vmap(attend_backward, in_axes=(0, 0, 0, None, 0, None, None, 0, 0))
    tree_parts = []
    saved_totals = []
    for tree_index in range(TPG):
        tree_slice = slice(tree_index * TREE, (tree_index + 1) * TREE)
        valid_tree = valid_all[tree_slice]
        head_parts = []
        for group_index in range(mix_count):
            head_pick = slice(2 * group_index, 2 * group_index + 2)
            trunk_in, path_in = block_inputs(
                queries3[tree_slice], keys3[tree_slice], values3[tree_slice], head_pick
            )
            conv_grp = conv_weight[head_pick]
            mix_grp = head_mix[group_index]
            trunk_out, trunk_lse = attend_forward(
                *trunk_in, trunk_pos, valid_tree[:TRUNK], conv_grp, mix_grp
            )
            path_out, path_lse = path_forward(
                *path_in, path_pos, along_paths(valid_tree), conv_grp, mix_grp
            )
            head_parts.append(owned_rows(trunk_out, path_out))
            saved_totals.append((trunk_lse, path_lse))
        tree_parts.append(jnp.concatenate(head_parts, axis=1))
    head_out = jnp.concatenate(tree_parts, axis=0)
    centered = head_out - jnp.mean(head_out, axis=-1, keepdims=True)
    inv_gn = lax.rsqrt(jnp.mean(centered * centered, axis=-1, keepdims=True) + 1e-05)
    unit_heads = centered * inv_gn
    normed_heads = (unit_heads * gn_gain).reshape(group_rows, width_local).astype(jnp.bfloat16)
    row_block = normed_heads
    attn_rows = lax.psum_scatter(
        jnp.einsum("rk,dk->rd", row_block, w_out, preferred_element_type=jnp.float32),
        "tensor",
        scatter_dimension=0,
        tiled=True,
    )
    hidden_in = inputs + attn_rows
    inv_two = lax.rsqrt(jnp.mean(hidden_in * hidden_in, axis=-1, keepdims=True) + 1e-06)
    normed_two = (hidden_in * inv_two * norm2_gain).astype(jnp.bfloat16)
    ffn_inputs = lax.all_gather(normed_two, "tensor", axis=0, tiled=True)
    gate_val = jnp.dot(ffn_inputs, w_gate, preferred_element_type=jnp.float32)
    up_val = jnp.dot(ffn_inputs, w_up, preferred_element_type=jnp.float32)
    hidden_low = (jax.nn.silu(gate_val) * up_val).astype(jnp.bfloat16)
    row_block = hidden_low
    ffn_rows = lax.psum_scatter(
        jnp.einsum("rf,df->rd", row_block, w_down, preferred_element_type=jnp.float32),
        "tensor",
        scatter_dimension=0,
        tiled=True,
    )
    final_rows = hidden_in + ffn_rows
    output = final_rows.astype(jnp.bfloat16)
    mine_valid = lax.dynamic_slice_in_dim(
        valid_mask, tensor_index * local_rows, local_rows, 0
    ).astype(jnp.float32)
    error_rows = mine_valid[:, None] * (final_rows - teacher.astype(jnp.float32))
    squared_sum = jnp.sum(error_rows * error_rows)
    count_sum = jnp.sum(mine_valid)
    d_low = error_rows.astype(jnp.bfloat16)
    d_all = lax.all_gather(d_low, "tensor", axis=0, tiled=True)
    grad_down = jnp.einsum("rd,rf->df", d_all, hidden_low, preferred_element_type=jnp.float32)
    d_hidden = jnp.dot(d_all, w_down, preferred_element_type=jnp.float32)
    sigmoid_gate = jax.nn.sigmoid(gate_val)
    d_gate = (d_hidden * up_val * sigmoid_gate * (1.0 + gate_val * (1.0 - sigmoid_gate))).astype(
        jnp.bfloat16
    )
    d_up = (d_hidden * gate_val * sigmoid_gate).astype(jnp.bfloat16)
    grad_gate = jnp.einsum("rd,rf->df", ffn_inputs, d_gate, preferred_element_type=jnp.float32)
    grad_up = jnp.einsum("rd,rf->df", ffn_inputs, d_up, preferred_element_type=jnp.float32)
    d_normed_two = lax.psum_scatter(
        jnp.einsum("rf,df->rd", d_gate, w_gate, preferred_element_type=jnp.float32)
        + jnp.einsum("rf,df->rd", d_up, w_up, preferred_element_type=jnp.float32),
        "tensor",
        scatter_dimension=0,
        tiled=True,
    )
    scaled_two = d_normed_two * norm2_gain
    grad_gain_two = jnp.sum(d_normed_two * hidden_in * inv_two, axis=0)
    d_hidden_in = (
        error_rows
        + inv_two * scaled_two
        - hidden_in * inv_two**3 * jnp.mean(scaled_two * hidden_in, axis=-1, keepdims=True)
    )
    d_attn_all = lax.all_gather(d_hidden_in.astype(jnp.bfloat16), "tensor", axis=0, tiled=True)
    grad_out = jnp.einsum("rd,rk->dk", d_attn_all, normed_heads, preferred_element_type=jnp.float32)
    d_normed_heads = jnp.dot(d_attn_all, w_out, preferred_element_type=jnp.float32).reshape(
        group_rows, heads_local, HD
    )
    grad_gn_local = jnp.sum(d_normed_heads * unit_heads, axis=0)
    scaled_heads = d_normed_heads * gn_gain
    d_head = (
        inv_gn
        * (
            scaled_heads
            - jnp.mean(scaled_heads, axis=-1, keepdims=True)
            - unit_heads * jnp.mean(scaled_heads * unit_heads, axis=-1, keepdims=True)
        )
    ).astype(jnp.bfloat16)
    tail_rows = TREE - TRUNK
    lead_rows = TRUNK - (CQ - 1)
    dq_trees, dk_trees, dv_trees = ([], [], [])
    kernel_sums = [jnp.zeros((2, CQ, CK), jnp.float32) for group_index in range(mix_count)]
    mix_sums = [jnp.zeros((2, 2), jnp.float32) for group_index in range(mix_count)]
    for tree_index in range(TPG):
        tree_slice = slice(tree_index * TREE, (tree_index + 1) * TREE)
        valid_tree = valid_all[tree_slice]
        dq_parts, dk_parts, dv_parts = ([], [], [])
        for group_index in range(mix_count):
            head_pick = slice(2 * group_index, 2 * group_index + 2)
            trunk_in, path_in = block_inputs(
                queries3[tree_slice], keys3[tree_slice], values3[tree_slice], head_pick
            )
            conv_grp = conv_weight[head_pick]
            mix_grp = head_mix[group_index]
            trunk_lse, path_lse = saved_totals[tree_index * mix_count + group_index]
            trunk_dout, path_dout = owned_split(d_head[tree_slice][:, head_pick])
            trunk_dq, trunk_dk, trunk_dv, trunk_kernel, trunk_mix = attend_backward(
                *trunk_in, trunk_pos, valid_tree[:TRUNK], conv_grp, mix_grp, trunk_lse, trunk_dout
            )
            path_dq, path_dk, path_dv, path_kernel, path_mix = path_backward(
                *path_in, path_pos, along_paths(valid_tree), conv_grp, mix_grp, path_lse, path_dout
            )
            path_dq = jnp.pad(path_dq, ((0, 0), (lead_rows, 0), (0, 0), (0, 0)))
            dq_parts.append(
                from_paths(path_dq) + jnp.pad(trunk_dq[CQ - 1 :], ((0, tail_rows), (0, 0), (0, 0)))
            )
            dk_parts.append(
                from_paths(path_dk) + jnp.pad(trunk_dk, ((0, tail_rows), (0, 0), (0, 0)))
            )
            dv_parts.append(
                from_paths(path_dv) + jnp.pad(trunk_dv, ((0, tail_rows), (0, 0), (0, 0)))
            )
            kernel_sums[group_index] = (
                kernel_sums[group_index] + trunk_kernel + jnp.sum(path_kernel, axis=0)
            )
            mix_sums[group_index] = mix_sums[group_index] + trunk_mix + jnp.sum(path_mix, axis=0)
        dq_trees.append(jnp.concatenate(dq_parts, axis=1))
        dk_trees.append(jnp.concatenate(dk_parts, axis=1))
        dv_trees.append(jnp.concatenate(dv_parts, axis=1))
    d_q_low = (
        jnp.concatenate(dq_trees, axis=0).reshape(group_rows, width_local).astype(jnp.bfloat16)
    )
    d_k_low = (
        jnp.concatenate(dk_trees, axis=0).reshape(group_rows, width_local).astype(jnp.bfloat16)
    )
    d_v_low = (
        jnp.concatenate(dv_trees, axis=0).reshape(group_rows, width_local).astype(jnp.bfloat16)
    )
    grad_kernel_local = jnp.concatenate(kernel_sums, axis=0)
    grad_mix_local = jnp.stack(mix_sums, axis=0)
    grad_query = jnp.einsum("rd,rk->dk", normed_all, d_q_low, preferred_element_type=jnp.float32)
    grad_key = jnp.einsum("rd,rk->dk", normed_all, d_k_low, preferred_element_type=jnp.float32)
    grad_value = jnp.einsum("rd,rk->dk", normed_all, d_v_low, preferred_element_type=jnp.float32)
    summed_terms = jnp.einsum("rk,dk->rd", d_q_low, w_query, preferred_element_type=jnp.float32)
    summed_terms = summed_terms + jnp.einsum(
        "rk,dk->rd", d_k_low, w_key, preferred_element_type=jnp.float32
    )
    d_normed_one = lax.psum_scatter(
        (
            summed_terms
            + jnp.einsum("rk,dk->rd", d_v_low, w_value, preferred_element_type=jnp.float32)
        ).astype(jnp.bfloat16),
        "tensor",
        scatter_dimension=0,
        tiled=True,
    ).astype(jnp.float32)
    scaled_one = d_normed_one * norm1_gain
    grad_gain_one = jnp.sum(d_normed_one * inputs * inv_one, axis=0)
    grad_input = (
        d_hidden_in
        + inv_one * scaled_one
        - inputs * inv_one**3 * jnp.mean(scaled_one * inputs, axis=-1, keepdims=True)
    )
    head_start = tensor_index * heads_local
    group_start = tensor_index * mix_count
    gn_full = lax.dynamic_update_slice(
        jnp.zeros((H, HD), jnp.float32), grad_gn_local, (head_start, 0)
    )
    kernel_full = lax.dynamic_update_slice(
        jnp.zeros((H, CQ, CK), jnp.float32), grad_kernel_local, (head_start, 0, 0)
    )
    mix_full = lax.dynamic_update_slice(
        jnp.zeros((H // 2, 2, 2), jnp.float32), grad_mix_local, (group_start, 0, 0)
    )
    sum_one, sum_two, sum_gn, sum_kernel, sum_mix, sum_squares, sum_count = lax.psum(
        (grad_gain_one, grad_gain_two, gn_full, kernel_full, mix_full, squared_sum, count_sum),
        ("dp", "tensor"),
    )
    loss = sum_squares / (sum_count * model_width)
    gain_slice = model_width // tensor_size
    gain_one_out = lax.dynamic_slice_in_dim(sum_one, tensor_index * gain_slice, gain_slice, 0)
    gain_two_out = lax.dynamic_slice_in_dim(sum_two, tensor_index * gain_slice, gain_slice, 0)
    gn_out = lax.dynamic_slice_in_dim(sum_gn, head_start, heads_local, 0)
    kernel_out = lax.dynamic_slice_in_dim(sum_kernel, head_start, heads_local, 0)
    mix_out = lax.dynamic_slice_in_dim(sum_mix, group_start, mix_count, 0)
    reduced = (
        lax.psum_scatter(grad_query, "dp", scatter_dimension=0, tiled=True),
        lax.psum_scatter(grad_key, "dp", scatter_dimension=0, tiled=True),
        lax.psum_scatter(grad_value, "dp", scatter_dimension=0, tiled=True),
        lax.psum_scatter(grad_out, "dp", scatter_dimension=0, tiled=True),
        lax.psum_scatter(grad_gate, "dp", scatter_dimension=0, tiled=True),
        lax.psum_scatter(grad_up, "dp", scatter_dimension=0, tiled=True),
        lax.psum_scatter(grad_down, "dp", scatter_dimension=0, tiled=True),
    )
    summed = (
        lax.all_gather(reduced[0].astype(jnp.bfloat16), "dp", axis=0, tiled=True).astype(
            jnp.float32
        ),
        lax.all_gather(reduced[1].astype(jnp.bfloat16), "dp", axis=0, tiled=True).astype(
            jnp.float32
        ),
        lax.all_gather(reduced[2].astype(jnp.bfloat16), "dp", axis=0, tiled=True).astype(
            jnp.float32
        ),
        lax.all_gather(reduced[3].astype(jnp.bfloat16), "dp", axis=0, tiled=True).astype(
            jnp.float32
        ),
        lax.all_gather(reduced[4].astype(jnp.bfloat16), "dp", axis=0, tiled=True).astype(
            jnp.float32
        ),
        lax.all_gather(reduced[5].astype(jnp.bfloat16), "dp", axis=0, tiled=True).astype(
            jnp.float32
        ),
        lax.all_gather(reduced[6].astype(jnp.bfloat16), "dp", axis=0, tiled=True).astype(
            jnp.float32
        ),
    )
    return (
        output,
        loss,
        grad_input,
        gain_one_out,
        summed[0],
        summed[1],
        summed[2],
        kernel_out,
        mix_out,
        gn_out,
        summed[3],
        gain_two_out,
        summed[4],
        summed[5],
        summed[6],
    )


def solution(mesh):
    return jax.shard_map(
        local,
        mesh=mesh,
        in_specs=(
            P(("dp", "tensor"), None),
            P(("dp", "tensor"), None),
            P("dp"),
            P(),
            P(None, "tensor"),
            P(None, "tensor"),
            P(None, "tensor"),
            P("tensor", None, None),
            P("tensor", None, None),
            P("tensor", None),
            P(None, "tensor"),
            P(),
            P(None, "tensor"),
            P(None, "tensor"),
            P(None, "tensor"),
        ),
        out_specs=(
            P(("dp", "tensor"), None),
            P(),
            P(("dp", "tensor"), None),
            P("tensor"),
            P(None, "tensor"),
            P(None, "tensor"),
            P(None, "tensor"),
            P("tensor", None, None),
            P("tensor", None, None),
            P("tensor", None),
            P(None, "tensor"),
            P("tensor"),
            P(None, "tensor"),
            P(None, "tensor"),
            P(None, "tensor"),
        ),
        check_vma=False,
    )
```

profile of v0, /device:TPU:0, one launch (start us, length us, event | category | flops | bytes accessed | tf_op | source)
XLA Modules:
  0.0 4814.2 jit_solution(15878675256563608252)
XLA Ops:
  30.7 112.6 %all-gather.12.cloned.1.call-done = bf16[2304,1536]{1,0:T(8,128)(2,1)} async-done(((bf16[576,1536]{1,0:T(8,128)(2,1)}), bf16[2304,1536]{1,0:T(8,128)(2,1)}) %all-gather.12.cloned.1.call-update) | async-done | bytes 7077904 | tf_op jit(solution)/shard_map/all_gather | solution.py:186
  256.7 48.9 %fusion.1474 = (f32[8,2,64]{2,1,0:T(2,128)S(1)}, f32[8,2,64,256]{3,2,1,0:T(8,128)}) fusion(f32[2]{0:T(128)} %get-tuple-element.1189, f32[2]{0:T(128)} %get-tuple-element.1190, f32[2]{0:T(128)} %get-tuple-element.1191, f32[2]{0:T(128)} %get-tuple-element.1192, f32[2]{0:T(128)} %get-tuple-element.1193, f32[8,2,69,256]{3,2,1,0:T(8,128)} %fusion.41, ...), kind=kLoop, calls=%fused_computation.4134 | loop fusion | flops 34864128 | bytes 8688640 | tf_op jit(solution)/shard_map/vmap()/reduce_max | solution.py:87
  324.7 46.7 fusion.1475
  390.5 50.1 %fusion.1476 = (f32[8,2,64]{2,1,0:T(2,128)S(1)}, f32[8,2,64,256]{3,2,1,0:T(8,128)}) fusion(f32[2]{0:T(128)} %get-tuple-element.1189, f32[2]{0:T(128)} %get-tuple-element.1190, f32[2]{0:T(128)} %get-tuple-element.1191, f32[2]{0:T(128)} %get-tuple-element.1192, f32[2]{0:T(128)} %get-tuple-element.1193, f32[8,2,69,256]{3,2,1,0:T(8,128)} %fusion.39, ...), kind=kLoop, calls=%fused_computation.4136 | loop fusion | flops 34864128 | bytes 8688640 | tf_op jit(solution)/shard_map/vmap()/reduce_max | solution.py:87
  458.9 45.9 fusion.1477
  595.7 47.6 fusion.1482
  663.3 47.6 fusion.1483
  730.8 46.7 fusion.1484
  797.5 49.4 %fusion.1485 = (f32[8,2,64]{2,1,0:T(2,128)S(1)}, f32[8,2,64,256]{3,2,1,0:T(8,128)}) fusion(f32[2]{0:T(128)} %get-tuple-element.1463, f32[2]{0:T(128)} %get-tuple-element.1462, f32[2]{0:T(128)} %get-tuple-element.1254, f32[2]{0:T(128)} %get-tuple-element.1255, f32[2]{0:T(128)} %get-tuple-element.1256, f32[8,2,69,256]{3,2,1,0:T(8,128)} %fusion.34, ...), kind=kLoop, calls=%fused_computation.4145 | loop fusion | flops 34864128 | bytes 8688640 | tf_op jit(solution)/shard_map/vmap()/reduce_max | solution.py:87
  913.7 23.5 fusion.1472
  940.3 23.3 fusion.1471
  966.6 23.7 fusion.1470
  993.3 22.8 fusion.1478
  1019.1 23.6 fusion.1479
  1045.8 25.0 fusion.1480
  1169.7 235.6 %reduce-scatter.12.cloned.1.call-done = f32[576,1536]{1,0:T(8,128)} async-done(((f32[2304,1536]{1,0:T(8,128)}), f32[576,1536]{1,0:T(8,128)}) %reduce-scatter.12.cloned.1.call-update) | async-done | bytes 3538960 | tf_op jit(solution)/shard_map/reduce_scatter | solution.py:228
  1411.8 129.3 %all-gather.14.cloned.1.call-done = bf16[2304,1536]{1,0:T(8,128)(2,1)} async-done(((bf16[576,1536]{1,0:T(8,128)(2,1)}), bf16[2304,1536]{1,0:T(8,128)(2,1)}) %all-gather.14.cloned.1.call-update) | async-done | bytes 7077904 | tf_op jit(solution)/shard_map/all_gather | solution.py:237
  1580.3 234.2 %reduce-scatter.14.cloned.1.call-done = f32[576,1536]{1,0:T(8,128)} async-done(((f32[2304,1536]{1,0:T(8,128)}), f32[576,1536]{1,0:T(8,128)}) %reduce-scatter.14.cloned.1.call-update) | async-done | bytes 3538960 | tf_op jit(solution)/shard_map/reduce_scatter | solution.py:242
  1821.7 129.4 %all-gather.16.cloned.1.call-done = bf16[2304,1536]{1,0:T(8,128)(2,1)} async-done(((bf16[576,1536]{1,0:T(8,128)(2,1)}), bf16[2304,1536]{1,0:T(8,128)(2,1)}) %all-gather.16.cloned.1.call-update) | async-done | bytes 7077904 | tf_op jit(solution)/shard_map/all_gather | solution.py:257
  1964.0 19.7 multiply_convert_fusion
  2026.3 17.4 convolution_add_fusion
  2045.8 44.4 reduce-scatter.28.cloned.1.call-done
  2092.2 63.7 %reduce-scatter.30.cloned.1.call-done = f32[192,1024]{1,0:T(8,128)} async-done(((f32[1536,1024]{1,0:T(8,128)}), f32[192,1024]{1,0:T(8,128)}) %reduce-scatter.30.cloned.1.call-update) | async-done | bytes 786448 | tf_op jit(solution)/shard_map/reduce_scatter | solution.py:399
  2158.0 237.7 %reduce-scatter.16.cloned.1.call-done = f32[576,1536]{1,0:T(8,128)} async-done(((f32[2304,1536]{1,0:T(8,128)}), f32[576,1536]{1,0:T(8,128)}) %reduce-scatter.16.cloned.1.call-update) | async-done | bytes 3538960 | tf_op jit(solution)/shard_map/reduce_scatter | solution.py:267
  2414.7 16.8 all-gather.32.cloned.1.call-done
  2436.9 29.6 all-gather.28.cloned.1.call-done
  2471.8 29.5 all-gather.30.cloned.1.call-done
  2506.6 125.1 %all-gather.18.cloned.1.call-done = bf16[2304,1536]{1,0:T(8,128)(2,1)} async-done(((bf16[576,1536]{1,0:T(8,128)(2,1)}), bf16[2304,1536]{1,0:T(8,128)(2,1)}) %all-gather.18.cloned.1.call-update) | async-done | bytes 7077904 | tf_op jit(solution)/shard_map/all_gather | solution.py:281
  2738.5 21.3 select_convert_fusion.1
  2770.3 21.3 select_convert_fusion
  2802.2 21.5 select_convert_fusion.3
  2834.2 21.3 select_convert_fusion.2
  2933.8 21.6 select_convert_fusion.5
  2965.9 22.2 select_convert_fusion.4
  2999.9 44.5 select_convert_fusion.7
  3054.9 43.5 select_convert_fusion.6
  3312.2 23.1 select_convert_fusion.14
  3337.1 15.5 multiply_reduce_fusion.502
  3837.7 17.4 multiply_reduce_fusion.472
  3880.2 18.2 multiply_reduce_fusion.454
  3923.4 16.4 multiply_reduce_fusion.436
  4087.1 16.9 multiply_reduce_fusion.406
  4127.3 17.9 multiply_reduce_fusion.388
  4172.0 16.1 multiply_reduce_fusion.370
  4295.2 16.1 multiply_reduce_fusion.340
  4350.3 16.5 multiply_reduce_fusion.322
  4435.0 17.0 add_convert_fusion
  4755.9 39.5 all-reduce.80
  (3379 shorter events, 2391.0 us)
Async XLA Ops:
  7.2 1561.3 %copy-start = (bf16[1536,1024]{1,0:T(8,128)(2,1)S(1)}, bf16[1536,1024]{1,0:T(8,128)(2,1)}, u32[]{:S(2)}) copy-start(bf16[1536,1024]{1,0:T(8,128)(2,1)} %param.29) | copy-start | bytes 9437188
  7.2 136.1 %all-gather.12.cloned.1.call-start = ((), (), s32[]{:S(2)}) async-start(), calls=%async_computation.11 | async-start | bytes 8847360 | tf_op jit(solution)/shard_map/all_gather | solution.py:186
  12.2 1393.1 %reduce-scatter.12.cloned.1.call-start = ((), (), s32[]{:S(2)}) async-start(), calls=%async_computation.12 | async-start | bytes 17694720 | tf_op jit(solution)/shard_map/reduce_scatter | solution.py:228
  15.2 239.9 %copy-start.148 = (pred[8,69,256]{2,1,0:T(8,128)(4,1)}, pred[8,69,256]{2,1,0:T(8,128)(4,1)S(1)}, u32[]{:S(2)}) copy-start(pred[8,69,256]{2,1,0:T(8,128)(4,1)S(1)} %get-tuple-element.1458) | copy-start | bytes 423940
  15.2 372.8 %copy-start.151 = (pred[8,69,256]{2,1,0:T(8,128)(4,1)}, pred[8,69,256]{2,1,0:T(8,128)(4,1)S(1)}, u32[]{:S(2)}) copy-start(pred[8,69,256]{2,1,0:T(8,128)(4,1)S(1)} %get-tuple-element.1459) | copy-start | bytes 423940
  18.5 549.7 %copy-start.182 = (pred[197,192]{0,1:T(8,128)(4,1)}, pred[197,192]{0,1:T(8,128)(4,1)S(1)}, u32[]{:S(2)}) copy-start(pred[197,192]{0,1:T(8,128)(4,1)S(1)} %get-tuple-element.1494) | copy-start | bytes 113476
  18.5 556.1 %copy-start.184 = (pred[197,192]{0,1:T(8,128)(4,1)}, pred[197,192]{0,1:T(8,128)(4,1)S(1)}, u32[]{:S(2)}) copy-start(pred[197,192]{0,1:T(8,128)(4,1)S(1)} %get-tuple-element.1496) | copy-start | bytes 113476
  578.5 495.3 %copy-start.13 = (f32[2,197,192]{1,2,0:T(8,128)}, f32[2,197,192]{1,2,0:T(8,128)S(1)}, u32[]{:S(2)}) copy-start(f32[2,197,192]{1,2,0:T(8,128)S(1)} %fusion.89) | copy-start | bytes 907780
  1169.7 240.5 %copy-start.508 = (f32[1536]{0:T(1024)S(1)}, f32[1536]{0:T(1024)}, u32[]{:S(2)}) copy-start(f32[1536]{0:T(1024)} %param.26) | copy-start | bytes 18436
  1169.7 371.5 %all-gather.14.cloned.1.call-start = ((), (), s32[]{:S(2)}) async-start(), calls=%async_computation.13 | async-start | bytes 8847360 | tf_op jit(solution)/shard_map/all_gather | solution.py:237
  1411.7 402.8 %reduce-scatter.14.cloned.1.call-start = ((), (), s32[]{:S(2)}) async-start(), calls=%async_computation.14 | async-start | bytes 17694720 | tf_op jit(solution)/shard_map/reduce_scatter | solution.py:242
  1578.8 372.3 %all-gather.16.cloned.1.call-start = ((), (), s32[]{:S(2)}) async-start(), calls=%async_computation.15 | async-start | bytes 8847360 | tf_op jit(solution)/shard_map/all_gather | solution.py:257
  1821.7 222.1 %reduce-scatter.32.cloned.1.call-start = ((), (), s32[]{:S(2)}) async-start(), calls=%async_computation.31 | async-start | bytes 7077888 | tf_op jit(solution)/shard_map/reduce_scatter | solution.py:400
  1964.0 126.2 %reduce-scatter.28.cloned.1.call-start = ((), (), s32[]{:S(2)}) async-start(), calls=%async_computation.27 | async-start | bytes 7077888 | tf_op jit(solution)/shard_map/reduce_scatter | solution.py:398
  1998.0 157.9 %reduce-scatter.30.cloned.1.call-start = ((), (), s32[]{:S(2)}) async-start(), calls=%async_computation.29 | async-start | bytes 7077888 | tf_op jit(solution)/shard_map/reduce_scatter | solution.py:399
  2011.0 384.7 %reduce-scatter.16.cloned.1.call-start = ((), (), s32[]{:S(2)}) async-start(), calls=%async_computation.16 | async-start | bytes 17694720 | tf_op jit(solution)/shard_map/reduce_scatter | solution.py:267
  2043.7 387.8 %all-gather.32.cloned.1.call-start = ((), (), s32[]{:S(2)}) async-start(), calls=%async_computation.32 | async-start | bytes 3538944 | tf_op jit(solution)/shard_map/all_gather | solution.py:421
  2045.8 420.7 %all-gather.28.cloned.1.call-start = ((), (), s32[]{:S(2)}) async-start(), calls=%async_computation.28 | async-start | bytes 3538944 | tf_op jit(solution)/shard_map/all_gather | solution.py:415
  2092.1 303.5 %copy-start.509 = (f32[1536]{0:T(1024)S(1)}, f32[1536]{0:T(1024)}, u32[]{:S(2)}) copy-start(f32[1536]{0:T(1024)} %param.26) | copy-start | bytes 18436
  2092.1 303.5 %copy-start.513 = (f32[576]{0:T(1024)S(1)}, f32[576]{0:T(1024)}, u32[]{:S(2)}) copy-start(f32[576]{0:T(1024)} %copy-done.512) | copy-start | bytes 6916
  2092.2 409.1 %all-gather.30.cloned.1.call-start = ((), (), s32[]{:S(2)}) async-start(), calls=%async_computation.30 | async-start | bytes 3538944 | tf_op jit(solution)/shard_map/all_gather | solution.py:418
  2157.9 242.5 %copy-start.519 = (f32[576]{0:T(1024)S(1)}, f32[576]{0:T(1024)}, u32[]{:S(2)}) copy-start(f32[576]{0:T(1024)} %get-tuple-element.1478) | copy-start | bytes 6916
  2157.9 473.9 %all-gather.18.cloned.1.call-start = ((), (), s32[]{:S(2)}) async-start(), calls=%async_computation.17 | async-start | bytes 8847360 | tf_op jit(solution)/shard_map/all_gather | solution.py:281
  2406.2 1611.3 %reduce-scatter.24.cloned.1.call-start = ((), (), s32[]{:S(2)}) async-start(), calls=%async_computation.23 | async-start | bytes 2654208 | tf_op jit(solution)/shard_map/reduce_scatter | solution.py:396
  2471.8 160.0 %copy-start.81 = (bf16[1536,384]{1,0:T(8,128)(2,1)S(1)}, bf16[1536,384]{1,0:T(8,128)(2,1)}, u32[]{:S(2)}) copy-start(bf16[1536,384]{1,0:T(8,128)(2,1)} %param.25) | copy-start | bytes 3538948
  2471.8 160.0 %copy-start.276 = (f32[2304,4]{0,1:T(4,128)S(1)}, f32[2304,4]{0,1:T(4,128)}, u32[]{:S(2)}) copy-start(f32[2304,4]{0,1:T(4,128)} %copy-done.275) | copy-start | bytes 110596
  2471.8 160.0 %copy-start.309 = (f32[2304,4]{0,1:T(4,128)S(1)}, f32[2304,4]{0,1:T(4,128)}, u32[]{:S(2)}) copy-start(f32[2304,4]{0,1:T(4,128)} %copy-done.308) | copy-start | bytes 110596
  2662.3 30.0 copy-start.69
  2999.9 44.5 copy-start.100
  2999.9 44.5 copy-start.383
  2999.9 44.5 copy-start.397
  3054.9 43.5 copy-start.104
  3244.2 926.0 %reduce-scatter.26.cloned.1.call-start = ((), (), s32[]{:S(2)}) async-start(), calls=%async_computation.25 | async-start | bytes 2654208 | tf_op jit(solution)/shard_map/reduce_scatter | solution.py:397
  3373.6 937.7 %reduce-scatter.22.cloned.1.call-start = ((), (), s32[]{:S(2)}) async-start(), calls=%async_computation.21 | async-start | bytes 2654208 | tf_op jit(solution)/shard_map/reduce_scatter | solution.py:395
  3594.0 828.2 %reduce-scatter.20.cloned.1.call-start = ((), (), s32[]{:S(2)}) async-start(), calls=%async_computation.19 | async-start | bytes 2654208 | tf_op jit(solution)/shard_map/reduce_scatter | solution.py:394
  3728.6 1013.0 %all-gather.24.cloned.1.call-start = ((), (), s32[]{:S(2)}) async-start(), calls=%async_computation.24 | async-start | bytes 1327104 | tf_op jit(solution)/shard_map/all_gather | solution.py:409
  4019.1 725.3 %all-gather.26.cloned.1.call-start = ((), (), s32[]{:S(2)}) async-start(), calls=%async_computation.26 | async-start | bytes 1327104 | tf_op jit(solution)/shard_map/all_gather | solution.py:412
  4171.9 575.4 %all-gather.22.cloned.1.call-start = ((), (), s32[]{:S(2)}) async-start(), calls=%async_computation.22 | async-start | bytes 1327104 | tf_op jit(solution)/shard_map/all_gather | solution.py:406
  4313.0 437.2 %all-gather.20.cloned.1.call-start = ((), (), s32[]{:S(2)}) async-start(), calls=%async_computation.20 | async-start | bytes 1327104 | tf_op jit(solution)/shard_map/all_gather | solution.py:403
  4423.8 329.3 %reduce-scatter.18.cloned.1.call-start = ((), (), s32[]{:S(2)}) async-start(), calls=%async_computation.18 | async-start | bytes 8847360 | tf_op jit(solution)/shard_map/reduce_scatter | solution.py:355
  4498.3 26.0 copy-start.672
  4498.3 26.6 copy-start.35
  4547.4 25.5 copy-start.664
  4547.4 26.1 copy-start.663
  4624.7 25.6 copy-start.654
  4624.7 26.3 copy-start.5
  4624.7 26.3 copy-start.44
  4753.1 46.7 copy-start.518
  (663 other events, 3634.4 us)
Sparse Core Ops, SparseCore 0:
  12.3 130.9 all-gather.11
  1169.8 235.4 reduce-scatter.11
  1411.8 129.2 all-gather.13
  1578.9 235.5 reduce-scatter.13
  1821.8 129.2 all-gather.15
  1964.1 59.9 reduce-scatter.31
  2028.4 61.7 reduce-scatter.27
  2094.2 61.7 reduce-scatter.29
  2158.4 237.2 reduce-scatter.15
  2398.1 33.3 all-gather.31
  2434.1 32.3 all-gather.27
  2469.0 32.3 all-gather.29
  2503.5 128.1 all-gather.17
  3244.4 40.6 reduce-scatter.23
  3373.8 40.6 reduce-scatter.25
  3594.1 40.5 reduce-scatter.21
  3728.7 40.5 reduce-scatter.19
  4019.3 22.0 all-gather.23
  4172.1 22.0 all-gather.25
  4313.1 22.1 all-gather.21
  4423.9 22.0 all-gather.19
  4452.5 121.4 reduce-scatter.17
where the time goes:
time: 4850 us; the launch traced here: 4810 us
  other arithmetic  1550 us (32%)
  local copies, waits for them, and re-layouts  1460 us (30%)
  waiting for transfers between devices  1390 us (29%)
  matrix products  354 us (7%)
    another operation x1072, local copies, waits for them, and re-layouts, attend_backward(): d_kernel = jnp.stack(kernel_grads, axis=-1).reshape(conv_w.shape)  815 us
    reduce_max x16, other arithmetic, attend_forward(): row_top = jnp.max(logits, axis=-1, keepdims=True)  541 us
    reduce_sum x72, other arithmetic, attend_backward(): kernel_grads.append(jnp.sum(d_conv_out * window, axis=(1, 2)))  376 us
    convert_element_type x16, other arithmetic, attend_backward(): d_scores = jnp.where(allowed[None], d_pre, 0.0).astype(jnp.bfloat16)  298 us
    reduce_scatter x1, waiting for transfers between devices, local(): lax.psum_scatter(jnp.einsum('rf,df->rd', d_gate, w_gate, preferred_elemen...  238 us
    reduce_scatter x1, waiting for transfers between devices, local(): lax.psum_scatter(jnp.einsum('rk,dk->rd', row_block, w_out, preferred_elem...  236 us
    reduce_scatter x1, waiting for transfers between devices, local(): lax.psum_scatter(jnp.einsum('rf,df->rd', row_block, w_down, preferred_ele...  234 us
    all_gather x1, waiting for transfers between devices, local(): d_all = lax.all_gather(d_low, 'tensor', axis=0, tiled=True)  129 us
  transfers between devices with their start and end apart: 22, of which 12 were waited for; matrix products, arithmetic and copies ran while one was open for 34% of the time, Pallas kernels for 0%

commit v1 on v0

v1 whole, which is shorter than its diff:
```python
import math
import jax
import jax.numpy as jnp
from jax import lax
from jax.experimental import pallas as pl
from jax.experimental.pallas import tpu as pltpu
from jax.sharding import PartitionSpec as P

HD = 96
CQ = 6
CK = 11
TRUNK = 192
SEG = 32
TREE = 576
WIN = 256
FAM = 96
EXT = 680
F32 = jnp.float32
BF16 = jnp.bfloat16


def segments():
    rows = [(0, TRUNK, 0, 0, -1)]
    for b in range(4):
        base, ext = TRUNK + FAM * b, 200 + 120 * b
        rows.append((TRUNK + SEG * b, SEG, base, ext, TRUNK - 8))
        for c in range(2):
            rows.append((320 + 64 * b + SEG * c, SEG, base + SEG * (c + 1), ext + 40 * (c + 1), TRUNK + SEG * b + SEG - 8))
    return rows


SEGS = segments()


def nn(a, b):
    return lax.dot_general(a, b, (((1,), (0,)), ((), ())), preferred_element_type=F32)


def nt(a, b):
    return lax.dot_general(a, b, (((1,), (1,)), ((), ())), preferred_element_type=F32)


def tn(a, b):
    return lax.dot_general(a, b, (((0,), (0,)), ((), ())), preferred_element_type=F32)


def head_masks(g):
    lane = lax.broadcasted_iota(jnp.int32, (1, WIN), 1)
    first = 64 * g
    m0 = (lane >= first) & (lane < first + HD)
    m1 = (lane >= first + HD) & (lane < first + 2 * HD)
    return m0, m1, lane >= first


def fill_distance(jj_ref, dist_ref):
    for index, (_, size, row, _, _) in enumerate(SEGS):
        start = 0 if index == 0 else (TRUNK if (index - 1) % 3 == 0 else TRUNK + SEG)
        pos = lax.broadcasted_iota(jnp.int32, (size, WIN), 0) + start
        dist_ref[row : row + size] = pos - jj_ref[index : index + 1, :]


def path_rows(ref, b, c, column):
    if b is None:
        parts = [ref[0:TRUNK, pl.ds(column, WIN)], ref[TRUNK : TRUNK + SEG, pl.ds(column, WIN)], ref[320 : 320 + SEG, pl.ds(column, WIN)]]
    else:
        parts = [
            ref[0:TRUNK, pl.ds(column, WIN)],
            ref[pl.ds(pl.multiple_of(TRUNK + SEG * b, SEG), SEG), pl.ds(column, WIN)],
            ref[pl.ds(pl.multiple_of(320 + 64 * b + SEG * c, SEG), SEG), pl.ds(column, WIN)],
        ]
    return jnp.concatenate(parts, axis=0)


def fam_rows(b, c):
    base = TRUNK + FAM * b
    return (pl.ds(pl.multiple_of(base, 32), 64), 64) if c == 0 else (pl.ds(pl.multiple_of(base + 64, 32), SEG), SEG)


def group_norm(ho, m0, m1):
    def stat(v):
        s0 = jnp.sum(jnp.where(m0, v, 0.0), axis=-1, keepdims=True) * (1.0 / HD)
        s1 = jnp.sum(jnp.where(m1, v, 0.0), axis=-1, keepdims=True) * (1.0 / HD)
        return jnp.where(m0, s0, s1)

    centered = jnp.where(m0 | m1, ho - stat(ho), 0.0)
    inv = lax.rsqrt(stat(centered * centered) + 1e-05)
    return centered * inv, inv, stat


def fwd_kernel(mix_ref, qkv_ref, t_ref, gn_ref, jj_ref, nh_ref, att_ref, pre_ref, qs_ref, ho_ref, dist_ref, qx_ref, mx_ref):
    g = pl.program_id(1)
    w0 = pl.multiple_of(g * 128, 128)
    m0, m1, from_first = head_masks(g)
    m0f, m1f = m0.astype(F32), m1.astype(F32)
    fill_distance(jj_ref, dist_ref)
    qx_ref[0:8] = jnp.zeros((8, WIN), F32)
    for token, size, _, ext, parent in SEGS:
        if parent >= 0:
            low = qkv_ref[parent - 8 : parent + 8, pl.ds(w0, WIN)].astype(F32)
            qx_ref[ext : ext + 8] = low[8:16]
        qx_ref[ext + 8 : ext + 8 + size] = qkv_ref[token : token + size, pl.ds(w0, WIN)].astype(F32)
    for a in range(CQ):
        for _, size, row, ext, _ in SEGS:
            part = qx_ref[ext + 8 - a : ext + 8 - a + size]
            qs_ref[0, a, row : row + size] = (part * m0f).astype(BF16)
            qs_ref[1, a, row : row + size] = (part * m1f).astype(BF16)
    k0, v0 = w0 + 384, w0 + 768
    k_trunk = path_rows(qkv_ref, None, 0, k0)

    def trunk_scores(a, carry):
        scores = nt(qs_ref[:, a, 0:TRUNK].reshape(2 * TRUNK, WIN), k_trunk).reshape(2, TRUNK, WIN)
        kept = dist_ref[0:TRUNK] >= a
        for e in range(2):
            pre_ref[e, 0:TRUNK, pl.ds(pl.multiple_of(a * WIN, WIN), WIN)] = jnp.where(kept, scores[e], 0.0).astype(BF16)
        return carry

    lax.fori_loop(0, CQ, trunk_scores, 0)

    def fam_scores(b, carry):
        for c in range(2):
            rows, size = fam_rows(b, c)
            keys = path_rows(qkv_ref, b, c, k0)
            scores = nt(qs_ref[:, :, rows].reshape(2 * CQ * size, WIN), keys).reshape(2, CQ, size, WIN)
            dist = dist_ref[rows]
            for a in range(CQ):
                kept = dist >= a
                for e in range(2):
                    pre_ref[e, rows, a * WIN : (a + 1) * WIN] = jnp.where(kept, scores[e, a], 0.0).astype(BF16)
        return carry

    lax.fori_loop(0, 4, fam_scores, 0)
    for e in range(2):
        conv = nn(pre_ref[e], t_ref[e])
        logits = jnp.where(dist_ref[...] >= 0, conv, -1e30)
        shifted = jnp.exp(logits - jnp.max(logits, axis=-1, keepdims=True))
        att_ref[e] = shifted / jnp.sum(shifted, axis=-1, keepdims=True)
    for c in range(2):
        mx_ref[c] = (mix_ref[4 * g + 2 * c] * att_ref[0] + mix_ref[4 * g + 2 * c + 1] * att_ref[1]).astype(BF16)

    def put_out(rows, size, values):
        out = nn(mx_ref[:, rows].reshape(2 * size, WIN), values).reshape(2, size, WIN)
        ho_ref[rows] = jnp.where(m0, out[0], jnp.where(m1, out[1], 0.0))

    put_out(pl.ds(0, TRUNK), TRUNK, path_rows(qkv_ref, None, 0, v0))

    def fam_out(b, carry):
        for c in range(2):
            rows, size = fam_rows(b, c)
            put_out(rows, size, path_rows(qkv_ref, b, c, v0))
        return carry

    lax.fori_loop(0, 4, fam_out, 0)
    gain = gn_ref[0:1, pl.ds(w0, WIN)]
    for token, size, row, _, _ in SEGS:
        unit, _, _ = group_norm(ho_ref[row : row + size], m0, m1)
        old = nh_ref[token : token + size, pl.ds(w0, WIN)].astype(F32)
        nh_ref[token : token + size, pl.ds(w0, WIN)] = jnp.where(from_first, unit * gain, old).astype(BF16)


def bwd_kernel(
    mix_ref, qkv_ref, t_ref, gn_ref, jj_ref, dn_ref, att_ref, pre_ref, qs_ref, ho_ref,
    dqkv_ref, ggn_ref, gmix_ref, gconv_ref,
    dist_ref, dh_ref, mx_ref, dm_ref, dc_ref, es_ref, dqx_ref, dk_ref, dv_ref,
):
    t, g = pl.program_id(0), pl.program_id(1)
    w0 = pl.multiple_of(g * 128, 128)
    m0, m1, from_first = head_masks(g)
    both = m0 | m1
    fill_distance(jj_ref, dist_ref)
    gain = gn_ref[0:1, pl.ds(w0, WIN)]
    gn_sum = jnp.zeros((1, WIN), F32)
    for token, size, row, _, _ in SEGS:
        unit, inv, stat = group_norm(ho_ref[row : row + size], m0, m1)
        dn = jnp.where(both, dn_ref[token : token + size, pl.ds(w0, WIN)].astype(F32), 0.0)
        gn_sum = gn_sum + jnp.sum(dn * unit, axis=0, keepdims=True)
        scaled = dn * gain
        d_head = inv * (scaled - stat(scaled) - unit * stat(scaled * unit))
        dh_ref[0, row : row + size] = jnp.where(m0, d_head, 0.0).astype(BF16)
        dh_ref[1, row : row + size] = jnp.where(m1, d_head, 0.0).astype(BF16)

    @pl.when((t == 0) & (g == 0))
    def _():
        ggn_ref[...] = jnp.zeros_like(ggn_ref)

    ggn_ref[0:1, pl.ds(w0, WIN)] += gn_sum
    k0, v0 = w0 + 384, w0 + 768
    for c in range(2):
        mx_ref[c] = (mix_ref[4 * g + 2 * c] * att_ref[0] + mix_ref[4 * g + 2 * c + 1] * att_ref[1]).astype(BF16)

    def add_keys(acc_ref, b, c, grads):
        acc_ref[0:TRUNK] += grads[0:TRUNK]
        branch = pl.ds(pl.multiple_of(TRUNK + SEG * b, SEG), SEG)
        if c == 0:
            acc_ref[branch] = grads[TRUNK : TRUNK + SEG]
        else:
            acc_ref[branch] += grads[TRUNK : TRUNK + SEG]
        acc_ref[pl.ds(pl.multiple_of(320 + 64 * b + SEG * c, SEG), SEG)] = grads[TRUNK + SEG :]

    def value_part(rows, size, values):
        heads = dh_ref[:, rows].reshape(2 * size, WIN)
        dm_ref[:, rows] = nt(heads, values).reshape(2, size, WIN)
        return tn(mx_ref[:, rows].reshape(2 * size, WIN), heads)

    dv_ref[0:TRUNK] = value_part(pl.ds(0, TRUNK), TRUNK, path_rows(qkv_ref, None, 0, v0))[0:TRUNK]

    def fam_values(b, carry):
        for c in range(2):
            rows, size = fam_rows(b, c)
            add_keys(dv_ref, b, c, value_part(rows, size, path_rows(qkv_ref, b, c, v0)))
        return carry

    lax.fori_loop(0, 4, fam_values, 0)

    def soft_part(block, sums):
        rows = pl.ds(pl.multiple_of(block * FAM, 32), FAM)
        dm = [dm_ref[c, rows] for c in range(2)]
        att = [att_ref[e, rows] for e in range(2)]
        out = []
        for e in range(2):
            d_att = mix_ref[4 * g + e] * dm[0] + mix_ref[4 * g + 2 + e] * dm[1]
            d_conv = att[e] * (d_att - jnp.sum(d_att * att[e], axis=-1, keepdims=True))
            dc_ref[e, rows] = d_conv.astype(BF16)
        for c in range(2):
            for e in range(2):
                out.append(sums[2 * c + e] + jnp.sum(dm[c] * att[e], axis=0, keepdims=True))
        return tuple(out)

    mix_sums = lax.fori_loop(0, 6, soft_part, tuple(jnp.zeros((1, WIN), F32) for _ in range(4)))
    gmix_ref[...] = jnp.zeros_like(gmix_ref)
    gconv_ref[...] = jnp.zeros_like(gconv_ref)
    for index in range(4):
        gmix_ref[index : index + 1] = mix_sums[index]
    mirror = lax.broadcasted_iota(jnp.int32, (WIN, WIN), 0) + lax.broadcasted_iota(jnp.int32, (WIN, WIN), 1) - (WIN - 1)
    band = jnp.abs(mirror) <= CK // 2
    flip = jnp.where(mirror == 0, 1.0, 0.0).astype(BF16)
    for e in range(2):
        flipped = nn(dc_ref[e], flip).astype(BF16)
        for a in range(CQ):
            cols = slice(a * WIN, (a + 1) * WIN)
            products = jnp.where(band, tn(flipped, pre_ref[e, :, cols]), 0.0)
            rolled = pltpu.roll(products, 24, 1, stride=1, stride_axis=0)
            gconv_ref[e, a : a + 1] = jnp.sum(rolled, axis=0, keepdims=True)
            grads = nt(dc_ref[e], t_ref[e, cols, :])
            es_ref[e, a] = jnp.where(dist_ref[...] >= a, grads, 0.0).astype(BF16)

    def score_part(rows, size, keys):
        grads = es_ref[:, :, rows].reshape(2 * CQ * size, WIN)
        back = nn(grads, keys).reshape(2, CQ, size, WIN)
        d_query = [jnp.where(m0, back[0, a], jnp.where(m1, back[1, a], 0.0)) for a in range(CQ)]
        return d_query, tn(grads, qs_ref[:, :, rows].reshape(2 * CQ * size, WIN))

    def shifted_sum(parts, start, size):
        zeros = jnp.zeros((8, WIN), F32)
        total = None
        for a in range(CQ):
            padded = jnp.concatenate([zeros, parts[a][start : start + size]], axis=0)
            if a:
                padded = pltpu.roll(padded, size + 8 - a, 0)
            total = padded if total is None else total + padded
        return total

    d_query, d_keys = score_part(pl.ds(0, TRUNK), TRUNK, path_rows(qkv_ref, None, 0, k0))
    dqx_ref[0:200] = shifted_sum(d_query, 0, TRUNK)
    dk_ref[0:TRUNK] = d_keys[0:TRUNK]

    def fam_scores(b, carry):
        ext = 200 + 120 * b
        for c in range(2):
            rows, size = fam_rows(b, c)
            d_query, d_keys = score_part(rows, size, path_rows(qkv_ref, b, c, k0))
            add_keys(dk_ref, b, c, d_keys)
            if c == 0:
                dqx_ref[pl.ds(pl.multiple_of(ext, 8), 40)] = shifted_sum(d_query, 0, SEG)
                dqx_ref[pl.ds(pl.multiple_of(ext + 40, 8), 40)] = shifted_sum(d_query, SEG, SEG)
            else:
                dqx_ref[pl.ds(pl.multiple_of(ext + 80, 8), 40)] = shifted_sum(d_query, 0, SEG)
        return carry

    lax.fori_loop(0, 4, fam_scores, 0)
    for b in range(4):
        ext = 200 + 120 * b
        dqx_ref[192:200] += dqx_ref[ext : ext + 8]
        dqx_ref[ext + 32 : ext + 40] += dqx_ref[ext + 40 : ext + 48] + dqx_ref[ext + 80 : ext + 88]

    def put(token, size, column, value):
        old = dqkv_ref[token : token + size, pl.ds(column, WIN)].astype(F32)
        dqkv_ref[token : token + size, pl.ds(column, WIN)] = jnp.where(from_first, value, old).astype(BF16)

    for token, size, _, ext, _ in SEGS:
        put(token, size, w0, dqx_ref[ext + 8 : ext + 8 + size])
        put(token, size, k0, dk_ref[token : token + size])
        put(token, size, v0, dv_ref[token : token + size])


def by_tree(shape, last):
    return pl.BlockSpec(shape, lambda t, g: (t,) + (0,) * last)


def by_group(shape):
    tail = (0,) * (len(shape) - 2)
    return pl.BlockSpec((None, None) + shape[2:], lambda t, g: (t, g) + tail)


def common_specs():
    return [
        pl.BlockSpec(memory_space=pltpu.SMEM),
        pl.BlockSpec((TREE, 1152), lambda t, g: (t, 0)),
        pl.BlockSpec((None, 2, CQ * WIN, WIN), lambda t, g: (g, 0, 0, 0)),
        pl.BlockSpec((8, 384), lambda t, g: (0, 0)),
        pl.BlockSpec((None, 16, WIN), lambda t, g: (t, 0, 0)),
    ]


PARAMS = dict(vmem_limit_bytes=60 * 1024 * 1024, dimension_semantics=("arbitrary", "arbitrary"))


def saved_shapes(trees):
    return [(trees, 2, 2, TREE, WIN), (trees, 2, 2, TREE, CQ * WIN), (trees, 2, 2, CQ, TREE, WIN), (trees, 2, TREE, WIN)]


def attention_forward(mix, qkv, toeplitz, gains, jj):
    trees = qkv.shape[0] // TREE
    shapes = saved_shapes(trees)
    kinds = (F32, BF16, BF16, F32)
    return pl.pallas_call(
        fwd_kernel,
        grid=(trees, 2),
        in_specs=common_specs(),
        out_specs=[pl.BlockSpec((TREE, 384), lambda t, g: (t, 0))] + [by_group(s) for s in shapes],
        out_shape=[jax.ShapeDtypeStruct((trees * TREE, 384), BF16)] + [jax.ShapeDtypeStruct(s, k) for s, k in zip(shapes, kinds)],
        scratch_shapes=[pltpu.VMEM((TREE, WIN), jnp.int32), pltpu.VMEM((EXT, WIN), F32), pltpu.VMEM((2, TREE, WIN), BF16)],
        compiler_params=pltpu.CompilerParams(**PARAMS),
        cost_estimate=pl.CostEstimate(flops=40_000_000_000, bytes_accessed=60_000_000, transcendentals=0),
    )(mix, qkv, toeplitz, gains, jj)


def attention_backward(mix, qkv, toeplitz, gains, jj, d_normed, saved):
    trees = qkv.shape[0] // TREE
    shapes = saved_shapes(trees)
    return pl.pallas_call(
        bwd_kernel,
        grid=(trees, 2),
        in_specs=common_specs() + [pl.BlockSpec((TREE, 384), lambda t, g: (t, 0))] + [by_group(s) for s in shapes],
        out_specs=[
            pl.BlockSpec((TREE, 1152), lambda t, g: (t, 0)),
            pl.BlockSpec((8, 384), lambda t, g: (0, 0)),
            by_group((trees, 2, 8, WIN)),
            by_group((trees, 2, 2, 8, WIN)),
        ],
        out_shape=[
            jax.ShapeDtypeStruct((trees * TREE, 1152), BF16),
            jax.ShapeDtypeStruct((8, 384), F32),
            jax.ShapeDtypeStruct((trees, 2, 8, WIN), F32),
            jax.ShapeDtypeStruct((trees, 2, 2, 8, WIN), F32),
        ],
        scratch_shapes=[
            pltpu.VMEM((TREE, WIN), jnp.int32),
            pltpu.VMEM((2, TREE, WIN), BF16),
            pltpu.VMEM((2, TREE, WIN), BF16),
            pltpu.VMEM((2, TREE, WIN), F32),
            pltpu.VMEM((2, TREE, WIN), BF16),
            pltpu.VMEM((2, CQ, TREE, WIN), BF16),
            pltpu.VMEM((EXT, WIN), F32),
            pltpu.VMEM((TREE, WIN), F32),
            pltpu.VMEM((TREE, WIN), F32),
        ],
        compiler_params=pltpu.CompilerParams(**PARAMS),
        cost_estimate=pl.CostEstimate(flops=80_000_000_000, bytes_accessed=60_000_000, transcendentals=0),
    )(mix, qkv, toeplitz, gains, jj, d_normed, *saved)


def toeplitz_of(conv_w):
    heads = conv_w.shape[0]
    offset = lax.broadcasted_iota(jnp.int32, (WIN, WIN), 1) - lax.broadcasted_iota(jnp.int32, (WIN, WIN), 0) + CK // 2
    total = jnp.zeros((heads, CQ, WIN, WIN), F32)
    for b in range(CK):
        total = total + jnp.where(offset == b, 1.0, 0.0) * (conv_w[:, :, b] * (1.0 / math.sqrt(HD)))[:, :, None, None]
    return total.astype(BF16).reshape(heads // 2, 2, CQ * WIN, WIN)


def key_positions(valid):
    trees = valid.shape[0] // TREE
    valid = valid.reshape(trees, TREE)
    far = jnp.int32(1 << 20)

    def places(part, start):
        return jnp.where(part > 0, lax.broadcasted_iota(jnp.int32, part.shape, 1) + start, far)

    trunk = places(valid[:, :TRUNK], 0)
    empty = jnp.full((trees, SEG), far, jnp.int32)
    rows = [jnp.concatenate([trunk, empty, empty], axis=1)]
    for b in range(4):
        branch = places(valid[:, TRUNK + SEG * b : TRUNK + SEG * (b + 1)], TRUNK)
        rows.append(jnp.concatenate([trunk, branch, empty], axis=1))
        for c in range(2):
            first = 320 + 64 * b + SEG * c
            leaf = places(valid[:, first : first + SEG], TRUNK + SEG)
            rows.append(jnp.concatenate([trunk, branch, leaf], axis=1))
    rows += [jnp.zeros((trees, WIN), jnp.int32)] * 3
    return jnp.stack(rows, axis=1)


def conv_grads(gconv):
    lanes = gconv[..., :CQ, 18:29][..., ::-1] * (1.0 / math.sqrt(HD))
    return jnp.sum(lanes, axis=0).reshape(-1, CQ, CK)


def mix_grads(gmix):
    return jnp.sum(gmix[:, :, :4], axis=(0, 3)).reshape(-1, 2, 2)


BACK = (0, 2, 1, 3)


def rows_dot(lhs, rhs):
    return tn(lhs, rhs).astype(BF16)


def unfused(value):
    return lax.optimization_barrier(value)


def make_local(planes, tensors):
    every = ("plane", "core", "tensor")
    sides = [(c, z) for c in range(2) for z in range(tensors)]

    def spot(q, c, z):
        return (q * 2 + c) * tensors + z

    def is_home(c, z):
        return z // 2 == c

    far_pairs = [(spot(q, c, z), spot(q, 1 - c, z ^ 2)) for q in range(planes) for c, z in sides if not is_home(c, z)]
    near_pairs = [
        (spot(q, c, z), spot(q, c, z ^ 1) if is_home(c, z) else spot(q, 1 - c, z ^ 3)) for q in range(planes) for c, z in sides
    ]

    def plane_pairs(flip, away_only):
        return [(spot(q, c, z), spot(q ^ flip, c, z)) for q in range(planes) for c, z in sides if not (away_only and is_home(c, z))]

    def over_plane(value, flip, away_only=False):
        return lax.ppermute(value, every, plane_pairs(flip, away_only))

    def over_core(value):
        return lax.ppermute(value, "core", [(0, 1), (1, 0)])

    def first_from(value):
        return lax.ppermute(value, every, far_pairs)

    def second_from(value):
        return lax.ppermute(value, every, near_pairs)

    square = planes == 4

    def local(
        tokens, teacher, valid_mask, norm1_gain, w_query, w_key, w_value, conv_weight, head_mix, gn_gain, w_out, norm2_gain,
        w_gate, w_up, w_down,
    ):
        q, c, z = lax.axis_index("plane"), lax.axis_index("core"), lax.axis_index("tensor")
        own_rows, width = tokens.shape
        home = (z // 2) == c
        chunk = width // planes
        heads = conv_weight.shape[0]
        wide = w_query.shape[1]

        def place(k):
            return jnp.bitwise_xor(q, k)

        def cut(value, index, axis):
            return lax.dynamic_slice_in_dim(value, index * chunk, chunk, axis)

        def turn(value, axis):
            if not square:
                return value
            return jnp.concatenate([cut(value, place(k), axis) for k in BACK], axis=axis)

        def turn_back(value, axis):
            if not square:
                return value
            parts = []
            for j in range(4):
                k = place(j)
                parts.append(cut(value, (k % 2) * 2 + k // 2, axis))
            return jnp.concatenate(parts, axis=axis)

        def spread(piece, away_only):
            if not square:
                return lax.all_gather(piece, "plane", axis=0, tiled=True)
            half = piece.shape[0] // 2
            by_x = over_plane(piece, 1, away_only)
            by_y = over_plane(piece, 2, away_only)
            top = over_plane(by_x[:half], 2, away_only)
            low = over_plane(by_y[half:], 1, away_only)
            return jnp.concatenate([piece, by_y, by_x, top, low], axis=0)

        def collect(parts):
            piece = jnp.concatenate([cut(p, q, 0) for p in parts], axis=1)
            second = spread(second_from(piece), False)
            first = spread(first_from(piece), True)
            mine = turn(jnp.concatenate(parts, axis=1), 0)
            return jnp.where(home, mine, first), second

        def reduce(lhs, rhs_first, rhs_second):
            if square:
                order = [lhs[:, k * chunk : (k + 1) * chunk] for k in range(4)]
                other = jnp.concatenate([order[1], order[3]], axis=1)
                keep = jnp.concatenate([order[0], order[2]], axis=1)
                recv_a = over_plane(rows_dot(lhs[:, 2 * chunk :], rhs_first), 1)
                recv_b = over_plane(rows_dot(other, rhs_second), 2)
                top_a = unfused(rows_dot(lhs[:, : 2 * chunk], rhs_first))
                top_b = unfused(rows_dot(keep, rhs_second))
                sum_a = top_a.astype(F32) + recv_a.astype(F32)
                sum_b = top_b.astype(F32) + recv_b.astype(F32)
                last_a = over_plane(sum_a[chunk:].astype(BF16), 2)
                last_b = over_plane(sum_b[chunk:].astype(BF16), 1)
                part_a = (sum_a[:chunk] + last_a.astype(F32)).astype(BF16)
                part_b = (sum_b[:chunk] + last_b.astype(F32)).astype(BF16)
            else:
                part_a = lax.psum_scatter(rows_dot(lhs, rhs_first), "plane", scatter_dimension=0, tiled=True)
                part_b = lax.psum_scatter(rows_dot(lhs, rhs_second), "plane", scatter_dimension=0, tiled=True)
            from_a = first_from(part_a)
            from_b = second_from(part_b)
            here = (jnp.where(home, part_a, from_a).astype(F32) + from_b.astype(F32)).astype(BF16)
            there = over_core(here)
            total = (here.astype(F32) + there.astype(F32)).astype(BF16)
            if not square:
                return lax.all_gather(total, "plane", axis=0, tiled=True).astype(F32)
            half = chunk // 2
            mine = spread(lax.dynamic_slice_in_dim(total, c * half, half, 0), False)
            theirs = over_core(mine)
            low = jnp.where(c == 0, mine, theirs).reshape(4, half, -1)
            high = jnp.where(c == 0, theirs, mine).reshape(4, half, -1)
            whole = jnp.concatenate([low, high], axis=1).reshape(width, -1)
            return turn_back(whole, 0).astype(F32)

        small = jnp.concatenate([conv_weight.reshape(-1), head_mix.reshape(-1), gn_gain.reshape(-1)])
        small_first = jnp.where(home, small, first_from(small))
        small_second = second_from(small)
        conv_size, mix_size = conv_weight.size, head_mix.size

        tokens = turn(tokens, 1)
        teacher = turn(teacher, 1)
        gain_one = turn(norm1_gain, 0)
        gain_two = turn(norm2_gain, 0)
        own_valid = lax.dynamic_slice_in_dim(valid_mask, z * own_rows, own_rows, 0)
        jj = key_positions(jnp.concatenate([own_valid, over_core(own_valid)]))

        qkv_weights = collect([w_query, w_key, w_value])
        out_weights = collect([w_out])
        gu_weights = collect([w_gate, w_up])
        down_weights = collect([w_down])

        def with_partner(value):
            return jnp.concatenate([value, over_core(value)], axis=0)

        def summed(lefts, rights):
            def half(rows):
                total = nt(lefts[0][rows], rights[0])
                return total + nt(lefts[1][rows], rights[1])

            sent = over_core(half(slice(own_rows, None)).astype(BF16))
            return half(slice(0, own_rows)) + sent.astype(F32)

        inputs = tokens.astype(F32)
        inv_one = lax.rsqrt(jnp.mean(inputs * inputs, axis=-1, keepdims=True) + 1e-06)
        normed_one = with_partner((inputs * inv_one * gain_one).astype(BF16))
        sides_small = []
        for vec in (small_first, small_second):
            conv = vec[:conv_size].reshape(conv_weight.shape)
            mix = vec[conv_size : conv_size + mix_size]
            gains = jnp.broadcast_to(vec[conv_size + mix_size :][None], (8, wide))
            sides_small.append((mix, toeplitz_of(conv), gains))
        qkv, heads_out, saved = [], [], []
        for (mix, toep, gains), weight in zip(sides_small, qkv_weights):
            projected = nn(normed_one, weight).astype(BF16)
            result = attention_forward(mix, projected, toep, gains, jj)
            qkv.append(projected)
            heads_out.append(result[0])
            saved.append(result[1:])
        hidden_in = inputs + summed(heads_out, out_weights)
        inv_two = lax.rsqrt(jnp.mean(hidden_in * hidden_in, axis=-1, keepdims=True) + 1e-06)
        normed_two = with_partner((hidden_in * inv_two * gain_two).astype(BF16))
        units = w_gate.shape[1]
        gates, ups, hiddens = [], [], []
        for weight in gu_weights:
            both = nn(normed_two, weight)
            gate, up = both[:, :units], both[:, units:]
            gates.append(gate.astype(BF16))
            ups.append(up.astype(BF16))
            hiddens.append((jax.nn.silu(gate) * up).astype(BF16))
        final_rows = hidden_in + summed(hiddens, down_weights)
        output = turn_back(final_rows.astype(BF16), 1)
        own_mask = own_valid.astype(F32)
        error = own_mask[:, None] * (final_rows - teacher.astype(F32))
        squared_sum = jnp.sum(error * error)
        count_sum = jnp.sum(own_mask)

        d_all = with_partner(error.astype(BF16))
        grad_down = reduce(d_all, hiddens[0], hiddens[1])
        d_gus = []
        for index, weight in enumerate(down_weights):
            d_hidden = nn(d_all, weight)
            gate, up = gates[index].astype(F32), ups[index].astype(F32)
            s = jax.nn.sigmoid(gate)
            d_gate = (d_hidden * up * s * (1.0 + gate * (1.0 - s))).astype(BF16)
            d_up = (d_hidden * gate * s).astype(BF16)
            d_gus.append(jnp.concatenate([d_gate, d_up], axis=1))
        grad_gu = reduce(normed_two, d_gus[0], d_gus[1])
        d_normed_two = summed(d_gus, gu_weights)
        scaled_two = d_normed_two * gain_two
        grad_gain_two = jnp.sum(d_normed_two * hidden_in * inv_two, axis=0)
        d_hidden_in = (
            error + inv_two * scaled_two - hidden_in * inv_two**3 * jnp.mean(scaled_two * hidden_in, axis=-1, keepdims=True)
        )
        d_attn = with_partner(d_hidden_in.astype(BF16))
        grad_out = reduce(d_attn, heads_out[0], heads_out[1])
        d_qkv, small_grads = [], []
        for index, (mix, toep, gains) in enumerate(sides_small):
            d_normed = nn(d_attn, out_weights[index])
            dqkv, ggn, gmix, gconv = attention_backward(mix, qkv[index], toep, gains, jj, d_normed, saved[index])
            d_qkv.append(dqkv)
            small_grads.append(jnp.concatenate([conv_grads(gconv).reshape(-1), mix_grads(gmix).reshape(-1), ggn[0]]))
        grad_qkv = reduce(normed_one, d_qkv[0], d_qkv[1])
        d_normed_one = summed(d_qkv, qkv_weights)
        scaled_one = d_normed_one * gain_one
        grad_gain_one = jnp.sum(d_normed_one * inputs * inv_one, axis=0)
        grad_input = (
            d_hidden_in + inv_one * scaled_one - inputs * inv_one**3 * jnp.mean(scaled_one * inputs, axis=-1, keepdims=True)
        )
        grad_input = turn_back(grad_input, 1)

        table = jnp.zeros((tensors, small.size), F32)
        table = lax.dynamic_update_slice(table, small_grads[0][None], (2 * c + z % 2, 0))
        table = lax.dynamic_update_slice(table, small_grads[1][None], (2 * c + 1 - z % 2, 0))
        packed = jnp.concatenate(
            [table.reshape(-1), turn_back(grad_gain_one, 0), turn_back(grad_gain_two, 0), squared_sum[None], count_sum[None]]
        )
        packed = lax.psum(packed, every)
        table_size = tensors * small.size
        small_sum = lax.dynamic_slice_in_dim(packed, z * small.size, small.size, 0)
        gain_slice = width // tensors
        gain_one_out = lax.dynamic_slice_in_dim(packed, table_size + z * gain_slice, gain_slice, 0)
        gain_two_out = lax.dynamic_slice_in_dim(packed, table_size + width + z * gain_slice, gain_slice, 0)
        loss = packed[-2] / (packed[-1] * width)
        return (
            output,
            loss,
            grad_input,
            gain_one_out,
            grad_qkv[:, :wide],
            grad_qkv[:, wide : 2 * wide],
            grad_qkv[:, 2 * wide :],
            small_sum[:conv_size].reshape(conv_weight.shape),
            small_sum[conv_size : conv_size + mix_size].reshape(head_mix.shape),
            small_sum[conv_size + mix_size :].reshape(gn_gain.shape),
            grad_out,
            gain_two_out,
            grad_gu[:, :units],
            grad_gu[:, units:],
            grad_down,
        )

    return local


def solution(mesh):
    tensors = mesh.shape["tensor"]
    planes = mesh.shape["dp"] // 2
    inner = jax.sharding.Mesh(mesh.devices.reshape(planes, 2, tensors), ("plane", "core", "tensor"))
    rows = P(("plane", "core", "tensor"), None)
    columns = P(None, "tensor")
    cube = P("tensor", None, None)
    return jax.shard_map(
        make_local(planes, tensors),
        mesh=inner,
        in_specs=(
            rows, rows, P(("plane", "core")), P(), columns, columns, columns, cube, cube, P("tensor", None), columns, P(),
            columns, columns, columns,
        ),
        out_specs=(
            rows, P(), rows, P("tensor"), columns, columns, columns, cube, cube, P("tensor", None), columns, P("tensor"),
            columns, columns, columns,
        ),
        check_vma=False,
    )
```

time: 4850 us -> 1240 us (0.26)
  other arithmetic: 1550 us -> 147 us
  local copies, waits for them, and re-layouts: 1460 us -> 143 us
  waiting for transfers between devices: 1390 us -> 248 us
  starting transfers between devices: 1.74 us -> 246 us
  Pallas kernels: 0 us -> 172 us
  matrix products: 354 us -> 195 us
    reduce_scatter x11 -> x0, waiting for transfers between devices: 816 us -> none  [the longest x1 238 us: local(): lax.psum_scatter(jnp.einsum('rf,df->rd', d_gate, w_gate, preferred_elemen...]
    another operation x1072 -> x20, local copies, waits for them, and re-layouts: 815 us -> 4.5 us  [the longest x2 1.82 us: local(): mix_grads(gmix).reshape(-1)]
    all_gather x11 -> x0, waiting for transfers between devices: 572 us -> none  [the longest x1 129 us: local(): d_all = lax.all_gather(d_low, 'tensor', axis=0, tiled=True)]
    reduce_max x16 -> x0, other arithmetic: 541 us -> none  [attend_forward(): row_top = jnp.max(logits, axis=-1, keepdims=True)]
    reduce_sum x156 -> x7, other arithmetic: 502 us -> 11.5 us  [the longest x1 3.82 us: local(): jnp.mean(scaled_one * inputs, axis=-1, keepdims=True)]
    convert_element_type x36 -> x25, other arithmetic: 363 us -> 60.8 us  [the longest x2 26.2 us: toeplitz_of(): return total.astype(BF16).reshape(heads // 2, 2, CQ * WIN, WIN)]
    ppermute x0 -> x99, waiting for transfers between devices: none -> 248 us  [the longest x64 232 us: over_plane(): return lax.ppermute(value, every, plane_pairs(flip, away_only))]
    ppermute x0 -> x99, starting transfers between devices: none -> 246 us  [the longest x17 154 us: over_core(): return lax.ppermute(value, 'core', [(0, 1), (1, 0)])]
  transfers between devices with their start and end apart: 22 -> 99, of which waited for: 12 -> 30; matrix products, arithmetic and copies ran while one was open for 34% -> 30% of each run, Pallas kernels for 0% -> 14%
where the time goes in v1:
time: 1240 us; the launch traced here: 1230 us
  waiting for transfers between devices  248 us (20%)
  starting transfers between devices  246 us (20%)
  matrix products  195 us (16%)
  Pallas kernels  172 us (14%)
  other arithmetic  147 us (12%)
  local copies, waits for them, and re-layouts  143 us (12%)
  blocking collectives  75.8 us (6%)
    ppermute x64, waiting for transfers between devices, over_plane(): return lax.ppermute(value, every, plane_pairs(flip, away_only))  232 us
    ppermute x17, starting transfers between devices, over_core(): return lax.ppermute(value, 'core', [(0, 1), (1, 0)])  154 us
    pallas_call x2, Pallas kernels, attention_backward(): pl.pallas_call(bwd_kernel, grid=(trees, 2), in_specs=common_specs() + [pl...  101 us
    psum x1, blocking collectives, local(): packed = lax.psum(packed, every)  75.8 us
    ppermute x64, starting transfers between devices, over_plane(): return lax.ppermute(value, every, plane_pairs(flip, away_only))  74.6 us
    pallas_call x2, Pallas kernels, attention_forward(): pl.pallas_call(fwd_kernel, grid=(trees, 2), in_specs=common_specs(), out_...  71.2 us
    dot_general x16, matrix products, tn(): lax.dot_general(a, b, (((0,), (0,)), ((), ())), preferred_element_type=F32)  68.9 us
    dot_general x8, matrix products, nn(): lax.dot_general(a, b, (((1,), (0,)), ((), ())), preferred_element_type=F32)  63.2 us
  transfers between devices with their start and end apart: 99, of which 30 were waited for; matrix products, arithmetic and copies ran while one was open for 30% of the time, Pallas kernels for 14%

profile of v1, /device:TPU:0, one launch (start us, length us, event | category | flops | bytes accessed | tf_op | source)
XLA Modules:
  0.0 1233.0 jit_solution(11526539559710720279)
XLA Ops:
  12.6 5.9 collective-permute-start.7
  61.8 11.5 add_convert_fusion.t_ref
  89.1 14.7 %add_convert_fusion.1.t_ref = bf16[2,2,1536,256]{3,2,1,0:T(8,128)(2,1)} fusion(f32[2,2,1536]{2,1,0:T(2,128)S(1)} %mul.1144, f32[1536,256]{1,0:T(8,128)S(1)} %bitcast.92, f32[2,2,1536]{2,1,0:T(2,128)S(1)} %mul.1135, f32[1536,256]{1,0:T(8,128)S(1)} %bitcast.94, f32[2,2,1536]{2,1,0:T(2,128)} %mul.1126, f32[1536,256]{1,0:T(8,128)} %bitcast.96, ...), kind=kLoop, calls=%fused_computation.72 | loop fusion | flops 34603008 | bytes 20717568 | tf_op jit(solution)/shard_map/convert_element_type | solution.py:378
  124.2 11.8 collective-permute-done.14
  139.7 8.4 collective-permute-done.42
  148.1 67.3 %collective-permute-start.1 = (bf16[576,1536]{1,0:T(8,128)(2,1)S(1)}, bf16[576,1536]{1,0:T(8,128)(2,1)S(1)}, u32[]{:S(2)}, u32[]{:S(2)}) collective-permute-start(bf16[576,1536]{1,0:T(8,128)(2,1)S(1)} %copy-done.43), channel_id=1, source_target_pairs={{0,4},{4,0},{1,5},{5,1},{2,6},{6,2},{3,7},{7,3},{8,12},{12,8},{9,1... | collective-permute-start | bytes 5308424 | tf_op jit(solution)/shard_map/ppermute | solution.py:445
  223.9 6.0 collective-permute-done.15
  249.8 34.5 %collective-permute-done.17 = bf16[192,1152]{1,0:T(8,128)(2,1)S(1)} collective-permute-done((bf16[192,1152]{1,0:T(8,128)(2,1)S(1)}, bf16[192,1152]{1,0:T(8,128)(2,1)S(1)}, u32[]{:S(2)}, u32[]{:S(2)}) %collective-permute-start.17) | collective-permute-done | bytes 442400 | tf_op jit(solution)/shard_map/ppermute | solution.py:442
  289.8 7.1 convolution_convert_fusion.qkv_ref
  297.5 35.7 %shard_map.263 = (bf16[1152,384]{1,0:T(8,128)(2,1)}, f32[2,2,2,576,256]{4,3,2,1,0:T(8,128)}, bf16[2,2,2,576,1536]{4,3,2,1,0:T(8,128)(2,1)}, bf16[2,2,2,6,576,256]{5,4,3,2,1,0:T(8,128)(2,1)}, f32[2,2,576,256]{3,2,1,0:T(8,128)}) custom-call(f32[8]{0:T(128)} %slice.471.mix_ref, bf16[1152,1152]{1,0:T(8,128)(2,1)} %convolution_convert_fusion.qkv_ref, ...), custom_call_target="tpu_custom_call" | custom-call | flops 40000000000 | bytes 60000000 | tf_op jit(solution)/shard_map/pallas_call | solution.py:325
  339.0 6.3 maximum_select_fusion.1
  345.3 7.2 convolution_convert_fusion.1.qkv_ref
  353.1 35.5 %shard_map.262 = (bf16[1152,384]{1,0:T(8,128)(2,1)}, f32[2,2,2,576,256]{4,3,2,1,0:T(8,128)}, bf16[2,2,2,576,1536]{4,3,2,1,0:T(8,128)(2,1)}, bf16[2,2,2,6,576,256]{5,4,3,2,1,0:T(8,128)(2,1)}, f32[2,2,576,256]{3,2,1,0:T(8,128)}) custom-call(f32[8]{0:T(128)} %slice.439.mix_ref, bf16[1152,1152]{1,0:T(8,128)(2,1)} %convolution_convert_fusion.1.qkv_ref, ...), custom_call_target="tpu_custom_call" | custom-call | flops 40000000000 | bytes 60000000 | tf_op jit(solution)/shard_map/pallas_call | solution.py:325
  390.9 23.0 %collective-permute-start.24 = (bf16[576,1536]{1,0:T(8,128)(2,1)S(1)}, bf16[576,1536]{1,0:T(8,128)(2,1)S(1)}, u32[]{:S(2)}, u32[]{:S(2)}) collective-permute-start(bf16[576,1536]{1,0:T(8,128)(2,1)S(1)} %add_convert_fusion.5), channel_id=1, source_target_pairs={{0,4},{4,0},{1,5},{5,1},{2,6},{6,2},{3,7},{7,3},{8,12},{12,8},{9,1... | collective-permute-start | bytes 5308424 | tf_op jit(solution)/shard_map/ppermute | solution.py:445
  451.8 12.5 %fusion.41 = f32[1152,2048]{1,0:T(8,128)S(1)} fusion(bf16[1536,2048]{1,0:T(8,128)(2,1)} %constant_dynamic-update-slice_fusion.35, bf16[576,1536]{1,0:T(8,128)(2,1)} %collective-permute-done.25, bf16[576,1536]{1,0:T(8,128)(2,1)S(1)} %multiply_convert_fusion.2), kind=kOutput, calls=%fused_computation.166 | convolution fusion | flops 7254835200 | bytes 19267584 | tf_op jit(solution)/shard_map/dot_general | solution.py:36
  469.5 9.9 fusion.42
  498.4 4.1 fusion.145
  506.6 10.6 fusion.15
  517.3 9.3 fusion.30
  526.6 9.4 fusion.7
  536.0 5.5 fusion.33
  541.5 6.4 add_convert_fusion.3
  548.5 8.8 convolution_convert_fusion.2
  558.0 5.9 convolution_convert_fusion.3
  563.9 7.0 convolution_convert_fusion.4
  579.5 4.8 fusion.99
  585.0 8.8 convolution_convert_fusion.5
  599.9 7.1 fusion.27
  607.0 54.3 %collective-permute-done.90 = bf16[768,1024]{1,0:T(8,128)(2,1)S(1)} collective-permute-done((bf16[768,1024]{1,0:T(8,128)(2,1)}, bf16[768,1024]{1,0:T(8,128)(2,1)S(1)}, u32[]{:S(2)}, u32[]{:S(2)}) %collective-permute-start.90) | collective-permute-done | bytes 1572896 | tf_op jit(solution)/shard_map/ppermute | solution.py:442
  663.6 12.2 collective-permute-done.87
  711.8 25.6 %collective-permute-start.93 = (bf16[384,1024]{1,0:T(8,128)(2,1)}, bf16[384,1024]{1,0:T(8,128)(2,1)}, u32[]{:S(2)}, u32[]{:S(2)}) collective-permute-start(bf16[384,1024]{1,0:T(8,128)(2,1)} %add_convert_fusion.8), channel_id=1, source_target_pairs={{0,4},{4,0},{1,5},{5,1},{2,6},{6,2},{3,7},{7,3},{8,12},{12,8},{9,1... | collective-permute-start | bytes 2359304 | tf_op jit(solution)/shard_map/ppermute | solution.py:445
  740.6 50.6 %shard_map.265 = (bf16[1152,1152]{1,0:T(8,128)(2,1)}, f32[8,384]{1,0:T(8,128)}, f32[2,2,8,256]{3,2,1,0:T(8,128)}, f32[2,2,2,8,256]{4,3,2,1,0:T(8,128)}) custom-call(f32[8]{0:T(128)} %slice.471.mix_ref, bf16[1152,1152]{1,0:T(8,128)(2,1)} %convolution_convert_fusion.qkv_ref, bf16[2,2,1536,256]{3,2,1,0:T(8,128)(2,1)} %add_convert_fusion.t_ref, ...), custom_call_target="tpu_custom_call" | custom-call | flops 80000000000 | bytes 60000000 | tf_op jit(solution)/shard_map/pallas_call | solution.py:340
  791.2 6.8 fusion.107
  798.0 4.3 fusion.110
  805.5 50.2 %shard_map.264 = (bf16[1152,1152]{1,0:T(8,128)(2,1)}, f32[8,384]{1,0:T(8,128)}, f32[2,2,8,256]{3,2,1,0:T(8,128)}, f32[2,2,2,8,256]{4,3,2,1,0:T(8,128)}) custom-call(f32[8]{0:T(128)} %slice.439.mix_ref, bf16[1152,1152]{1,0:T(8,128)(2,1)} %convolution_convert_fusion.1.qkv_ref, bf16[2,2,1536,256]{3,2,1,0:T(8,128)(2,1)} %add_convert_fusion.1.t_ref, ...), custom_call_target="tpu_custom_call" | custom-call | flops 80000000000 | bytes 60000000 | tf_op jit(solution)/shard_map/pallas_call | solution.py:340
  869.2 6.8 fusion.112
  885.6 4.1 convolution_convert_fusion.6
  919.2 7.4 collective-permute-done.63
  928.5 6.5 collective-permute-done.95
  967.7 28.4 %collective-permute-done.71 = bf16[192,384]{1,0:T(8,128)(2,1)S(1)} collective-permute-done((bf16[192,384]{1,0:T(8,128)(2,1)S(1)}, bf16[192,384]{1,0:T(8,128)(2,1)S(1)}, u32[]{:S(2)}, u32[]{:S(2)}) %collective-permute-start.71) | collective-permute-done | bytes 147488 | tf_op jit(solution)/shard_map/ppermute | solution.py:442
  1021.7 75.8 %psum.7 = f32[5698]{0:T(1024)S(1)} all-reduce(f32[5698]{0:T(1024)S(1)} %concatenate.243), channel_id=1, replica_groups=mesh['plane'=4,'core'=2,'tensor'=4] {'plane','core','tensor'}, use_global_device_ids=true, to_apply=%region_11.12 | all-reduce | flops 5698 | bytes 45584 | tf_op jit(solution)/shard_map/psum | solution.py:638
  1107.3 13.8 %collective-permute-done.52 = bf16[384,1152]{1,0:T(8,128)(2,1)S(1)} collective-permute-done((bf16[384,1152]{1,0:T(8,128)(2,1)S(1)}, bf16[384,1152]{1,0:T(8,128)(2,1)S(1)}, u32[]{:S(2)}, u32[]{:S(2)}) %collective-permute-start.52) | collective-permute-done | bytes 884768 | tf_op jit(solution)/shard_map/ppermute | solution.py:442
  1130.1 17.6 %collective-permute-start.57 = (bf16[384,1152]{1,0:T(8,128)(2,1)S(1)}, bf16[384,1152]{1,0:T(8,128)(2,1)S(1)}, u32[]{:S(2)}, u32[]{:S(2)}) collective-permute-start(bf16[384,1152]{1,0:T(8,128)(2,1)S(1)} %add_convert_fusion.7), channel_id=1, source_target_pairs={{0,4},{4,0},{1,5},{5,1},{2,6},{6,2},{3,7},{7,3},{8,12},{12,8},{9,1... | collective-permute-start | bytes 2654216 | tf_op jit(solution)/shard_map/ppermute | solution.py:445
  1163.0 6.8 collective-permute-done.59
  1172.0 17.0 %collective-permute-done.60 = bf16[96,1152]{1,0:T(8,128)(2,1)S(1)} collective-permute-done((bf16[96,1152]{1,0:T(8,128)(2,1)S(1)}, bf16[96,1152]{1,0:T(8,128)(2,1)S(1)}, u32[]{:S(2)}, u32[]{:S(2)}) %collective-permute-start.60) | collective-permute-done | bytes 221216 | tf_op jit(solution)/shard_map/ppermute | solution.py:442
  1196.5 9.3 collective-permute-done.84
  1214.2 5.2 maximum_convert_fusion
  1219.4 12.1 fusion.236
  (867 shorter events, 426.7 us)
Async XLA Ops:
  3.0 81.7 %collective-permute-start.19 = (bf16[384,384]{1,0:T(8,128)(2,1)S(1)}, bf16[384,384]{1,0:T(8,128)(2,1)}, u32[]{:S(2)}, u32[]{:S(2)}) collective-permute-start(bf16[384,384]{1,0:T(8,128)(2,1)S(1)} %get-tuple-element.204), channel_id=1, source_target_pairs={{0,1},{1,0},{2,5},{3,4},{4,3},{5,2},{6,7},{7,6},{8,9},{9,8},{10,13... | collective-permute-start | bytes 884744 | tf_op jit(solution)/shard_map/ppermute | solution.py:451
  6.0 81.7 %collective-permute-start.8 = (bf16[384,384]{1,0:T(8,128)(2,1)S(1)}, bf16[384,384]{1,0:T(8,128)(2,1)}, u32[]{:S(2)}, u32[]{:S(2)}) collective-permute-start(bf16[384,384]{1,0:T(8,128)(2,1)S(1)} %get-tuple-element.204), channel_id=1, source_target_pairs={{2,4},{3,5},{4,2},{5,3},{10,12},{11,13},{12,10},{13,11},{18,20},{1... | collective-permute-start | bytes 884744 | tf_op jit(solution)/shard_map/ppermute | solution.py:448
  9.8 39.8 %collective-permute-start.13 = (f32[656]{0:T(1024)S(1)}, f32[656]{0:T(1024)S(1)}, u32[]{:S(2)}, u32[]{:S(2)}) collective-permute-start(f32[656]{0:T(1024)S(1)} %pad_maximum_fusion.29), channel_id=1, source_target_pairs={{0,1},{1,0},{2,5},{3,4},{4,3},{5,2},{6,7},{7,6},{8,9},{9,8},{10,13... | collective-permute-start | bytes 7880 | tf_op jit(solution)/shard_map/ppermute | solution.py:451
  10.0 63.3 %collective-permute-start = (f32[656]{0:T(1024)S(1)}, f32[656]{0:T(1024)}, u32[]{:S(2)}, u32[]{:S(2)}) collective-permute-start(f32[656]{0:T(1024)S(1)} %pad_maximum_fusion.29), channel_id=1, source_target_pairs={{2,4},{3,5},{4,2},{5,3},{10,12},{11,13},{12,10},{13,11},{18,20},{1... | collective-permute-start | bytes 7880 | tf_op jit(solution)/shard_map/ppermute | solution.py:448
  12.6 33.5 %collective-permute-start.7 = (s32[576]{0:T(1024)S(1)}, s32[576]{0:T(1024)S(1)}, u32[]{:S(2)}, u32[]{:S(2)}) collective-permute-start(s32[576]{0:T(1024)S(1)} %get-tuple-element.116), channel_id=1, source_target_pairs={{0,4},{4,0},{1,5},{5,1},{2,6},{6,2},{3,7},{7,3},{8,12},{12,8},{9,1... | collective-permute-start | bytes 6920 | tf_op jit(solution)/shard_map/ppermute | solution.py:445
  46.2 69.5 %collective-permute-start.41 = (bf16[384,1024]{1,0:T(8,128)(2,1)}, bf16[384,1024]{1,0:T(8,128)(2,1)}, u32[]{:S(2)}, u32[]{:S(2)}) collective-permute-start(bf16[384,1024]{1,0:T(8,128)(2,1)} %get-tuple-element.182), channel_id=1, source_target_pairs={{0,1},{1,0},{2,5},{3,4},{4,3},{5,2},{6,7},{7,6},{8,9},{9,8},{10,13... | collective-permute-start | bytes 2359304 | tf_op jit(solution)/shard_map/ppermute | solution.py:451
  84.7 25.1 %collective-permute-start.20 = (bf16[384,384]{1,0:T(8,128)(2,1)}, bf16[384,384]{1,0:T(8,128)(2,1)S(1)}, u32[]{:S(2)}, u32[]{:S(2)}) collective-permute-start(bf16[384,384]{1,0:T(8,128)(2,1)} %collective-permute-done.19), channel_id=1, source_target_pairs={{0,16},{1,17},{2,18},{3,19},{4,20},{5,21},{6,22},{7,23},{8,24},{9,... | collective-permute-start | bytes 884744 | tf_op jit(solution)/shard_map/ppermute | solution.py:442
  113.7 22.2 %collective-permute-start.14 = (bf16[384,1152]{1,0:T(8,128)(2,1)S(1)}, bf16[384,1152]{1,0:T(8,128)(2,1)S(1)}, u32[]{:S(2)}, u32[]{:S(2)}) collective-permute-start(bf16[384,1152]{1,0:T(8,128)(2,1)S(1)} %copy-done.100), channel_id=1, source_target_pairs={{0,1},{1,0},{2,5},{3,4},{4,3},{5,2},{6,7},{7,6},{8,9},{9,8},{10,13... | collective-permute-start | bytes 2654216 | tf_op jit(solution)/shard_map/ppermute | solution.py:451
  120.3 96.7 %collective-permute-start.36 = (bf16[384,2048]{1,0:T(8,128)(2,1)S(1)}, bf16[384,2048]{1,0:T(8,128)(2,1)}, u32[]{:S(2)}, u32[]{:S(2)}) collective-permute-start(bf16[384,2048]{1,0:T(8,128)(2,1)S(1)} %copy-done.81), channel_id=1, source_target_pairs={{0,1},{1,0},{2,5},{3,4},{4,3},{5,2},{6,7},{7,6},{8,9},{9,8},{10,13... | collective-permute-start | bytes 4718600 | tf_op jit(solution)/shard_map/ppermute | solution.py:451
  122.1 98.3 %collective-permute-start.26 = (bf16[384,2048]{1,0:T(8,128)(2,1)S(1)}, bf16[384,2048]{1,0:T(8,128)(2,1)}, u32[]{:S(2)}, u32[]{:S(2)}) collective-permute-start(bf16[384,2048]{1,0:T(8,128)(2,1)S(1)} %copy-done.81), channel_id=1, source_target_pairs={{2,4},{3,5},{4,2},{5,3},{10,12},{11,13},{12,10},{13,11},{18,20},{1... | collective-permute-start | bytes 4718600 | tf_op jit(solution)/shard_map/ppermute | solution.py:448
  135.9 80.2 %collective-permute-start.32 = (bf16[384,1024]{1,0:T(8,128)(2,1)S(1)}, bf16[384,1024]{1,0:T(8,128)(2,1)S(1)}, u32[]{:S(2)}, u32[]{:S(2)}) collective-permute-start(bf16[384,1024]{1,0:T(8,128)(2,1)S(1)} %collective-permute-done.31), channel_id=1, source_target_pairs={{2,18},{3,19},{4,20},{5,21},{10,26},{11,27},{12,28},{13,29},{18,2}... | collective-permute-start | bytes 2359304 | tf_op jit(solution)/shard_map/ppermute | solution.py:442
  136.7 78.8 %collective-permute-start.33 = (bf16[384,1024]{1,0:T(8,128)(2,1)S(1)}, bf16[384,1024]{1,0:T(8,128)(2,1)S(1)}, u32[]{:S(2)}, u32[]{:S(2)}) collective-permute-start(bf16[384,1024]{1,0:T(8,128)(2,1)S(1)} %collective-permute-done.31), channel_id=1, source_target_pairs={{2,10},{3,11},{4,12},{5,13},{10,2},{11,3},{12,4},{13,5},{18,26},{1... | collective-permute-start | bytes 2359304 | tf_op jit(solution)/shard_map/ppermute | solution.py:442
  148.1 139.6 %collective-permute-start.1 = (bf16[576,1536]{1,0:T(8,128)(2,1)S(1)}, bf16[576,1536]{1,0:T(8,128)(2,1)S(1)}, u32[]{:S(2)}, u32[]{:S(2)}) collective-permute-start(bf16[576,1536]{1,0:T(8,128)(2,1)S(1)} %copy-done.43), channel_id=1, source_target_pairs={{0,4},{4,0},{1,5},{5,1},{2,6},{6,2},{3,7},{7,3},{8,12},{12,8},{9,1... | collective-permute-start | bytes 5308424 | tf_op jit(solution)/shard_map/ppermute | solution.py:445
  241.7 177.4 %collective-permute-start.37 = (bf16[384,2048]{1,0:T(8,128)(2,1)}, bf16[384,2048]{1,0:T(8,128)(2,1)}, u32[]{:S(2)}, u32[]{:S(2)}) collective-permute-start(bf16[384,2048]{1,0:T(8,128)(2,1)} %collective-permute-done.36), channel_id=1, source_target_pairs={{0,16},{1,17},{2,18},{3,19},{4,20},{5,21},{6,22},{7,23},{8,24},{9,... | collective-permute-start | bytes 4718600 | tf_op jit(solution)/shard_map/ppermute | solution.py:442
  241.7 42.7 %collective-permute-start.17 = (bf16[192,1152]{1,0:T(8,128)(2,1)S(1)}, bf16[192,1152]{1,0:T(8,128)(2,1)S(1)}, u32[]{:S(2)}, u32[]{:S(2)}) collective-permute-start(bf16[192,1152]{1,0:T(8,128)(2,1)S(1)} %slice.608), channel_id=1, source_target_pairs={{0,16},{1,17},{2,18},{3,19},{4,20},{5,21},{6,22},{7,23},{8,24},{9,... | collective-permute-start | bytes 1327112 | tf_op jit(solution)/shard_map/ppermute | solution.py:442
  247.7 38.5 %collective-permute-start.18 = (bf16[192,1152]{1,0:T(8,128)(2,1)S(1)}, bf16[192,1152]{1,0:T(8,128)(2,1)S(1)}, u32[]{:S(2)}, u32[]{:S(2)}) collective-permute-start(bf16[192,1152]{1,0:T(8,128)(2,1)S(1)} %slice.609), channel_id=1, source_target_pairs={{0,8},{1,9},{2,10},{3,11},{4,12},{5,13},{6,14},{7,15},{8,0},{9,1},... | collective-permute-start | bytes 1327112 | tf_op jit(solution)/shard_map/ppermute | solution.py:442
  248.5 167.7 %collective-permute-start.38 = (bf16[384,2048]{1,0:T(8,128)(2,1)}, bf16[384,2048]{1,0:T(8,128)(2,1)}, u32[]{:S(2)}, u32[]{:S(2)}) collective-permute-start(bf16[384,2048]{1,0:T(8,128)(2,1)} %collective-permute-done.36), channel_id=1, source_target_pairs={{0,8},{1,9},{2,10},{3,11},{4,12},{5,13},{6,14},{7,15},{8,0},{9,1},... | collective-permute-start | bytes 4718600 | tf_op jit(solution)/shard_map/ppermute | solution.py:442
  284.4 141.1 %collective-permute-start.27 = (bf16[384,2048]{1,0:T(8,128)(2,1)}, bf16[384,2048]{1,0:T(8,128)(2,1)}, u32[]{:S(2)}, u32[]{:S(2)}) collective-permute-start(bf16[384,2048]{1,0:T(8,128)(2,1)} %collective-permute-done.26), channel_id=1, source_target_pairs={{2,18},{3,19},{4,20},{5,21},{10,26},{11,27},{12,28},{13,29},{18,2}... | collective-permute-start | bytes 4718600 | tf_op jit(solution)/shard_map/ppermute | solution.py:442
  286.2 46.9 %collective-permute-start.5 = (bf16[192,1152]{1,0:T(8,128)(2,1)}, bf16[192,1152]{1,0:T(8,128)(2,1)}, u32[]{:S(2)}, u32[]{:S(2)}) collective-permute-start(bf16[192,1152]{1,0:T(8,128)(2,1)} %slice.580), channel_id=1, source_target_pairs={{2,18},{3,19},{4,20},{5,21},{10,26},{11,27},{12,28},{13,29},{18,2}... | collective-permute-start | bytes 1327112 | tf_op jit(solution)/shard_map/ppermute | solution.py:442
  287.8 49.4 %collective-permute-start.6 = (bf16[192,1152]{1,0:T(8,128)(2,1)}, bf16[192,1152]{1,0:T(8,128)(2,1)}, u32[]{:S(2)}, u32[]{:S(2)}) collective-permute-start(bf16[192,1152]{1,0:T(8,128)(2,1)} %slice.581), channel_id=1, source_target_pairs={{2,10},{3,11},{4,12},{5,13},{10,2},{11,3},{12,4},{13,5},{18,26},{1... | collective-permute-start | bytes 1327112 | tf_op jit(solution)/shard_map/ppermute | solution.py:442
  333.2 88.6 %collective-permute-start.28 = (bf16[384,2048]{1,0:T(8,128)(2,1)}, bf16[384,2048]{1,0:T(8,128)(2,1)}, u32[]{:S(2)}, u32[]{:S(2)}) collective-permute-start(bf16[384,2048]{1,0:T(8,128)(2,1)} %collective-permute-done.26), channel_id=1, source_target_pairs={{2,10},{3,11},{4,12},{5,13},{10,2},{11,3},{12,4},{13,5},{18,26},{1... | collective-permute-start | bytes 4718600 | tf_op jit(solution)/shard_map/ppermute | solution.py:442
  390.9 50.8 %collective-permute-start.24 = (bf16[576,1536]{1,0:T(8,128)(2,1)S(1)}, bf16[576,1536]{1,0:T(8,128)(2,1)S(1)}, u32[]{:S(2)}, u32[]{:S(2)}) collective-permute-start(bf16[576,1536]{1,0:T(8,128)(2,1)S(1)} %add_convert_fusion.5), channel_id=1, source_target_pairs={{0,4},{4,0},{1,5},{5,1},{2,6},{6,2},{3,7},{7,3},{8,12},{12,8},{9,1... | collective-permute-start | bytes 5308424 | tf_op jit(solution)/shard_map/ppermute | solution.py:445
  547.9 131.0 %collective-permute-start.48 = (bf16[576,1536]{1,0:T(8,128)(2,1)S(1)}, bf16[576,1536]{1,0:T(8,128)(2,1)}, u32[]{:S(2)}, u32[]{:S(2)}) collective-permute-start(bf16[576,1536]{1,0:T(8,128)(2,1)S(1)} %add_convert_fusion.3), channel_id=1, source_target_pairs={{0,4},{4,0},{1,5},{5,1},{2,6},{6,2},{3,7},{7,3},{8,12},{12,8},{9,1... | collective-permute-start | bytes 5308424 | tf_op jit(solution)/shard_map/ppermute | solution.py:445
  557.3 139.8 %collective-permute-start.78 = (bf16[768,2048]{1,0:T(8,128)(2,1)}, bf16[768,2048]{1,0:T(8,128)(2,1)}, u32[]{:S(2)}, u32[]{:S(2)}) collective-permute-start(bf16[768,2048]{1,0:T(8,128)(2,1)} %convolution_convert_fusion.2), channel_id=1, source_target_pairs={{0,16},{1,17},{2,18},{3,19},{4,20},{5,21},{6,22},{7,23},{8,24},{9,... | collective-permute-start | bytes 9437192 | tf_op jit(solution)/shard_map/ppermute | solution.py:442
  570.9 133.1 %collective-permute-start.75 = (bf16[768,2048]{1,0:T(8,128)(2,1)}, bf16[768,2048]{1,0:T(8,128)(2,1)}, u32[]{:S(2)}, u32[]{:S(2)}) collective-permute-start(bf16[768,2048]{1,0:T(8,128)(2,1)} %convolution_convert_fusion.4), channel_id=1, source_target_pairs={{0,8},{1,9},{2,10},{3,11},{4,12},{5,13},{6,14},{7,15},{8,0},{9,1},... | collective-permute-start | bytes 9437192 | tf_op jit(solution)/shard_map/ppermute | solution.py:442
  578.0 83.3 %collective-permute-start.90 = (bf16[768,1024]{1,0:T(8,128)(2,1)}, bf16[768,1024]{1,0:T(8,128)(2,1)S(1)}, u32[]{:S(2)}, u32[]{:S(2)}) collective-permute-start(bf16[768,1024]{1,0:T(8,128)(2,1)} %fusion.93), channel_id=1, source_target_pairs={{0,16},{1,17},{2,18},{3,19},{4,20},{5,21},{6,22},{7,23},{8,24},{9,... | collective-permute-start | bytes 4718600 | tf_op jit(solution)/shard_map/ppermute | solution.py:442
  584.3 91.5 %collective-permute-start.87 = (bf16[768,1024]{1,0:T(8,128)(2,1)}, bf16[768,1024]{1,0:T(8,128)(2,1)S(1)}, u32[]{:S(2)}, u32[]{:S(2)}) collective-permute-start(bf16[768,1024]{1,0:T(8,128)(2,1)} %fusion.99), channel_id=1, source_target_pairs={{0,8},{1,9},{2,10},{3,11},{4,12},{5,13},{6,14},{7,15},{8,0},{9,1},... | collective-permute-start | bytes 4718600 | tf_op jit(solution)/shard_map/ppermute | solution.py:442
  662.1 29.5 %collective-permute-start.91 = (bf16[384,1024]{1,0:T(8,128)(2,1)S(1)}, bf16[384,1024]{1,0:T(8,128)(2,1)}, u32[]{:S(2)}, u32[]{:S(2)}) collective-permute-start(bf16[384,1024]{1,0:T(8,128)(2,1)S(1)} %slice.1097), channel_id=1, source_target_pairs={{0,8},{1,9},{2,10},{3,11},{4,12},{5,13},{6,14},{7,15},{8,0},{9,1},... | collective-permute-start | bytes 2359304 | tf_op jit(solution)/shard_map/ppermute | solution.py:442
  685.9 51.4 %collective-permute-start.49 = (bf16[576,1536]{1,0:T(8,128)(2,1)S(1)}, bf16[576,1536]{1,0:T(8,128)(2,1)S(1)}, u32[]{:S(2)}, u32[]{:S(2)}) collective-permute-start(bf16[576,1536]{1,0:T(8,128)(2,1)S(1)} %get-tuple-element.120), channel_id=1, source_target_pairs={{0,4},{4,0},{1,5},{5,1},{2,6},{6,2},{3,7},{7,3},{8,12},{12,8},{9,1... | collective-permute-start | bytes 5308424 | tf_op jit(solution)/shard_map/ppermute | solution.py:445
  701.7 254.8 %collective-permute-start.79 = (bf16[384,2048]{1,0:T(8,128)(2,1)}, bf16[384,2048]{1,0:T(8,128)(2,1)}, u32[]{:S(2)}, u32[]{:S(2)}) collective-permute-start(bf16[384,2048]{1,0:T(8,128)(2,1)} %slice.1093), channel_id=1, source_target_pairs={{0,8},{1,9},{2,10},{3,11},{4,12},{5,13},{6,14},{7,15},{8,0},{9,1},... | collective-permute-start | bytes 4718600 | tf_op jit(solution)/shard_map/ppermute | solution.py:442
  709.0 256.4 %collective-permute-start.76 = (bf16[384,2048]{1,0:T(8,128)(2,1)}, bf16[384,2048]{1,0:T(8,128)(2,1)}, u32[]{:S(2)}, u32[]{:S(2)}) collective-permute-start(bf16[384,2048]{1,0:T(8,128)(2,1)} %slice.1094), channel_id=1, source_target_pairs={{0,16},{1,17},{2,18},{3,19},{4,20},{5,21},{6,22},{7,23},{8,24},{9,... | collective-permute-start | bytes 4718600 | tf_op jit(solution)/shard_map/ppermute | solution.py:442
  711.8 202.6 %collective-permute-start.93 = (bf16[384,1024]{1,0:T(8,128)(2,1)}, bf16[384,1024]{1,0:T(8,128)(2,1)}, u32[]{:S(2)}, u32[]{:S(2)}) collective-permute-start(bf16[384,1024]{1,0:T(8,128)(2,1)} %add_convert_fusion.8), channel_id=1, source_target_pairs={{0,4},{4,0},{1,5},{5,1},{2,6},{6,2},{3,7},{7,3},{8,12},{12,8},{9,1... | collective-permute-start | bytes 2359304 | tf_op jit(solution)/shard_map/ppermute | solution.py:445
  884.7 32.8 %collective-permute-start.66 = (bf16[768,384]{1,0:T(8,128)(2,1)}, bf16[768,384]{1,0:T(8,128)(2,1)}, u32[]{:S(2)}, u32[]{:S(2)}) collective-permute-start(bf16[768,384]{1,0:T(8,128)(2,1)} %fusion.114), channel_id=1, source_target_pairs={{0,16},{1,17},{2,18},{3,19},{4,20},{5,21},{6,22},{7,23},{8,24},{9,... | collective-permute-start | bytes 1769480 | tf_op jit(solution)/shard_map/ppermute | solution.py:442
  947.9 66.7 %collective-permute-start.50 = (bf16[576,1536]{1,0:T(8,128)(2,1)S(1)}, bf16[576,1536]{1,0:T(8,128)(2,1)S(1)}, u32[]{:S(2)}, u32[]{:S(2)}) collective-permute-start(bf16[576,1536]{1,0:T(8,128)(2,1)S(1)} %copy-done.146), channel_id=1, source_target_pairs={{0,4},{4,0},{1,5},{5,1},{2,6},{6,2},{3,7},{7,3},{8,12},{12,8},{9,1... | collective-permute-start | bytes 5308424 | tf_op jit(solution)/shard_map/ppermute | solution.py:445
  953.5 55.8 %collective-permute-start.54 = (bf16[768,1152]{1,0:T(8,128)(2,1)S(1)}, bf16[768,1152]{1,0:T(8,128)(2,1)S(1)}, u32[]{:S(2)}, u32[]{:S(2)}) collective-permute-start(bf16[768,1152]{1,0:T(8,128)(2,1)S(1)} %copy-done.147), channel_id=1, source_target_pairs={{0,16},{1,17},{2,18},{3,19},{4,20},{5,21},{6,22},{7,23},{8,24},{9,... | collective-permute-start | bytes 5308424 | tf_op jit(solution)/shard_map/ppermute | solution.py:442
  954.6 143.0 %collective-permute-start.51 = (bf16[768,1152]{1,0:T(8,128)(2,1)}, bf16[768,1152]{1,0:T(8,128)(2,1)}, u32[]{:S(2)}, u32[]{:S(2)}) collective-permute-start(bf16[768,1152]{1,0:T(8,128)(2,1)} %convolution_convert_fusion.8), channel_id=1, source_target_pairs={{0,8},{1,9},{2,10},{3,11},{4,12},{5,13},{6,14},{7,15},{8,0},{9,1},... | collective-permute-start | bytes 5308424 | tf_op jit(solution)/shard_map/ppermute | solution.py:442
  964.3 34.9 %collective-permute-start.70 = (bf16[192,384]{1,0:T(8,128)(2,1)S(1)}, bf16[192,384]{1,0:T(8,128)(2,1)S(1)}, u32[]{:S(2)}, u32[]{:S(2)}) collective-permute-start(bf16[192,384]{1,0:T(8,128)(2,1)S(1)} %get-tuple-element.112), channel_id=1, source_target_pairs={{0,16},{1,17},{2,18},{3,19},{4,20},{5,21},{6,22},{7,23},{8,24},{9,... | collective-permute-start | bytes 442376 | tf_op jit(solution)/shard_map/ppermute | solution.py:442
  965.4 30.7 %collective-permute-start.71 = (bf16[192,384]{1,0:T(8,128)(2,1)S(1)}, bf16[192,384]{1,0:T(8,128)(2,1)S(1)}, u32[]{:S(2)}, u32[]{:S(2)}) collective-permute-start(bf16[192,384]{1,0:T(8,128)(2,1)S(1)} %get-tuple-element.112), channel_id=1, source_target_pairs={{0,8},{1,9},{2,10},{3,11},{4,12},{5,13},{6,14},{7,15},{8,0},{9,1},... | collective-permute-start | bytes 442376 | tf_op jit(solution)/shard_map/ppermute | solution.py:442
  996.1 161.7 %collective-permute-start.98 = (bf16[768,1024]{1,0:T(8,128)(2,1)}, bf16[768,1024]{1,0:T(8,128)(2,1)}, u32[]{:S(2)}, u32[]{:S(2)}) collective-permute-start(bf16[768,1024]{1,0:T(8,128)(2,1)} %constant_dynamic-update-slice_fusion.60), channel_id=1, source_target_pairs={{0,4},{4,0},{1,5},{5,1},{2,6},{6,2},{3,7},{7,3},{8,12},{12,8},{9,1... | collective-permute-start | bytes 4718600 | tf_op jit(solution)/shard_map/ppermute | solution.py:445
  1008.1 116.2 %collective-permute-start.80 = (bf16[384,2048]{1,0:T(8,128)(2,1)}, bf16[384,2048]{1,0:T(8,128)(2,1)}, u32[]{:S(2)}, u32[]{:S(2)}) collective-permute-start(bf16[384,2048]{1,0:T(8,128)(2,1)} %fusion.24), channel_id=1, source_target_pairs={{0,1},{1,0},{2,5},{3,4},{4,3},{5,2},{6,7},{7,6},{8,9},{9,8},{10,13... | collective-permute-start | bytes 4718600 | tf_op jit(solution)/shard_map/ppermute | solution.py:451
  1009.3 117.1 %collective-permute-start.77 = (bf16[384,2048]{1,0:T(8,128)(2,1)S(1)}, bf16[384,2048]{1,0:T(8,128)(2,1)}, u32[]{:S(2)}, u32[]{:S(2)}) collective-permute-start(bf16[384,2048]{1,0:T(8,128)(2,1)S(1)} %fusion.25), channel_id=1, source_target_pairs={{2,4},{3,5},{4,2},{5,3},{10,12},{11,13},{12,10},{13,11},{18,20},{1... | collective-permute-start | bytes 4718600 | tf_op jit(solution)/shard_map/ppermute | solution.py:448
  1014.6 90.2 %collective-permute-start.55 = (bf16[384,1152]{1,0:T(8,128)(2,1)}, bf16[384,1152]{1,0:T(8,128)(2,1)}, u32[]{:S(2)}, u32[]{:S(2)}) collective-permute-start(bf16[384,1152]{1,0:T(8,128)(2,1)} %slice.1095), channel_id=1, source_target_pairs={{0,8},{1,9},{2,10},{3,11},{4,12},{5,13},{6,14},{7,15},{8,0},{9,1},... | collective-permute-start | bytes 2654216 | tf_op jit(solution)/shard_map/ppermute | solution.py:442
  1107.2 22.6 %collective-permute-start.56 = (bf16[384,1152]{1,0:T(8,128)(2,1)S(1)}, bf16[384,1152]{1,0:T(8,128)(2,1)S(1)}, u32[]{:S(2)}, u32[]{:S(2)}) collective-permute-start(bf16[384,1152]{1,0:T(8,128)(2,1)S(1)} %fusion.63), channel_id=1, source_target_pairs={{0,1},{1,0},{2,5},{3,4},{4,3},{5,2},{6,7},{7,6},{8,9},{9,8},{10,13... | collective-permute-start | bytes 2654216 | tf_op jit(solution)/shard_map/ppermute | solution.py:451
  1124.3 27.6 %collective-permute-start.74 = (bf16[768,384]{1,0:T(8,128)(2,1)}, bf16[768,384]{1,0:T(8,128)(2,1)}, u32[]{:S(2)}, u32[]{:S(2)}) collective-permute-start(bf16[768,384]{1,0:T(8,128)(2,1)} %constant_dynamic-update-slice_fusion.50), channel_id=1, source_target_pairs={{0,4},{4,0},{1,5},{5,1},{2,6},{6,2},{3,7},{7,3},{8,12},{12,8},{9,1... | collective-permute-start | bytes 1769480 | tf_op jit(solution)/shard_map/ppermute | solution.py:445
  1128.6 31.3 %collective-permute-start.81 = (bf16[384,2048]{1,0:T(8,128)(2,1)S(1)}, bf16[384,2048]{1,0:T(8,128)(2,1)}, u32[]{:S(2)}, u32[]{:S(2)}) collective-permute-start(bf16[384,2048]{1,0:T(8,128)(2,1)S(1)} %add_convert_fusion.6), channel_id=1, source_target_pairs={{0,4},{4,0},{1,5},{5,1},{2,6},{6,2},{3,7},{7,3},{8,12},{12,8},{9,1... | collective-permute-start | bytes 4718600 | tf_op jit(solution)/shard_map/ppermute | solution.py:445
  1130.1 25.0 %collective-permute-start.57 = (bf16[384,1152]{1,0:T(8,128)(2,1)S(1)}, bf16[384,1152]{1,0:T(8,128)(2,1)S(1)}, u32[]{:S(2)}, u32[]{:S(2)}) collective-permute-start(bf16[384,1152]{1,0:T(8,128)(2,1)S(1)} %add_convert_fusion.7), channel_id=1, source_target_pairs={{0,4},{4,0},{1,5},{5,1},{2,6},{6,2},{3,7},{7,3},{8,12},{12,8},{9,1... | collective-permute-start | bytes 2654216 | tf_op jit(solution)/shard_map/ppermute | solution.py:445
  1161.4 33.5 %collective-permute-start.82 = (bf16[192,2048]{1,0:T(8,128)(2,1)S(1)}, bf16[192,2048]{1,0:T(8,128)(2,1)S(1)}, u32[]{:S(2)}, u32[]{:S(2)}) collective-permute-start(bf16[192,2048]{1,0:T(8,128)(2,1)S(1)} %get-tuple-element.110), channel_id=1, source_target_pairs={{0,16},{1,17},{2,18},{3,19},{4,20},{5,21},{6,22},{7,23},{8,24},{9,... | collective-permute-start | bytes 2359304 | tf_op jit(solution)/shard_map/ppermute | solution.py:442
  1162.3 31.9 %collective-permute-start.83 = (bf16[192,2048]{1,0:T(8,128)(2,1)S(1)}, bf16[192,2048]{1,0:T(8,128)(2,1)S(1)}, u32[]{:S(2)}, u32[]{:S(2)}) collective-permute-start(bf16[192,2048]{1,0:T(8,128)(2,1)S(1)} %get-tuple-element.110), channel_id=1, source_target_pairs={{0,8},{1,9},{2,10},{3,11},{4,12},{5,13},{6,14},{7,15},{8,0},{9,1},... | collective-permute-start | bytes 2359304 | tf_op jit(solution)/shard_map/ppermute | solution.py:442
  (221 other events, 2876.7 us)

commit v2 on v1

--- a/solution.py
+++ b/solution.py
@@ -409,15 +409,467 @@
     return jnp.sum(gmix[:, :, :4], axis=(0, 3)).reshape(-1, 2, 2)
 
 
-BACK = (0, 2, 1, 3)
+MESH = pl.DeviceIdType.MESH
+
+GATHERS = ((0, 0, 0), (1, 0, 1), (2, 0, 2), (3, 1, 0), (4, 2, 0), (5, 2, 1), (6, 3, 0))
+
+
+def greet(peers):
+    sem = pltpu.get_barrier_semaphore()
+    for peer in peers:
+        pl.semaphore_signal(sem, inc=1, device_id=peer, device_id_type=MESH)
+    pl.semaphore_wait(sem, len(peers))
+
+
+class Gather:
+    def __init__(self, items, weights, firsts, seconds, send, recv, local, held):
+        self.held = held
+        self.items, self.weights, self.firsts, self.seconds = items, weights, firsts, seconds
+        self.send, self.recv, self.local = send, recv, local
+        q, c, z = lax.axis_index("plane"), lax.axis_index("core"), lax.axis_index("tensor")
+        self.home = (z // 2) == c
+        self.q = q
+        self.far = (q, 1 - c, (z + 2) % 4)
+        self.near = (q, c, (z // 2) * 2 + (1 - z % 2))
+        self.by_x = ((q // 2) * 2 + (1 - q % 2), c, z)
+        self.by_y = ((q + 2) % 4, c, z)
+
+    def barrier(self):
+        greet((self.near, self.far, self.by_x, self.by_y))
+
+    def whole(self, item, side):
+        _, out, part = self.items[item]
+        ref = (self.firsts, self.seconds)[side][out]
+        width = self.weights[item].shape[1]
+        return ref, pl.ds(part * width, width)
+
+    def z_copy(self, item, side, relay=False):
+        rows = self.weights[item].shape[0] // 4
+        mine = pl.ds(pl.multiple_of(self.q * rows, 128), rows)
+        ref, cols = self.whole(item, side)
+        source = self.whole(item, 0)[0].at[mine, cols] if relay else self.weights[item].at[mine]
+        return pltpu.make_async_remote_copy(
+            src_ref=source, dst_ref=ref.at[mine, cols], send_sem=self.send.at[item, side],
+            recv_sem=self.recv.at[item, side], device_id=(self.far, self.near)[side], device_id_type=MESH)
+
+    def plane_copy(self, item, side, step, receiving=False):
+        ref, cols = self.whole(item, side)
+        rows = ref.shape[0] // 4
+        if step < 2:
+            owner, first, size = self.q, 0, rows
+        elif step == 2:
+            owner, first, size = self.by_x[0], 0, rows // 2
+        else:
+            owner, first, size = self.by_y[0], rows // 2, rows // 2
+        span = pl.ds(pl.multiple_of(owner * rows + first, 64), size)
+        slot = 2 + 4 * side + step
+        return pltpu.make_async_remote_copy(
+            src_ref=ref.at[span, cols], dst_ref=ref.at[span, cols], send_sem=self.send.at[item, slot], recv_sem=self.recv.at[item, slot],
+            device_id=(self.by_x, self.by_y, self.by_y, self.by_x)[step], device_id_type=MESH)
+
+    def own_load(self, item):
+        return pltpu.make_async_copy(self.weights[item], self.held[item], self.local.at[item, 0])
+
+    def own_store(self, item):
+        ref, cols = self.whole(item, 0)
+        return pltpu.make_async_copy(self.held[item], ref.at[:, cols], self.local.at[item, 1])
+
+    def each(self, action):
+        action(1)
+
+        @pl.when(jnp.logical_not(self.home))
+        def _():
+            action(0)
+
+    def start_z(self, item):
+        @pl.when(self.home)
+        def _():
+            self.z_copy(item, 1).start()
+
+        @pl.when(jnp.logical_not(self.home))
+        def _():
+            self.z_copy(item, 0).start()
+
+    def relay_z(self, item):
+        @pl.when(jnp.logical_not(self.home))
+        def _():
+            self.z_copy(item, 0).wait_recv()
+            self.z_copy(item, 1, True).start()
+            self.plane_copy(item, 0, 0).start()
+            self.plane_copy(item, 0, 1).start()
+
+    def own(self, item):
+        @pl.when(self.home)
+        def _():
+            self.own_load(item).start()
+
+    def pass_own(self, item):
+        @pl.when(self.home)
+        def _():
+            self.own_load(item).wait()
+            self.own_store(item).start()
+
+    def wait_own(self, item):
+        @pl.when(self.home)
+        def _():
+            self.own_store(item).wait()
+
+    def start_plane(self, item):
+        self.z_copy(item, 1).wait_recv()
+        self.plane_copy(item, 1, 0).start()
+        self.plane_copy(item, 1, 1).start()
+
+    def forward(self, item):
+        def act(side):
+            self.plane_copy(item, side, 0).wait_recv()
+            self.plane_copy(item, side, 2).start()
+            self.plane_copy(item, side, 1).wait_recv()
+            self.plane_copy(item, side, 3).start()
+
+        self.each(act)
+
+    def finish(self, item):
+        def act(side):
+            self.plane_copy(item, side, 2).wait_recv()
+            self.plane_copy(item, side, 3).wait_recv()
+            self.z_copy(item, side).wait_send()
+            for step in range(4):
+                self.plane_copy(item, side, step).wait_send()
+
+        self.each(act)
+        self.wait_own(item)
+
+
+def gather_kernel(items, weights, outs, send, recv, local, *held, ahead=3):
+    count = len(items)
+    half = len(outs) // 2
+    work = Gather(items, weights, outs[:half], outs[half:], send, recv, local, held)
+    for item in range(count):
+        work.own(item)
+    work.barrier()
+    for item in range(min(ahead, count)):
+        work.start_z(item)
+    for step in range(count + 1):
+        if step < count:
+            work.relay_z(step)
+            if step + ahead < count:
+                work.start_z(step + ahead)
+            work.start_plane(step)
+            work.pass_own(step)
+        if step >= 1:
+            work.forward(step - 1)
+    for item in range(count):
+        work.finish(item)
+
+
+def gather_weights(weights, items, widths, collective_id):
+    depth = weights[0].shape[0]
+    count = len(items)
+
+    def kernel(*refs):
+        gather_kernel(items, refs[:count], refs[count : count + 2 * len(widths)], *refs[count + 2 * len(widths) :])
+
+    shapes = [jax.ShapeDtypeStruct((depth, w), BF16) for w in widths] * 2
+    outs = pl.pallas_call(
+        kernel,
+        in_specs=[pl.BlockSpec(memory_space=pl.ANY)] * count,
+        out_specs=[pl.BlockSpec(memory_space=pl.ANY)] * len(shapes),
+        out_shape=shapes,
+        scratch_shapes=[pltpu.SemaphoreType.DMA((count, 10)), pltpu.SemaphoreType.DMA((count, 10)), pltpu.SemaphoreType.DMA((count, 2))]
+        + [pltpu.VMEM(w.shape, BF16) for w in weights],
+        compiler_params=pltpu.CompilerParams(collective_id=collective_id, has_side_effects=True, vmem_limit_bytes=60 * 1024 * 1024),
+    )(*weights)
+    return [(outs[i], outs[len(widths) + i]) for i in range(len(widths))]
+
+
+class Finish:
+    def __init__(self, plan, parts, raw, outs, small, bufs):
+        q, c, z = lax.axis_index("plane"), lax.axis_index("core"), lax.axis_index("tensor")
+        self.q, self.c = q, c
+        self.home = (z // 2) == c
+        self.by_x = ((q // 2) * 2 + (1 - q % 2), c, z)
+        self.by_y = ((q + 2) % 4, c, z)
+        self.core = (q, 1 - c, z)
+        self.near = (q, c, (z // 2) * 2 + (1 - z % 2))
+        self.far = (q, 1 - c, (z + 2) % 4)
+        self.across = (q, c, (z + 2) % 4)
+        self.plan, self.parts, self.raw, self.outs, self.small = plan, parts, raw, outs, small
+        (self.near_buf, self.far_buf, self.core_buf, self.here_buf, self.total_buf, self.raw_part, self.raw_own, self.raw_first,
+         self.raw_second, self.small_buf, self.small_in, self.send, self.recv, self.raw_send, self.raw_recv, self.small_send,
+         self.small_recv, self.local) = bufs
+
+    def remote(self, src, dst, sems, index, peer):
+        return pltpu.make_async_remote_copy(
+            src_ref=src, dst_ref=dst, send_sem=sems[0].at[index], recv_sem=sems[1].at[index], device_id=peer, device_id_type=MESH)
+
+    def columns(self, item):
+        _, first_a, first_b, size, _, _, at = self.plan[item]
+        return pl.ds(first_a, size), pl.ds(first_b, size), pl.ds(at, size)
+
+    def part(self, item):
+        source = self.plan[item][0]
+        return self.raw_part if source < 0 else self.parts[source]
+
+    def away(self, action):
+        pl.when(jnp.logical_not(self.home))(action)
+
+    def raw_copies(self, item):
+        cols_a, cols_b, _ = self.columns(item)
+        sems = (self.raw_send, self.raw_recv)
+
+        def rows(owner):
+            return pl.ds(pl.multiple_of(owner * 384, 128), 384)
+
+        across = 3 - self.q
+        x, y = self.by_x[0], self.by_y[0]
+        return [
+            self.remote(self.raw.at[rows(x), cols_a], self.raw_first.at[0, :, cols_a], sems, (item, 0), self.by_x),
+            self.remote(self.raw.at[rows(across), cols_a], self.raw_first.at[1, :, cols_a], sems, (item, 1), self.by_x),
+            self.remote(self.raw.at[rows(y), cols_b], self.raw_first.at[0, :, cols_b], sems, (item, 2), self.by_y),
+            self.remote(self.raw.at[rows(across), cols_b], self.raw_first.at[1, :, cols_b], sems, (item, 3), self.by_y),
+        ], [
+            pltpu.make_async_copy(self.raw.at[rows(self.q), cols_a], self.raw_own.at[0, :, cols_a], self.local.at[item, 0]),
+            pltpu.make_async_copy(self.raw.at[rows(y), cols_a], self.raw_own.at[1, :, cols_a], self.local.at[item, 1]),
+            pltpu.make_async_copy(self.raw.at[rows(self.q), cols_b], self.raw_own.at[0, :, cols_b], self.local.at[item, 2]),
+            pltpu.make_async_copy(self.raw.at[rows(x), cols_b], self.raw_own.at[1, :, cols_b], self.local.at[item, 3]),
+        ]
+
+    def raw_second_copies(self, item):
+        cols_a, cols_b, _ = self.columns(item)
+        sems = (self.raw_send, self.raw_recv)
+        return [
+            self.remote(self.raw_own.at[1, :, cols_a], self.raw_second.at[:, cols_a], sems, (item, 4), self.by_y),
+            self.remote(self.raw_own.at[1, :, cols_b], self.raw_second.at[:, cols_b], sems, (item, 5), self.by_x),
+        ]
+
+    def r1(self, item):
+        for group in self.raw_copies(item):
+            for copy in group:
+                copy.start()
+
+    def r2(self, item):
+        remote, own = self.raw_copies(item)
+        for copy in own:
+            copy.wait()
+        for side, cols in enumerate(self.columns(item)[:2]):
+            remote[2 * side + 1].wait_recv()
+            self.raw_own[1, :, cols] = added(self.raw_own[1, :, cols], self.raw_first[1, :, cols])
+            self.raw_second_copies(item)[side].start()
+
+    def r3(self, item):
+        remote, _ = self.raw_copies(item)
+        for side, cols in enumerate(self.columns(item)[:2]):
+            remote[2 * side].wait_recv()
+            self.raw_second_copies(item)[side].wait_recv()
+            total = self.raw_own[0, :, cols].astype(F32) + self.raw_first[0, :, cols].astype(F32) + self.raw_second[:, cols].astype(F32)
+            self.raw_part[:, cols] = total.astype(BF16)
+
+    def near_copy(self, item):
+        _, cols_b, at = self.columns(item)
+        return self.remote(self.part(item).at[:, cols_b], self.near_buf.at[:, self.spot(item)], (self.send, self.recv), (item, 0), self.near)
+
+    def spot(self, item):
+        return pl.ds(self.plan[item][5], self.plan[item][3])
+
+    def far_copy(self, item):
+        spot = self.spot(item)
+        return self.remote(self.here_buf.at[:, spot], self.far_buf.at[:, spot], (self.send, self.recv), (item, 1), self.far)
+
+    def core_copy(self, item, relayed):
+        spot = self.spot(item)
+        source = self.far_buf if relayed else self.here_buf
+        return self.remote(source.at[:, spot], self.core_buf.at[:, spot], (self.send, self.recv), (item, 2), self.core)
+
+    def s1(self, item):
+        self.near_copy(item).start()
+
+    def s2(self, item):
+        spot, cols_a = self.spot(item), self.columns(item)[0]
+        self.near_copy(item).wait_recv()
+        self.here_buf[:, spot] = added(self.part(item)[:, cols_a], self.near_buf[:, spot])
+
+        @pl.when(self.home)
+        def _():
+            self.core_copy(item, False).start()
+
+        @self.away
+        def _():
+            self.far_copy(item).start()
+
+    def s3(self, item):
+        @self.away
+        def _():
+            self.far_copy(item).wait_recv()
+            self.core_copy(item, True).start()
+
+    def plane_copies(self, item):
+        out = self.outs[self.plan[item][4]]
+        at, spot = self.columns(item)[2], self.spot(item)
+        sems = (self.send, self.recv)
+        half = self.c * 192
+
+        def rows(owner, first, size):
+            return pl.ds(pl.multiple_of(owner * 384 + half + first, 32), size)
+
+        mine = self.total_buf.at[pl.ds(pl.multiple_of(half, 32), 192), spot]
+        x, y, across = self.by_x[0], self.by_y[0], 3 - self.q
+        own = out.at[rows(self.q, 0, 192), at]
+        top, low = out.at[rows(x, 0, 96), at], out.at[rows(y, 96, 96), at]
+        return [
+            self.remote(mine, own, sems, (item, 3), self.by_x),
+            self.remote(mine, own, sems, (item, 4), self.by_y),
+            self.remote(top, top, sems, (item, 5), self.by_y),
+            self.remote(low, low, sems, (item, 6), self.by_x),
+        ] + [
+            self.remote(out.at[rows(o, 0, 192), at], out.at[rows(o, 0, 192), at], sems, (item, 7 + i), self.core)
+            for i, o in enumerate((x, y, across))
+        ]
+
+    def own_copy(self, item):
+        out = self.outs[self.plan[item][4]]
+        rows = pl.ds(pl.multiple_of(self.q * 384, 128), 384)
+        return pltpu.make_async_copy(self.total_buf.at[:, self.spot(item)], out.at[rows, self.columns(item)[2]], self.local.at[item, 4])
+
+    def s4(self, item):
+        spot = self.spot(item)
+
+        @pl.when(self.home)
+        def _():
+            self.core_copy(item, False).wait_recv()
+            self.total_buf[:, spot] = added(self.here_buf[:, spot], self.core_buf[:, spot])
+
+        @self.away
+        def _():
+            self.core_copy(item, True).wait_recv()
+            self.total_buf[:, spot] = added(self.far_buf[:, spot], self.core_buf[:, spot])
+
+        self.own_copy(item).start()
+        copies = self.plane_copies(item)
+        copies[0].start()
+        copies[1].start()
+
+    def s5(self, item):
+        copies = self.plane_copies(item)
+        copies[0].wait_recv()
+        copies[2].start()
+        copies[4].start()
+        copies[1].wait_recv()
+        copies[3].start()
+        copies[5].start()
+
+    def s6(self, item):
+        copies = self.plane_copies(item)
+        copies[2].wait_recv()
+        copies[3].wait_recv()
+        copies[6].start()
+
+    def s7(self, item):
+        copies = self.plane_copies(item)
+        self.own_copy(item).wait()
+        for copy in copies[4:]:
+            copy.wait_recv()
+        for copy in copies:
+            copy.wait_send()
+        self.near_copy(item).wait_send()
+
+        @pl.when(self.home)
+        def _():
+            self.core_copy(item, False).wait_send()
+
+        @self.away
+        def _():
+            self.core_copy(item, True).wait_send()
+            self.far_copy(item).wait_send()
+
+        if self.plan[item][0] < 0:
+            for copy in self.raw_copies(item)[0] + self.raw_second_copies(item):
+                copy.wait_send()
+
+    def small_copy(self, turn):
+        peer = (self.core, self.by_x, self.by_y, self.near, self.across)[turn]
+        return self.remote(self.small_buf.at[turn], self.small_in.at[turn], (self.small_send, self.small_recv), turn, peer)
+
+    def small_start(self):
+        self.small_buf[0] = self.small[...]
+        self.small_copy(0).start()
+
+    def small_next(self, turn):
+        self.small_copy(turn).wait_recv()
+        self.small_buf[turn + 1] = self.small_buf[turn] + self.small_in[turn]
+        if turn < 4:
+            self.small_copy(turn + 1).start()
+
+    def small_done(self, out):
+        for turn in range(5):
+            self.small_copy(turn).wait_send()
+        out[...] = self.small_buf[5]
+
+
+def added(left, right):
+    return (left.astype(F32) + right.astype(F32)).astype(BF16)
+
+
+FINISH = (
+    (0, 0, 1024, 1024, 0, 0, 0),
+    (1, 0, 2048, 1024, 1, 1024, 0),
+    (1, 1024, 3072, 1024, 1, 2048, 1024),
+    (2, 0, 384, 384, 2, 3072, 0),
+    (-1, 0, 1152, 384, 3, 3456, 0),
+    (-1, 384, 1536, 384, 3, 3840, 384),
+    (-1, 768, 1920, 384, 3, 4224, 768),
+)
+
+
+def finish_kernel(small, down, gu, out, raw, small_out, o_down, o_gu, o_out, o_qkv, *bufs):
+    work = Finish(FINISH, (down, gu, out), raw, (o_down, o_gu, o_out, o_qkv), small, bufs)
+    greet((work.near, work.far, work.by_x, work.by_y, work.core, work.across))
+    for item in (4, 5, 6):
+        work.r1(item)
+    work.s1(0)
+    work.s1(1)
+    work.small_start()
+    script = (
+        ("s2", 0), ("s1", 2), ("r2", 4), ("s3", 0), ("m", 0),
+        ("s2", 1), ("s1", 3), ("r2", 5), ("s4", 0), ("s3", 1), ("m", 1),
+        ("r2", 6), ("s2", 2), ("r3", 4), ("s1", 4), ("s5", 0), ("s4", 1), ("s3", 2), ("m", 2),
+        ("r3", 5), ("s1", 5), ("s2", 3), ("r3", 6), ("s1", 6), ("s6", 0), ("s5", 1), ("s4", 2), ("s3", 3), ("m", 3),
+        ("s2", 4), ("s6", 1), ("s5", 2), ("s4", 3), ("s3", 4), ("m", 4),
+        ("s2", 5), ("s6", 2), ("s5", 3), ("s4", 4), ("s3", 5),
+        ("s2", 6), ("s6", 3), ("s5", 4), ("s4", 5), ("s3", 6),
+        ("s6", 4), ("s5", 5), ("s4", 6), ("s6", 5), ("s5", 6), ("s6", 6),
+    )
+    for name, item in script:
+        (work.small_next if name == "m" else getattr(work, name))(item)
+    for item in range(len(FINISH)):
+        work.s7(item)
+    work.small_done(small_out)
+
+
+def finish_gradients(small, down, gu, out, raw, collective_id):
+    vmem = pl.BlockSpec(memory_space=pltpu.VMEM)
+    anywhere = pl.BlockSpec(memory_space=pl.ANY)
+    rows, width, count = 384, 4608, len(FINISH)
+    wide = (rows, width)
+    return pl.pallas_call(
+        finish_kernel,
+        in_specs=[vmem] * 4 + [anywhere],
+        out_specs=[vmem] + [anywhere] * 4,
+        out_shape=[jax.ShapeDtypeStruct(small.shape, F32)] + [jax.ShapeDtypeStruct((1536, n), BF16) for n in (1024, 2048, 384, 1152)],
+        scratch_shapes=[pltpu.VMEM(wide, BF16)] * 5
+        + [pltpu.VMEM((rows, 2304), BF16)]
+        + [pltpu.VMEM((2, rows, 2304), BF16)] * 2
+        + [pltpu.VMEM((rows, 2304), BF16)]
+        + [pltpu.VMEM((6,) + small.shape, F32), pltpu.VMEM((5,) + small.shape, F32)]
+        + [pltpu.SemaphoreType.DMA((count, 10))] * 2
+        + [pltpu.SemaphoreType.DMA((count, 6))] * 2
+        + [pltpu.SemaphoreType.DMA((5,))] * 2
+        + [pltpu.SemaphoreType.DMA((count, 5))],
+        compiler_params=pltpu.CompilerParams(collective_id=collective_id, has_side_effects=True, vmem_limit_bytes=60 * 1024 * 1024),
+    )(small, down, gu, out, raw)
 
 
 def rows_dot(lhs, rhs):
     return tn(lhs, rhs).astype(BF16)
-
-
-def unfused(value):
-    return lax.optimization_barrier(value)
 
 
 def make_local(planes, tensors):
@@ -434,12 +886,6 @@
     near_pairs = [
         (spot(q, c, z), spot(q, c, z ^ 1) if is_home(c, z) else spot(q, 1 - c, z ^ 3)) for q in range(planes) for c, z in sides
     ]
-
-    def plane_pairs(flip, away_only):
-        return [(spot(q, c, z), spot(q ^ flip, c, z)) for q in range(planes) for c, z in sides if not (away_only and is_home(c, z))]
-
-    def over_plane(value, flip, away_only=False):
-        return lax.ppermute(value, every, plane_pairs(flip, away_only))
 
     def over_core(value):
         return lax.ppermute(value, "core", [(0, 1), (1, 0)])
@@ -459,96 +905,43 @@
         q, c, z = lax.axis_index("plane"), lax.axis_index("core"), lax.axis_index("tensor")
         own_rows, width = tokens.shape
         home = (z // 2) == c
-        chunk = width // planes
         heads = conv_weight.shape[0]
         wide = w_query.shape[1]
 
-        def place(k):
-            return jnp.bitwise_xor(q, k)
-
-        def cut(value, index, axis):
-            return lax.dynamic_slice_in_dim(value, index * chunk, chunk, axis)
-
-        def turn(value, axis):
-            if not square:
-                return value
-            return jnp.concatenate([cut(value, place(k), axis) for k in BACK], axis=axis)
-
-        def turn_back(value, axis):
-            if not square:
-                return value
-            parts = []
-            for j in range(4):
-                k = place(j)
-                parts.append(cut(value, (k % 2) * 2 + k // 2, axis))
-            return jnp.concatenate(parts, axis=axis)
-
-        def spread(piece, away_only):
-            if not square:
-                return lax.all_gather(piece, "plane", axis=0, tiled=True)
-            half = piece.shape[0] // 2
-            by_x = over_plane(piece, 1, away_only)
-            by_y = over_plane(piece, 2, away_only)
-            top = over_plane(by_x[:half], 2, away_only)
-            low = over_plane(by_y[half:], 1, away_only)
-            return jnp.concatenate([piece, by_y, by_x, top, low], axis=0)
-
-        def collect(parts):
-            piece = jnp.concatenate([cut(p, q, 0) for p in parts], axis=1)
-            second = spread(second_from(piece), False)
-            first = spread(first_from(piece), True)
-            mine = turn(jnp.concatenate(parts, axis=1), 0)
-            return jnp.where(home, mine, first), second
-
-        def reduce(lhs, rhs_first, rhs_second):
-            if square:
-                order = [lhs[:, k * chunk : (k + 1) * chunk] for k in range(4)]
-                other = jnp.concatenate([order[1], order[3]], axis=1)
-                keep = jnp.concatenate([order[0], order[2]], axis=1)
-                recv_a = over_plane(rows_dot(lhs[:, 2 * chunk :], rhs_first), 1)
-                recv_b = over_plane(rows_dot(other, rhs_second), 2)
-                top_a = unfused(rows_dot(lhs[:, : 2 * chunk], rhs_first))
-                top_b = unfused(rows_dot(keep, rhs_second))
-                sum_a = top_a.astype(F32) + recv_a.astype(F32)
-                sum_b = top_b.astype(F32) + recv_b.astype(F32)
-                last_a = over_plane(sum_a[chunk:].astype(BF16), 2)
-                last_b = over_plane(sum_b[chunk:].astype(BF16), 1)
-                part_a = (sum_a[:chunk] + last_a.astype(F32)).astype(BF16)
-                part_b = (sum_b[:chunk] + last_b.astype(F32)).astype(BF16)
-            else:
-                part_a = lax.psum_scatter(rows_dot(lhs, rhs_first), "plane", scatter_dimension=0, tiled=True)
-                part_b = lax.psum_scatter(rows_dot(lhs, rhs_second), "plane", scatter_dimension=0, tiled=True)
-            from_a = first_from(part_a)
-            from_b = second_from(part_b)
-            here = (jnp.where(home, part_a, from_a).astype(F32) + from_b.astype(F32)).astype(BF16)
-            there = over_core(here)
-            total = (here.astype(F32) + there.astype(F32)).astype(BF16)
-            if not square:
-                return lax.all_gather(total, "plane", axis=0, tiled=True).astype(F32)
-            half = chunk // 2
-            mine = spread(lax.dynamic_slice_in_dim(total, c * half, half, 0), False)
-            theirs = over_core(mine)
-            low = jnp.where(c == 0, mine, theirs).reshape(4, half, -1)
-            high = jnp.where(c == 0, theirs, mine).reshape(4, half, -1)
-            whole = jnp.concatenate([low, high], axis=1).reshape(width, -1)
-            return turn_back(whole, 0).astype(F32)
+        def collect_all(weights):
+            groups = ((0, 1, 2), (3,), (4, 5), (6,))
+            if square and tensors == 4:
+                widths = [sum(weights[i].shape[1] for i in group) for group in groups]
+                return gather_weights(weights, GATHERS, widths, 1)
+            pairs = []
+            for group in groups:
+                whole = jnp.concatenate([weights[i] for i in group], axis=1)
+                pairs.append((jnp.where(home, whole, first_from(whole)), second_from(whole)))
+            return pairs
+
+        fused = square and tensors == 4
+
+        def plane_sum(grads):
+            return lax.psum_scatter(grads, "plane", scatter_dimension=0, tiled=True)
+
+        def reduce(part):
+            count = part.shape[1] // 2
+            first, second = part[:, :count], part[:, count:]
+            here = added(first, lax.ppermute(second, "tensor", [(i, i ^ 1) for i in range(tensors)]))
+            here = jnp.where(home, here, first_from(here))
+            total = added(here, over_core(here))
+            return lax.all_gather(total, "plane", axis=0, tiled=True)
 
         small = jnp.concatenate([conv_weight.reshape(-1), head_mix.reshape(-1), gn_gain.reshape(-1)])
         small_first = jnp.where(home, small, first_from(small))
         small_second = second_from(small)
         conv_size, mix_size = conv_weight.size, head_mix.size
 
-        tokens = turn(tokens, 1)
-        teacher = turn(teacher, 1)
-        gain_one = turn(norm1_gain, 0)
-        gain_two = turn(norm2_gain, 0)
+        gain_one, gain_two = norm1_gain, norm2_gain
         own_valid = lax.dynamic_slice_in_dim(valid_mask, z * own_rows, own_rows, 0)
         jj = key_positions(jnp.concatenate([own_valid, over_core(own_valid)]))
 
-        qkv_weights = collect([w_query, w_key, w_value])
-        out_weights = collect([w_out])
-        gu_weights = collect([w_gate, w_up])
-        down_weights = collect([w_down])
+        qkv_weights, out_weights, gu_weights, down_weights = collect_all([w_query, w_key, w_value, w_out, w_gate, w_up, w_down])
 
         def with_partner(value):
             return jnp.concatenate([value, over_core(value)], axis=0)
@@ -589,14 +982,16 @@
             ups.append(up.astype(BF16))
             hiddens.append((jax.nn.silu(gate) * up).astype(BF16))
         final_rows = hidden_in + summed(hiddens, down_weights)
-        output = turn_back(final_rows.astype(BF16), 1)
+        output = final_rows.astype(BF16)
         own_mask = own_valid.astype(F32)
         error = own_mask[:, None] * (final_rows - teacher.astype(F32))
         squared_sum = jnp.sum(error * error)
         count_sum = jnp.sum(own_mask)
 
         d_all = with_partner(error.astype(BF16))
-        grad_down = reduce(d_all, hiddens[0], hiddens[1])
+        down_grads = rows_dot(d_all, jnp.concatenate(hiddens, axis=1))
+        down_grads, d_all = lax.optimization_barrier((down_grads, d_all))
+        down_part = plane_sum(down_grads)
         d_gus = []
         for index, weight in enumerate(down_weights):
             d_hidden = nn(d_all, weight)
@@ -605,7 +1000,9 @@
             d_gate = (d_hidden * up * s * (1.0 + gate * (1.0 - s))).astype(BF16)
             d_up = (d_hidden * gate * s).astype(BF16)
             d_gus.append(jnp.concatenate([d_gate, d_up], axis=1))
-        grad_gu = reduce(normed_two, d_gus[0], d_gus[1])
+        gu_grads = rows_dot(normed_two, jnp.concatenate(d_gus, axis=1))
+        gu_grads, d_gus = lax.optimization_barrier((gu_grads, d_gus))
+        gu_part = plane_sum(gu_grads)
         d_normed_two = summed(d_gus, gu_weights)
         scaled_two = d_normed_two * gain_two
         grad_gain_two = jnp.sum(d_normed_two * hidden_in * inv_two, axis=0)
@@ -613,29 +1010,43 @@
             error + inv_two * scaled_two - hidden_in * inv_two**3 * jnp.mean(scaled_two * hidden_in, axis=-1, keepdims=True)
         )
         d_attn = with_partner(d_hidden_in.astype(BF16))
-        grad_out = reduce(d_attn, heads_out[0], heads_out[1])
+        out_grads = rows_dot(d_attn, jnp.concatenate(heads_out, axis=1))
+        out_grads, d_attn = lax.optimization_barrier((out_grads, d_attn))
+        out_part = plane_sum(out_grads)
         d_qkv, small_grads = [], []
         for index, (mix, toep, gains) in enumerate(sides_small):
             d_normed = nn(d_attn, out_weights[index])
+            if index == 0:
+                d_normed, down_part = lax.optimization_barrier((d_normed, down_part))
+            else:
+                d_normed, gu_part = lax.optimization_barrier((d_normed, gu_part))
             dqkv, ggn, gmix, gconv = attention_backward(mix, qkv[index], toep, gains, jj, d_normed, saved[index])
             d_qkv.append(dqkv)
             small_grads.append(jnp.concatenate([conv_grads(gconv).reshape(-1), mix_grads(gmix).reshape(-1), ggn[0]]))
-        grad_qkv = reduce(normed_one, d_qkv[0], d_qkv[1])
+        qkv_grads = rows_dot(normed_one, jnp.concatenate(d_qkv, axis=1))
         d_normed_one = summed(d_qkv, qkv_weights)
         scaled_one = d_normed_one * gain_one
         grad_gain_one = jnp.sum(d_normed_one * inputs * inv_one, axis=0)
         grad_input = (
             d_hidden_in + inv_one * scaled_one - inputs * inv_one**3 * jnp.mean(scaled_one * inputs, axis=-1, keepdims=True)
         )
-        grad_input = turn_back(grad_input, 1)
 
         table = jnp.zeros((tensors, small.size), F32)
         table = lax.dynamic_update_slice(table, small_grads[0][None], (2 * c + z % 2, 0))
         table = lax.dynamic_update_slice(table, small_grads[1][None], (2 * c + 1 - z % 2, 0))
         packed = jnp.concatenate(
-            [table.reshape(-1), turn_back(grad_gain_one, 0), turn_back(grad_gain_two, 0), squared_sum[None], count_sum[None]]
+            [table.reshape(-1), grad_gain_one, grad_gain_two, squared_sum[None], count_sum[None]]
         )
-        packed = lax.psum(packed, every)
+        if fused:
+            length = packed.size
+            lines = -(-length // 1024) * 8
+            packed = jnp.pad(packed, (0, lines * 128 - length)).reshape(lines, 128)
+            packed, *sums = finish_gradients(packed, down_part, gu_part, out_part, qkv_grads, 2)
+            packed = packed.reshape(-1)[:length]
+        else:
+            packed = lax.psum(packed, every)
+            sums = [reduce(part) for part in (down_part, gu_part, out_part, plane_sum(qkv_grads))]
+        grad_down, grad_gu, grad_out, grad_qkv = [value.astype(F32) for value in sums]
         table_size = tensors * small.size
         small_sum = lax.dynamic_slice_in_dim(packed, z * small.size, small.size, 0)
         gain_slice = width // tensors

time: 1240 us -> 904 us (0.73)
  Pallas kernels: 172 us -> 467 us
  waiting for transfers between devices: 248 us -> 38.7 us
  starting transfers between devices: 246 us -> 60.5 us
  local copies, waits for them, and re-layouts: 143 us -> 56.2 us
  other arithmetic: 147 us -> 70.8 us
  blocking collectives: 75.8 us -> 0 us
    pallas_call x0 -> x2, Pallas kernels: none -> 295 us  [the longest x1 149 us: finish_gradients(): pl.pallas_call(finish_kernel, in_specs=[vmem] * 4 + [anywhere], out_specs...]
    ppermute x64 -> x0, waiting for transfers between devices: 232 us -> none  [over_plane(): return lax.ppermute(value, every, plane_pairs(flip, away_only))]
    ppermute x17 -> x9, starting transfers between devices: 154 us -> 56.4 us  [over_core(): return lax.ppermute(value, 'core', [(0, 1), (1, 0)])]
    psum x1 -> x0, blocking collectives: 75.8 us -> none  [local(): packed = lax.psum(packed, every)]
    ppermute x64 -> x0, starting transfers between devices: 74.6 us -> none  [over_plane(): return lax.ppermute(value, every, plane_pairs(flip, away_only))]
    unnamed x389 -> x166, local copies, waits for them, and re-layouts: 51.4 us -> 14.9 us
    reduce_scatter x0 -> x3, waiting for transfers between devices: none -> 25.1 us  [plane_sum(): return lax.psum_scatter(grads, 'plane', scatter_dimension=0, tiled=True)]
    convert_element_type x17 -> x2, other arithmetic: 26.1 us -> 5.49 us  [local(): value.astype(F32)]
  transfers between devices with their start and end apart: 99 -> 14, of which waited for: 30 -> 6; matrix products, arithmetic and copies ran while one was open for 30% -> 22% of each run, Pallas kernels for 14% -> 27%
where the time goes in v2:
time: 904 us; the launch traced here: 898 us
  Pallas kernels  467 us (52%)
  matrix products  187 us (21%)
  other arithmetic  70.8 us (8%)
  starting transfers between devices  60.5 us (7%)
  local copies, waits for them, and re-layouts  56.2 us (6%)
  waiting for transfers between devices  38.7 us (4%)
  between operations  18.5 us (2%)
    pallas_call x1, Pallas kernels, finish_gradients(): pl.pallas_call(finish_kernel, in_specs=[vmem] * 4 + [anywhere], out_specs...  149 us
    pallas_call x1, Pallas kernels, gather_weights(): pl.pallas_call(kernel, in_specs=[pl.BlockSpec(memory_space=pl.ANY)] * cou...  146 us
    pallas_call x2, Pallas kernels, attention_backward(): pl.pallas_call(bwd_kernel, grid=(trees, 2), in_specs=common_specs() + [pl...  101 us
    dot_general x16, matrix products, nt(): lax.dot_general(a, b, (((1,), (1,)), ((), ())), preferred_element_type=F32)  73.2 us
    pallas_call x2, Pallas kernels, attention_forward(): pl.pallas_call(fwd_kernel, grid=(trees, 2), in_specs=common_specs(), out_...  71.3 us
    dot_general x8, matrix products, nn(): lax.dot_general(a, b, (((1,), (0,)), ((), ())), preferred_element_type=F32)  56.8 us
    dot_general x4, matrix products, tn(): lax.dot_general(a, b, (((0,), (0,)), ((), ())), preferred_element_type=F32)  56.6 us
    ppermute x9, starting transfers between devices, over_core(): return lax.ppermute(value, 'core', [(0, 1), (1, 0)])  56.4 us
  transfers between devices with their start and end apart: 14, of which 6 were waited for; matrix products, arithmetic and copies ran while one was open for 22% of the time, Pallas kernels for 27%

profile of v2, /device:TPU:0, one launch (start us, length us, event | category | flops | bytes accessed | tf_op | source)
XLA Modules:
  0.0 898.4 jit_solution(3073332536062987498)
XLA Ops:
  10.9 3.1 collective-permute-start.3
  17.1 3.2 fusion.31
  20.3 3.4 collective-permute-start.1
  31.7 145.8 %shard_map.262 = (bf16[1536,1152]{1,0:T(8,128)(2,1)}, bf16[1536,384]{1,0:T(8,128)(2,1)}, bf16[1536,2048]{1,0:T(8,128)(2,1)}, bf16[1536,1024]{1,0:T(8,128)(2,1)},...) custom-call(bf16[1536,384]{1,0:T(8,128)(2,1)} %refs_0_.1, ...), custom_call_target="tpu_custom_call" | custom-call | tf_op jit(solution)/shard_map/pallas_call | solution.py:573
  191.2 12.0 %add_convert_fusion.1.t_ref = bf16[2,2,1536,256]{3,2,1,0:T(8,128)(2,1)} fusion(f32[2,2,1536]{2,1,0:T(2,128)S(1)} %mul.1007, f32[1536,256]{1,0:T(8,128)S(1)} %bitcast.70, f32[2,2,1536]{2,1,0:T(2,128)S(1)} %mul.998, f32[1536,256]{1,0:T(8,128)S(1)} %bitcast.72, f32[2,2,1536]{2,1,0:T(2,128)S(1)} %mul.989, f32[1536,256]{1,0:T(8,128)S(1)} %bitcast.74, ...), kind=kLoop, calls=%fused_computation.25 | loop fusion | flops 34603008 | bytes 20717568 | tf_op jit(solution)/shard_map/convert_element_type | solution.py:378
  208.0 13.4 %add_convert_fusion.t_ref = bf16[2,2,1536,256]{3,2,1,0:T(8,128)(2,1)} fusion(f32[2,2,1536]{2,1,0:T(2,128)S(1)} %mul.1074, f32[2,2,1536]{2,1,0:T(2,128)S(1)} %mul.1068, f32[2,2,1536]{2,1,0:T(2,128)S(1)} %mul.1062, f32[2,2,1536]{2,1,0:T(2,128)S(1)} %mul.1056, f32[2,2,1536]{2,1,0:T(2,128)S(1)} %mul.1050, f32[2,2,1536]{2,1,0:T(2,128)S(1)} %mul.1044, ...), kind=kLoop, calls=%fused_computation.24 | loop fusion | flops 34603008 | bytes 20717568 | tf_op jit(solution)/shard_map/convert_element_type | solution.py:378
  221.4 8.3 convolution_convert_fusion.4.qkv_ref
  230.4 35.7 %shard_map.263 = (bf16[1152,384]{1,0:T(8,128)(2,1)}, f32[2,2,2,576,256]{4,3,2,1,0:T(8,128)}, bf16[2,2,2,576,1536]{4,3,2,1,0:T(8,128)(2,1)}, bf16[2,2,2,6,576,256]{5,4,3,2,1,0:T(8,128)(2,1)}, f32[2,2,576,256]{3,2,1,0:T(8,128)}) custom-call(f32[8]{0:T(128)} %slice.244.mix_ref, bf16[1152,1152]{1,0:T(8,128)(2,1)} %convolution_convert_fusion.4.qkv_ref, ...), custom_call_target="tpu_custom_call" | custom-call | flops 40000000000 | bytes 60000000 | tf_op jit(solution)/shard_map/pallas_call | solution.py:325
  266.1 2.7 fusion.61
  268.7 8.3 convolution_convert_fusion.3.qkv_ref
  277.7 35.6 %shard_map.264 = (bf16[1152,384]{1,0:T(8,128)(2,1)}, f32[2,2,2,576,256]{4,3,2,1,0:T(8,128)}, bf16[2,2,2,576,1536]{4,3,2,1,0:T(8,128)(2,1)}, bf16[2,2,2,6,576,256]{5,4,3,2,1,0:T(8,128)(2,1)}, f32[2,2,576,256]{3,2,1,0:T(8,128)}) custom-call(f32[8]{0:T(128)} %slice.272.mix_ref, bf16[1152,1152]{1,0:T(8,128)(2,1)} %convolution_convert_fusion.3.qkv_ref, ...), custom_call_target="tpu_custom_call" | custom-call | flops 40000000000 | bytes 60000000 | tf_op jit(solution)/shard_map/pallas_call | solution.py:325
  313.3 2.7 add_convert_fusion.5
  316.0 51.3 %collective-permute-start.4 = (bf16[576,1536]{1,0:T(8,128)(2,1)S(1)}, bf16[576,1536]{1,0:T(8,128)(2,1)S(1)}, u32[]{:S(2)}, u32[]{:S(2)}) collective-permute-start(bf16[576,1536]{1,0:T(8,128)(2,1)S(1)} %add_convert_fusion.5), channel_id=1, source_target_pairs={{0,4},{4,0},{1,5},{5,1},{2,6},{6,2},{3,7},{7,3},{8,12},{12,8},{9,1... | collective-permute-start | bytes 5308424 | tf_op jit(solution)/shard_map/ppermute | solution.py:891
  373.6 3.3 collective-permute-done.5
  376.9 7.5 fusion.58
  388.0 7.5 fusion.59
  397.6 2.3 copy-done.14
  407.7 4.5 fusion.122
  412.6 3.3 collective-permute-done.7
  417.1 10.3 %convolution_convert_fusion.2 = bf16[1536,2048]{1,0:T(8,128)(2,1)} fusion(bf16[1152,1024]{1,0:T(8,128)(2,1)S(1)} %multiply_convert_fusion, bf16[1152,1024]{1,0:T(8,128)(2,1)S(1)} %multiply_convert_fusion.1, bf16[576,1536]{1,0:T(8,128)(2,1)S(1)} %collective-permute-done.7, bf16[576,1536]{1,0:T(8,128)(2,1)S(1)} %get-tuple-element.209), kind=kOutput, calls=%fused_computation.15 | convolution fusion | flops 7267418112 | bytes 14548992 | tf_op jit(solution)/shard_map/dot_general | solution.py:44
  427.4 4.0 pad_maximum_fusion.4
  431.7 10.8 %fusion.15 = (bf16[1152,1024]{1,0:T(8,128)(2,1)S(1)}, bf16[1152,1024]{1,0:T(8,128)(2,1)S(1)}) fusion(f32[1152,2048]{1,0:T(8,128)} %copy-done.14, bf16[1152,1536]{1,0:T(8,128)(2,1)} %pad_maximum_fusion.4, bf16[1536,1024]{1,0:T(8,128)(2,1)} %get-tuple-element.64), kind=kOutput, calls=%fused_computation.34 | convolution fusion | flops 3641573376 | bytes 16121856 | tf_op jit(solution)/shard_map/dot_general | solution.py:36
  442.6 2.7 pad_maximum_fusion
  448.8 7.9 fusion.23
  458.9 2.6 pad_maximum_fusion.1
  461.5 24.4 %convolution_convert_fusion = bf16[1536,4096]{1,0:T(8,128)(2,1)} fusion(bf16[1152,1024]{1,0:T(8,128)(2,1)} %copy-done.30, bf16[1152,1024]{1,0:T(8,128)(2,1)} %copy-done.29, bf16[1152,1024]{1,0:T(8,128)(2,1)} %copy-done.28, bf16[1152,1024]{1,0:T(8,128)(2,1)} %copy-done.27, bf16[576,1536]{1,0:T(8,128)(2,1)} %copy-done.68, bf16[576,1536]{1,0:T(8,128)(2,1)} %copy-done.32), kind=kOutput, calls=%fused_computation | convolution fusion | flops 14546632704 | bytes 25559040 | tf_op jit(solution)/shard_map/dot_general | solution.py:44
  486.0 7.1 fusion.38
  493.1 8.8 add_convert_fusion.3
  502.1 5.7 fusion.41
  507.9 9.5 %multiply_reduce_fusion.1 = (f32[1536]{0:T(1024)}, f32[576]{0:T(1024)S(1)}, f32[576,1536]{1,0:T(8,128)S(1)}) fusion(f32[576,1536]{1,0:T(8,128)S(1)} %get-tuple-element.208, f32[576]{0:T(1024)S(1)} %get-tuple-element.193, f32[1536]{0:T(1024)S(1)} %copy-done.51, bf16[576,1536]{1,0:T(8,128)(2,1)} %collective-permute-done.8, f32[576,1536]{1,0:T(8,128)} %fusion.41, ...), kind=kOutput, calls=%fused_computation.69 | convolution fusion | flops 3631839232 | bytes 21057792 | tf_op jit(solution)/shard_map/dot_general | solution.py:40
  517.4 5.0 fusion.123
  522.8 3.5 collective-permute-done.9
  526.3 6.9 convolution_convert_fusion.5
  535.0 3.2 fusion.128.dn_ref
  538.3 3.2 fusion.129.dn_ref
  541.5 50.7 %shard_map.265 = (bf16[1152,1152]{1,0:T(8,128)(2,1)}, f32[8,384]{1,0:T(8,128)}, f32[2,2,8,256]{3,2,1,0:T(8,128)}, f32[2,2,2,8,256]{4,3,2,1,0:T(8,128)}) custom-call(f32[8]{0:T(128)} %slice.244.mix_ref, bf16[1152,1152]{1,0:T(8,128)(2,1)} %convolution_convert_fusion.4.qkv_ref, bf16[2,2,1536,256]{3,2,1,0:T(8,128)(2,1)} %add_convert_fusion.1.t_ref, ...), custom_call_target="tpu_custom_call" | custom-call | flops 80000000000 | bytes 60000000 | tf_op jit(solution)/shard_map/pallas_call | solution.py:340
  592.3 5.7 fusion.47
  598.0 4.3 fusion.50
  603.6 25.0 %reduce-scatter.6.cloned.1.call-done.gu = bf16[384,4096]{1,0:T(8,128)(2,1)} async-done(((bf16[1536,4096]{1,0:T(8,128)(2,1)}), bf16[384,4096]{1,0:T(8,128)(2,1)}) %reduce-scatter.6.cloned.1.call-update) | async-done | bytes 3145744 | tf_op jit(solution)/shard_map/reduce_scatter | solution.py:925
  628.7 49.9 %shard_map.266 = (bf16[1152,1152]{1,0:T(8,128)(2,1)}, f32[8,384]{1,0:T(8,128)}, f32[2,2,8,256]{3,2,1,0:T(8,128)}, f32[2,2,2,8,256]{4,3,2,1,0:T(8,128)}) custom-call(f32[8]{0:T(128)} %slice.272.mix_ref, bf16[1152,1152]{1,0:T(8,128)(2,1)} %convolution_convert_fusion.3.qkv_ref, bf16[2,2,1536,256]{3,2,1,0:T(8,128)(2,1)} %add_convert_fusion.t_ref, ...), custom_call_target="tpu_custom_call" | custom-call | flops 80000000000 | bytes 60000000 | tf_op jit(solution)/shard_map/pallas_call | solution.py:340
  678.6 7.2 add_convert_fusion.2
  687.3 14.9 %convolution_convert_fusion.1.raw = bf16[1536,2304]{1,0:T(8,128)(2,1)} fusion(bf16[1152,1152]{1,0:T(8,128)(2,1)} %get-tuple-element.90, bf16[1152,1152]{1,0:T(8,128)(2,1)} %get-tuple-element.89, bf16[576,1536]{1,0:T(8,128)(2,1)} %collective-permute-done.1, bf16[576,1536]{1,0:T(8,128)(2,1)} %fusion.31), kind=kOutput, calls=%fused_computation.1 | convolution fusion | flops 8174960640 | bytes 15925248 | tf_op jit(solution)/shard_map/dot_general | solution.py:44
  702.3 6.3 fusion.36
  710.6 149.4 %shard_map.267 = (f32[48,128]{1,0:T(8,128)}, bf16[1536,1024]{1,0:T(8,128)(2,1)}, bf16[1536,2048]{1,0:T(8,128)(2,1)}, bf16[1536,384]{1,0:T(8,128)(2,1)}, bf16[1536,1152]{1,0:T(8,128)(2,1)}) custom-call(f32[48,128]{1,0:T(8,128)} %pad_bitcast_fusion.small, bf16[384,2048]{1,0:T(8,128)(2,1)} %reduce-scatter.4.cloned.1.call-done.down, ...), custom_call_target="tpu_custom_call" | custom-call | tf_op jit(solution)/shard_map/pallas_call | solution.py:853
  862.3 5.2 fusion.125
  871.1 9.3 %fusion.124 = (f32[1536,1024]{1,0:T(8,128)}, f32[1536,1024]{1,0:T(8,128)}) fusion(bf16[1536,2048]{1,0:T(8,128)(2,1)} %get-tuple-element.97), kind=kLoop, calls=%fused_computation.244 | loop fusion | bytes 25165824 | tf_op jit(solution)/shard_map/slice | solution.py:1070
  880.4 3.9 convert_element_type.171
  887.5 2.7 fusion.35
  (351 shorter events, 75.5 us)
Async XLA Ops:
  7.2 534.4 %reduce-scatter.4.cloned.1.call-start = ((), (), s32[]{:S(2)}) async-start(), calls=%async_computation.3 | async-start | bytes 7864320 | tf_op jit(solution)/shard_map/reduce_scatter | solution.py:925
  10.2 169.1 %collective-permute-start = (f32[656]{0:T(1024)}, f32[656]{0:T(1024)S(1)}, u32[]{:S(2)}, u32[]{:S(2)}) collective-permute-start(f32[656]{0:T(1024)} %pad_maximum_fusion.12), channel_id=1, source_target_pairs={{2,4},{3,5},{4,2},{5,3},{10,12},{11,13},{12,10},{13,11},{18,20},{1... | collective-permute-start | bytes 7880 | tf_op jit(solution)/shard_map/ppermute | solution.py:894
  10.9 193.0 %collective-permute-start.3 = (f32[656]{0:T(1024)}, f32[656]{0:T(1024)}, u32[]{:S(2)}, u32[]{:S(2)}) collective-permute-start(f32[656]{0:T(1024)} %pad_maximum_fusion.12), channel_id=1, source_target_pairs={{0,1},{1,0},{2,5},{3,4},{4,3},{5,2},{6,7},{7,6},{8,9},{9,8},{10,13... | collective-permute-start | bytes 7880 | tf_op jit(solution)/shard_map/ppermute | solution.py:897
  20.3 201.2 %collective-permute-start.1 = (bf16[576,1536]{1,0:T(8,128)(2,1)}, bf16[576,1536]{1,0:T(8,128)(2,1)}, u32[]{:S(2)}, u32[]{:S(2)}) collective-permute-start(bf16[576,1536]{1,0:T(8,128)(2,1)} %fusion.31), channel_id=1, source_target_pairs={{0,4},{4,0},{1,5},{5,1},{2,6},{6,2},{3,7},{7,3},{8,12},{12,8},{9,1... | collective-permute-start | bytes 5308424 | tf_op jit(solution)/shard_map/ppermute | solution.py:891
  25.0 152.5 %copy-start.47 = (s32[576]{0:T(1024)}, s32[576]{0:T(1024)S(1)}, u32[]{:S(2)}) copy-start(s32[576]{0:T(1024)S(1)} %get-tuple-element.156) | copy-start | bytes 6916
  25.0 152.4 %collective-permute-start.2 = (s32[576]{0:T(1024)S(1)}, s32[576]{0:T(1024)S(1)}, u32[]{:S(2)}, u32[]{:S(2)}) collective-permute-start(s32[576]{0:T(1024)S(1)} %get-tuple-element.156), channel_id=1, source_target_pairs={{0,4},{4,0},{1,5},{5,1},{2,6},{6,2},{3,7},{7,3},{8,12},{12,8},{9,1... | collective-permute-start | bytes 6920 | tf_op jit(solution)/shard_map/ppermute | solution.py:891
  189.1 14.1 %copy-start.7 = (f32[6,256,256]{2,1,0:T(8,128)}, f32[6,256,256]{2,1,0:T(8,128)S(1)}, u32[]{:S(2)}) copy-start(f32[6,256,256]{2,1,0:T(8,128)S(1)} %mul.938) | copy-start | bytes 4718596
  189.8 13.4 %copy-start.8 = (f32[6,256,256]{2,1,0:T(8,128)}, f32[6,256,256]{2,1,0:T(8,128)S(1)}, u32[]{:S(2)}) copy-start(f32[6,256,256]{2,1,0:T(8,128)S(1)} %mul.929) | copy-start | bytes 4718596
  190.0 13.2 %copy-start.9 = (f32[6,256,256]{2,1,0:T(8,128)}, f32[6,256,256]{2,1,0:T(8,128)S(1)}, u32[]{:S(2)}) copy-start(f32[6,256,256]{2,1,0:T(8,128)S(1)} %mul.920) | copy-start | bytes 4718596
  190.2 13.0 %copy-start.10 = (f32[6,256,256]{2,1,0:T(8,128)}, f32[6,256,256]{2,1,0:T(8,128)S(1)}, u32[]{:S(2)}) copy-start(f32[6,256,256]{2,1,0:T(8,128)S(1)} %mul.911) | copy-start | bytes 4718596
  191.2 12.1 %copy-start.56 = (f32[656]{0:T(1024)S(1)}, f32[656]{0:T(1024)}, u32[]{:S(2)}) copy-start(f32[656]{0:T(1024)} %copy-done.55) | copy-start | bytes 7876
  208.0 13.4 %copy-start.64 = (bf16[1536,1152]{1,0:T(8,128)(2,1)S(1)}, bf16[1536,1152]{1,0:T(8,128)(2,1)}, u32[]{:S(2)}) copy-start(bf16[1536,1152]{1,0:T(8,128)(2,1)} %get-tuple-element.57) | copy-start | bytes 10616836
  313.3 54.0 %copy-start.18 = (bf16[1536,384]{1,0:T(8,128)(2,1)S(1)}, bf16[1536,384]{1,0:T(8,128)(2,1)}, u32[]{:S(2)}) copy-start(bf16[1536,384]{1,0:T(8,128)(2,1)} %get-tuple-element.59) | copy-start | bytes 3538948
  313.3 54.0 %copy-start.40 = (bf16[1152,384]{1,0:T(8,128)(2,1)S(1)}, bf16[1152,384]{1,0:T(8,128)(2,1)}, u32[]{:S(2)}) copy-start(bf16[1152,384]{1,0:T(8,128)(2,1)} %get-tuple-element.58) | copy-start | bytes 2654212
  316.0 54.6 %copy-start = (bf16[576,1536]{1,0:T(8,128)(2,1)S(1)}, bf16[576,1536]{1,0:T(8,128)(2,1)}, u32[]{:S(2)}) copy-start(bf16[576,1536]{1,0:T(8,128)(2,1)} %param.15) | copy-start | bytes 5308420
  316.0 54.6 %copy-start.20 = (bf16[1536,384]{1,0:T(8,128)(2,1)S(1)}, bf16[1536,384]{1,0:T(8,128)(2,1)}, u32[]{:S(2)}) copy-start(bf16[1536,384]{1,0:T(8,128)(2,1)} %get-tuple-element.62) | copy-start | bytes 3538948
  316.0 54.6 %copy-start.41 = (bf16[1152,384]{1,0:T(8,128)(2,1)S(1)}, bf16[1152,384]{1,0:T(8,128)(2,1)}, u32[]{:S(2)}) copy-start(bf16[1152,384]{1,0:T(8,128)(2,1)} %get-tuple-element.61) | copy-start | bytes 2654212
  316.0 54.6 %collective-permute-start.4 = (bf16[576,1536]{1,0:T(8,128)(2,1)S(1)}, bf16[576,1536]{1,0:T(8,128)(2,1)S(1)}, u32[]{:S(2)}, u32[]{:S(2)}) collective-permute-start(bf16[576,1536]{1,0:T(8,128)(2,1)S(1)} %add_convert_fusion.5), channel_id=1, source_target_pairs={{0,4},{4,0},{1,5},{5,1},{2,6},{6,2},{3,7},{7,3},{8,12},{12,8},{9,1... | collective-permute-start | bytes 5308424 | tf_op jit(solution)/shard_map/ppermute | solution.py:891
  367.3 9.6 %slice-start.4 = ((s8[6291456]{0:T(1024)(128)(4,1)}), s8[4194304]{0:T(1024)(128)(4,1)S(1)}, s32[]{:S(2)}) async-start(s8[6291456]{0:T(1024)(128)(4,1)} %bitcast.99), calls=%async_computation.10 | async-start | bytes 8388608
  372.8 15.3 %slice-start.6 = ((s8[6291456]{0:T(1024)(128)(4,1)}), s8[4194304]{0:T(1024)(128)(4,1)S(1)}, s32[]{:S(2)}) async-start(s8[6291456]{0:T(1024)(128)(4,1)} %bitcast.101), calls=%async_computation.12 | async-start | bytes 8388608
  373.1 14.9 %copy-start.32 = (bf16[576,1536]{1,0:T(8,128)(2,1)}, bf16[576,1536]{1,0:T(8,128)(2,1)S(1)}, u32[]{:S(2)}) copy-start(bf16[576,1536]{1,0:T(8,128)(2,1)S(1)} %multiply_convert_fusion.2) | copy-start | bytes 5308420
  373.1 3.8 collective-permute-start.5
  376.9 11.1 %copy-start.68 = (bf16[576,1536]{1,0:T(8,128)(2,1)}, bf16[576,1536]{1,0:T(8,128)(2,1)S(1)}, u32[]{:S(2)}) copy-start(bf16[576,1536]{1,0:T(8,128)(2,1)S(1)} %collective-permute-done.5) | copy-start | bytes 5308420
  376.9 11.1 %slice-start.7 = ((s8[6291456]{0:T(1024)(128)(4,1)}), s8[2097152]{0:T(1024)(128)(4,1)S(1)}, s32[]{:S(2)}) async-start(s8[6291456]{0:T(1024)(128)(4,1)} %bitcast.101), calls=%async_computation.13 | async-start | bytes 4194304
  404.0 3.8 collective-permute-start.6
  412.2 3.7 collective-permute-start.7
  431.5 197.2 %reduce-scatter.6.cloned.1.call-start = ((), (), s32[]{:S(2)}) async-start(), calls=%async_computation.4 | async-start | bytes 15728640 | tf_op jit(solution)/shard_map/reduce_scatter | solution.py:925
  485.9 224.7 %reduce-scatter.8.cloned.1.call-start = ((), (), s32[]{:S(2)}) async-start(), calls=%async_computation.5 | async-start | bytes 2949120 | tf_op jit(solution)/shard_map/reduce_scatter | solution.py:925
  486.0 16.1 %slice-start.2 = ((s8[4718592]{0:T(1024)(128)(4,1)}), s8[4194304]{0:T(1024)(128)(4,1)S(1)}, s32[]{:S(2)}) async-start(s8[4718592]{0:T(1024)(128)(4,1)} %bitcast.94), calls=%async_computation.8 | async-start | bytes 8388608
  486.0 16.1 %slice-start.8 = ((s8[6291456]{0:T(1024)(128)(4,1)}), s8[4194304]{0:T(1024)(128)(4,1)S(1)}, s32[]{:S(2)}) async-start(s8[6291456]{0:T(1024)(128)(4,1)} %bitcast.103), calls=%async_computation.14 | async-start | bytes 8388608
  486.0 21.8 %slice-start = ((s8[4718592]{0:T(1024)(128)(4,1)}), s8[4194304]{0:T(1024)(128)(4,1)S(1)}, s32[]{:S(2)}) async-start(s8[4718592]{0:T(1024)(128)(4,1)} %bitcast.92), calls=%async_computation.6 | async-start | bytes 8388608
  493.1 9.0 slice-start.3
  493.1 9.0 slice-start.9
  493.1 14.7 %slice-start.1 = ((s8[4718592]{0:T(1024)(128)(4,1)}), s8[524288]{0:T(1024)(128)(4,1)S(1)}, s32[]{:S(2)}) async-start(s8[4718592]{0:T(1024)(128)(4,1)} %bitcast.92), calls=%async_computation.7 | async-start | bytes 1048576
  501.9 5.9 collective-permute-start.8
  507.8 9.5 %copy-start.12 = (f32[576,1536]{1,0:T(8,128)S(1)}, f32[576,1536]{1,0:T(8,128)}, u32[]{:S(2)}) copy-start(f32[576,1536]{1,0:T(8,128)} %get-tuple-element.210) | copy-start | bytes 10616836
  507.8 9.5 %copy-start.16 = (bf16[576,1536]{1,0:T(8,128)(2,1)S(1)}, bf16[576,1536]{1,0:T(8,128)(2,1)}, u32[]{:S(2)}) copy-start(bf16[576,1536]{1,0:T(8,128)(2,1)} %param.16) | copy-start | bytes 5308420
  507.8 9.5 %copy-start.54 = (f32[576]{0:T(1024)S(1)}, f32[576]{0:T(1024)}, u32[]{:S(2)}) copy-start(f32[576]{0:T(1024)} %get-tuple-element.192) | copy-start | bytes 6916
  522.4 3.9 collective-permute-start.9
  541.5 50.7 %copy-start.65 = (bf16[1536,1152]{1,0:T(8,128)(2,1)S(1)}, bf16[1536,1152]{1,0:T(8,128)(2,1)}, u32[]{:S(2)}) copy-start(bf16[1536,1152]{1,0:T(8,128)(2,1)} %get-tuple-element.57) | copy-start | bytes 10616836
  685.8 16.4 %collective-permute-start.10 = (bf16[576,1536]{1,0:T(8,128)(2,1)}, bf16[576,1536]{1,0:T(8,128)(2,1)}, u32[]{:S(2)}, u32[]{:S(2)}) collective-permute-start(bf16[576,1536]{1,0:T(8,128)(2,1)} %add_convert_fusion.2), channel_id=1, source_target_pairs={{0,4},{4,0},{1,5},{5,1},{2,6},{6,2},{3,7},{7,3},{8,12},{12,8},{9,1... | collective-permute-start | bytes 5308424 | tf_op jit(solution)/shard_map/ppermute | solution.py:891
  687.2 15.0 %copy-start.1 = (bf16[576,1536]{1,0:T(8,128)(2,1)S(1)}, bf16[576,1536]{1,0:T(8,128)(2,1)}, u32[]{:S(2)}) copy-start(bf16[576,1536]{1,0:T(8,128)(2,1)} %param.15) | copy-start | bytes 5308420
  687.2 15.0 %copy-start.50 = (f32[576]{0:T(1024)S(1)}, f32[576]{0:T(1024)}, u32[]{:S(2)}) copy-start(f32[576]{0:T(1024)} %copy-done.49) | copy-start | bytes 6916
  687.2 15.0 %copy-start.52 = (f32[1536]{0:T(1024)S(1)}, f32[1536]{0:T(1024)}, u32[]{:S(2)}) copy-start(f32[1536]{0:T(1024)} %param.18) | copy-start | bytes 18436
  687.2 15.0 %copy-start.63 = (bf16[1536,1152]{1,0:T(8,128)(2,1)S(1)}, bf16[1536,1152]{1,0:T(8,128)(2,1)}, u32[]{:S(2)}) copy-start(bf16[1536,1152]{1,0:T(8,128)(2,1)} %get-tuple-element.60) | copy-start | bytes 10616836
  687.2 15.0 %copy-start.69 = (f32[576,1536]{1,0:T(8,128)S(1)}, f32[576,1536]{1,0:T(8,128)}, u32[]{:S(2)}) copy-start(f32[576,1536]{1,0:T(8,128)} %fusion.50) | copy-start | bytes 10616836
  687.3 15.0 %copy-start.70 = (bf16[1152,1152]{1,0:T(8,128)(2,1)S(1)}, bf16[1152,1152]{1,0:T(8,128)(2,1)}, u32[]{:S(2)}) copy-start(bf16[1152,1152]{1,0:T(8,128)(2,1)} %get-tuple-element.90) | copy-start | bytes 7962628
  871.1 9.3 %copy-start.24 = (bf16[1536,1024]{1,0:T(8,128)(2,1)S(1)}, bf16[1536,1024]{1,0:T(8,128)(2,1)}, u32[]{:S(2)}) copy-start(bf16[1536,1024]{1,0:T(8,128)(2,1)} %get-tuple-element.98) | copy-start | bytes 9437188
  (48 other events, 176.3 us)
Sparse Core Ops, SparseCore 0:
  431.6 73.1 reduce-scatter.3
  507.9 120.7 reduce-scatter.5
  632.3 37.4 reduce-scatter.7

commit v3 on v2

--- a/solution.py
+++ b/solution.py
@@ -87,8 +87,11 @@
     return centered * inv, inv, stat
 
 
-def fwd_kernel(mix_ref, qkv_ref, t_ref, gn_ref, jj_ref, nh_ref, att_ref, pre_ref, qs_ref, ho_ref, dist_ref, qx_ref, mx_ref):
-    g = pl.program_id(1)
+def fwd_kernel(hook, mix_ref, qkv_ref, t_ref, gn_ref, jj_ref, nh_ref, att_ref, pre_ref, qs_ref, ho_ref, dist_ref, qx_ref, mx_ref):
+    side, t, g = pl.program_id(0), pl.program_id(1), pl.program_id(2)
+    step = (side * 2 + t) * 2 + g
+    mix0 = 8 * side + 4 * g
+    hook(step, 0)
     w0 = pl.multiple_of(g * 128, 128)
     m0, m1, from_first = head_masks(g)
     m0f, m1f = m0.astype(F32), m1.astype(F32)
@@ -129,13 +132,14 @@
         return carry
 
     lax.fori_loop(0, 4, fam_scores, 0)
+    hook(step, 1)
     for e in range(2):
         conv = nn(pre_ref[e], t_ref[e])
         logits = jnp.where(dist_ref[...] >= 0, conv, -1e30)
         shifted = jnp.exp(logits - jnp.max(logits, axis=-1, keepdims=True))
         att_ref[e] = shifted / jnp.sum(shifted, axis=-1, keepdims=True)
     for c in range(2):
-        mx_ref[c] = (mix_ref[4 * g + 2 * c] * att_ref[0] + mix_ref[4 * g + 2 * c + 1] * att_ref[1]).astype(BF16)
+        mx_ref[c] = (mix_ref[mix0 + 2 * c] * att_ref[0] + mix_ref[mix0 + 2 * c + 1] * att_ref[1]).astype(BF16)
 
     def put_out(rows, size, values):
         out = nn(mx_ref[:, rows].reshape(2 * size, WIN), values).reshape(2, size, WIN)
@@ -155,6 +159,7 @@
         unit, _, _ = group_norm(ho_ref[row : row + size], m0, m1)
         old = nh_ref[token : token + size, pl.ds(w0, WIN)].astype(F32)
         nh_ref[token : token + size, pl.ds(w0, WIN)] = jnp.where(from_first, unit * gain, old).astype(BF16)
+    hook(step, 2)
 
 
 def bwd_kernel(
@@ -162,7 +167,8 @@
     dqkv_ref, ggn_ref, gmix_ref, gconv_ref,
     dist_ref, dh_ref, mx_ref, dm_ref, dc_ref, es_ref, dqx_ref, dk_ref, dv_ref,
 ):
-    t, g = pl.program_id(0), pl.program_id(1)
+    side, t, g = pl.program_id(0), pl.program_id(1), pl.program_id(2)
+    mix0 = 8 * side + 4 * g
     w0 = pl.multiple_of(g * 128, 128)
     m0, m1, from_first = head_masks(g)
     both = m0 | m1
@@ -185,7 +191,7 @@
     ggn_ref[0:1, pl.ds(w0, WIN)] += gn_sum
     k0, v0 = w0 + 384, w0 + 768
     for c in range(2):
-        mx_ref[c] = (mix_ref[4 * g + 2 * c] * att_ref[0] + mix_ref[4 * g + 2 * c + 1] * att_ref[1]).astype(BF16)
+        mx_ref[c] = (mix_ref[mix0 + 2 * c] * att_ref[0] + mix_ref[mix0 + 2 * c + 1] * att_ref[1]).astype(BF16)
 
     def add_keys(acc_ref, b, c, grads):
         acc_ref[0:TRUNK] += grads[0:TRUNK]
@@ -217,7 +223,7 @@
         att = [att_ref[e, rows] for e in range(2)]
         out = []
         for e in range(2):
-            d_att = mix_ref[4 * g + e] * dm[0] + mix_ref[4 * g + 2 + e] * dm[1]
+            d_att = mix_ref[mix0 + e] * dm[0] + mix_ref[mix0 + 2 + e] * dm[1]
             d_conv = att[e] * (d_att - jnp.sum(d_att * att[e], axis=-1, keepdims=True))
             dc_ref[e, rows] = d_conv.astype(BF16)
         for c in range(2):
@@ -292,46 +298,66 @@
         put(token, size, v0, dv_ref[token : token + size])
 
 
-def by_tree(shape, last):
-    return pl.BlockSpec(shape, lambda t, g: (t,) + (0,) * last)
-
-
 def by_group(shape):
-    tail = (0,) * (len(shape) - 2)
-    return pl.BlockSpec((None, None) + shape[2:], lambda t, g: (t, g) + tail)
+    tail = (0,) * (len(shape) - 3)
+    return pl.BlockSpec((None, None, None) + shape[3:], lambda s, t, g: (s, t, g) + tail)
+
+
+def by_side(shape):
+    return pl.BlockSpec((None,) + shape, lambda s, t, g: (s, 0, 0))
 
 
 def common_specs():
     return [
         pl.BlockSpec(memory_space=pltpu.SMEM),
-        pl.BlockSpec((TREE, 1152), lambda t, g: (t, 0)),
-        pl.BlockSpec((None, 2, CQ * WIN, WIN), lambda t, g: (g, 0, 0, 0)),
-        pl.BlockSpec((8, 384), lambda t, g: (0, 0)),
-        pl.BlockSpec((None, 16, WIN), lambda t, g: (t, 0, 0)),
+        pl.BlockSpec((TREE, 1152), lambda s, t, g: (t, s)),
+        pl.BlockSpec((None, None, 2, CQ * WIN, WIN), lambda s, t, g: (s, g, 0, 0, 0)),
+        by_side((8, 384)),
+        pl.BlockSpec((None, 16, WIN), lambda s, t, g: (t, 0, 0)),
     ]
 
 
-PARAMS = dict(vmem_limit_bytes=60 * 1024 * 1024, dimension_semantics=("arbitrary", "arbitrary"))
+PARAMS = dict(vmem_limit_bytes=60 * 1024 * 1024, dimension_semantics=("arbitrary",) * 3)
 
 
 def saved_shapes(trees):
-    return [(trees, 2, 2, TREE, WIN), (trees, 2, 2, TREE, CQ * WIN), (trees, 2, 2, CQ, TREE, WIN), (trees, 2, TREE, WIN)]
-
-
-def attention_forward(mix, qkv, toeplitz, gains, jj):
+    lead = (2, trees, 2)
+    return [lead + (2, TREE, WIN), lead + (2, TREE, CQ * WIN), lead + (2, CQ, TREE, WIN), lead + (TREE, WIN)]
+
+
+def attention_forward(mix, qkv, toeplitz, gains, jj, gather=None):
     trees = qkv.shape[0] // TREE
     shapes = saved_shapes(trees)
     kinds = (F32, BF16, BF16, F32)
-    return pl.pallas_call(
-        fwd_kernel,
-        grid=(trees, 2),
-        in_specs=common_specs(),
-        out_specs=[pl.BlockSpec((TREE, 384), lambda t, g: (t, 0))] + [by_group(s) for s in shapes],
-        out_shape=[jax.ShapeDtypeStruct((trees * TREE, 384), BF16)] + [jax.ShapeDtypeStruct(s, k) for s, k in zip(shapes, kinds)],
-        scratch_shapes=[pltpu.VMEM((TREE, WIN), jnp.int32), pltpu.VMEM((EXT, WIN), F32), pltpu.VMEM((2, TREE, WIN), BF16)],
-        compiler_params=pltpu.CompilerParams(**PARAMS),
-        cost_estimate=pl.CostEstimate(flops=40_000_000_000, bytes_accessed=60_000_000, transcendentals=0),
-    )(mix, qkv, toeplitz, gains, jj)
+    weights, wide, count, collective = gather if gather else ((), (), 0, {})
+    many, held = len(weights), len(wide)
+
+    def kernel(*refs):
+        inputs, loads, refs = refs[:5], refs[5 : 5 + many], refs[5 + many :]
+        outs, full, refs = refs[:5], refs[5 : 5 + held], refs[5 + held :]
+        work = Gather(LATER, loads, full, *refs[3:]) if gather else None
+
+        def hook(step, place):
+            if work:
+                background(work, step, place)
+
+        fwd_kernel(hook, *inputs, *outs, *refs[:3])
+
+    anywhere = pl.BlockSpec(memory_space=pl.ANY)
+    result = pl.pallas_call(
+        kernel,
+        grid=(2, trees, 2),
+        in_specs=common_specs() + [anywhere] * many,
+        out_specs=[pl.BlockSpec((TREE, 384), lambda s, t, g: (t, s))] + [by_group(s) for s in shapes] + [anywhere] * held,
+        out_shape=[jax.ShapeDtypeStruct((trees * TREE, 768), BF16)]
+        + [jax.ShapeDtypeStruct(s, k) for s, k in zip(shapes, kinds)]
+        + [jax.ShapeDtypeStruct((1536, w), BF16) for w in wide],
+        scratch_shapes=[pltpu.VMEM((TREE, WIN), jnp.int32), pltpu.VMEM((EXT, WIN), F32), pltpu.VMEM((2, TREE, WIN), BF16)]
+        + gather_scratch(weights, count),
+        compiler_params=pltpu.CompilerParams(**PARAMS, **collective),
+        cost_estimate=pl.CostEstimate(flops=80_000_000_000, bytes_accessed=120_000_000, transcendentals=0),
+    )(mix, qkv, toeplitz, gains, jj, *weights)
+    return result[0], result[1:5], result[5:]
 
 
 def attention_backward(mix, qkv, toeplitz, gains, jj, d_normed, saved):
@@ -339,19 +365,19 @@
     shapes = saved_shapes(trees)
     return pl.pallas_call(
         bwd_kernel,
-        grid=(trees, 2),
-        in_specs=common_specs() + [pl.BlockSpec((TREE, 384), lambda t, g: (t, 0))] + [by_group(s) for s in shapes],
+        grid=(2, trees, 2),
+        in_specs=common_specs() + [pl.BlockSpec((TREE, 384), lambda s, t, g: (t, s))] + [by_group(s) for s in shapes],
         out_specs=[
-            pl.BlockSpec((TREE, 1152), lambda t, g: (t, 0)),
-            pl.BlockSpec((8, 384), lambda t, g: (0, 0)),
-            by_group((trees, 2, 8, WIN)),
-            by_group((trees, 2, 2, 8, WIN)),
+            pl.BlockSpec((TREE, 1152), lambda s, t, g: (t, s)),
+            by_side((8, 384)),
+            by_group((2, trees, 2, 8, WIN)),
+            by_group((2, trees, 2, 2, 8, WIN)),
         ],
         out_shape=[
-            jax.ShapeDtypeStruct((trees * TREE, 1152), BF16),
-            jax.ShapeDtypeStruct((8, 384), F32),
-            jax.ShapeDtypeStruct((trees, 2, 8, WIN), F32),
-            jax.ShapeDtypeStruct((trees, 2, 2, 8, WIN), F32),
+            jax.ShapeDtypeStruct((trees * TREE, 2304), BF16),
+            jax.ShapeDtypeStruct((2, 8, 384), F32),
+            jax.ShapeDtypeStruct((2, trees, 2, 8, WIN), F32),
+            jax.ShapeDtypeStruct((2, trees, 2, 2, 8, WIN), F32),
         ],
         scratch_shapes=[
             pltpu.VMEM((TREE, WIN), jnp.int32),
@@ -365,17 +391,24 @@
             pltpu.VMEM((TREE, WIN), F32),
         ],
         compiler_params=pltpu.CompilerParams(**PARAMS),
-        cost_estimate=pl.CostEstimate(flops=80_000_000_000, bytes_accessed=60_000_000, transcendentals=0),
+        cost_estimate=pl.CostEstimate(flops=160_000_000_000, bytes_accessed=120_000_000, transcendentals=0),
     )(mix, qkv, toeplitz, gains, jj, d_normed, *saved)
 
 
-def toeplitz_of(conv_w):
-    heads = conv_w.shape[0]
-    offset = lax.broadcasted_iota(jnp.int32, (WIN, WIN), 1) - lax.broadcasted_iota(jnp.int32, (WIN, WIN), 0) + CK // 2
-    total = jnp.zeros((heads, CQ, WIN, WIN), F32)
-    for b in range(CK):
-        total = total + jnp.where(offset == b, 1.0, 0.0) * (conv_w[:, :, b] * (1.0 / math.sqrt(HD)))[:, :, None, None]
-    return total.astype(BF16).reshape(heads // 2, 2, CQ * WIN, WIN)
+def band_rows(conv_w):
+    rows = conv_w.reshape(-1, CK) * (1.0 / math.sqrt(HD))
+    middle = jnp.zeros((rows.shape[0], WIN - CK), F32)
+    return jnp.concatenate([rows[:, CK // 2 :], middle, rows[:, : CK // 2]], axis=1)
+
+
+def fill_toeplitz(rows_ref, side, out_ref):
+    offset = lax.broadcasted_iota(jnp.int32, (WIN, WIN), 1) - lax.broadcasted_iota(jnp.int32, (WIN, WIN), 0)
+    band = jnp.abs(offset) <= CK // 2
+    for head in range(4):
+        for a in range(CQ):
+            row = rows_ref[side, head * CQ + a : head * CQ + a + 1, :]
+            rolled = pltpu.roll(jnp.broadcast_to(row, (WIN, WIN)), 0, 1, stride=1, stride_axis=0)
+            out_ref[side, head // 2, head % 2, a * WIN : (a + 1) * WIN, :] = jnp.where(band, rolled, 0.0).astype(BF16)
 
 
 def key_positions(valid):
@@ -402,16 +435,25 @@
 
 def conv_grads(gconv):
     lanes = gconv[..., :CQ, 18:29][..., ::-1] * (1.0 / math.sqrt(HD))
-    return jnp.sum(lanes, axis=0).reshape(-1, CQ, CK)
+    return jnp.sum(lanes, axis=1).reshape(2, -1)
 
 
 def mix_grads(gmix):
-    return jnp.sum(gmix[:, :, :4], axis=(0, 3)).reshape(-1, 2, 2)
+    return jnp.sum(gmix[:, :, :, :4], axis=(1, 4)).reshape(2, -1)
 
 
 MESH = pl.DeviceIdType.MESH
 
-GATHERS = ((0, 0, 0), (1, 0, 1), (2, 0, 2), (3, 1, 0), (4, 2, 0), (5, 2, 1), (6, 3, 0))
+FIRST = ((0, 0, 0, 0, 1152, 384), (1, 0, 0, 384, 1536, 384), (2, 0, 0, 768, 1920, 384))
+LATER = (
+    (0, 0, 0, 0, 384, 384),
+    (1, 1, 0, 0, 1024, 512),
+    (1, 1, 512, 512, 1536, 512),
+    (2, 1, 0, 2048, 3072, 512),
+    (2, 1, 512, 2560, 3584, 512),
+    (3, 2, 0, 0, 1024, 512),
+    (3, 2, 512, 512, 1536, 512),
+)
 
 
 def greet(peers):
@@ -422,62 +464,83 @@
 
 
 class Gather:
-    def __init__(self, items, weights, firsts, seconds, send, recv, local, held):
-        self.held = held
-        self.items, self.weights, self.firsts, self.seconds = items, weights, firsts, seconds
+    def __init__(self, items, weights, fulls, send, recv, local, *held):
+        self.items, self.weights, self.fulls, self.held = items, weights, fulls, held
         self.send, self.recv, self.local = send, recv, local
         q, c, z = lax.axis_index("plane"), lax.axis_index("core"), lax.axis_index("tensor")
         self.home = (z // 2) == c
         self.q = q
+        self.core = (q, 1 - c, z)
         self.far = (q, 1 - c, (z + 2) % 4)
         self.near = (q, c, (z // 2) * 2 + (1 - z % 2))
         self.by_x = ((q // 2) * 2 + (1 - q % 2), c, z)
         self.by_y = ((q + 2) % 4, c, z)
 
-    def barrier(self):
-        greet((self.near, self.far, self.by_x, self.by_y))
+    def away(self, action):
+        pl.when(jnp.logical_not(self.home))(action)
 
     def whole(self, item, side):
-        _, out, part = self.items[item]
-        ref = (self.firsts, self.seconds)[side][out]
-        width = self.weights[item].shape[1]
-        return ref, pl.ds(part * width, width)
+        _, out, _, first, second, size = self.items[item]
+        return self.fulls[out], pl.ds((first, second)[side], size)
 
     def z_copy(self, item, side, relay=False):
-        rows = self.weights[item].shape[0] // 4
-        mine = pl.ds(pl.multiple_of(self.q * rows, 128), rows)
+        weight, _, source_col, _, _, size = self.items[item]
+        mine = pl.ds(pl.multiple_of(self.q * 384, 128), 384)
         ref, cols = self.whole(item, side)
-        source = self.whole(item, 0)[0].at[mine, cols] if relay else self.weights[item].at[mine]
+        source = ref.at[mine, self.whole(item, 0)[1]] if relay else self.weights[weight].at[mine, pl.ds(source_col, size)]
         return pltpu.make_async_remote_copy(
             src_ref=source, dst_ref=ref.at[mine, cols], send_sem=self.send.at[item, side],
             recv_sem=self.recv.at[item, side], device_id=(self.far, self.near)[side], device_id_type=MESH)
 
-    def plane_copy(self, item, side, step, receiving=False):
+    def plane_copy(self, item, side, step):
         ref, cols = self.whole(item, side)
-        rows = ref.shape[0] // 4
         if step < 2:
-            owner, first, size = self.q, 0, rows
+            owner, first, size = self.q, 0, 384
         elif step == 2:
-            owner, first, size = self.by_x[0], 0, rows // 2
+            owner, first, size = self.by_x[0], 0, 192
         else:
-            owner, first, size = self.by_y[0], rows // 2, rows // 2
-        span = pl.ds(pl.multiple_of(owner * rows + first, 64), size)
+            owner, first, size = self.by_y[0], 192, 192
+        span = pl.ds(pl.multiple_of(owner * 384 + first, 64), size)
         slot = 2 + 4 * side + step
         return pltpu.make_async_remote_copy(
             src_ref=ref.at[span, cols], dst_ref=ref.at[span, cols], send_sem=self.send.at[item, slot], recv_sem=self.recv.at[item, slot],
             device_id=(self.by_x, self.by_y, self.by_y, self.by_x)[step], device_id_type=MESH)
 
-    def own_load(self, item):
-        return pltpu.make_async_copy(self.weights[item], self.held[item], self.local.at[item, 0])
-
-    def own_store(self, item):
-        ref, cols = self.whole(item, 0)
-        return pltpu.make_async_copy(self.held[item], ref.at[:, cols], self.local.at[item, 1])
+    def own_load(self, weight):
+        return pltpu.make_async_copy(self.weights[weight], self.held[weight], self.local.at[weight, 0])
+
+    def own_stores(self, weight):
+        copies = []
+        for number, (index, out, source_col, first, _, size) in enumerate(self.items):
+            if index == weight:
+                source = self.held[weight].at[:, pl.ds(source_col, size)]
+                copies.append(pltpu.make_async_copy(source, self.fulls[out].at[:, pl.ds(first, size)], self.local.at[number, 1]))
+        return copies
+
+    def own(self):
+        @pl.when(self.home)
+        def _():
+            for weight in range(len(self.weights)):
+                self.own_load(weight).start()
+
+    def pass_own(self, weight):
+        @pl.when(self.home)
+        def _():
+            self.own_load(weight).wait()
+            for copy in self.own_stores(weight):
+                copy.start()
+
+    def wait_own(self):
+        @pl.when(self.home)
+        def _():
+            for weight in range(len(self.weights)):
+                for copy in self.own_stores(weight):
+                    copy.wait()
 
     def each(self, action):
         action(1)
 
-        @pl.when(jnp.logical_not(self.home))
+        @self.away
         def _():
             action(0)
 
@@ -486,33 +549,17 @@
         def _():
             self.z_copy(item, 1).start()
 
-        @pl.when(jnp.logical_not(self.home))
+        @self.away
         def _():
             self.z_copy(item, 0).start()
 
     def relay_z(self, item):
-        @pl.when(jnp.logical_not(self.home))
+        @self.away
         def _():
             self.z_copy(item, 0).wait_recv()
             self.z_copy(item, 1, True).start()
             self.plane_copy(item, 0, 0).start()
             self.plane_copy(item, 0, 1).start()
-
-    def own(self, item):
-        @pl.when(self.home)
-        def _():
-            self.own_load(item).start()
-
-    def pass_own(self, item):
-        @pl.when(self.home)
-        def _():
-            self.own_load(item).wait()
-            self.own_store(item).start()
-
-    def wait_own(self, item):
-        @pl.when(self.home)
-        def _():
-            self.own_store(item).wait()
 
     def start_plane(self, item):
         self.z_copy(item, 1).wait_recv()
@@ -537,49 +584,135 @@
                 self.plane_copy(item, side, step).wait_send()
 
         self.each(act)
-        self.wait_own(item)
-
-
-def gather_kernel(items, weights, outs, send, recv, local, *held, ahead=3):
-    count = len(items)
-    half = len(outs) // 2
-    work = Gather(items, weights, outs[:half], outs[half:], send, recv, local, held)
-    for item in range(count):
-        work.own(item)
-    work.barrier()
-    for item in range(min(ahead, count)):
+
+
+def gather_scratch(weights, count):
+    if not weights:
+        return []
+    return [pltpu.SemaphoreType.DMA((count, 10)), pltpu.SemaphoreType.DMA((count, 10)), pltpu.SemaphoreType.DMA((max(count, len(weights)), 2))] + [
+        pltpu.VMEM(w.shape, BF16) for w in weights
+    ]
+
+
+AHEAD = 3
+
+
+def background(work, step, place):
+    count = len(work.items)
+    if place == 2:
+
+        @pl.when(step == 7)
+        def _():
+            work.forward(count - 1)
+            for item in range(count):
+                work.finish(item)
+            work.wait_own()
+
+        return
+
+    for turn in range(8):
+        slot = 2 * turn + place
+
+        @pl.when(step == turn)
+        def _(slot=slot):
+            if slot == 0:
+                work.own()
+                greet((work.near, work.far, work.by_x, work.by_y))
+                for item in range(AHEAD):
+                    work.start_z(item)
+            elif slot <= 2 * count:
+                item = (slot - 1) // 2
+                if slot % 2:
+                    work.relay_z(item)
+                    if item + AHEAD < count:
+                        work.start_z(item + AHEAD)
+                    if item < len(work.weights):
+                        work.pass_own(item)
+                else:
+                    work.start_plane(item)
+                    if item >= 1:
+                        work.forward(item - 1)
+
+
+def opening_kernel(tokens_ref, gain_ref, small_ref, wq_ref, wk_ref, wv_ref, full_ref, normed_ref, toep_ref, both_ref, send, recv, local, held0, held1, held2, extra_send, extra_recv):
+    work = Gather(FIRST, (wq_ref, wk_ref, wv_ref), (full_ref,), send, recv, local, held0, held1, held2)
+    rows = tokens_ref.shape[0]
+
+    def extra(source, target, index, peer):
+        return pltpu.make_async_remote_copy(
+            src_ref=source, dst_ref=target, send_sem=extra_send.at[index], recv_sem=extra_recv.at[index], device_id=peer, device_id_type=MESH)
+
+    far_small = extra(small_ref, both_ref.at[0], 0, work.far)
+    near_small = extra(both_ref.at[0], both_ref.at[1], 1, work.near)
+    normed_out = extra(normed_ref.at[0:rows], normed_ref.at[rows : 2 * rows], 2, work.core)
+    work.own()
+    greet((work.near, work.far, work.by_x, work.by_y, work.core))
+
+    @work.away
+    def _():
+        far_small.start()
+
+    @pl.when(work.home)
+    def _():
+        both_ref[0] = small_ref[...]
+        near_small.start()
+
+    for item in range(3):
         work.start_z(item)
-    for step in range(count + 1):
-        if step < count:
-            work.relay_z(step)
-            if step + ahead < count:
-                work.start_z(step + ahead)
-            work.start_plane(step)
-            work.pass_own(step)
-        if step >= 1:
-            work.forward(step - 1)
-    for item in range(count):
+    for start in range(0, rows, 96):
+        x = tokens_ref[start : start + 96].astype(F32)
+        inv = lax.rsqrt(jnp.mean(x * x, axis=-1, keepdims=True) + 1e-06)
+        normed_ref[start : start + 96] = (x * inv * gain_ref[...]).astype(BF16)
+    normed_out.start()
+
+    @work.away
+    def _():
+        far_small.wait_recv()
+        near_small.start()
+
+    work.relay_z(0)
+    work.start_plane(0)
+    fill_toeplitz(both_ref, 0, toep_ref)
+    work.relay_z(1)
+    work.start_plane(1)
+    work.forward(0)
+    for weight in range(3):
+        work.pass_own(weight)
+    near_small.wait_recv()
+    work.relay_z(2)
+    work.start_plane(2)
+    work.forward(1)
+    fill_toeplitz(both_ref, 1, toep_ref)
+    work.forward(2)
+    for item in range(3):
         work.finish(item)
-
-
-def gather_weights(weights, items, widths, collective_id):
-    depth = weights[0].shape[0]
-    count = len(items)
-
-    def kernel(*refs):
-        gather_kernel(items, refs[:count], refs[count : count + 2 * len(widths)], *refs[count + 2 * len(widths) :])
-
-    shapes = [jax.ShapeDtypeStruct((depth, w), BF16) for w in widths] * 2
-    outs = pl.pallas_call(
-        kernel,
-        in_specs=[pl.BlockSpec(memory_space=pl.ANY)] * count,
-        out_specs=[pl.BlockSpec(memory_space=pl.ANY)] * len(shapes),
-        out_shape=shapes,
-        scratch_shapes=[pltpu.SemaphoreType.DMA((count, 10)), pltpu.SemaphoreType.DMA((count, 10)), pltpu.SemaphoreType.DMA((count, 2))]
-        + [pltpu.VMEM(w.shape, BF16) for w in weights],
+    work.wait_own()
+    near_small.wait_send()
+
+    @work.away
+    def _():
+        far_small.wait_send()
+
+    normed_out.wait()
+
+
+def opening(tokens, gain, small, weights, collective_id):
+    vmem = pl.BlockSpec(memory_space=pltpu.VMEM)
+    anywhere = pl.BlockSpec(memory_space=pl.ANY)
+    rows, width = tokens.shape
+    return pl.pallas_call(
+        opening_kernel,
+        in_specs=[vmem] * 3 + [anywhere] * 3,
+        out_specs=[anywhere] + [vmem] * 3,
+        out_shape=[
+            jax.ShapeDtypeStruct((width, 2304), BF16),
+            jax.ShapeDtypeStruct((2 * rows, width), BF16),
+            jax.ShapeDtypeStruct((2, 2, 2, CQ * WIN, WIN), BF16),
+            jax.ShapeDtypeStruct((2,) + small.shape, F32),
+        ],
+        scratch_shapes=gather_scratch(weights, 3) + [pltpu.SemaphoreType.DMA((3,)), pltpu.SemaphoreType.DMA((3,))],
         compiler_params=pltpu.CompilerParams(collective_id=collective_id, has_side_effects=True, vmem_limit_bytes=60 * 1024 * 1024),
-    )(*weights)
-    return [(outs[i], outs[len(widths) + i]) for i in range(len(widths))]
+    )(tokens, gain, small, *weights)
 
 
 class Finish:
@@ -811,8 +944,8 @@
 
 FINISH = (
     (0, 0, 1024, 1024, 0, 0, 0),
-    (1, 0, 2048, 1024, 1, 1024, 0),
-    (1, 1024, 3072, 1024, 1, 2048, 1024),
+    (1, 0, 1024, 1024, 1, 1024, 0),
+    (1, 2048, 3072, 1024, 1, 2048, 1024),
     (2, 0, 384, 384, 2, 3072, 0),
     (-1, 0, 1152, 384, 3, 3456, 0),
     (-1, 384, 1536, 384, 3, 3840, 384),
@@ -872,6 +1005,18 @@
     return tn(lhs, rhs).astype(BF16)
 
 
+def toeplitz_alone(both):
+    def kernel(rows_ref, out_ref):
+        fill_toeplitz(rows_ref, 0, out_ref)
+        fill_toeplitz(rows_ref, 1, out_ref)
+
+    return pl.pallas_call(
+        kernel,
+        out_shape=jax.ShapeDtypeStruct((2, 2, 2, CQ * WIN, WIN), BF16),
+        compiler_params=pltpu.CompilerParams(vmem_limit_bytes=60 * 1024 * 1024),
+    )(both)
+
+
 def make_local(planes, tensors):
     every = ("plane", "core", "tensor")
     sides = [(c, z) for c in range(2) for z in range(tensors)]
@@ -905,18 +1050,13 @@
         q, c, z = lax.axis_index("plane"), lax.axis_index("core"), lax.axis_index("tensor")
         own_rows, width = tokens.shape
         home = (z // 2) == c
-        heads = conv_weight.shape[0]
         wide = w_query.shape[1]
 
-        def collect_all(weights):
-            groups = ((0, 1, 2), (3,), (4, 5), (6,))
-            if square and tensors == 4:
-                widths = [sum(weights[i].shape[1] for i in group) for group in groups]
-                return gather_weights(weights, GATHERS, widths, 1)
+        def collect(weights):
             pairs = []
-            for group in groups:
-                whole = jnp.concatenate([weights[i] for i in group], axis=1)
-                pairs.append((jnp.where(home, whole, first_from(whole)), second_from(whole)))
+            for weight in weights:
+                pairs.append(jnp.where(home, weight, first_from(weight)))
+                pairs.append(second_from(weight))
             return pairs
 
         fused = square and tensors == 4
@@ -924,64 +1064,64 @@
         def plane_sum(grads):
             return lax.psum_scatter(grads, "plane", scatter_dimension=0, tiled=True)
 
-        def reduce(part):
-            count = part.shape[1] // 2
-            first, second = part[:, :count], part[:, count:]
+        def reduce(first, second):
             here = added(first, lax.ppermute(second, "tensor", [(i, i ^ 1) for i in range(tensors)]))
             here = jnp.where(home, here, first_from(here))
             total = added(here, over_core(here))
             return lax.all_gather(total, "plane", axis=0, tiled=True)
 
-        small = jnp.concatenate([conv_weight.reshape(-1), head_mix.reshape(-1), gn_gain.reshape(-1)])
-        small_first = jnp.where(home, small, first_from(small))
-        small_second = second_from(small)
+        small = jnp.concatenate(
+            [
+                band_rows(conv_weight),
+                jnp.pad(head_mix.reshape(1, -1), ((0, 0), (0, WIN - head_mix.size))),
+                jnp.pad(gn_gain.reshape(1, -1), ((0, 0), (0, 2 * WIN - wide))).reshape(2, WIN),
+                jnp.zeros((5, WIN), F32),
+            ]
+        )
         conv_size, mix_size = conv_weight.size, head_mix.size
-
+        small_size = conv_size + mix_size + wide
         gain_one, gain_two = norm1_gain, norm2_gain
         own_valid = lax.dynamic_slice_in_dim(valid_mask, z * own_rows, own_rows, 0)
         jj = key_positions(jnp.concatenate([own_valid, over_core(own_valid)]))
 
-        qkv_weights, out_weights, gu_weights, down_weights = collect_all([w_query, w_key, w_value, w_out, w_gate, w_up, w_down])
-
         def with_partner(value):
             return jnp.concatenate([value, over_core(value)], axis=0)
 
-        def summed(lefts, rights):
-            def half(rows):
-                total = nt(lefts[0][rows], rights[0])
-                return total + nt(lefts[1][rows], rights[1])
-
-            sent = over_core(half(slice(own_rows, None)).astype(BF16))
-            return half(slice(0, own_rows)) + sent.astype(F32)
+        def summed(left, right):
+            sent = over_core(nt(left[own_rows:], right).astype(BF16))
+            return nt(left[:own_rows], right) + sent.astype(F32)
 
         inputs = tokens.astype(F32)
         inv_one = lax.rsqrt(jnp.mean(inputs * inputs, axis=-1, keepdims=True) + 1e-06)
-        normed_one = with_partner((inputs * inv_one * gain_one).astype(BF16))
-        sides_small = []
-        for vec in (small_first, small_second):
-            conv = vec[:conv_size].reshape(conv_weight.shape)
-            mix = vec[conv_size : conv_size + mix_size]
-            gains = jnp.broadcast_to(vec[conv_size + mix_size :][None], (8, wide))
-            sides_small.append((mix, toeplitz_of(conv), gains))
-        qkv, heads_out, saved = [], [], []
-        for (mix, toep, gains), weight in zip(sides_small, qkv_weights):
-            projected = nn(normed_one, weight).astype(BF16)
-            result = attention_forward(mix, projected, toep, gains, jj)
-            qkv.append(projected)
-            heads_out.append(result[0])
-            saved.append(result[1:])
-        hidden_in = inputs + summed(heads_out, out_weights)
+        if fused:
+            qkv_weight, normed_one, toep, both_small = opening(tokens, gain_one[None], small, [w_query, w_key, w_value], 1)
+            gather = ([w_out, w_gate, w_up, w_down], (768, 4096, 2048), len(LATER), dict(collective_id=3, has_side_effects=True))
+        else:
+            both_small = jnp.stack([jnp.where(home, small, first_from(small)), second_from(small)])
+            toep = toeplitz_alone(both_small)
+            normed_one = with_partner((inputs * inv_one * gain_one).astype(BF16))
+            parts = collect([w_query, w_key, w_value])
+            qkv_weight = jnp.concatenate(parts[0::2] + parts[1::2], axis=1)
+            gather = None
+        mix = both_small[:, 24, :mix_size].reshape(-1)
+        gains = jnp.broadcast_to(both_small[:, 25:27].reshape(2, 1, 2 * WIN)[:, :, :wide], (2, 8, wide))
+        qkv = nn(normed_one, qkv_weight).astype(BF16)
+        heads_out, saved, later = attention_forward(mix, qkv, toep, gains, jj, gather)
+        if fused:
+            out_weight, gu_weight, down_weight = later
+        else:
+            out_weight = jnp.concatenate(collect([w_out]), axis=1)
+            gu_weight = jnp.concatenate(collect([w_gate, w_up]), axis=1)
+            down_weight = jnp.concatenate(collect([w_down]), axis=1)
+        hidden_in = inputs + summed(heads_out, out_weight)
         inv_two = lax.rsqrt(jnp.mean(hidden_in * hidden_in, axis=-1, keepdims=True) + 1e-06)
         normed_two = with_partner((hidden_in * inv_two * gain_two).astype(BF16))
         units = w_gate.shape[1]
-        gates, ups, hiddens = [], [], []
-        for weight in gu_weights:
-            both = nn(normed_two, weight)
-            gate, up = both[:, :units], both[:, units:]
-            gates.append(gate.astype(BF16))
-            ups.append(up.astype(BF16))
-            hiddens.append((jax.nn.silu(gate) * up).astype(BF16))
-        final_rows = hidden_in + summed(hiddens, down_weights)
+        both = nn(normed_two, gu_weight)
+        gate, up = both[:, : 2 * units], both[:, 2 * units :]
+        hidden = (jax.nn.silu(gate) * up).astype(BF16)
+        gate, up = gate.astype(BF16), up.astype(BF16)
+        final_rows = hidden_in + summed(hidden, down_weight)
         output = final_rows.astype(BF16)
         own_mask = own_valid.astype(F32)
         error = own_mask[:, None] * (final_rows - teacher.astype(F32))
@@ -989,51 +1129,43 @@
         count_sum = jnp.sum(own_mask)
 
         d_all = with_partner(error.astype(BF16))
-        down_grads = rows_dot(d_all, jnp.concatenate(hiddens, axis=1))
+        down_grads = rows_dot(d_all, hidden)
         down_grads, d_all = lax.optimization_barrier((down_grads, d_all))
         down_part = plane_sum(down_grads)
-        d_gus = []
-        for index, weight in enumerate(down_weights):
-            d_hidden = nn(d_all, weight)
-            gate, up = gates[index].astype(F32), ups[index].astype(F32)
-            s = jax.nn.sigmoid(gate)
-            d_gate = (d_hidden * up * s * (1.0 + gate * (1.0 - s))).astype(BF16)
-            d_up = (d_hidden * gate * s).astype(BF16)
-            d_gus.append(jnp.concatenate([d_gate, d_up], axis=1))
-        gu_grads = rows_dot(normed_two, jnp.concatenate(d_gus, axis=1))
-        gu_grads, d_gus = lax.optimization_barrier((gu_grads, d_gus))
+        d_hidden = nn(d_all, down_weight)
+        gate, up = gate.astype(F32), up.astype(F32)
+        s = jax.nn.sigmoid(gate)
+        d_gate = (d_hidden * up * s * (1.0 + gate * (1.0 - s))).astype(BF16)
+        d_up = (d_hidden * gate * s).astype(BF16)
+        d_gu = jnp.concatenate([d_gate, d_up], axis=1)
+        gu_grads = rows_dot(normed_two, d_gu)
+        gu_grads, d_gu = lax.optimization_barrier((gu_grads, d_gu))
         gu_part = plane_sum(gu_grads)
-        d_normed_two = summed(d_gus, gu_weights)
+        d_normed_two = summed(d_gu, gu_weight)
         scaled_two = d_normed_two * gain_two
         grad_gain_two = jnp.sum(d_normed_two * hidden_in * inv_two, axis=0)
         d_hidden_in = (
             error + inv_two * scaled_two - hidden_in * inv_two**3 * jnp.mean(scaled_two * hidden_in, axis=-1, keepdims=True)
         )
         d_attn = with_partner(d_hidden_in.astype(BF16))
-        out_grads = rows_dot(d_attn, jnp.concatenate(heads_out, axis=1))
+        out_grads = rows_dot(d_attn, heads_out)
         out_grads, d_attn = lax.optimization_barrier((out_grads, d_attn))
         out_part = plane_sum(out_grads)
-        d_qkv, small_grads = [], []
-        for index, (mix, toep, gains) in enumerate(sides_small):
-            d_normed = nn(d_attn, out_weights[index])
-            if index == 0:
-                d_normed, down_part = lax.optimization_barrier((d_normed, down_part))
-            else:
-                d_normed, gu_part = lax.optimization_barrier((d_normed, gu_part))
-            dqkv, ggn, gmix, gconv = attention_backward(mix, qkv[index], toep, gains, jj, d_normed, saved[index])
-            d_qkv.append(dqkv)
-            small_grads.append(jnp.concatenate([conv_grads(gconv).reshape(-1), mix_grads(gmix).reshape(-1), ggn[0]]))
-        qkv_grads = rows_dot(normed_one, jnp.concatenate(d_qkv, axis=1))
-        d_normed_one = summed(d_qkv, qkv_weights)
+        d_normed = nn(d_attn, out_weight)
+        d_normed, down_part = lax.optimization_barrier((d_normed, down_part))
+        d_qkv, ggn, gmix, gconv = attention_backward(mix, qkv, toep, gains, jj, d_normed, saved)
+        small_grads = jnp.concatenate([conv_grads(gconv), mix_grads(gmix), ggn[:, 0]], axis=1)
+        qkv_grads = rows_dot(normed_one, d_qkv)
+        d_normed_one = summed(d_qkv, qkv_weight)
         scaled_one = d_normed_one * gain_one
         grad_gain_one = jnp.sum(d_normed_one * inputs * inv_one, axis=0)
         grad_input = (
             d_hidden_in + inv_one * scaled_one - inputs * inv_one**3 * jnp.mean(scaled_one * inputs, axis=-1, keepdims=True)
         )
 
-        table = jnp.zeros((tensors, small.size), F32)
-        table = lax.dynamic_update_slice(table, small_grads[0][None], (2 * c + z % 2, 0))
-        table = lax.dynamic_update_slice(table, small_grads[1][None], (2 * c + 1 - z % 2, 0))
+        table = jnp.zeros((tensors, small_size), F32)
+        table = lax.dynamic_update_slice(table, small_grads[:1], (2 * c + z % 2, 0))
+        table = lax.dynamic_update_slice(table, small_grads[1:], (2 * c + 1 - z % 2, 0))
         packed = jnp.concatenate(
             [table.reshape(-1), grad_gain_one, grad_gain_two, squared_sum[None], count_sum[None]]
         )
@@ -1045,10 +1177,14 @@
             packed = packed.reshape(-1)[:length]
         else:
             packed = lax.psum(packed, every)
-            sums = [reduce(part) for part in (down_part, gu_part, out_part, plane_sum(qkv_grads))]
+            qkv_part = plane_sum(qkv_grads)
+            sums = [reduce(part[:, : part.shape[1] // 2], part[:, part.shape[1] // 2 :]) for part in (down_part, out_part, qkv_part)]
+            places = [slice(i * units, (i + 1) * units) for i in range(4)]
+            first, second = [jnp.concatenate([gu_part[:, places[i]], gu_part[:, places[i + 2]]], axis=1) for i in range(2)]
+            sums.insert(1, reduce(first, second))
         grad_down, grad_gu, grad_out, grad_qkv = [value.astype(F32) for value in sums]
-        table_size = tensors * small.size
-        small_sum = lax.dynamic_slice_in_dim(packed, z * small.size, small.size, 0)
+        table_size = tensors * small_size
+        small_sum = lax.dynamic_slice_in_dim(packed, z * small_size, small_size, 0)
         gain_slice = width // tensors
         gain_one_out = lax.dynamic_slice_in_dim(packed, table_size + z * gain_slice, gain_slice, 0)
         gain_two_out = lax.dynamic_slice_in_dim(packed, table_size + width + z * gain_slice, gain_slice, 0)

time: 904 us -> 774 us (0.86)
  Pallas kernels: 467 us -> 388 us
  local copies, waits for them, and re-layouts: 56.2 us -> 30 us
  other arithmetic: 70.8 us -> 49.8 us
  matrix products: 187 us -> 174 us
    pallas_call x5 -> x3, Pallas kernels: 318 us -> 239 us  [the longest x1 91.4 us: attention_backward(): pl.pallas_call(bwd_kernel, grid=(2, trees, 2), in_specs=common_specs() +...]
    convert_element_type x5 -> x1, other arithmetic: 32.3 us -> 7.78 us  [local(): hidden = (jax.nn.silu(gate) * up).astype(BF16)]
    dot_general x16 -> x8, matrix products: 73.2 us -> 57.6 us  [nt(): lax.dot_general(a, b, (((1,), (1,)), ((), ())), preferred_element_type=F32)]
    unnamed x166 -> x66, local copies, waits for them, and re-layouts: 14.9 us -> 1.88 us
    ppermute x9 -> x8, starting transfers between devices: 56.4 us -> 68.6 us  [over_core(): return lax.ppermute(value, 'core', [(0, 1), (1, 0)])]
    reduce_scatter x3, waiting for transfers between devices: 25.1 us -> 15.4 us  [plane_sum(): return lax.psum_scatter(grads, 'plane', scatter_dimension=0, tiled=True)]
    mul x55 -> x2, local copies, waits for them, and re-layouts: 9.64 us -> 0.01 us  [band_rows(): rows = conv_w.reshape(-1, CK) * (1.0 / math.sqrt(HD))]
    dot_general x8 -> x4, matrix products: 56.8 us -> 64.3 us  [nn(): lax.dot_general(a, b, (((1,), (0,)), ((), ())), preferred_element_type=F32)]
  transfers between devices with their start and end apart: 14 -> 11, of which waited for: 6 -> 7; matrix products, arithmetic and copies ran while one was open for 22% -> 19% of each run, Pallas kernels for 27% -> 19%
where the time goes in v3:
time: 774 us; the launch traced here: 764 us
  Pallas kernels  388 us (50%)
  matrix products  174 us (22%)
  starting transfers between devices  68.7 us (9%)
  other arithmetic  49.8 us (6%)
  waiting for transfers between devices  36.4 us (5%)
  local copies, waits for them, and re-layouts  30 us (4%)
  between operations  17 us (2%)
    pallas_call x1, Pallas kernels, finish_gradients(): pl.pallas_call(finish_kernel, in_specs=[vmem] * 4 + [anywhere], out_specs...  149 us
    pallas_call x1, Pallas kernels, attention_backward(): pl.pallas_call(bwd_kernel, grid=(2, trees, 2), in_specs=common_specs() +...  91.4 us
    pallas_call x1, Pallas kernels, attention_forward(): pl.pallas_call(kernel, grid=(2, trees, 2), in_specs=common_specs() + [any...  89.8 us
    ppermute x8, starting transfers between devices, over_core(): return lax.ppermute(value, 'core', [(0, 1), (1, 0)])  68.6 us
    dot_general x4, matrix products, nn(): lax.dot_general(a, b, (((1,), (0,)), ((), ())), preferred_element_type=F32)  64.3 us
    dot_general x8, matrix products, nt(): lax.dot_general(a, b, (((1,), (1,)), ((), ())), preferred_element_type=F32)  57.6 us
    pallas_call x1, Pallas kernels, opening(): pl.pallas_call(opening_kernel, in_specs=[vmem] * 3 + [anywhere] * 3, out_...  57.4 us
    dot_general x4, matrix products, tn(): lax.dot_general(a, b, (((0,), (0,)), ((), ())), preferred_element_type=F32)  52 us
  transfers between devices with their start and end apart: 11, of which 7 were waited for; matrix products, arithmetic and copies ran while one was open for 19% of the time, Pallas kernels for 19%

profile of v3, /device:TPU:0, one launch (start us, length us, event | category | flops | bytes accessed | tf_op | source)
XLA Modules:
  0.0 763.9 jit_solution(9006627936716906299)
XLA Ops:
  7.2 1.4 convert_reduce_fusion
  9.9 0.8 reshape.123
  10.7 0.8 reshape.122
  11.4 1.3 broadcast_in_dim.53.gain_ref
  13.5 57.4 %shard_map.262 = (bf16[1536,2304]{1,0:T(8,128)(2,1)}, bf16[1152,1536]{1,0:T(8,128)(2,1)}, bf16[2,2,2,1536,256]{4,3,2,1,0:T(8,128)(2,1)}, f32[2,32,256]{2,1,0:T(8,128)}) custom-call(bf16[576,1536]{1,0:T(8,128)(2,1)} %tokens_ref.1, f32[1,1536]{1,0:T(1,128)} %broadcast_in_dim.53.gain_ref, f32[32,256]{1,0:T(8,128)} %fusion.38.small_ref, ...), custom_call_target="tpu_custom_call" | custom-call | tf_op jit(solution)/shard_map/pallas_call | solution.py:703
  72.4 13.8 %convolution_convert_fusion.2.refs_1_.qkv_ref = bf16[1152,2304]{1,0:T(8,128)(2,1)} fusion(bf16[1152,1536]{1,0:T(8,128)(2,1)} %get-tuple-element.45, bf16[1536,2304]{1,0:T(8,128)(2,1)} %get-tuple-element.46), kind=kOutput, calls=%fused_computation.5 | convolution fusion | flops 8156381184 | bytes 15925248 | tf_op jit(solution)/shard_map/dot_general | solution.py:36
  87.3 1.3 stack.59.refs_4_.jj_ref
  89.2 89.8 %shard_map.263 = (bf16[1152,768]{1,0:T(8,128)(2,1)}, f32[2,2,2,2,576,256]{5,4,3,2,1,0:T(8,128)}, bf16[2,2,2,2,576,1536]{5,4,3,2,1,0:T(8,128)(2,1)}, bf16[2,2,2,2...) custom-call(f32[16]{0:T(128)} %reshape_squeeze.3.refs_0_.mix_ref, ...), custom_call_target="tpu_custom_call" | custom-call | flops 80000000000 | bytes 120000000 | tf_op jit(solution)/shard_map/pallas_call | solution.py:347
  179.1 3.7 convolution_convert_fusion.6
  182.8 66.2 %collective-permute-start.1 = (bf16[576,1536]{1,0:T(8,128)(2,1)S(1)}, bf16[576,1536]{1,0:T(8,128)(2,1)S(1)}, u32[]{:S(2)}, u32[]{:S(2)}) collective-permute-start(bf16[576,1536]{1,0:T(8,128)(2,1)S(1)} %convolution_convert_fusion.6), channel_id=1, source_target_pairs={{0,4},{4,0},{1,5},{5,1},{2,6},{6,2},{3,7},{7,3},{8,12},{12,8},{9,1... | collective-permute-start | bytes 5308424 | tf_op jit(solution)/shard_map/ppermute | solution.py:1036
  248.9 3.3 collective-permute-done.1
  252.2 1.8 multiply_reduce_fusion.3
  255.5 3.3 collective-permute-done.2
  258.8 23.0 %fusion.31 = f32[1152,4096]{1,0:T(8,128)} fusion(bf16[1536,4096]{1,0:T(8,128)(2,1)} %get-tuple-element.50, bf16[576,1536]{1,0:T(8,128)(2,1)S(1)} %collective-permute-done.2, bf16[576,1536]{1,0:T(8,128)(2,1)S(1)} %multiply_convert_fusion.1), kind=kOutput, calls=%fused_computation.58 | convolution fusion | flops 14502592512 | bytes 34996224 | tf_op jit(solution)/shard_map/dot_general | solution.py:36
  281.8 7.8 %multiply_convert_fusion = bf16[1152,2048]{1,0:T(8,128)(2,1)S(1)} fusion(f32[1152,4096]{1,0:T(8,128)} %fusion.31), kind=kLoop, calls=%fused_computation.15 | loop fusion | flops 14155776 | bytes 23592960 | tf_op jit(solution)/shard_map/convert_element_type | solution.py:1122
  289.7 3.9 convolution_convert_fusion.5
  294.0 3.3 collective-permute-done.3
  297.3 6.1 fusion.46
  303.7 3.3 collective-permute-done.4
  307.1 2.0 pad_maximum_fusion.2
  309.1 10.3 %convolution_convert_fusion.3 = bf16[1536,2048]{1,0:T(8,128)(2,1)} fusion(bf16[1152,2048]{1,0:T(8,128)(2,1)S(1)} %multiply_convert_fusion, bf16[576,1536]{1,0:T(8,128)(2,1)S(1)} %collective-permute-done.4, bf16[576,1536]{1,0:T(8,128)(2,1)S(1)} %get-tuple-element.146), kind=kOutput, calls=%fused_computation.18 | convolution fusion | flops 7257980928 | bytes 14548992 | tf_op jit(solution)/shard_map/dot_general | solution.py:44
  319.4 19.7 %fusion.5 = (bf16[1152,2048]{1,0:T(8,128)(2,1)}, bf16[1152,2048]{1,0:T(8,128)(2,1)}) fusion(f32[1152,4096]{1,0:T(8,128)} %fusion.31, bf16[1152,1536]{1,0:T(8,128)(2,1)} %pad_maximum_fusion.2, bf16[1536,2048]{1,0:T(8,128)(2,1)} %get-tuple-element.51), kind=kOutput, calls=%fused_computation.11 | convolution fusion | flops 7283146752 | bytes 28704768 | tf_op jit(solution)/shard_map/dot_general | solution.py:36
  339.2 10.8 %pad_maximum_fusion = bf16[1152,4096]{1,0:T(8,128)(2,1)} fusion(bf16[1152,2048]{1,0:T(8,128)(2,1)} %get-tuple-element.97, bf16[1152,2048]{1,0:T(8,128)(2,1)} %get-tuple-element.96), kind=kLoop, calls=%fused_computation.14 | loop fusion | flops 18874368 | bytes 18874368 | tf_op jit(solution)/shard_map/concatenate | solution.py:1140
  350.0 22.3 %convolution_convert_fusion = bf16[1536,4096]{1,0:T(8,128)(2,1)} fusion(bf16[576,1536]{1,0:T(8,128)(2,1)} %copy-done.25, bf16[576,1536]{1,0:T(8,128)(2,1)S(1)} %copy-done.10, bf16[1152,2048]{1,0:T(8,128)(2,1)} %get-tuple-element.97, bf16[1152,2048]{1,0:T(8,128)(2,1)S(1)} %copy-done.6), kind=kOutput, calls=%fused_computation | convolution fusion | flops 14527758336 | bytes 25559040 | tf_op jit(solution)/shard_map/dot_general | solution.py:44
  372.3 12.1 %fusion.18 = bf16[576,1536]{1,0:T(8,128)(2,1)S(1)} fusion(bf16[1536,4096]{1,0:T(8,128)(2,1)} %get-tuple-element.50, bf16[1152,4096]{1,0:T(8,128)(2,1)} %pad_maximum_fusion), kind=kOutput, calls=%fused_computation.48 | convolution fusion | flops 7248642048 | bytes 19070976 | tf_op jit(solution)/shard_map/dot_general | solution.py:40
  384.7 3.6 collective-permute-done.5
  388.3 13.0 %multiply_reduce_fusion.1 = (f32[1536]{0:T(1024)}, f32[576]{0:T(1024)S(1)}, f32[576,1536]{1,0:T(8,128)}) fusion(f32[576,1536]{1,0:T(8,128)S(1)} %get-tuple-element.145, f32[576]{0:T(1024)S(1)} %copy-done.13, bf16[576,1536]{1,0:T(8,128)(2,1)} %collective-permute-done.5, f32[1536]{0:T(1024)S(1)} %copy-done.15, bf16[1536,4096]{1,0:T(8,128)(2,1)} %get-tuple-element.50, ...), kind=kOutput, calls=%fused_computation.38 | convolution fusion | flops 7254833152 | bytes 26169600 | tf_op jit(solution)/shard_map/dot_general | solution.py:40
  401.3 9.4 %fusion.47 = (bf16[576,1536]{1,0:T(8,128)(2,1)S(1)}, f32[576,1536]{1,0:T(8,128)}, f32[]{:T(128)}, bf16[576,1536]{1,0:T(8,128)(2,1)}) fusion(f32[576]{0:T(1024)S(1)} %broadcast_multiply_fusion.2, f32[576,1536]{1,0:T(8,128)S(1)} %get-tuple-element.145, f32[576]{0:T(1024)S(1)} %copy-done.20, f32[1536]{0:T(1024)S(1)} %copy-done.15, ...), kind=kLoop, calls=%fused_computation.124 | loop fusion | flops 13271039 | bytes 21249028 | tf_op jit(solution)/shard_map/convert_element_type | solution.py:1150
  411.0 3.4 collective-permute-done.6
  414.4 4.6 convolution_convert_fusion.4
  419.0 3.5 pad_maximum_fusion.3
  425.0 7.8 %fusion.53.dn_ref = f32[1152,768]{1,0:T(8,128)} fusion(bf16[1152,1536]{1,0:T(8,128)(2,1)} %pad_maximum_fusion.3, bf16[1536,768]{1,0:T(8,128)(2,1)} %get-tuple-element.49), kind=kOutput, calls=%fused_computation.130 | convolution fusion | flops 2717908992 | bytes 9437184 | tf_op jit(solution)/shard_map/dot_general | solution.py:36
  432.8 91.4 %shard_map.264 = (bf16[1152,2304]{1,0:T(8,128)(2,1)}, f32[2,8,384]{2,1,0:T(8,128)}, f32[2,2,2,8,256]{4,3,2,1,0:T(8,128)}, f32[2,2,2,2,8,256]{5,4,3,2,1,0:T(8,128)}) custom-call(f32[16]{0:T(128)} %reshape_squeeze.3.refs_0_.mix_ref, bf16[1152,2304]{1,0:T(8,128)(2,1)} %convolution_convert_fusion.2.refs_1_.qkv_ref, ...), custom_call_target="tpu_custom_call" | custom-call | flops 160000000000 | bytes 120000000 | tf_op jit(solution)/shard_map/pallas_call | solution.py:366
  524.3 9.5 %convolution_convert_fusion.7 = bf16[576,1536]{1,0:T(8,128)(2,1)} fusion(bf16[1536,2304]{1,0:T(8,128)(2,1)} %get-tuple-element.46, bf16[1152,2304]{1,0:T(8,128)(2,1)} %get-tuple-element.64), kind=kOutput, calls=%fused_computation.51 | convolution fusion | flops 4077748224 | bytes 11501568 | tf_op jit(solution)/shard_map/dot_general | solution.py:40
  534.2 0.7 slice.170
  535.5 14.9 %convolution_convert_fusion.1.raw = bf16[1536,2304]{1,0:T(8,128)(2,1)} fusion(bf16[1152,1536]{1,0:T(8,128)(2,1)} %get-tuple-element.45, bf16[1152,2304]{1,0:T(8,128)(2,1)} %get-tuple-element.64), kind=kOutput, calls=%fused_computation.4 | convolution fusion | flops 8157265920 | bytes 15925248 | tf_op jit(solution)/shard_map/dot_general | solution.py:44
  550.5 7.6 fusion.17
  558.1 1.4 concatenate.88
  560.0 6.0 fusion.16
  566.1 15.4 %reduce-scatter.6.cloned.1.call-done.gu = bf16[384,4096]{1,0:T(8,128)(2,1)} async-done(((bf16[1536,4096]{1,0:T(8,128)(2,1)}), bf16[384,4096]{1,0:T(8,128)(2,1)}) %reduce-scatter.6.cloned.1.call-update) | async-done | bytes 3145744 | tf_op jit(solution)/shard_map/reduce_scatter | solution.py:1065
  581.5 149.3 %shard_map.265 = (f32[48,128]{1,0:T(8,128)}, bf16[1536,1024]{1,0:T(8,128)(2,1)}, bf16[1536,2048]{1,0:T(8,128)(2,1)}, bf16[1536,384]{1,0:T(8,128)(2,1)}, bf16[1536,1152]{1,0:T(8,128)(2,1)}) custom-call(f32[48,128]{1,0:T(8,128)} %pad_bitcast_fusion.small, bf16[384,2048]{1,0:T(8,128)(2,1)} %reduce-scatter.4.cloned.1.call-done.down, ...), custom_call_target="tpu_custom_call" | custom-call | tf_op jit(solution)/shard_map/pallas_call | solution.py:986
  730.8 0.8 dynamic_slice.14
  731.7 1.4 fusion.51
  733.1 9.3 %fusion.48 = (f32[1536,1024]{1,0:T(8,128)}, f32[1536,1024]{1,0:T(8,128)}) fusion(bf16[1536,2048]{1,0:T(8,128)(2,1)} %get-tuple-element.71), kind=kLoop, calls=%fused_computation.125 | loop fusion | bytes 25165824 | tf_op jit(solution)/shard_map/slice | solution.py:1206
  742.5 3.4 fusion.49
  746.2 3.4 convert_element_type.129
  749.7 1.6 convert_element_type.127
  753.3 1.4 fusion.50
  (150 shorter events, 14.8 us)
Async XLA Ops:
  7.2 425.6 %reduce-scatter.4.cloned.1.call-start = ((), (), s32[]{:S(2)}) async-start(), calls=%async_computation.3 | async-start | bytes 7864320 | tf_op jit(solution)/shard_map/reduce_scatter | solution.py:1065
  8.6 78.1 %collective-permute-start = (s32[576]{0:T(1024)S(1)}, s32[576]{0:T(1024)S(1)}, u32[]{:S(2)}, u32[]{:S(2)}) collective-permute-start(s32[576]{0:T(1024)S(1)} %get-tuple-element.93), channel_id=1, source_target_pairs={{0,4},{4,0},{1,5},{5,1},{2,6},{6,2},{3,7},{7,3},{8,12},{12,8},{9,1... | collective-permute-start | bytes 6920 | tf_op jit(solution)/shard_map/ppermute | solution.py:1036
  179.1 73.2 %copy-start = (bf16[576,1536]{1,0:T(8,128)(2,1)S(1)}, bf16[576,1536]{1,0:T(8,128)(2,1)}, u32[]{:S(2)}) copy-start(bf16[576,1536]{1,0:T(8,128)(2,1)} %tokens_ref.1) | copy-start | bytes 5308420
  179.1 73.2 %copy-start.26 = (bf16[1536,768]{1,0:T(8,128)(2,1)S(1)}, bf16[1536,768]{1,0:T(8,128)(2,1)}, u32[]{:S(2)}) copy-start(bf16[1536,768]{1,0:T(8,128)(2,1)} %get-tuple-element.49) | copy-start | bytes 7077892
  179.1 73.2 %copy-start.27 = (bf16[1152,768]{1,0:T(8,128)(2,1)S(1)}, bf16[1152,768]{1,0:T(8,128)(2,1)}, u32[]{:S(2)}) copy-start(bf16[1152,768]{1,0:T(8,128)(2,1)} %get-tuple-element.48) | copy-start | bytes 5308420
  182.7 71.9 %copy-start.14 = (f32[1536]{0:T(1024)S(1)}, f32[1536]{0:T(1024)}, u32[]{:S(2)}) copy-start(f32[1536]{0:T(1024)} %param.26) | copy-start | bytes 18436
  182.8 69.5 %collective-permute-start.1 = (bf16[576,1536]{1,0:T(8,128)(2,1)S(1)}, bf16[576,1536]{1,0:T(8,128)(2,1)S(1)}, u32[]{:S(2)}, u32[]{:S(2)}) collective-permute-start(bf16[576,1536]{1,0:T(8,128)(2,1)S(1)} %convolution_convert_fusion.6), channel_id=1, source_target_pairs={{0,4},{4,0},{1,5},{5,1},{2,6},{6,2},{3,7},{7,3},{8,12},{12,8},{9,1... | collective-permute-start | bytes 5308424 | tf_op jit(solution)/shard_map/ppermute | solution.py:1036
  254.7 27.1 %copy-start.12 = (f32[576]{0:T(1024)}, f32[576]{0:T(1024)S(1)}, u32[]{:S(2)}) copy-start(f32[576]{0:T(1024)S(1)} %get-tuple-element.130) | copy-start | bytes 6916
  254.7 34.9 %slice-start.1 = ((s8[6291456]{0:T(1024)(128)(4,1)}), s8[4194304]{0:T(1024)(128)(4,1)S(1)}, s32[]{:S(2)}) async-start(s8[6291456]{0:T(1024)(128)(4,1)} %bitcast.61), calls=%async_computation.7 | async-start | bytes 8388608
  255.1 26.8 %copy-start.9 = (bf16[576,1536]{1,0:T(8,128)(2,1)}, bf16[576,1536]{1,0:T(8,128)(2,1)S(1)}, u32[]{:S(2)}) copy-start(bf16[576,1536]{1,0:T(8,128)(2,1)S(1)} %multiply_convert_fusion.1) | copy-start | bytes 5308420
  255.1 3.8 collective-permute-start.2
  258.8 23.0 %copy-start.25 = (bf16[576,1536]{1,0:T(8,128)(2,1)}, bf16[576,1536]{1,0:T(8,128)(2,1)S(1)}, u32[]{:S(2)}) copy-start(bf16[576,1536]{1,0:T(8,128)(2,1)S(1)} %collective-permute-done.2) | copy-start | bytes 5308420
  258.8 30.8 %slice-start.2 = ((s8[6291456]{0:T(1024)(128)(4,1)}), s8[2097152]{0:T(1024)(128)(4,1)S(1)}, s32[]{:S(2)}) async-start(s8[6291456]{0:T(1024)(128)(4,1)} %bitcast.61), calls=%async_computation.8 | async-start | bytes 4194304
  289.6 7.6 %copy-start.8 = (bf16[576,1536]{1,0:T(8,128)(2,1)S(1)}, bf16[576,1536]{1,0:T(8,128)(2,1)}, u32[]{:S(2)}) copy-start(bf16[576,1536]{1,0:T(8,128)(2,1)} %param.16) | copy-start | bytes 5308420
  293.5 3.8 collective-permute-start.3
  303.4 3.7 collective-permute-start.4
  339.1 227.0 %reduce-scatter.8.cloned.1.call-start = ((), (), s32[]{:S(2)}) async-start(), calls=%async_computation.5 | async-start | bytes 2949120 | tf_op jit(solution)/shard_map/reduce_scatter | solution.py:1065
  339.1 10.9 %copy-start.6 = (bf16[1152,2048]{1,0:T(8,128)(2,1)S(1)}, bf16[1152,2048]{1,0:T(8,128)(2,1)}, u32[]{:S(2)}) copy-start(bf16[1152,2048]{1,0:T(8,128)(2,1)} %get-tuple-element.96) | copy-start | bytes 14155780
  339.2 10.9 %copy-start.10 = (bf16[576,1536]{1,0:T(8,128)(2,1)S(1)}, bf16[576,1536]{1,0:T(8,128)(2,1)}, u32[]{:S(2)}) copy-start(bf16[576,1536]{1,0:T(8,128)(2,1)} %copy-done.9) | copy-start | bytes 5308420
  372.3 16.0 %copy-start.4 = (bf16[1152,4096]{1,0:T(8,128)(2,1)S(1)}, bf16[1152,4096]{1,0:T(8,128)(2,1)}, u32[]{:S(2)}) copy-start(bf16[1152,4096]{1,0:T(8,128)(2,1)} %pad_maximum_fusion) | copy-start | bytes 28311556
  372.3 16.0 %copy-start.13 = (f32[576]{0:T(1024)S(1)}, f32[576]{0:T(1024)}, u32[]{:S(2)}) copy-start(f32[576]{0:T(1024)} %copy-done.12) | copy-start | bytes 6916
  372.3 16.0 %copy-start.15 = (f32[1536]{0:T(1024)S(1)}, f32[1536]{0:T(1024)}, u32[]{:S(2)}) copy-start(f32[1536]{0:T(1024)} %param.26) | copy-start | bytes 18436
  384.4 17.0 %copy-start.20 = (f32[576]{0:T(1024)S(1)}, f32[576]{0:T(1024)}, u32[]{:S(2)}) copy-start(f32[576]{0:T(1024)} %get-tuple-element.129) | copy-start | bytes 6916
  384.4 3.9 collective-permute-start.5
  401.3 13.1 %copy-start.28 = (bf16[1152,768]{1,0:T(8,128)(2,1)S(1)}, bf16[1152,768]{1,0:T(8,128)(2,1)}, u32[]{:S(2)}) copy-start(bf16[1152,768]{1,0:T(8,128)(2,1)} %get-tuple-element.48) | copy-start | bytes 5308420
  410.7 3.7 copy-start.5
  410.7 3.7 collective-permute-start.6
  422.5 1.5 copy-start.1
  422.5 159.0 %reduce-scatter.6.cloned.1.call-start = ((), (), s32[]{:S(2)}) async-start(), calls=%async_computation.4 | async-start | bytes 15728640 | tf_op jit(solution)/shard_map/reduce_scatter | solution.py:1065
  524.2 9.7 %copy-start.16 = (f32[2,2,2,2,8,256]{5,4,3,2,1,0:T(8,128)S(1)}, f32[2,2,2,2,8,256]{5,4,3,2,1,0:T(8,128)}, u32[]{:S(2)}) copy-start(f32[2,2,2,2,8,256]{5,4,3,2,1,0:T(8,128)} %get-tuple-element.61) | copy-start | bytes 393220
  524.2 10.7 %copy-start.21 = (f32[2,2,2,8,256]{4,3,2,1,0:T(8,128)S(1)}, f32[2,2,2,8,256]{4,3,2,1,0:T(8,128)}, u32[]{:S(2)}) copy-start(f32[2,2,2,8,256]{4,3,2,1,0:T(8,128)} %get-tuple-element.62) | copy-start | bytes 196612
  533.7 16.7 %collective-permute-start.7 = (bf16[576,1536]{1,0:T(8,128)(2,1)}, bf16[576,1536]{1,0:T(8,128)(2,1)}, u32[]{:S(2)}, u32[]{:S(2)}) collective-permute-start(bf16[576,1536]{1,0:T(8,128)(2,1)} %convolution_convert_fusion.7), channel_id=1, source_target_pairs={{0,4},{4,0},{1,5},{5,1},{2,6},{6,2},{3,7},{7,3},{8,12},{12,8},{9,1... | collective-permute-start | bytes 5308424 | tf_op jit(solution)/shard_map/ppermute | solution.py:1036
  535.4 14.9 %copy-start.2 = (bf16[576,1536]{1,0:T(8,128)(2,1)S(1)}, bf16[576,1536]{1,0:T(8,128)(2,1)}, u32[]{:S(2)}) copy-start(bf16[576,1536]{1,0:T(8,128)(2,1)} %tokens_ref.1) | copy-start | bytes 5308420
  535.5 15.0 %copy-start.17 = (f32[1536]{0:T(1024)S(1)}, f32[1536]{0:T(1024)}, u32[]{:S(2)}) copy-start(f32[1536]{0:T(1024)} %param.18) | copy-start | bytes 18436
  535.5 14.9 %copy-start.19 = (f32[576]{0:T(1024)S(1)}, f32[576]{0:T(1024)}, u32[]{:S(2)}) copy-start(f32[576]{0:T(1024)} %get-tuple-element.128) | copy-start | bytes 6916
  535.5 14.9 %copy-start.24 = (bf16[1536,2304]{1,0:T(8,128)(2,1)S(1)}, bf16[1536,2304]{1,0:T(8,128)(2,1)}, u32[]{:S(2)}) copy-start(bf16[1536,2304]{1,0:T(8,128)(2,1)} %get-tuple-element.46) | copy-start | bytes 21233668
  535.5 14.9 %copy-start.29 = (bf16[1152,2304]{1,0:T(8,128)(2,1)S(1)}, bf16[1152,2304]{1,0:T(8,128)(2,1)}, u32[]{:S(2)}) copy-start(bf16[1152,2304]{1,0:T(8,128)(2,1)} %get-tuple-element.64) | copy-start | bytes 15925252
  550.4 7.6 copy-start.23
  550.4 9.6 %copy-start.18 = (f32[576]{0:T(1024)S(1)}, f32[576]{0:T(1024)}, u32[]{:S(2)}) copy-start(f32[576]{0:T(1024)} %get-tuple-element.127) | copy-start | bytes 6916
  731.6 10.9 %copy-start.22 = (f32[656]{0:T(1024)}, f32[656]{0:T(1024)S(1)}, u32[]{:S(2)}) copy-start(f32[656]{0:T(1024)S(1)} %dynamic_slice.14) | copy-start | bytes 7876
  733.1 9.3 %copy-start.3 = (bf16[1536,1152]{1,0:T(8,128)(2,1)S(1)}, bf16[1536,1152]{1,0:T(8,128)(2,1)}, u32[]{:S(2)}) copy-start(bf16[1536,1152]{1,0:T(8,128)(2,1)} %get-tuple-element.69) | copy-start | bytes 10616836
  742.4 3.8 copy-start.7
  746.2 3.4 copy-start.11
  749.7 1.6 slice-start
Sparse Core Ops, SparseCore 0:
  339.2 67.4 reduce-scatter.3
  422.6 34.9 reduce-scatter.7
  460.7 120.7 reduce-scatter.5

commit v4 on v3

--- a/solution.py
+++ b/solution.py
@@ -163,12 +163,14 @@
 
 
 def bwd_kernel(
-    mix_ref, qkv_ref, t_ref, gn_ref, jj_ref, dn_ref, att_ref, pre_ref, qs_ref, ho_ref,
+    hook, mix_ref, qkv_ref, t_ref, gn_ref, jj_ref, dn_ref, att_ref, pre_ref, qs_ref, ho_ref,
     dqkv_ref, ggn_ref, gmix_ref, gconv_ref,
     dist_ref, dh_ref, mx_ref, dm_ref, dc_ref, es_ref, dqx_ref, dk_ref, dv_ref,
 ):
     side, t, g = pl.program_id(0), pl.program_id(1), pl.program_id(2)
     mix0 = 8 * side + 4 * g
+    step = (side * 2 + t) * 2 + g
+    hook(step, 0)
     w0 = pl.multiple_of(g * 128, 128)
     m0, m1, from_first = head_masks(g)
     both = m0 | m1
@@ -238,6 +240,7 @@
         gmix_ref[index : index + 1] = mix_sums[index]
     mirror = lax.broadcasted_iota(jnp.int32, (WIN, WIN), 0) + lax.broadcasted_iota(jnp.int32, (WIN, WIN), 1) - (WIN - 1)
     band = jnp.abs(mirror) <= CK // 2
+    hook(step, 1)
     flip = jnp.where(mirror == 0, 1.0, 0.0).astype(BF16)
     for e in range(2):
         flipped = nn(dc_ref[e], flip).astype(BF16)
@@ -296,6 +299,7 @@
         put(token, size, w0, dqx_ref[ext + 8 : ext + 8 + size])
         put(token, size, k0, dk_ref[token : token + size])
         put(token, size, v0, dv_ref[token : token + size])
+    hook(step, 2)
 
 
 def by_group(shape):
@@ -360,25 +364,43 @@
     return result[0], result[1:5], result[5:]
 
 
-def attention_backward(mix, qkv, toeplitz, gains, jj, d_normed, saved):
+def attention_backward(mix, qkv, toeplitz, gains, jj, d_normed, saved, sums=None):
     trees = qkv.shape[0] // TREE
     shapes = saved_shapes(trees)
-    return pl.pallas_call(
-        bwd_kernel,
+    collective = dict(collective_id=4, has_side_effects=True) if sums else {}
+    many = len(sums or ())
+
+    def kernel(*refs):
+        inputs, extra, refs = refs[:10], refs[10 : 10 + many], refs[10 + many :]
+        outs, full, refs = refs[:4], refs[4 : 4 + many], refs[4 + many :]
+        work = Finish(BESIDE, extra, None, full, None, refs[9:]) if sums else None
+
+        def hook(step, place):
+            if work:
+                beside(work, step, place)
+
+        bwd_kernel(hook, *inputs, *outs, *refs[:9])
+
+    anywhere = pl.BlockSpec(memory_space=pl.ANY)
+    extra_in = [pl.BlockSpec((384, 2048), lambda s, t, g: (0, 0))] if sums else []
+    result = pl.pallas_call(
+        kernel,
         grid=(2, trees, 2),
-        in_specs=common_specs() + [pl.BlockSpec((TREE, 384), lambda s, t, g: (t, s))] + [by_group(s) for s in shapes],
+        in_specs=common_specs() + [pl.BlockSpec((TREE, 384), lambda s, t, g: (t, s))] + [by_group(s) for s in shapes] + extra_in,
         out_specs=[
             pl.BlockSpec((TREE, 1152), lambda s, t, g: (t, s)),
             by_side((8, 384)),
             by_group((2, trees, 2, 8, WIN)),
             by_group((2, trees, 2, 2, 8, WIN)),
-        ],
+        ]
+        + [anywhere] * many,
         out_shape=[
             jax.ShapeDtypeStruct((trees * TREE, 2304), BF16),
             jax.ShapeDtypeStruct((2, 8, 384), F32),
             jax.ShapeDtypeStruct((2, trees, 2, 8, WIN), F32),
             jax.ShapeDtypeStruct((2, trees, 2, 2, 8, WIN), F32),
-        ],
+        ]
+        + [jax.ShapeDtypeStruct((1536, n), BF16) for n in (1024,)[:many]],
         scratch_shapes=[
             pltpu.VMEM((TREE, WIN), jnp.int32),
             pltpu.VMEM((2, TREE, WIN), BF16),
@@ -389,10 +411,12 @@
             pltpu.VMEM((EXT, WIN), F32),
             pltpu.VMEM((TREE, WIN), F32),
             pltpu.VMEM((TREE, WIN), F32),
-        ],
-        compiler_params=pltpu.CompilerParams(**PARAMS),
-        cost_estimate=pl.CostEstimate(flops=160_000_000_000, bytes_accessed=120_000_000, transcendentals=0),
-    )(mix, qkv, toeplitz, gains, jj, d_normed, *saved)
+        ]
+        + (finish_scratch(BESIDE, 128) if sums else []),
+        compiler_params=pltpu.CompilerParams(**PARAMS, **collective),
+        cost_estimate=pl.CostEstimate(flops=1_000_000_000, bytes_accessed=1_000_000, transcendentals=0),
+    )(mix, qkv, toeplitz, gains, jj, d_normed, *saved, *(sums or ()))
+    return result[:4], result[4:]
 
 
 def band_rows(conv_w):
@@ -716,7 +740,8 @@
 
 
 class Finish:
-    def __init__(self, plan, parts, raw, outs, small, bufs):
+    def __init__(self, plan, parts, raw, outs, small, bufs, made=False):
+        self.made = made
         q, c, z = lax.axis_index("plane"), lax.axis_index("core"), lax.axis_index("tensor")
         self.q, self.c = q, c
         self.home = (z // 2) == c
@@ -727,9 +752,10 @@
         self.far = (q, 1 - c, (z + 2) % 4)
         self.across = (q, c, (z + 2) % 4)
         self.plan, self.parts, self.raw, self.outs, self.small = plan, parts, raw, outs, small
-        (self.near_buf, self.far_buf, self.core_buf, self.here_buf, self.total_buf, self.raw_part, self.raw_own, self.raw_first,
-         self.raw_second, self.small_buf, self.small_in, self.send, self.recv, self.raw_send, self.raw_recv, self.small_send,
-         self.small_recv, self.local) = bufs
+        (self.near_buf, self.far_buf, self.core_buf, self.here_buf, self.raw_part, self.raw_own, self.raw_first,
+         self.raw_second, self.send, self.recv, self.raw_send, self.raw_recv, self.local) = bufs[:13]
+        if small is not None:
+            self.small_buf, self.small_in, self.small_send, self.small_recv = bufs[13:]
 
     def remote(self, src, dst, sems, index, peer):
         return pltpu.make_async_remote_copy(
@@ -741,39 +767,53 @@
 
     def part(self, item):
         source = self.plan[item][0]
-        return self.raw_part if source < 0 else self.parts[source]
+        if source >= 0:
+            return self.parts[source]
+        return self.raw.at[self.rows(self.q)] if self.made else self.raw_part
 
     def away(self, action):
         pl.when(jnp.logical_not(self.home))(action)
+
+    def rows(self, owner):
+        return pl.ds(pl.multiple_of(owner * 384, 128), 384)
 
     def raw_copies(self, item):
         cols_a, cols_b, _ = self.columns(item)
         sems = (self.raw_send, self.raw_recv)
-
-        def rows(owner):
-            return pl.ds(pl.multiple_of(owner * 384, 128), 384)
-
         across = 3 - self.q
         x, y = self.by_x[0], self.by_y[0]
-        return [
-            self.remote(self.raw.at[rows(x), cols_a], self.raw_first.at[0, :, cols_a], sems, (item, 0), self.by_x),
-            self.remote(self.raw.at[rows(across), cols_a], self.raw_first.at[1, :, cols_a], sems, (item, 1), self.by_x),
-            self.remote(self.raw.at[rows(y), cols_b], self.raw_first.at[0, :, cols_b], sems, (item, 2), self.by_y),
-            self.remote(self.raw.at[rows(across), cols_b], self.raw_first.at[1, :, cols_b], sems, (item, 3), self.by_y),
-        ], [
-            pltpu.make_async_copy(self.raw.at[rows(self.q), cols_a], self.raw_own.at[0, :, cols_a], self.local.at[item, 0]),
-            pltpu.make_async_copy(self.raw.at[rows(y), cols_a], self.raw_own.at[1, :, cols_a], self.local.at[item, 1]),
-            pltpu.make_async_copy(self.raw.at[rows(self.q), cols_b], self.raw_own.at[0, :, cols_b], self.local.at[item, 2]),
-            pltpu.make_async_copy(self.raw.at[rows(x), cols_b], self.raw_own.at[1, :, cols_b], self.local.at[item, 3]),
+        remote = [
+            self.remote(self.raw.at[self.rows(x), cols_a], self.raw_first.at[0, :, cols_a], sems, (item, 0), self.by_x),
+            self.remote(self.raw.at[self.rows(across), cols_a], self.raw_first.at[1, :, cols_a], sems, (item, 1), self.by_x),
+            self.remote(self.raw.at[self.rows(y), cols_b], self.raw_first.at[0, :, cols_b], sems, (item, 2), self.by_y),
+            self.remote(self.raw.at[self.rows(across), cols_b], self.raw_first.at[1, :, cols_b], sems, (item, 3), self.by_y),
         ]
+        if self.made:
+            return remote, []
+        return remote, [
+            pltpu.make_async_copy(self.raw.at[self.rows(self.q), cols_a], self.raw_own.at[0, :, cols_a], self.local.at[item, 0]),
+            pltpu.make_async_copy(self.raw.at[self.rows(y), cols_a], self.raw_own.at[1, :, cols_a], self.local.at[item, 1]),
+            pltpu.make_async_copy(self.raw.at[self.rows(self.q), cols_b], self.raw_own.at[0, :, cols_b], self.local.at[item, 2]),
+            pltpu.make_async_copy(self.raw.at[self.rows(x), cols_b], self.raw_own.at[1, :, cols_b], self.local.at[item, 3]),
+        ]
+
+    def raw_place(self, which, side, cols):
+        if self.made:
+            owner = self.q if which == 0 else (self.by_y[0], self.by_x[0])[side]
+            return self.raw, (self.rows(owner), cols)
+        return self.raw_own, (which, slice(None), cols)
 
     def raw_second_copies(self, item):
-        cols_a, cols_b, _ = self.columns(item)
         sems = (self.raw_send, self.raw_recv)
-        return [
-            self.remote(self.raw_own.at[1, :, cols_a], self.raw_second.at[:, cols_a], sems, (item, 4), self.by_y),
-            self.remote(self.raw_own.at[1, :, cols_b], self.raw_second.at[:, cols_b], sems, (item, 5), self.by_x),
-        ]
+        copies = []
+        for side, cols in enumerate(self.columns(item)[:2]):
+            ref, place = self.raw_place(1, side, cols)
+            copies.append(self.remote(ref.at[place], self.raw_second.at[:, cols], sems, (item, 4 + side), (self.by_y, self.by_x)[side]))
+        return copies
+
+    def r1_side(self, item, side):
+        for copy in self.raw_copies(item)[0][2 * side : 2 * side + 2]:
+            copy.start()
 
     def r1(self, item):
         for group in self.raw_copies(item):
@@ -786,7 +826,8 @@
             copy.wait()
         for side, cols in enumerate(self.columns(item)[:2]):
             remote[2 * side + 1].wait_recv()
-            self.raw_own[1, :, cols] = added(self.raw_own[1, :, cols], self.raw_first[1, :, cols])
+            ref, place = self.raw_place(1, side, cols)
+            ref[place] = added(ref[place], self.raw_first[1, :, cols])
             self.raw_second_copies(item)[side].start()
 
     def r3(self, item):
@@ -794,8 +835,9 @@
         for side, cols in enumerate(self.columns(item)[:2]):
             remote[2 * side].wait_recv()
             self.raw_second_copies(item)[side].wait_recv()
-            total = self.raw_own[0, :, cols].astype(F32) + self.raw_first[0, :, cols].astype(F32) + self.raw_second[:, cols].astype(F32)
-            self.raw_part[:, cols] = total.astype(BF16)
+            ref, place = self.raw_place(0, side, cols)
+            total = ref[place].astype(F32) + self.raw_first[0, :, cols].astype(F32) + self.raw_second[:, cols].astype(F32)
+            self.part(item)[:, cols] = total.astype(BF16)
 
     def near_copy(self, item):
         _, cols_b, at = self.columns(item)
@@ -844,7 +886,7 @@
         def rows(owner, first, size):
             return pl.ds(pl.multiple_of(owner * 384 + half + first, 32), size)
 
-        mine = self.total_buf.at[pl.ds(pl.multiple_of(half, 32), 192), spot]
+        mine = self.core_buf.at[pl.ds(pl.multiple_of(half, 32), 192), spot]
         x, y, across = self.by_x[0], self.by_y[0], 3 - self.q
         own = out.at[rows(self.q, 0, 192), at]
         top, low = out.at[rows(x, 0, 96), at], out.at[rows(y, 96, 96), at]
@@ -861,7 +903,7 @@
     def own_copy(self, item):
         out = self.outs[self.plan[item][4]]
         rows = pl.ds(pl.multiple_of(self.q * 384, 128), 384)
-        return pltpu.make_async_copy(self.total_buf.at[:, self.spot(item)], out.at[rows, self.columns(item)[2]], self.local.at[item, 4])
+        return pltpu.make_async_copy(self.core_buf.at[:, self.spot(item)], out.at[rows, self.columns(item)[2]], self.local.at[item, 4])
 
     def s4(self, item):
         spot = self.spot(item)
@@ -869,12 +911,12 @@
         @pl.when(self.home)
         def _():
             self.core_copy(item, False).wait_recv()
-            self.total_buf[:, spot] = added(self.here_buf[:, spot], self.core_buf[:, spot])
+            self.core_buf[:, spot] = added(self.here_buf[:, spot], self.core_buf[:, spot])
 
         @self.away
         def _():
             self.core_copy(item, True).wait_recv()
-            self.total_buf[:, spot] = added(self.far_buf[:, spot], self.core_buf[:, spot])
+            self.core_buf[:, spot] = added(self.far_buf[:, spot], self.core_buf[:, spot])
 
         self.own_copy(item).start()
         copies = self.plane_copies(item)
@@ -923,7 +965,6 @@
         return self.remote(self.small_buf.at[turn], self.small_in.at[turn], (self.small_send, self.small_recv), turn, peer)
 
     def small_start(self):
-        self.small_buf[0] = self.small[...]
         self.small_copy(0).start()
 
     def small_next(self, turn):
@@ -944,61 +985,219 @@
 
 FINISH = (
     (0, 0, 1024, 1024, 0, 0, 0),
-    (1, 0, 1024, 1024, 1, 1024, 0),
-    (1, 2048, 3072, 1024, 1, 2048, 1024),
-    (2, 0, 384, 384, 2, 3072, 0),
-    (-1, 0, 1152, 384, 3, 3456, 0),
-    (-1, 384, 1536, 384, 3, 3840, 384),
-    (-1, 768, 1920, 384, 3, 4224, 768),
+    (0, 2048, 3072, 1024, 0, 1024, 1024),
+    (-1, 0, 1152, 384, 1, 2048, 0),
+    (-1, 384, 1536, 384, 1, 2432, 384),
+    (-1, 768, 1920, 384, 1, 2816, 768),
 )
-
-
-def finish_kernel(small, down, gu, out, raw, small_out, o_down, o_gu, o_out, o_qkv, *bufs):
-    work = Finish(FINISH, (down, gu, out), raw, (o_down, o_gu, o_out, o_qkv), small, bufs)
+LONE = ((-1, 0, 384, 384, 0, 0, 0),)
+BESIDE = (
+    (0, 0, 1024, 512, 0, 0, 0),
+    (0, 512, 1536, 512, 0, 512, 512),
+)
+BESIDE_STEPS = (
+    (("greet", 0), ("s1", 0), ("s1", 1)),
+    (),
+    (("s2", 0),),
+    (("s2", 1),),
+    (("s3", 0),),
+    (("s3", 1),),
+    (("s4", 0),),
+    (("s4", 1),),
+    (),
+    (),
+    (("s5", 0),),
+    (("s5", 1),),
+    (),
+    (("s6", 0),),
+    (("s6", 1),),
+)
+
+
+def finish_scratch(plan, raw_width, made=False):
+    count, width = len(plan), sum(item[3] for item in plan)
+    return (
+        [pltpu.VMEM((384, width), BF16)] * 4
+        + [pltpu.VMEM((384, 128 if made else raw_width), BF16)]
+        + [pltpu.VMEM((2, 384, 128 if made else raw_width), BF16), pltpu.VMEM((2, 384, raw_width), BF16)]
+        + [pltpu.VMEM((384, raw_width), BF16)]
+        + [pltpu.SemaphoreType.DMA((count, 10))] * 2
+        + [pltpu.SemaphoreType.DMA((count, 6))] * 2
+        + [pltpu.SemaphoreType.DMA((count, 5))]
+    )
+
+
+def beside(work, step, place):
+    if place == 2:
+
+        @pl.when(step == 7)
+        def _():
+            for item in range(len(work.plan)):
+                work.s7(item)
+
+        return
+
+    for slot, names in enumerate(BESIDE_STEPS):
+        if slot % 2 == place:
+
+            @pl.when(step == slot // 2)
+            def _(names=names):
+                for name, item in names:
+                    if name == "greet":
+                        greet((work.near, work.far, work.by_x, work.by_y, work.core))
+                    else:
+                        getattr(work, name)(item)
+
+
+def finish_kernel(
+    small, gu, out, normed_t, d_qkv, weight, tokens, gain, d_hidden, small_out, d_input, o_gu, o_qkv, o_out,
+    made, partner, arrived, loaded, load_sem, hidden_buf, tokens_buf, hidden_sem, core_send, core_recv, *bufs,
+):
+    lone = Finish(LONE, (), out, (o_out,), None, bufs[-13:])
+    work = Finish(FINISH, (gu,), made, (o_gu, o_qkv), small, bufs[:-13], True)
+    rows = tokens.shape[0]
+
+    def load(part):
+        return pltpu.make_async_copy(weight.at[384 * part : 384 * (part + 1)], loaded.at[part % 2], load_sem.at[part % 2])
+
+    def exchange(part):
+        cols = pl.ds(384 * part, 384)
+        return work.remote(partner.at[:, cols], arrived.at[:, cols], (core_send, core_recv), part, work.core)
+
+    def load_hidden(part):
+        span = pl.ds(64 * part, 64)
+        return (
+            pltpu.make_async_copy(d_hidden.at[span], hidden_buf.at[part % 2], hidden_sem.at[0, part % 2]),
+            pltpu.make_async_copy(tokens.at[span], tokens_buf.at[part % 2], hidden_sem.at[1, part % 2]),
+        )
+
+    load(0).start()
+    load(1).start()
+    for copy in load_hidden(0):
+        copy.start()
     greet((work.near, work.far, work.by_x, work.by_y, work.core, work.across))
-    for item in (4, 5, 6):
-        work.r1(item)
+    lone.r1(0)
     work.s1(0)
+
+    def make(side, owner):
+        cols = slice(1152 * side, 1152 * (side + 1))
+        made[work.rows(owner), cols] = nn(normed_t[work.rows(owner), :], d_qkv[:, cols]).astype(BF16)
+
+    across = 3 - work.q
+    for side, owners in enumerate(((across, work.by_x[0]), (across, work.by_y[0]))):
+        for owner in owners:
+            make(side, owner)
+        for item in (2, 3, 4):
+            work.r1_side(item, side)
+    work.s2(0)
     work.s1(1)
+    lone.r2(0)
+    make(0, work.by_y[0])
+    make(1, work.by_x[0])
+    work.s3(0)
+    make(0, work.q)
+    make(1, work.q)
+    work.r2(2)
+    lone.r3(0)
+    lone.s1(0)
+    work.s4(0)
+
+    def back(part):
+        cols = slice(384 * part, 384 * (part + 1))
+        load(part).wait()
+        both = nt(d_qkv[...], loaded[part % 2])
+        d_input[:, cols] = both[:rows]
+        partner[:, cols] = both[rows:].astype(BF16)
+        if part < 2:
+            load(part + 2).start()
+        exchange(part).start()
+
+    back(0)
+    work.r2(3)
+    work.s2(1)
+    back(1)
+    work.r2(4)
+    work.r3(2)
+    work.s1(2)
+    back(2)
+    work.s3(1)
+    lone.s2(0)
+    work.r3(3)
+    work.s1(3)
+    work.s5(0)
+    back(3)
+    work.s2(2)
+    work.r3(4)
+    work.s1(4)
+    work.s4(1)
+    for part in range(4):
+        exchange(part).wait_recv()
+    gain_sum = jnp.zeros((1, tokens.shape[1]), F32)
+    for part in range(rows // 64):
+        span = slice(64 * part, 64 * (part + 1))
+        if part + 1 < rows // 64:
+            for copy in load_hidden(part + 1):
+                copy.start()
+        for copy in load_hidden(part):
+            copy.wait()
+        x = tokens_buf[part % 2].astype(F32)
+        inv = lax.rsqrt(jnp.mean(x * x, axis=-1, keepdims=True) + 1e-06)
+        d_normed = d_input[span] + arrived[span].astype(F32)
+        scaled = d_normed * gain[...]
+        gain_sum = gain_sum + jnp.sum(d_normed * x * inv, axis=0, keepdims=True)
+        d_input[span] = hidden_buf[part % 2] + inv * scaled - x * inv**3 * jnp.mean(scaled * x, axis=-1, keepdims=True)
+    work.small_buf[0] = small[...]
+    work.small_buf[0, 0:1] = gain_sum
     work.small_start()
     script = (
-        ("s2", 0), ("s1", 2), ("r2", 4), ("s3", 0), ("m", 0),
-        ("s2", 1), ("s1", 3), ("r2", 5), ("s4", 0), ("s3", 1), ("m", 1),
-        ("r2", 6), ("s2", 2), ("r3", 4), ("s1", 4), ("s5", 0), ("s4", 1), ("s3", 2), ("m", 2),
-        ("r3", 5), ("s1", 5), ("s2", 3), ("r3", 6), ("s1", 6), ("s6", 0), ("s5", 1), ("s4", 2), ("s3", 3), ("m", 3),
-        ("s2", 4), ("s6", 1), ("s5", 2), ("s4", 3), ("s3", 4), ("m", 4),
-        ("s2", 5), ("s6", 2), ("s5", 3), ("s4", 4), ("s3", 5),
-        ("s2", 6), ("s6", 3), ("s5", 4), ("s4", 5), ("s3", 6),
-        ("s6", 4), ("s5", 5), ("s4", 6), ("s6", 5), ("s5", 6), ("s6", 6),
+        ("s3", 2), ("s2", 3), ("s3", 5), ("s6", 0), ("m", 0),
+        ("s5", 1), ("s4", 2), ("s3", 3), ("s2", 4), ("s4", 5), ("m", 1),
+        ("s6", 1), ("s5", 2), ("s4", 3), ("s3", 4), ("s5", 5), ("m", 2),
+        ("s6", 2), ("s5", 3), ("s4", 4), ("s6", 5), ("m", 3), ("s6", 3), ("s5", 4), ("m", 4), ("s6", 4),
     )
     for name, item in script:
-        (work.small_next if name == "m" else getattr(work, name))(item)
+        if name == "m":
+            work.small_next(item)
+        elif item == 5:
+            getattr(lone, name)(0)
+        else:
+            getattr(work, name)(item)
     for item in range(len(FINISH)):
         work.s7(item)
+    lone.s7(0)
+    for part in range(4):
+        exchange(part).wait_send()
     work.small_done(small_out)
 
 
-def finish_gradients(small, down, gu, out, raw, collective_id):
+def finish_gradients(small, gu, out, normed_t, d_qkv, weight, tokens, gain, d_hidden, collective_id):
     vmem = pl.BlockSpec(memory_space=pltpu.VMEM)
     anywhere = pl.BlockSpec(memory_space=pl.ANY)
-    rows, width, count = 384, 4608, len(FINISH)
-    wide = (rows, width)
+    rows, width = tokens.shape
     return pl.pallas_call(
         finish_kernel,
-        in_specs=[vmem] * 4 + [anywhere],
-        out_specs=[vmem] + [anywhere] * 4,
-        out_shape=[jax.ShapeDtypeStruct(small.shape, F32)] + [jax.ShapeDtypeStruct((1536, n), BF16) for n in (1024, 2048, 384, 1152)],
-        scratch_shapes=[pltpu.VMEM(wide, BF16)] * 5
-        + [pltpu.VMEM((rows, 2304), BF16)]
-        + [pltpu.VMEM((2, rows, 2304), BF16)] * 2
-        + [pltpu.VMEM((rows, 2304), BF16)]
+        in_specs=[vmem] * 2 + [anywhere] + [vmem] * 2 + [anywhere] * 2 + [vmem] + [anywhere],
+        out_specs=[vmem] * 2 + [anywhere] * 3,
+        out_shape=[jax.ShapeDtypeStruct(small.shape, F32), jax.ShapeDtypeStruct((rows, width), F32)]
+        + [jax.ShapeDtypeStruct((1536, n), BF16) for n in (2048, 1152, 384)],
+        scratch_shapes=[
+            pltpu.VMEM((1536, 2304), BF16),
+            pltpu.VMEM((rows, width), BF16),
+            pltpu.VMEM((rows, width), BF16),
+            pltpu.VMEM((2, 384, 2304), BF16),
+            pltpu.SemaphoreType.DMA((2,)),
+            pltpu.VMEM((2, 64, width), F32),
+            pltpu.VMEM((2, 64, width), BF16),
+            pltpu.SemaphoreType.DMA((2, 2)),
+            pltpu.SemaphoreType.DMA((4,)),
+            pltpu.SemaphoreType.DMA((4,)),
+        ]
+        + finish_scratch(FINISH, 2304, True)
         + [pltpu.VMEM((6,) + small.shape, F32), pltpu.VMEM((5,) + small.shape, F32)]
-        + [pltpu.SemaphoreType.DMA((count, 10))] * 2
-        + [pltpu.SemaphoreType.DMA((count, 6))] * 2
         + [pltpu.SemaphoreType.DMA((5,))] * 2
-        + [pltpu.SemaphoreType.DMA((count, 5))],
+        + finish_scratch(LONE, 768),
         compiler_params=pltpu.CompilerParams(collective_id=collective_id, has_side_effects=True, vmem_limit_bytes=60 * 1024 * 1024),
-    )(small, down, gu, out, raw)
+    )(small, gu, out, normed_t, d_qkv, weight, tokens, gain, d_hidden)
 
 
 def rows_dot(lhs, rhs):
@@ -1150,45 +1349,43 @@
         d_attn = with_partner(d_hidden_in.astype(BF16))
         out_grads = rows_dot(d_attn, heads_out)
         out_grads, d_attn = lax.optimization_barrier((out_grads, d_attn))
-        out_part = plane_sum(out_grads)
         d_normed = nn(d_attn, out_weight)
         d_normed, down_part = lax.optimization_barrier((d_normed, down_part))
-        d_qkv, ggn, gmix, gconv = attention_backward(mix, qkv, toep, gains, jj, d_normed, saved)
+        (d_qkv, ggn, gmix, gconv), done = attention_backward(
+            mix, qkv, toep, gains, jj, d_normed, saved, (down_part,) if fused else None
+        )
         small_grads = jnp.concatenate([conv_grads(gconv), mix_grads(gmix), ggn[:, 0]], axis=1)
-        qkv_grads = rows_dot(normed_one, d_qkv)
-        d_normed_one = summed(d_qkv, qkv_weight)
-        scaled_one = d_normed_one * gain_one
-        grad_gain_one = jnp.sum(d_normed_one * inputs * inv_one, axis=0)
-        grad_input = (
-            d_hidden_in + inv_one * scaled_one - inputs * inv_one**3 * jnp.mean(scaled_one * inputs, axis=-1, keepdims=True)
-        )
-
         table = jnp.zeros((tensors, small_size), F32)
         table = lax.dynamic_update_slice(table, small_grads[:1], (2 * c + z % 2, 0))
         table = lax.dynamic_update_slice(table, small_grads[1:], (2 * c + 1 - z % 2, 0))
-        packed = jnp.concatenate(
-            [table.reshape(-1), grad_gain_one, grad_gain_two, squared_sum[None], count_sum[None]]
-        )
+        table = jnp.pad(table.reshape(-1), (0, 4 * width - table.size)).reshape(4, width)
+        last = jnp.pad(jnp.stack([squared_sum, count_sum]), (0, 2 * width - 2)).reshape(2, width)
+        packed = jnp.concatenate([jnp.zeros((1, width), F32), grad_gain_two[None], table, last])
         if fused:
-            length = packed.size
-            lines = -(-length // 1024) * 8
-            packed = jnp.pad(packed, (0, lines * 128 - length)).reshape(lines, 128)
-            packed, *sums = finish_gradients(packed, down_part, gu_part, out_part, qkv_grads, 2)
-            packed = packed.reshape(-1)[:length]
+            packed, grad_input, sum_gu, sum_qkv, sum_out = finish_gradients(
+                packed, gu_part, out_grads, normed_one.T, d_qkv, qkv_weight, tokens, gain_one[None], d_hidden_in, 2
+            )
+            sums = [done[0], sum_gu, sum_out, sum_qkv]
         else:
+            qkv_grads = rows_dot(normed_one, d_qkv)
+            d_normed_one = summed(d_qkv, qkv_weight)
+            scaled_one = d_normed_one * gain_one
+            packed = packed.at[0].set(jnp.sum(d_normed_one * inputs * inv_one, axis=0))
+            grad_input = (
+                d_hidden_in + inv_one * scaled_one - inputs * inv_one**3 * jnp.mean(scaled_one * inputs, axis=-1, keepdims=True)
+            )
             packed = lax.psum(packed, every)
-            qkv_part = plane_sum(qkv_grads)
+            out_part, qkv_part = plane_sum(out_grads), plane_sum(qkv_grads)
             sums = [reduce(part[:, : part.shape[1] // 2], part[:, part.shape[1] // 2 :]) for part in (down_part, out_part, qkv_part)]
             places = [slice(i * units, (i + 1) * units) for i in range(4)]
             first, second = [jnp.concatenate([gu_part[:, places[i]], gu_part[:, places[i + 2]]], axis=1) for i in range(2)]
             sums.insert(1, reduce(first, second))
         grad_down, grad_gu, grad_out, grad_qkv = [value.astype(F32) for value in sums]
-        table_size = tensors * small_size
-        small_sum = lax.dynamic_slice_in_dim(packed, z * small_size, small_size, 0)
+        small_sum = lax.dynamic_slice_in_dim(packed[2:6].reshape(-1), z * small_size, small_size, 0)
         gain_slice = width // tensors
-        gain_one_out = lax.dynamic_slice_in_dim(packed, table_size + z * gain_slice, gain_slice, 0)
-        gain_two_out = lax.dynamic_slice_in_dim(packed, table_size + width + z * gain_slice, gain_slice, 0)
-        loss = packed[-2] / (packed[-1] * width)
+        gain_one_out = lax.dynamic_slice_in_dim(packed[0], z * gain_slice, gain_slice, 0)
+        gain_two_out = lax.dynamic_slice_in_dim(packed[1], z * gain_slice, gain_slice, 0)
+        loss = packed[6, 0] / (packed[6, 1] * width)
         return (
             output,
             loss,

time: 774 us -> 723 us (0.934)
  matrix products: 174 us -> 141 us
  waiting for transfers between devices: 36.4 us -> 17 us
  local copies, waits for them, and re-layouts: 30 us -> 42.6 us
  other arithmetic: 49.8 us -> 39.5 us
    dot_general x8 -> x6, matrix products: 57.6 us -> 40.4 us  [nt(): lax.dot_general(a, b, (((1,), (1,)), ((), ())), preferred_element_type=F32)]
    reduce_scatter x3 -> x2, waiting for transfers between devices: 15.4 us -> 0.01 us  [plane_sum(): return lax.psum_scatter(grads, 'plane', scatter_dimension=0, tiled=True)]
    dot_general x4 -> x3, matrix products: 52 us -> 39.4 us  [tn(): lax.dot_general(a, b, (((0,), (0,)), ((), ())), preferred_element_type=F32)]
    ppermute x8 -> x7, waiting for transfers between devices: 20.3 us -> 17 us  [over_core(): return lax.ppermute(value, 'core', [(0, 1), (1, 0)])]
    ppermute x8 -> x7, starting transfers between devices: 68.6 us -> 68.2 us  [over_core(): return lax.ppermute(value, 'core', [(0, 1), (1, 0)])]
  transfers between devices with their start and end apart: 11 -> 9, of which waited for: 7 -> 5; matrix products, arithmetic and copies ran while one was open for 19% -> 18% of each run, Pallas kernels for 19% -> 23%
where the time goes in v4:
time: 723 us; the launch traced here: 719 us
  Pallas kernels  393 us (54%)
  matrix products  141 us (20%)
  starting transfers between devices  68.3 us (9%)
  local copies, waits for them, and re-layouts  42.6 us (6%)
  other arithmetic  39.5 us (5%)
  between operations  17.3 us (2%)
  waiting for transfers between devices  17 us (2%)
    pallas_call x1, Pallas kernels, finish_gradients(): pl.pallas_call(finish_kernel, in_specs=[vmem] * 2 + [anywhere] + [vmem] *...  139 us
    pallas_call x1, Pallas kernels, attention_backward(): pl.pallas_call(kernel, grid=(2, trees, 2), in_specs=common_specs() + [pl....  106 us
    pallas_call x1, Pallas kernels, attention_forward(): pl.pallas_call(kernel, grid=(2, trees, 2), in_specs=common_specs() + [any...  90 us
    ppermute x7, starting transfers between devices, over_core(): return lax.ppermute(value, 'core', [(0, 1), (1, 0)])  68.2 us
    dot_general x4, matrix products, nn(): lax.dot_general(a, b, (((1,), (0,)), ((), ())), preferred_element_type=F32)  61.5 us
    pallas_call x1, Pallas kernels, opening(): pl.pallas_call(opening_kernel, in_specs=[vmem] * 3 + [anywhere] * 3, out_...  57.4 us
    dot_general x6, matrix products, nt(): lax.dot_general(a, b, (((1,), (1,)), ((), ())), preferred_element_type=F32)  40.4 us
    dot_general x3, matrix products, tn(): lax.dot_general(a, b, (((0,), (0,)), ((), ())), preferred_element_type=F32)  39.4 us
  transfers between devices with their start and end apart: 9, of which 5 were waited for; matrix products, arithmetic and copies ran while one was open for 18% of the time, Pallas kernels for 23%

profile of v4, /device:TPU:0, one launch (start us, length us, event | category | flops | bytes accessed | tf_op | source)
XLA Modules:
  0.0 718.7 jit_solution(3959732623637113433)
XLA Ops:
  7.2 1.4 fusion.37
  11.4 1.3 broadcast_in_dim.51.gain_ref.gain
  13.5 57.4 %shard_map.262 = (bf16[1536,2304]{1,0:T(8,128)(2,1)}, bf16[1152,1536]{1,0:T(8,128)(2,1)}, bf16[2,2,2,1536,256]{4,3,2,1,0:T(8,128)(2,1)}, f32[2,32,256]{2,1,0:T(8,128)}) custom-call(bf16[576,1536]{1,0:T(8,128)(2,1)} %tokens.1, f32[1,1536]{1,0:T(1,128)} %broadcast_in_dim.51.gain_ref.gain, f32[32,256]{1,0:T(8,128)} %fusion.27.small_ref, ...), custom_call_target="tpu_custom_call" | custom-call | tf_op jit(solution)/shard_map/pallas_call | solution.py:727
  72.4 13.8 %convolution_convert_fusion.1.refs_1_ = bf16[1152,2304]{1,0:T(8,128)(2,1)} fusion(bf16[1152,1536]{1,0:T(8,128)(2,1)} %get-tuple-element.46, bf16[1536,2304]{1,0:T(8,128)(2,1)} %get-tuple-element.47.weight), kind=kOutput, calls=%fused_computation.4 | convolution fusion | flops 8156381184 | bytes 15925248 | tf_op jit(solution)/shard_map/dot_general | solution.py:36
  87.3 1.3 stack.68.refs_4_
  89.2 90.0 %shard_map.263 = (bf16[1152,768]{1,0:T(8,128)(2,1)}, f32[2,2,2,2,576,256]{5,4,3,2,1,0:T(8,128)}, bf16[2,2,2,2,576,1536]{5,4,3,2,1,0:T(8,128)(2,1)}, bf16[2,2,2,2...) custom-call(f32[16]{0:T(128)} %reshape_squeeze.3.refs_0_, ...), custom_call_target="tpu_custom_call" | custom-call | flops 80000000000 | bytes 120000000 | tf_op jit(solution)/shard_map/pallas_call | solution.py:351
  179.3 3.6 convolution_convert_fusion.5
  182.9 66.2 %collective-permute-start.1 = (bf16[576,1536]{1,0:T(8,128)(2,1)S(1)}, bf16[576,1536]{1,0:T(8,128)(2,1)S(1)}, u32[]{:S(2)}, u32[]{:S(2)}) collective-permute-start(bf16[576,1536]{1,0:T(8,128)(2,1)S(1)} %convolution_convert_fusion.5), channel_id=1, source_target_pairs={{0,4},{4,0},{1,5},{5,1},{2,6},{6,2},{3,7},{7,3},{8,12},{12,8},{9,1... | collective-permute-start | bytes 5308424 | tf_op jit(solution)/shard_map/ppermute | solution.py:1235
  249.1 3.3 collective-permute-done.1
  252.4 1.8 multiply_reduce_fusion.3
  255.7 3.3 collective-permute-done.2
  259.0 22.9 %fusion.20 = f32[1152,4096]{1,0:T(8,128)} fusion(bf16[1536,4096]{1,0:T(8,128)(2,1)} %get-tuple-element.51, bf16[576,1536]{1,0:T(8,128)(2,1)S(1)} %collective-permute-done.2, bf16[576,1536]{1,0:T(8,128)(2,1)S(1)} %multiply_convert_fusion.1), kind=kOutput, calls=%fused_computation.42 | convolution fusion | flops 14502592512 | bytes 34996224 | tf_op jit(solution)/shard_map/dot_general | solution.py:36
  281.9 7.8 %multiply_convert_fusion = bf16[1152,2048]{1,0:T(8,128)(2,1)S(1)} fusion(f32[1152,4096]{1,0:T(8,128)} %fusion.20), kind=kLoop, calls=%fused_computation.14 | loop fusion | flops 14155776 | bytes 23592960 | tf_op jit(solution)/shard_map/convert_element_type | solution.py:1321
  289.7 3.9 convolution_convert_fusion.4
  294.0 3.3 collective-permute-done.3
  297.3 6.1 fusion.35
  303.8 3.3 collective-permute-done.4
  307.1 2.1 pad_maximum_fusion.2
  309.2 10.3 %convolution_convert_fusion.2 = bf16[1536,2048]{1,0:T(8,128)(2,1)} fusion(bf16[1152,2048]{1,0:T(8,128)(2,1)S(1)} %multiply_convert_fusion, bf16[576,1536]{1,0:T(8,128)(2,1)S(1)} %collective-permute-done.4, bf16[576,1536]{1,0:T(8,128)(2,1)S(1)} %get-tuple-element.144), kind=kOutput, calls=%fused_computation.17 | convolution fusion | flops 7257980928 | bytes 14548992 | tf_op jit(solution)/shard_map/dot_general | solution.py:44
  319.6 20.1 %fusion.5 = (bf16[1152,2048]{1,0:T(8,128)(2,1)S(1)}, bf16[1152,2048]{1,0:T(8,128)(2,1)}) fusion(f32[1152,4096]{1,0:T(8,128)} %fusion.20, bf16[1152,1536]{1,0:T(8,128)(2,1)} %pad_maximum_fusion.2, bf16[1536,2048]{1,0:T(8,128)(2,1)} %get-tuple-element.52), kind=kOutput, calls=%fused_computation.10 | convolution fusion | flops 7283146752 | bytes 28704768 | tf_op jit(solution)/shard_map/dot_general | solution.py:36
  339.7 7.2 %pad_maximum_fusion = bf16[1152,4096]{1,0:T(8,128)(2,1)} fusion(bf16[1152,2048]{1,0:T(8,128)(2,1)} %get-tuple-element.97, bf16[1152,2048]{1,0:T(8,128)(2,1)S(1)} %get-tuple-element.96), kind=kLoop, calls=%fused_computation.13 | loop fusion | flops 18874368 | bytes 18874368 | tf_op jit(solution)/shard_map/concatenate | solution.py:1339
  346.9 22.0 %convolution_convert_fusion = bf16[1536,4096]{1,0:T(8,128)(2,1)} fusion(bf16[576,1536]{1,0:T(8,128)(2,1)} %copy-done.17, bf16[576,1536]{1,0:T(8,128)(2,1)S(1)} %copy-done.7, bf16[1152,2048]{1,0:T(8,128)(2,1)} %get-tuple-element.97, bf16[1152,2048]{1,0:T(8,128)(2,1)S(1)} %get-tuple-element.96), kind=kOutput, calls=%fused_computation | convolution fusion | flops 14527758336 | bytes 25559040 | tf_op jit(solution)/shard_map/dot_general | solution.py:44
  369.0 12.1 %fusion.12 = bf16[576,1536]{1,0:T(8,128)(2,1)S(1)} fusion(bf16[1536,4096]{1,0:T(8,128)(2,1)} %get-tuple-element.51, bf16[1152,4096]{1,0:T(8,128)(2,1)} %pad_maximum_fusion), kind=kOutput, calls=%fused_computation.36 | convolution fusion | flops 7248642048 | bytes 19070976 | tf_op jit(solution)/shard_map/dot_general | solution.py:40
  381.3 3.7 collective-permute-done.5
  385.0 12.9 %multiply_reduce_fusion.2 = (f32[1536]{0:T(1024)S(1)}, f32[576]{0:T(1024)S(1)}, f32[576,1536]{1,0:T(8,128)S(1)}) fusion(f32[576,1536]{1,0:T(8,128)S(1)} %get-tuple-element.143, f32[576]{0:T(1024)S(1)} %copy-done.10, bf16[576,1536]{1,0:T(8,128)(2,1)} %collective-permute-done.5, f32[1536]{0:T(1024)S(1)} %copy-done.14, ...), kind=kOutput, calls=%fused_computation.28 | convolution fusion | flops 7254833152 | bytes 26165760 | tf_op jit(solution)/shard_map/dot_general | solution.py:40
  398.0 5.9 fusion.36
  404.0 6.1 copy.57
  410.7 1.4 select_maximum_fusion.1
  412.2 7.1 convolution_convert_fusion.3.out
  419.2 1.9 pad_maximum_fusion.3
  421.4 4.7 fusion.43.refs_5_
  426.1 106.1 %shard_map.264 = (bf16[1152,2304]{1,0:T(8,128)(2,1)}, f32[2,8,384]{2,1,0:T(8,128)}, f32[2,2,2,8,256]{4,3,2,1,0:T(8,128)}, f32[2,2,2,2,8,256]{5,4,3,2,1,0:T(8,128)}, bf16[1536,1024]{1,0:T(8,128)(2,1)}) custom-call(f32[16]{0:T(128)} %reshape_squeeze.3.refs_0_, bf16[1152,2304]{1,0:T(8,128)(2,1)} %convolution_convert_fusion.1.refs_1_, ...), custom_call_target="tpu_custom_call" | custom-call | flops 1000000000 | bytes 1000000 | tf_op jit(solution)/shard_map/pallas_call | solution.py:386
  532.2 0.9 slice.166
  534.1 0.9 slice_reduce_fusion
  535.6 5.3 convert_element_type.119
  541.6 139.3 %shard_map.265 = (f32[8,1536]{1,0:T(8,128)}, f32[576,1536]{1,0:T(8,128)}, bf16[1536,2048]{1,0:T(8,128)(2,1)}, bf16[1536,1152]{1,0:T(8,128)(2,1)}, bf16[1536,384]{1,0:T(8,128)(2,1)}) custom-call(f32[8,1536]{1,0:T(8,128)} %pad_maximum_fusion.6.small, bf16[384,4096]{1,0:T(8,128)(2,1)} %reduce-scatter.5.cloned.1.call-done.gu, ...), custom_call_target="tpu_custom_call" | custom-call | tf_op jit(solution)/shard_map/pallas_call | solution.py:1177
  680.9 0.8 slice.177
  683.7 1.5 fusion.40
  685.1 1.3 fusion.41
  686.5 9.3 %fusion.38 = (f32[1536,1024]{1,0:T(8,128)}, f32[1536,1024]{1,0:T(8,128)}) fusion(bf16[1536,2048]{1,0:T(8,128)(2,1)} %get-tuple-element.73), kind=kLoop, calls=%fused_computation.111 | loop fusion | bytes 25165824 | tf_op jit(solution)/shard_map/slice | solution.py:1403
  695.8 3.1 fusion.39
  698.9 1.6 convert_element_type.117
  700.5 1.1 reshape.119
  702.2 1.3 reshape.121
  703.5 1.3 reshape.120
  704.9 1.3 dynamic-slice_reduce_fusion
  706.1 1.2 dynamic-slice_reduce_fusion.1
  708.6 1.8 copy.65
  (130 shorter events, 15.2 us)
Async XLA Ops:
  7.2 418.9 %reduce-scatter.3.cloned.1.call-start = ((), (), s32[]{:S(2)}) async-start(), calls=%async_computation.2 | async-start | bytes 7864320 | tf_op jit(solution)/shard_map/reduce_scatter | solution.py:1264
  8.6 78.2 %copy-start.11 = (s32[576]{0:T(1024)}, s32[576]{0:T(1024)S(1)}, u32[]{:S(2)}) copy-start(s32[576]{0:T(1024)S(1)} %get-tuple-element.95) | copy-start | bytes 6916
  8.6 78.2 %collective-permute-start = (s32[576]{0:T(1024)S(1)}, s32[576]{0:T(1024)S(1)}, u32[]{:S(2)}, u32[]{:S(2)}) collective-permute-start(s32[576]{0:T(1024)S(1)} %get-tuple-element.95), channel_id=1, source_target_pairs={{0,4},{4,0},{1,5},{5,1},{2,6},{6,2},{3,7},{7,3},{8,12},{12,8},{9,1... | collective-permute-start | bytes 6920 | tf_op jit(solution)/shard_map/ppermute | solution.py:1235
  179.2 73.2 %copy-start.1 = (bf16[576,1536]{1,0:T(8,128)(2,1)S(1)}, bf16[576,1536]{1,0:T(8,128)(2,1)}, u32[]{:S(2)}) copy-start(bf16[576,1536]{1,0:T(8,128)(2,1)} %tokens.1) | copy-start | bytes 5308420
  179.2 73.2 %copy-start.18 = (bf16[1536,768]{1,0:T(8,128)(2,1)S(1)}, bf16[1536,768]{1,0:T(8,128)(2,1)}, u32[]{:S(2)}) copy-start(bf16[1536,768]{1,0:T(8,128)(2,1)} %get-tuple-element.50) | copy-start | bytes 7077892
  179.3 73.2 %copy-start.20 = (bf16[1152,768]{1,0:T(8,128)(2,1)S(1)}, bf16[1152,768]{1,0:T(8,128)(2,1)}, u32[]{:S(2)}) copy-start(bf16[1152,768]{1,0:T(8,128)(2,1)} %get-tuple-element.49) | copy-start | bytes 5308420
  182.9 71.9 %copy-start.13 = (f32[1536]{0:T(1024)S(1)}, f32[1536]{0:T(1024)}, u32[]{:S(2)}) copy-start(f32[1536]{0:T(1024)} %param.26) | copy-start | bytes 18436
  182.9 69.5 %collective-permute-start.1 = (bf16[576,1536]{1,0:T(8,128)(2,1)S(1)}, bf16[576,1536]{1,0:T(8,128)(2,1)S(1)}, u32[]{:S(2)}, u32[]{:S(2)}) collective-permute-start(bf16[576,1536]{1,0:T(8,128)(2,1)S(1)} %convolution_convert_fusion.5), channel_id=1, source_target_pairs={{0,4},{4,0},{1,5},{5,1},{2,6},{6,2},{3,7},{7,3},{8,12},{12,8},{9,1... | collective-permute-start | bytes 5308424 | tf_op jit(solution)/shard_map/ppermute | solution.py:1235
  254.8 27.0 %copy-start.9 = (f32[576]{0:T(1024)}, f32[576]{0:T(1024)S(1)}, u32[]{:S(2)}) copy-start(f32[576]{0:T(1024)S(1)} %get-tuple-element.128) | copy-start | bytes 6916
  254.9 34.8 %slice-start = ((s8[6291456]{0:T(1024)(128)(4,1)}), s8[4194304]{0:T(1024)(128)(4,1)S(1)}, s32[]{:S(2)}) async-start(s8[6291456]{0:T(1024)(128)(4,1)} %bitcast.53), calls=%async_computation.4 | async-start | bytes 8388608
  255.2 26.6 %copy-start.6 = (bf16[576,1536]{1,0:T(8,128)(2,1)}, bf16[576,1536]{1,0:T(8,128)(2,1)S(1)}, u32[]{:S(2)}) copy-start(bf16[576,1536]{1,0:T(8,128)(2,1)S(1)} %multiply_convert_fusion.1) | copy-start | bytes 5308420
  255.2 3.8 collective-permute-start.2
  259.0 22.9 %copy-start.17 = (bf16[576,1536]{1,0:T(8,128)(2,1)}, bf16[576,1536]{1,0:T(8,128)(2,1)S(1)}, u32[]{:S(2)}) copy-start(bf16[576,1536]{1,0:T(8,128)(2,1)S(1)} %collective-permute-done.2) | copy-start | bytes 5308420
  259.0 30.7 %slice-start.1 = ((s8[6291456]{0:T(1024)(128)(4,1)}), s8[2097152]{0:T(1024)(128)(4,1)S(1)}, s32[]{:S(2)}) async-start(s8[6291456]{0:T(1024)(128)(4,1)} %bitcast.53), calls=%async_computation.5 | async-start | bytes 4194304
  289.7 7.7 %copy-start.4 = (bf16[576,1536]{1,0:T(8,128)(2,1)S(1)}, bf16[576,1536]{1,0:T(8,128)(2,1)}, u32[]{:S(2)}) copy-start(bf16[576,1536]{1,0:T(8,128)(2,1)} %param.16) | copy-start | bytes 5308420
  289.7 7.7 %copy-start.15 = (f32[576]{0:T(1024)S(1)}, f32[576]{0:T(1024)}, u32[]{:S(2)}) copy-start(f32[576]{0:T(1024)} %get-tuple-element.94) | copy-start | bytes 6916
  293.6 3.8 collective-permute-start.3
  303.4 3.7 collective-permute-start.4
  319.6 222.1 %reduce-scatter.5.cloned.1.call-start = ((), (), s32[]{:S(2)}) async-start(), calls=%async_computation.3 | async-start | bytes 15728640 | tf_op jit(solution)/shard_map/reduce_scatter | solution.py:1264
  339.7 7.2 %copy-start.7 = (bf16[576,1536]{1,0:T(8,128)(2,1)S(1)}, bf16[576,1536]{1,0:T(8,128)(2,1)}, u32[]{:S(2)}) copy-start(bf16[576,1536]{1,0:T(8,128)(2,1)} %copy-done.6) | copy-start | bytes 5308420
  369.0 16.1 %copy-start.10 = (f32[576]{0:T(1024)S(1)}, f32[576]{0:T(1024)}, u32[]{:S(2)}) copy-start(f32[576]{0:T(1024)} %copy-done.9) | copy-start | bytes 6916
  369.0 16.1 %copy-start.14 = (f32[1536]{0:T(1024)S(1)}, f32[1536]{0:T(1024)}, u32[]{:S(2)}) copy-start(f32[1536]{0:T(1024)} %param.26) | copy-start | bytes 18436
  381.1 16.9 %copy-start.2 = (f32[576,1536]{1,0:T(8,128)S(1)}, f32[576,1536]{1,0:T(8,128)}, u32[]{:S(2)}) copy-start(f32[576,1536]{1,0:T(8,128)} %get-tuple-element.145) | copy-start | bytes 10616836
  381.1 16.9 %copy-start.5 = (bf16[576,1536]{1,0:T(8,128)(2,1)S(1)}, bf16[576,1536]{1,0:T(8,128)(2,1)}, u32[]{:S(2)}) copy-start(bf16[576,1536]{1,0:T(8,128)(2,1)} %param.16) | copy-start | bytes 5308420
  381.1 16.9 %copy-start.16 = (f32[576]{0:T(1024)S(1)}, f32[576]{0:T(1024)}, u32[]{:S(2)}) copy-start(f32[576]{0:T(1024)} %get-tuple-element.127) | copy-start | bytes 6916
  381.1 3.9 collective-permute-start.5
  403.8 8.3 %collective-permute-start.6 = (bf16[576,1536]{1,0:T(8,128)(2,1)}, bf16[576,1536]{1,0:T(8,128)(2,1)S(1)}, u32[]{:S(2)}, u32[]{:S(2)}) collective-permute-start(bf16[576,1536]{1,0:T(8,128)(2,1)} %get-tuple-element.92), channel_id=1, source_target_pairs={{0,4},{4,0},{1,5},{5,1},{2,6},{6,2},{3,7},{7,3},{8,12},{12,8},{9,1... | collective-permute-start | bytes 5308424 | tf_op jit(solution)/shard_map/ppermute | solution.py:1235
  404.0 6.2 copy-start.12
  419.2 2.2 copy-start.19
  686.5 9.3 %copy-start = (bf16[1536,1152]{1,0:T(8,128)(2,1)S(1)}, bf16[1536,1152]{1,0:T(8,128)(2,1)}, u32[]{:S(2)}) copy-start(bf16[1536,1152]{1,0:T(8,128)(2,1)} %get-tuple-element.71) | copy-start | bytes 10616836
  695.8 3.1 copy-start.8
  698.9 9.7 %copy-start.3 = (f32[576,1536]{1,0:T(8,128)S(1)}, f32[576,1536]{1,0:T(8,128)}, u32[]{:S(2)}) copy-start(f32[576,1536]{1,0:T(8,128)} %get-tuple-element.166) | copy-start | bytes 10616836
Sparse Core Ops, SparseCore 0:
  319.7 67.4 reduce-scatter.2
  390.3 133.3 reduce-scatter.4

commit v5 on v4

--- a/solution.py
+++ b/solution.py
@@ -339,7 +339,7 @@
     def kernel(*refs):
         inputs, loads, refs = refs[:5], refs[5 : 5 + many], refs[5 + many :]
         outs, full, refs = refs[:5], refs[5 : 5 + held], refs[5 + held :]
-        work = Gather(LATER, loads, full, *refs[3:]) if gather else None
+        work = Gather(DIRECT, LATER, loads, full, *refs[3:]) if gather else None
 
         def hook(step, place):
             if work:
@@ -471,13 +471,16 @@
 FIRST = ((0, 0, 0, 0, 1152, 384), (1, 0, 0, 384, 1536, 384), (2, 0, 0, 768, 1920, 384))
 LATER = (
     (0, 0, 0, 0, 384, 384),
-    (1, 1, 0, 0, 1024, 512),
-    (1, 1, 512, 512, 1536, 512),
-    (2, 1, 0, 2048, 3072, 512),
-    (2, 1, 512, 2560, 3584, 512),
+    (1, 1, 0, 0, 2048, 512),
+    (2, 1, 0, 512, 2560, 512),
+    (1, 1, 512, 1024, 3072, 512),
+    (2, 1, 512, 1536, 3584, 512),
     (3, 2, 0, 0, 1024, 512),
     (3, 2, 512, 512, 1536, 512),
 )
+WHOLE = 5
+DIRECT = 0
+LAST = ((0, 0, 0, 0, 1024, 512), (0, 0, 512, 512, 1536, 512))
 
 
 def greet(peers):
@@ -488,7 +491,8 @@
 
 
 class Gather:
-    def __init__(self, items, weights, fulls, send, recv, local, *held):
+    def __init__(self, direct, items, weights, fulls, send, recv, local, *held):
+        self.direct = direct
         self.items, self.weights, self.fulls, self.held = items, weights, fulls, held
         self.send, self.recv, self.local = send, recv, local
         q, c, z = lax.axis_index("plane"), lax.axis_index("core"), lax.axis_index("tensor")
@@ -568,10 +572,20 @@
         def _():
             action(0)
 
+    def across_copy(self, item):
+        weight, _, source_col, _, _, size = self.items[item]
+        span = pl.ds(pl.multiple_of((3 - self.q) * 384, 128), 384)
+        ref, cols = self.whole(item, 1)
+        return pltpu.make_async_remote_copy(
+            src_ref=self.weights[weight].at[span, pl.ds(source_col, size)], dst_ref=ref.at[span, cols], send_sem=self.send.at[item, 8],
+            recv_sem=self.recv.at[item, 8], device_id=self.near, device_id_type=MESH)
+
     def start_z(self, item):
         @pl.when(self.home)
         def _():
             self.z_copy(item, 1).start()
+            if item < self.direct:
+                self.across_copy(item).start()
 
         @self.away
         def _():
@@ -584,6 +598,23 @@
             self.z_copy(item, 1, True).start()
             self.plane_copy(item, 0, 0).start()
             self.plane_copy(item, 0, 1).start()
+
+    def relay_only(self, item):
+        @self.away
+        def _():
+            self.z_copy(item, 0).wait_recv()
+            self.z_copy(item, 1, True).start()
+
+    def finish_z(self, item):
+        self.z_copy(item, 1).wait_recv()
+        self.each(lambda side: self.z_copy(item, side).wait_send())
+
+    def start_both(self, item):
+        def act(side):
+            self.plane_copy(item, side, 0).start()
+            self.plane_copy(item, side, 1).start()
+
+        self.each(act)
 
     def start_plane(self, item):
         self.z_copy(item, 1).wait_recv()
@@ -597,17 +628,40 @@
             self.plane_copy(item, side, 1).wait_recv()
             self.plane_copy(item, side, 3).start()
 
-        self.each(act)
+        if item < self.direct:
+
+            @self.away
+            def _():
+                act(1)
+                act(0)
+
+        else:
+            self.each(act)
 
     def finish(self, item):
         def act(side):
             self.plane_copy(item, side, 2).wait_recv()
             self.plane_copy(item, side, 3).wait_recv()
-            self.z_copy(item, side).wait_send()
+            if self.weights:
+                self.z_copy(item, side).wait_send()
             for step in range(4):
                 self.plane_copy(item, side, step).wait_send()
 
-        self.each(act)
+        if item >= self.direct:
+            self.each(act)
+            return
+
+        @self.away
+        def _():
+            act(1)
+            act(0)
+
+        @pl.when(self.home)
+        def _():
+            self.z_copy(item, 1).wait_send()
+            self.across_copy(item).wait()
+            for step in range(2):
+                self.plane_copy(item, 1, step).wait()
 
 
 def gather_scratch(weights, count):
@@ -622,14 +676,16 @@
 
 
 def background(work, step, place):
-    count = len(work.items)
     if place == 2:
 
         @pl.when(step == 7)
         def _():
-            work.forward(count - 1)
-            for item in range(count):
-                work.finish(item)
+            work.forward(WHOLE - 1)
+            for item in range(len(work.items)):
+                if item < WHOLE:
+                    work.finish(item)
+                else:
+                    work.finish_z(item)
             work.wait_own()
 
         return
@@ -644,11 +700,11 @@
                 greet((work.near, work.far, work.by_x, work.by_y))
                 for item in range(AHEAD):
                     work.start_z(item)
-            elif slot <= 2 * count:
+            elif slot <= 2 * WHOLE:
                 item = (slot - 1) // 2
                 if slot % 2:
                     work.relay_z(item)
-                    if item + AHEAD < count:
+                    if item + AHEAD < len(work.items):
                         work.start_z(item + AHEAD)
                     if item < len(work.weights):
                         work.pass_own(item)
@@ -656,10 +712,94 @@
                     work.start_plane(item)
                     if item >= 1:
                         work.forward(item - 1)
+            elif slot <= 2 * WHOLE + 2:
+                work.relay_only(slot - 2 * WHOLE - 1 + WHOLE)
+
+
+TILE = 512
+
+
+def beside_gate(work, step):
+    script = (("start_both", 0), ("start_both", 1)), (), (("forward", 0),), (("forward", 1),)
+    for turn, names in enumerate(script):
+        if names:
+
+            @pl.when(step == turn)
+            def _(names=names, turn=turn):
+                if turn == 0:
+                    greet((work.by_x, work.by_y))
+                for name, item in names:
+                    getattr(work, name)(item)
+
+
+def gated_forward(normed, weight, part=None):
+    rows, width = normed.shape
+    units = weight.shape[1] // 2
+    many = 0 if part is None else 1
+    count = len(LAST)
+
+    def kernel(x_ref, w_ref, *refs):
+        hidden_ref, gate_ref, up_ref, refs = refs[many], refs[many + 1], refs[many + 2], refs[many + 3 :]
+        step = pl.program_id(0)
+        work = Gather(0, LAST, (), refs[:1], refs[1], refs[2], None) if many else None
+        if work:
+            beside_gate(work, step)
+        gate = nn(x_ref[...], w_ref[:, :TILE])
+        gate_ref[...] = gate.astype(BF16)
+        up = nn(x_ref[...], w_ref[:, TILE:])
+        up_ref[...] = up.astype(BF16)
+        hidden_ref[...] = (gate * jax.nn.sigmoid(gate) * up).astype(BF16)
+        if work:
+
+            @pl.when(step == units // TILE - 1)
+            def _():
+                for item in range(count):
+                    work.finish(item)
+
+    anywhere = pl.BlockSpec(memory_space=pl.ANY)
+    tile = pl.BlockSpec((rows, TILE), lambda j: (0, j))
+    collective = dict(collective_id=5, has_side_effects=True) if many else {}
+    extra = [] if part is None else [part]
+    result = pl.pallas_call(
+        kernel,
+        grid=(units // TILE,),
+        in_specs=[pl.BlockSpec((rows, width), lambda j: (0, 0)), pl.BlockSpec((width, 2 * TILE), lambda j: (0, j))] + [anywhere] * many,
+        out_specs=[tile] * 3 + [anywhere] * many,
+        out_shape=[jax.ShapeDtypeStruct((rows, units), BF16)] * 3 + [jax.ShapeDtypeStruct(p.shape, BF16) for p in extra],
+        scratch_shapes=[pltpu.SemaphoreType.DMA((count, 10))] * 2 * many,
+        input_output_aliases={2: 3} if many else {},
+        compiler_params=pltpu.CompilerParams(vmem_limit_bytes=60 * 1024 * 1024, **collective),
+    )(normed, weight, *extra)
+    return result[:3], result[3:]
+
+
+def gated_backward(d_out, down, gate, up, normed):
+    rows, width = d_out.shape
+    units = gate.shape[1]
+
+    def kernel(d_ref, down_ref, gate_ref, up_ref, x_ref, d_gu_ref, grads_ref):
+        d_hidden = nn(d_ref[...], down_ref[...])
+        gate_value, up_value = gate_ref[...].astype(F32), up_ref[...].astype(F32)
+        s = jax.nn.sigmoid(gate_value)
+        d_gu_ref[:, :TILE] = (d_hidden * up_value * s * (1.0 + gate_value * (1.0 - s))).astype(BF16)
+        d_gu_ref[:, TILE:] = (d_hidden * gate_value * s).astype(BF16)
+        grads_ref[...] = tn(x_ref[...], d_gu_ref[...]).astype(BF16)
+
+    whole = pl.BlockSpec((rows, width), lambda j: (0, 0))
+    tile = pl.BlockSpec((rows, TILE), lambda j: (0, j))
+    return pl.pallas_call(
+        kernel,
+        grid=(units // TILE,),
+        in_specs=[whole, pl.BlockSpec((width, TILE), lambda j: (0, j)), tile, tile, whole],
+        out_specs=[pl.BlockSpec((rows, 2 * TILE), lambda j: (0, j)), pl.BlockSpec((width, 2 * TILE), lambda j: (0, j))],
+        out_shape=[jax.ShapeDtypeStruct((rows, 2 * units), BF16), jax.ShapeDtypeStruct((width, 2 * units), BF16)],
+        compiler_params=pltpu.CompilerParams(vmem_limit_bytes=60 * 1024 * 1024),
+        cost_estimate=pl.CostEstimate(flops=22_000_000_000, bytes_accessed=40_000_000, transcendentals=0),
+    )(d_out, down, gate, up, normed)
 
 
 def opening_kernel(tokens_ref, gain_ref, small_ref, wq_ref, wk_ref, wv_ref, full_ref, normed_ref, toep_ref, both_ref, send, recv, local, held0, held1, held2, extra_send, extra_recv):
-    work = Gather(FIRST, (wq_ref, wk_ref, wv_ref), (full_ref,), send, recv, local, held0, held1, held2)
+    work = Gather(3, FIRST, (wq_ref, wk_ref, wv_ref), (full_ref,), send, recv, local, held0, held1, held2)
     rows = tokens_ref.shape[0]
 
     def extra(source, target, index, peer):
@@ -984,11 +1124,13 @@
 
 
 FINISH = (
-    (0, 0, 1024, 1024, 0, 0, 0),
-    (0, 2048, 3072, 1024, 0, 1024, 1024),
-    (-1, 0, 1152, 384, 1, 2048, 0),
-    (-1, 384, 1536, 384, 1, 2432, 384),
-    (-1, 768, 1920, 384, 1, 2816, 768),
+    (0, 0, 2048, 512, 0, 0, 0),
+    (0, 512, 2560, 512, 1, 512, 0),
+    (0, 1024, 3072, 512, 0, 1024, 512),
+    (0, 1536, 3584, 512, 1, 1536, 512),
+    (-1, 0, 1152, 384, 2, 2048, 0),
+    (-1, 384, 1536, 384, 2, 2432, 384),
+    (-1, 768, 1920, 384, 2, 2816, 768),
 )
 LONE = ((-1, 0, 384, 384, 0, 0, 0),)
 BESIDE = (
@@ -1050,11 +1192,11 @@
 
 
 def finish_kernel(
-    small, gu, out, normed_t, d_qkv, weight, tokens, gain, d_hidden, small_out, d_input, o_gu, o_qkv, o_out,
+    small, gu, out, normed, d_qkv, weight, tokens, gain, d_hidden, small_out, d_input, o_gate, o_up, o_qkv, o_out,
     made, partner, arrived, loaded, load_sem, hidden_buf, tokens_buf, hidden_sem, core_send, core_recv, *bufs,
 ):
     lone = Finish(LONE, (), out, (o_out,), None, bufs[-13:])
-    work = Finish(FINISH, (gu,), made, (o_gu, o_qkv), small, bufs[:-13], True)
+    work = Finish(FINISH, (gu,), made, (o_gate, o_up, o_qkv), small, bufs[:-13], True)
     rows = tokens.shape[0]
 
     def load(part):
@@ -1078,26 +1220,31 @@
     greet((work.near, work.far, work.by_x, work.by_y, work.core, work.across))
     lone.r1(0)
     work.s1(0)
+    work.s1(1)
 
     def make(side, owner):
         cols = slice(1152 * side, 1152 * (side + 1))
-        made[work.rows(owner), cols] = nn(normed_t[work.rows(owner), :], d_qkv[:, cols]).astype(BF16)
+        made[work.rows(owner), cols] = tn(normed[:, work.rows(owner)], d_qkv[:, cols]).astype(BF16)
 
     across = 3 - work.q
     for side, owners in enumerate(((across, work.by_x[0]), (across, work.by_y[0]))):
         for owner in owners:
             make(side, owner)
-        for item in (2, 3, 4):
+        for item in (4, 5, 6):
             work.r1_side(item, side)
     work.s2(0)
-    work.s1(1)
+    work.s1(2)
     lone.r2(0)
     make(0, work.by_y[0])
+    work.s2(1)
+    work.s1(3)
     make(1, work.by_x[0])
     work.s3(0)
     make(0, work.q)
+    work.s2(2)
+    work.s3(1)
     make(1, work.q)
-    work.r2(2)
+    work.r2(4)
     lone.r3(0)
     lone.s1(0)
     work.s4(0)
@@ -1113,23 +1260,28 @@
         exchange(part).start()
 
     back(0)
-    work.r2(3)
-    work.s2(1)
+    work.r2(5)
+    work.s2(3)
+    work.s4(1)
     back(1)
-    work.r2(4)
-    work.r3(2)
-    work.s1(2)
-    back(2)
-    work.s3(1)
-    lone.s2(0)
-    work.r3(3)
-    work.s1(3)
-    work.s5(0)
-    back(3)
-    work.s2(2)
+    work.r2(6)
     work.r3(4)
     work.s1(4)
-    work.s4(1)
+    work.s3(2)
+    work.s5(0)
+    back(2)
+    lone.s2(0)
+    work.r3(5)
+    work.s1(5)
+    work.s3(3)
+    work.s4(2)
+    work.s5(1)
+    back(3)
+    work.s2(4)
+    work.r3(6)
+    work.s1(6)
+    work.s4(3)
+    work.s6(0)
     for part in range(4):
         exchange(part).wait_recv()
     gain_sum = jnp.zeros((1, tokens.shape[1]), F32)
@@ -1150,15 +1302,15 @@
     work.small_buf[0, 0:1] = gain_sum
     work.small_start()
     script = (
-        ("s3", 2), ("s2", 3), ("s3", 5), ("s6", 0), ("m", 0),
-        ("s5", 1), ("s4", 2), ("s3", 3), ("s2", 4), ("s4", 5), ("m", 1),
-        ("s6", 1), ("s5", 2), ("s4", 3), ("s3", 4), ("s5", 5), ("m", 2),
-        ("s6", 2), ("s5", 3), ("s4", 4), ("s6", 5), ("m", 3), ("s6", 3), ("s5", 4), ("m", 4), ("s6", 4),
+        ("s3", 4), ("s2", 5), ("s3", 7), ("s6", 1), ("s5", 2), ("m", 0),
+        ("s4", 4), ("s3", 5), ("s2", 6), ("s4", 7), ("s5", 3), ("s6", 2), ("m", 1),
+        ("s5", 4), ("s4", 5), ("s3", 6), ("s5", 7), ("s6", 3), ("m", 2),
+        ("s6", 4), ("s5", 5), ("s4", 6), ("s6", 7), ("m", 3), ("s6", 5), ("s5", 6), ("m", 4), ("s6", 6),
     )
     for name, item in script:
         if name == "m":
             work.small_next(item)
-        elif item == 5:
+        elif item == 7:
             getattr(lone, name)(0)
         else:
             getattr(work, name)(item)
@@ -1170,16 +1322,16 @@
     work.small_done(small_out)
 
 
-def finish_gradients(small, gu, out, normed_t, d_qkv, weight, tokens, gain, d_hidden, collective_id):
+def finish_gradients(small, gu, out, normed, d_qkv, weight, tokens, gain, d_hidden, collective_id):
     vmem = pl.BlockSpec(memory_space=pltpu.VMEM)
     anywhere = pl.BlockSpec(memory_space=pl.ANY)
     rows, width = tokens.shape
     return pl.pallas_call(
         finish_kernel,
         in_specs=[vmem] * 2 + [anywhere] + [vmem] * 2 + [anywhere] * 2 + [vmem] + [anywhere],
-        out_specs=[vmem] * 2 + [anywhere] * 3,
+        out_specs=[vmem] * 2 + [anywhere] * 4,
         out_shape=[jax.ShapeDtypeStruct(small.shape, F32), jax.ShapeDtypeStruct((rows, width), F32)]
-        + [jax.ShapeDtypeStruct((1536, n), BF16) for n in (2048, 1152, 384)],
+        + [jax.ShapeDtypeStruct((1536, n), BF16) for n in (1024, 1024, 1152, 384)],
         scratch_shapes=[
             pltpu.VMEM((1536, 2304), BF16),
             pltpu.VMEM((rows, width), BF16),
@@ -1197,7 +1349,7 @@
         + [pltpu.SemaphoreType.DMA((5,))] * 2
         + finish_scratch(LONE, 768),
         compiler_params=pltpu.CompilerParams(collective_id=collective_id, has_side_effects=True, vmem_limit_bytes=60 * 1024 * 1024),
-    )(small, gu, out, normed_t, d_qkv, weight, tokens, gain, d_hidden)
+    )(small, gu, out, normed, d_qkv, weight, tokens, gain, d_hidden)
 
 
 def rows_dot(lhs, rhs):
@@ -1259,6 +1411,7 @@
             return pairs
 
         fused = square and tensors == 4
+        units = w_gate.shape[1]
 
         def plane_sum(grads):
             return lax.psum_scatter(grads, "plane", scatter_dimension=0, tiled=True)
@@ -1310,16 +1463,14 @@
             out_weight, gu_weight, down_weight = later
         else:
             out_weight = jnp.concatenate(collect([w_out]), axis=1)
-            gu_weight = jnp.concatenate(collect([w_gate, w_up]), axis=1)
-            down_weight = jnp.concatenate(collect([w_down]), axis=1)
+            pieces = collect([w_gate, w_up])
+            pieces = [pieces[2 * kind + side][:, start : start + TILE] for side in range(2) for start in range(0, units, TILE) for kind in range(2)]
+            gu_weight = jnp.concatenate(pieces, axis=1)
         hidden_in = inputs + summed(heads_out, out_weight)
         inv_two = lax.rsqrt(jnp.mean(hidden_in * hidden_in, axis=-1, keepdims=True) + 1e-06)
         normed_two = with_partner((hidden_in * inv_two * gain_two).astype(BF16))
-        units = w_gate.shape[1]
-        both = nn(normed_two, gu_weight)
-        gate, up = both[:, : 2 * units], both[:, 2 * units :]
-        hidden = (jax.nn.silu(gate) * up).astype(BF16)
-        gate, up = gate.astype(BF16), up.astype(BF16)
+        (hidden, gate, up), last = gated_forward(normed_two, gu_weight, down_weight if fused else None)
+        down_weight = last[0] if fused else jnp.concatenate(collect([w_down]), axis=1)
         final_rows = hidden_in + summed(hidden, down_weight)
         output = final_rows.astype(BF16)
         own_mask = own_valid.astype(F32)
@@ -1331,13 +1482,7 @@
         down_grads = rows_dot(d_all, hidden)
         down_grads, d_all = lax.optimization_barrier((down_grads, d_all))
         down_part = plane_sum(down_grads)
-        d_hidden = nn(d_all, down_weight)
-        gate, up = gate.astype(F32), up.astype(F32)
-        s = jax.nn.sigmoid(gate)
-        d_gate = (d_hidden * up * s * (1.0 + gate * (1.0 - s))).astype(BF16)
-        d_up = (d_hidden * gate * s).astype(BF16)
-        d_gu = jnp.concatenate([d_gate, d_up], axis=1)
-        gu_grads = rows_dot(normed_two, d_gu)
+        d_gu, gu_grads = gated_backward(d_all, down_weight, gate, up, normed_two)
         gu_grads, d_gu = lax.optimization_barrier((gu_grads, d_gu))
         gu_part = plane_sum(gu_grads)
         d_normed_two = summed(d_gu, gu_weight)
@@ -1362,10 +1507,10 @@
         last = jnp.pad(jnp.stack([squared_sum, count_sum]), (0, 2 * width - 2)).reshape(2, width)
         packed = jnp.concatenate([jnp.zeros((1, width), F32), grad_gain_two[None], table, last])
         if fused:
-            packed, grad_input, sum_gu, sum_qkv, sum_out = finish_gradients(
-                packed, gu_part, out_grads, normed_one.T, d_qkv, qkv_weight, tokens, gain_one[None], d_hidden_in, 2
+            packed, grad_input, sum_gate, sum_up, sum_qkv, sum_out = finish_gradients(
+                packed, gu_part, out_grads, normed_one, d_qkv, qkv_weight, tokens, gain_one[None], d_hidden_in, 2
             )
-            sums = [done[0], sum_gu, sum_out, sum_qkv]
+            sums = [done[0], sum_gate, sum_up, sum_out, sum_qkv]
         else:
             qkv_grads = rows_dot(normed_one, d_qkv)
             d_normed_one = summed(d_qkv, qkv_weight)
@@ -1377,10 +1522,11 @@
             packed = lax.psum(packed, every)
             out_part, qkv_part = plane_sum(out_grads), plane_sum(qkv_grads)
             sums = [reduce(part[:, : part.shape[1] // 2], part[:, part.shape[1] // 2 :]) for part in (down_part, out_part, qkv_part)]
-            places = [slice(i * units, (i + 1) * units) for i in range(4)]
-            first, second = [jnp.concatenate([gu_part[:, places[i]], gu_part[:, places[i + 2]]], axis=1) for i in range(2)]
-            sums.insert(1, reduce(first, second))
-        grad_down, grad_gu, grad_out, grad_qkv = [value.astype(F32) for value in sums]
+            sum_gu = reduce(gu_part[:, : 2 * units], gu_part[:, 2 * units :])
+            for kind in range(2):
+                places = range(kind * TILE, 2 * units, 2 * TILE)
+                sums.insert(1 + kind, jnp.concatenate([sum_gu[:, i : i + TILE] for i in places], axis=1))
+        grad_down, grad_gate, grad_up, grad_out, grad_qkv = [value.astype(F32) for value in sums]
         small_sum = lax.dynamic_slice_in_dim(packed[2:6].reshape(-1), z * small_size, small_size, 0)
         gain_slice = width // tensors
         gain_one_out = lax.dynamic_slice_in_dim(packed[0], z * gain_slice, gain_slice, 0)
@@ -1399,8 +1545,8 @@
             small_sum[conv_size + mix_size :].reshape(gn_gain.shape),
             grad_out,
             gain_two_out,
-            grad_gu[:, :units],
-            grad_gu[:, units:],
+            grad_gate,
+            grad_up,
             grad_down,
         )
 

time: 723 us -> 698 us (0.965)
  matrix products: 141 us -> 81.2 us
  Pallas kernels: 393 us -> 451 us
  local copies, waits for them, and re-layouts: 42.6 us -> 30.1 us
    pallas_call x0 -> x2, Pallas kernels: none -> 68.9 us  [the longest x1 34.9 us: gated_forward(): pl.pallas_call(kernel, grid=(units // TILE,), in_specs=[pl.BlockSpec((row...]
    dot_general x4 -> x2, matrix products: 61.5 us -> 18.6 us  [nn(): lax.dot_general(a, b, (((1,), (0,)), ((), ())), preferred_element_type=F32)]
    dot_general x3 -> x2, matrix products: 39.4 us -> 17 us  [tn(): lax.dot_general(a, b, (((0,), (0,)), ((), ())), preferred_element_type=F32)]
    slice x1 -> x0, local copies, waits for them, and re-layouts: 9.31 us -> none  [local(): grad_gu[:, units:]]
    convert_element_type x1 -> x0, other arithmetic: 7.78 us -> none  [local(): hidden = (jax.nn.silu(gate) * up).astype(BF16)]
    concatenate x1 -> x0, other arithmetic: 7.23 us -> none  [local(): d_gu = jnp.concatenate([d_gate, d_up], axis=1)]
  transfers between devices with their start and end apart: 9 -> 9, of which waited for: 5 -> 6; matrix products, arithmetic and copies ran while one was open for 18% -> 11% of each run, Pallas kernels for 23% -> 28%
where the time goes in v5:
time: 698 us; the launch traced here: 693 us
  Pallas kernels  451 us (65%)
  matrix products  81.2 us (12%)
  starting transfers between devices  63.4 us (9%)
  other arithmetic  32.7 us (5%)
  local copies, waits for them, and re-layouts  30.1 us (4%)
  waiting for transfers between devices  17.6 us (3%)
  between operations  17.2 us (2%)
    pallas_call x1, Pallas kernels, finish_gradients(): pl.pallas_call(finish_kernel, in_specs=[vmem] * 2 + [anywhere] + [vmem] *...  138 us
    pallas_call x1, Pallas kernels, attention_backward(): pl.pallas_call(kernel, grid=(2, trees, 2), in_specs=common_specs() + [pl....  110 us
    pallas_call x1, Pallas kernels, attention_forward(): pl.pallas_call(kernel, grid=(2, trees, 2), in_specs=common_specs() + [any...  83.9 us
    ppermute x7, starting transfers between devices, over_core(): return lax.ppermute(value, 'core', [(0, 1), (1, 0)])  63.3 us
    pallas_call x1, Pallas kernels, opening(): pl.pallas_call(opening_kernel, in_specs=[vmem] * 3 + [anywhere] * 3, out_...  50.9 us
    dot_general x6, matrix products, nt(): lax.dot_general(a, b, (((1,), (1,)), ((), ())), preferred_element_type=F32)  45.6 us
    pallas_call x1, Pallas kernels, gated_forward(): pl.pallas_call(kernel, grid=(units // TILE,), in_specs=[pl.BlockSpec((row...  34.9 us
    pallas_call x1, Pallas kernels, gated_backward(): pl.pallas_call(kernel, grid=(units // TILE,), in_specs=[whole, pl.BlockSp...  34.1 us
  transfers between devices with their start and end apart: 9, of which 6 were waited for; matrix products, arithmetic and copies ran while one was open for 11% of the time, Pallas kernels for 28%

profile of v5, /device:TPU:0, one launch (start us, length us, event | category | flops | bytes accessed | tf_op | source)
XLA Modules:
  0.0 693.5 jit_solution(2420458124501210240)
XLA Ops:
  7.2 0.8 fusion.23
  10.8 1.3 broadcast_in_dim.51.gain_ref.gain
  12.9 50.9 %shard_map.262 = (bf16[1536,2304]{1,0:T(8,128)(2,1)}, bf16[1152,1536]{1,0:T(8,128)(2,1)}, bf16[2,2,2,1536,256]{4,3,2,1,0:T(8,128)(2,1)}, f32[2,32,256]{2,1,0:T(8,128)}) custom-call(bf16[576,1536]{1,0:T(8,128)(2,1)} %tokens.1, f32[1,1536]{1,0:T(1,128)} %broadcast_in_dim.51.gain_ref.gain, f32[32,256]{1,0:T(8,128)} %fusion.15.small_ref, ...), custom_call_target="tpu_custom_call" | custom-call | tf_op jit(solution)/shard_map/pallas_call | solution.py:867
  65.2 13.9 %convolution_convert_fusion.refs_1_ = bf16[1152,2304]{1,0:T(8,128)(2,1)} fusion(bf16[1152,1536]{1,0:T(8,128)(2,1)} %get-tuple-element.53.normed, bf16[1536,2304]{1,0:T(8,128)(2,1)} %get-tuple-element.54.weight), kind=kOutput, calls=%fused_computation | convolution fusion | flops 8156381184 | bytes 15925248 | tf_op jit(solution)/shard_map/dot_general | solution.py:36
  80.3 1.3 stack.68.refs_4_
  82.2 83.9 %shard_map.263 = (bf16[1152,768]{1,0:T(8,128)(2,1)}, f32[2,2,2,2,576,256]{5,4,3,2,1,0:T(8,128)}, bf16[2,2,2,2,576,1536]{5,4,3,2,1,0:T(8,128)(2,1)}, bf16[2,2,2,2...) custom-call(f32[16]{0:T(128)} %reshape_squeeze.3.refs_0_, ...), custom_call_target="tpu_custom_call" | custom-call | flops 80000000000 | bytes 120000000 | tf_op jit(solution)/shard_map/pallas_call | solution.py:351
  166.1 3.6 convolution_convert_fusion.4
  169.8 49.2 %collective-permute-start.1 = (bf16[576,1536]{1,0:T(8,128)(2,1)S(1)}, bf16[576,1536]{1,0:T(8,128)(2,1)S(1)}, u32[]{:S(2)}, u32[]{:S(2)}) collective-permute-start(bf16[576,1536]{1,0:T(8,128)(2,1)S(1)} %convolution_convert_fusion.4), channel_id=1, source_target_pairs={{0,4},{4,0},{1,5},{5,1},{2,6},{6,2},{3,7},{7,3},{8,12},{12,8},{9,1... | collective-permute-start | bytes 5308424 | tf_op jit(solution)/shard_map/ppermute | solution.py:1387
  219.0 3.3 collective-permute-done.1
  222.3 1.9 multiply_reduce_fusion.3
  225.6 3.3 collective-permute-done.2
  228.9 2.0 pad_maximum_fusion.x_ref
  231.0 34.9 %shard_map.264 = (bf16[1152,2048]{1,0:T(8,128)(2,1)}, bf16[1152,2048]{1,0:T(8,128)(2,1)}, bf16[1152,2048]{1,0:T(8,128)(2,1)}, bf16[1536,2048]{1,0:T(8,128)(2,1)}) custom-call(bf16[1152,1536]{1,0:T(8,128)(2,1)} %pad_maximum_fusion.x_ref, bf16[1536,4096]{1,0:T(8,128)(2,1)} %get-tuple-element.58.w_ref, ...), custom_call_target="tpu_custom_call", output_to_operand_aliasing={{3}: (2, {})} | custom-call | tf_op jit(solution)/shard_map/pallas_call | solution.py:763
  265.9 7.5 %convolution_convert_fusion.3 = bf16[576,1536]{1,0:T(8,128)(2,1)S(1)} fusion(bf16[1536,2048]{1,0:T(8,128)(2,1)} %get-tuple-element.61.down_ref, bf16[1152,2048]{1,0:T(8,128)(2,1)} %get-tuple-element.60), kind=kOutput, calls=%fused_computation.21 | convolution fusion | flops 3624763392 | bytes 10420224 | tf_op jit(solution)/shard_map/dot_general | solution.py:40
  273.4 12.0 %collective-permute-start.3 = (bf16[576,1536]{1,0:T(8,128)(2,1)S(1)}, bf16[576,1536]{1,0:T(8,128)(2,1)S(1)}, u32[]{:S(2)}, u32[]{:S(2)}) collective-permute-start(bf16[576,1536]{1,0:T(8,128)(2,1)S(1)} %convolution_convert_fusion.3), channel_id=1, source_target_pairs={{0,4},{4,0},{1,5},{5,1},{2,6},{6,2},{3,7},{7,3},{8,12},{12,8},{9,1... | collective-permute-start | bytes 5308424 | tf_op jit(solution)/shard_map/ppermute | solution.py:1387
  285.3 3.3 collective-permute-done.3
  288.7 6.1 fusion.21
  295.1 3.3 collective-permute-done.4
  298.4 2.0 pad_maximum_fusion.1.d_ref
  300.5 10.3 %convolution_convert_fusion.1 = bf16[1536,2048]{1,0:T(8,128)(2,1)} fusion(bf16[1152,2048]{1,0:T(8,128)(2,1)S(1)} %copy-done.15, bf16[576,1536]{1,0:T(8,128)(2,1)S(1)} %collective-permute-done.4, bf16[576,1536]{1,0:T(8,128)(2,1)S(1)} %get-tuple-element.154), kind=kOutput, calls=%fused_computation.1 | convolution fusion | flops 7257980928 | bytes 14548992 | tf_op jit(solution)/shard_map/dot_general | solution.py:44
  310.8 34.1 %shard_map.265 = (bf16[1152,4096]{1,0:T(8,128)(2,1)}, bf16[1536,4096]{1,0:T(8,128)(2,1)}) custom-call(bf16[1152,1536]{1,0:T(8,128)(2,1)} %pad_maximum_fusion.1.d_ref, bf16[1536,2048]{1,0:T(8,128)(2,1)} %get-tuple-element.61.down_ref, bf16[1152,2048]{1,0:T(8,128)(2,1)} %get-tuple-element.63.gate_ref, bf16[1152,2048]{1,0:T(8,128)(2,1)} %get-tuple-element.64.up_ref, ...), custom_call_target="tpu_custom_call" | custom-call | flops 22000001024 | bytes 40000000 | tf_op jit(solution)/shard_map/pallas_call | solution.py:790
  344.9 12.0 %fusion.4 = bf16[576,1536]{1,0:T(8,128)(2,1)S(1)} fusion(bf16[1536,4096]{1,0:T(8,128)(2,1)} %get-tuple-element.58.w_ref, bf16[1152,4096]{1,0:T(8,128)(2,1)} %get-tuple-element.67), kind=kOutput, calls=%fused_computation.20 | convolution fusion | flops 7248642048 | bytes 19070976 | tf_op jit(solution)/shard_map/dot_general | solution.py:40
  357.5 3.5 collective-permute-done.5
  360.9 14.4 %multiply_reduce_fusion.2 = (f32[1536]{0:T(1024)}, f32[576]{0:T(1024)S(1)}, f32[576,1536]{1,0:T(8,128)S(1)}) fusion(f32[576,1536]{1,0:T(8,128)S(1)} %get-tuple-element.153, f32[576]{0:T(1024)S(1)} %get-tuple-element.138, bf16[576,1536]{1,0:T(8,128)(2,1)} %collective-permute-done.5, f32[1536]{0:T(1024)S(1)} %copy-done.11, ...), kind=kOutput, calls=%fused_computation.12 | convolution fusion | flops 7254833152 | bytes 26165760 | tf_op jit(solution)/shard_map/dot_general | solution.py:40
  375.4 5.9 fusion.22
  382.3 1.4 select_maximum_fusion.1
  384.4 0.8 collective-permute-done.6
  385.2 6.7 convolution_convert_fusion.2.out
  391.9 1.9 pad_maximum_fusion.2
  394.1 4.7 fusion.28.refs_5_
  398.8 109.7 %shard_map.266 = (bf16[1152,2304]{1,0:T(8,128)(2,1)}, f32[2,8,384]{2,1,0:T(8,128)}, f32[2,2,2,8,256]{4,3,2,1,0:T(8,128)}, f32[2,2,2,2,8,256]{5,4,3,2,1,0:T(8,128)}, bf16[1536,1024]{1,0:T(8,128)(2,1)}) custom-call(f32[16]{0:T(128)} %reshape_squeeze.3.refs_0_, bf16[1152,2304]{1,0:T(8,128)(2,1)} %convolution_convert_fusion.refs_1_, ...), custom_call_target="tpu_custom_call" | custom-call | flops 1000000000 | bytes 1000000 | tf_op jit(solution)/shard_map/pallas_call | solution.py:386
  508.6 0.9 slice.152
  510.5 0.9 slice_reduce_fusion
  512.0 5.4 convert_element_type.91
  518.1 137.8 %shard_map.267 = (f32[8,1536]{1,0:T(8,128)}, f32[576,1536]{1,0:T(8,128)}, bf16[1536,1024]{1,0:T(8,128)(2,1)}, bf16[1536,1024]{1,0:T(8,128)(2,1)}, bf16[1536,1152]{1,0:T(8,128)(2,1)}, /*index=5*/bf16[1536,384]{1,0:T(8,128)(2,1)}) custom-call(f32[8,1536]{1,0:T(8,128)} %pad_maximum_fusion.3.small, bf16[384,4096]{1,0:T(8,128)(2,1)} %reduce-scatter.5.cloned.1.call-done.gu, ...), custom_call_target="tpu_custom_call" | custom-call | tf_op jit(solution)/shard_map/pallas_call | solution.py:1329
  655.9 0.8 slice.163
  658.7 1.5 fusion.25
  660.1 1.3 fusion.26
  661.5 5.3 fusion.24
  666.7 3.4 convert_element_type.89
  670.2 3.5 convert_element_type.90
  673.6 1.6 convert_element_type.88
  675.2 1.1 reshape.119
  676.9 1.3 reshape.121
  678.3 1.3 reshape.120
  679.6 1.3 dynamic-slice_reduce_fusion
  680.9 1.3 dynamic-slice_reduce_fusion.1
  683.5 1.8 copy.65
  (119 shorter events, 16.0 us)
Async XLA Ops:
  7.2 391.7 %reduce-scatter.3.cloned.1.call-start = ((), (), s32[]{:S(2)}) async-start(), calls=%async_computation.2 | async-start | bytes 7864320 | tf_op jit(solution)/shard_map/reduce_scatter | solution.py:1417
  8.0 71.8 %copy-start.9 = (s32[576]{0:T(1024)}, s32[576]{0:T(1024)S(1)}, u32[]{:S(2)}) copy-start(s32[576]{0:T(1024)S(1)} %get-tuple-element.109) | copy-start | bytes 6916
  8.0 280.6 %copy-start.12 = (f32[576]{0:T(1024)}, f32[576]{0:T(1024)S(1)}, u32[]{:S(2)}) copy-start(f32[576]{0:T(1024)S(1)} %get-tuple-element.108) | copy-start | bytes 6916
  8.0 71.8 %collective-permute-start = (s32[576]{0:T(1024)S(1)}, s32[576]{0:T(1024)S(1)}, u32[]{:S(2)}, u32[]{:S(2)}) collective-permute-start(s32[576]{0:T(1024)S(1)} %get-tuple-element.109), channel_id=1, source_target_pairs={{0,4},{4,0},{1,5},{5,1},{2,6},{6,2},{3,7},{7,3},{8,12},{12,8},{9,1... | collective-permute-start | bytes 6920 | tf_op jit(solution)/shard_map/ppermute | solution.py:1387
  166.1 56.2 %copy-start = (bf16[576,1536]{1,0:T(8,128)(2,1)S(1)}, bf16[576,1536]{1,0:T(8,128)(2,1)}, u32[]{:S(2)}) copy-start(bf16[576,1536]{1,0:T(8,128)(2,1)} %tokens.1) | copy-start | bytes 5308420
  166.1 56.2 %copy-start.16 = (bf16[1536,768]{1,0:T(8,128)(2,1)S(1)}, bf16[1536,768]{1,0:T(8,128)(2,1)}, u32[]{:S(2)}) copy-start(bf16[1536,768]{1,0:T(8,128)(2,1)} %get-tuple-element.57) | copy-start | bytes 7077892
  166.1 56.2 %copy-start.18 = (bf16[1152,768]{1,0:T(8,128)(2,1)S(1)}, bf16[1152,768]{1,0:T(8,128)(2,1)}, u32[]{:S(2)}) copy-start(bf16[1152,768]{1,0:T(8,128)(2,1)} %get-tuple-element.56) | copy-start | bytes 5308420
  169.8 55.0 %copy-start.11 = (f32[1536]{0:T(1024)S(1)}, f32[1536]{0:T(1024)}, u32[]{:S(2)}) copy-start(f32[1536]{0:T(1024)} %param.26) | copy-start | bytes 18436
  169.8 52.5 %collective-permute-start.1 = (bf16[576,1536]{1,0:T(8,128)(2,1)S(1)}, bf16[576,1536]{1,0:T(8,128)(2,1)S(1)}, u32[]{:S(2)}, u32[]{:S(2)}) collective-permute-start(bf16[576,1536]{1,0:T(8,128)(2,1)S(1)} %convolution_convert_fusion.4), channel_id=1, source_target_pairs={{0,4},{4,0},{1,5},{5,1},{2,6},{6,2},{3,7},{7,3},{8,12},{12,8},{9,1... | collective-permute-start | bytes 5308424 | tf_op jit(solution)/shard_map/ppermute | solution.py:1387
  225.2 3.8 collective-permute-start.2
  265.8 22.8 %copy-start.1 = (bf16[1536,2048]{1,0:T(8,128)(2,1)S(1)}, bf16[1536,2048]{1,0:T(8,128)(2,1)}, u32[]{:S(2)}) copy-start(bf16[1536,2048]{1,0:T(8,128)(2,1)} %get-tuple-element.61.down_ref) | copy-start | bytes 18874372
  265.8 22.8 %copy-start.6 = (bf16[576,1536]{1,0:T(8,128)(2,1)S(1)}, bf16[576,1536]{1,0:T(8,128)(2,1)}, u32[]{:S(2)}) copy-start(bf16[576,1536]{1,0:T(8,128)(2,1)} %param.16) | copy-start | bytes 5308420
  265.8 22.8 %copy-start.15 = (bf16[1152,2048]{1,0:T(8,128)(2,1)S(1)}, bf16[1152,2048]{1,0:T(8,128)(2,1)}, u32[]{:S(2)}) copy-start(bf16[1152,2048]{1,0:T(8,128)(2,1)} %get-tuple-element.60) | copy-start | bytes 14155780
  273.4 15.3 %collective-permute-start.3 = (bf16[576,1536]{1,0:T(8,128)(2,1)S(1)}, bf16[576,1536]{1,0:T(8,128)(2,1)S(1)}, u32[]{:S(2)}, u32[]{:S(2)}) collective-permute-start(bf16[576,1536]{1,0:T(8,128)(2,1)S(1)} %convolution_convert_fusion.3), channel_id=1, source_target_pairs={{0,4},{4,0},{1,5},{5,1},{2,6},{6,2},{3,7},{7,3},{8,12},{12,8},{9,1... | collective-permute-start | bytes 5308424 | tf_op jit(solution)/shard_map/ppermute | solution.py:1387
  294.7 3.7 collective-permute-start.4
  310.8 207.3 %reduce-scatter.5.cloned.1.call-start = ((), (), s32[]{:S(2)}) async-start(), calls=%async_computation.3 | async-start | bytes 15728640 | tf_op jit(solution)/shard_map/reduce_scatter | solution.py:1417
  357.0 18.3 %copy-start.2 = (f32[576,1536]{1,0:T(8,128)S(1)}, f32[576,1536]{1,0:T(8,128)}, u32[]{:S(2)}) copy-start(f32[576,1536]{1,0:T(8,128)} %get-tuple-element.155) | copy-start | bytes 10616836
  357.0 18.3 %copy-start.7 = (bf16[576,1536]{1,0:T(8,128)(2,1)S(1)}, bf16[576,1536]{1,0:T(8,128)(2,1)}, u32[]{:S(2)}) copy-start(bf16[576,1536]{1,0:T(8,128)(2,1)} %param.16) | copy-start | bytes 5308420
  357.0 18.3 %copy-start.13 = (f32[576]{0:T(1024)S(1)}, f32[576]{0:T(1024)}, u32[]{:S(2)}) copy-start(f32[576]{0:T(1024)} %copy-done.12) | copy-start | bytes 6916
  357.0 18.3 %copy-start.14 = (f32[576]{0:T(1024)S(1)}, f32[576]{0:T(1024)}, u32[]{:S(2)}) copy-start(f32[576]{0:T(1024)} %get-tuple-element.137) | copy-start | bytes 6916
  357.0 3.9 collective-permute-start.5
  375.4 6.3 copy-start.10
  381.2 4.0 collective-permute-start.6
  391.9 2.2 copy-start.17
  661.5 5.3 copy-start.5
  666.7 3.4 copy-start.4
  670.2 3.5 copy-start.8
  673.6 9.8 %copy-start.3 = (f32[576,1536]{1,0:T(8,128)S(1)}, f32[576,1536]{1,0:T(8,128)}, u32[]{:S(2)}) copy-start(f32[576,1536]{1,0:T(8,128)} %get-tuple-element.176) | copy-start | bytes 10616836
Sparse Core Ops, SparseCore 0:
  310.9 74.2 reduce-scatter.2
  388.4 129.6 reduce-scatter.4

commit v6 on v5

--- a/solution.py
+++ b/solution.py
@@ -87,11 +87,20 @@
     return centered * inv, inv, stat
 
 
-def fwd_kernel(hook, mix_ref, qkv_ref, t_ref, gn_ref, jj_ref, nh_ref, att_ref, pre_ref, qs_ref, ho_ref, dist_ref, qx_ref, mx_ref):
+def fwd_kernel(
+    hook, mix_ref, normed_ref, weight_ref, t_ref, gn_ref, jj_ref, nh_ref, att_ref, pre_ref, qs_ref, ho_ref, qkv_ref, dist_ref, qx_ref, mx_ref
+):
     side, t, g = pl.program_id(0), pl.program_id(1), pl.program_id(2)
     step = (side * 2 + t) * 2 + g
     mix0 = 8 * side + 4 * g
     hook(step, 0)
+
+    @pl.when(g == 0)
+    def _():
+        for part in range(3):
+            cols = slice(384 * part, 384 * (part + 1))
+            qkv_ref[:, cols] = nn(normed_ref[...], weight_ref[:, cols]).astype(BF16)
+
     w0 = pl.multiple_of(g * 128, 128)
     m0, m1, from_first = head_masks(g)
     m0f, m1f = m0.astype(F32), m1.astype(F32)
@@ -311,10 +320,10 @@
     return pl.BlockSpec((None,) + shape, lambda s, t, g: (s, 0, 0))
 
 
-def common_specs():
+def common_specs(first=None):
     return [
         pl.BlockSpec(memory_space=pltpu.SMEM),
-        pl.BlockSpec((TREE, 1152), lambda s, t, g: (t, s)),
+        *(first or [pl.BlockSpec((TREE, 1152), lambda s, t, g: (t, s))]),
         pl.BlockSpec((None, None, 2, CQ * WIN, WIN), lambda s, t, g: (s, g, 0, 0, 0)),
         by_side((8, 384)),
         pl.BlockSpec((None, 16, WIN), lambda s, t, g: (t, 0, 0)),
@@ -329,16 +338,16 @@
     return [lead + (2, TREE, WIN), lead + (2, TREE, CQ * WIN), lead + (2, CQ, TREE, WIN), lead + (TREE, WIN)]
 
 
-def attention_forward(mix, qkv, toeplitz, gains, jj, gather=None):
-    trees = qkv.shape[0] // TREE
+def attention_forward(mix, normed, weight, toeplitz, gains, jj, gather=None):
+    trees, width = normed.shape[0] // TREE, normed.shape[1]
     shapes = saved_shapes(trees)
     kinds = (F32, BF16, BF16, F32)
     weights, wide, count, collective = gather if gather else ((), (), 0, {})
     many, held = len(weights), len(wide)
 
     def kernel(*refs):
-        inputs, loads, refs = refs[:5], refs[5 : 5 + many], refs[5 + many :]
-        outs, full, refs = refs[:5], refs[5 : 5 + held], refs[5 + held :]
+        inputs, loads, refs = refs[:6], refs[6 : 6 + many], refs[6 + many :]
+        outs, full, refs = refs[:6], refs[6 : 6 + held], refs[6 + held :]
         work = Gather(DIRECT, LATER, loads, full, *refs[3:]) if gather else None
 
         def hook(step, place):
@@ -348,20 +357,25 @@
         fwd_kernel(hook, *inputs, *outs, *refs[:3])
 
     anywhere = pl.BlockSpec(memory_space=pl.ANY)
+    first = [pl.BlockSpec((TREE, width), lambda s, t, g: (t, 0)), pl.BlockSpec((width, 1152), lambda s, t, g: (0, s))]
     result = pl.pallas_call(
         kernel,
         grid=(2, trees, 2),
-        in_specs=common_specs() + [anywhere] * many,
-        out_specs=[pl.BlockSpec((TREE, 384), lambda s, t, g: (t, s))] + [by_group(s) for s in shapes] + [anywhere] * held,
+        in_specs=common_specs(first) + [anywhere] * many,
+        out_specs=[pl.BlockSpec((TREE, 384), lambda s, t, g: (t, s))]
+        + [by_group(s) for s in shapes]
+        + [pl.BlockSpec((TREE, 1152), lambda s, t, g: (t, s))]
+        + [anywhere] * held,
         out_shape=[jax.ShapeDtypeStruct((trees * TREE, 768), BF16)]
         + [jax.ShapeDtypeStruct(s, k) for s, k in zip(shapes, kinds)]
-        + [jax.ShapeDtypeStruct((1536, w), BF16) for w in wide],
+        + [jax.ShapeDtypeStruct((trees * TREE, 2304), BF16)]
+        + [jax.ShapeDtypeStruct((width, w), BF16) for w in wide],
         scratch_shapes=[pltpu.VMEM((TREE, WIN), jnp.int32), pltpu.VMEM((EXT, WIN), F32), pltpu.VMEM((2, TREE, WIN), BF16)]
         + gather_scratch(weights, count),
         compiler_params=pltpu.CompilerParams(**PARAMS, **collective),
-        cost_estimate=pl.CostEstimate(flops=80_000_000_000, bytes_accessed=120_000_000, transcendentals=0),
-    )(mix, qkv, toeplitz, gains, jj, *weights)
-    return result[0], result[1:5], result[5:]
+        cost_estimate=pl.CostEstimate(flops=90_000_000_000, bytes_accessed=120_000_000, transcendentals=0),
+    )(mix, normed, weight, toeplitz, gains, jj, *weights)
+    return result[0], result[1:5], result[5], result[6:]
 
 
 def attention_backward(mix, qkv, toeplitz, gains, jj, d_normed, saved, sums=None):
@@ -672,7 +686,21 @@
     ]
 
 
-AHEAD = 3
+SLOTS = {
+    1: (("relay_z", 0), ("start_z", 2), ("pass_own", 0)),
+    2: (("start_plane", 0),),
+    3: (("relay_z", 1), ("start_z", 3), ("pass_own", 1)),
+    4: (("start_plane", 1), ("forward", 0)),
+    5: (("relay_z", 2), ("start_z", 4), ("pass_own", 2)),
+    6: (("start_plane", 2), ("forward", 1)),
+    7: (("relay_z", 3), ("pass_own", 3)),
+    8: (("start_plane", 3), ("forward", 2), ("start_z", 5)),
+    9: (("relay_z", 4), ("start_z", 6)),
+    10: (("start_plane", 4), ("forward", 3)),
+    11: (("relay_only", 5),),
+    12: (("forward", 4),),
+    13: (("relay_only", 6),),
+}
 
 
 def background(work, step, place):
@@ -680,7 +708,6 @@
 
         @pl.when(step == 7)
         def _():
-            work.forward(WHOLE - 1)
             for item in range(len(work.items)):
                 if item < WHOLE:
                     work.finish(item)
@@ -698,31 +725,19 @@
             if slot == 0:
                 work.own()
                 greet((work.near, work.far, work.by_x, work.by_y))
-                for item in range(AHEAD):
+                for item in range(2):
                     work.start_z(item)
-            elif slot <= 2 * WHOLE:
-                item = (slot - 1) // 2
-                if slot % 2:
-                    work.relay_z(item)
-                    if item + AHEAD < len(work.items):
-                        work.start_z(item + AHEAD)
-                    if item < len(work.weights):
-                        work.pass_own(item)
-                else:
-                    work.start_plane(item)
-                    if item >= 1:
-                        work.forward(item - 1)
-            elif slot <= 2 * WHOLE + 2:
-                work.relay_only(slot - 2 * WHOLE - 1 + WHOLE)
+            for name, item in SLOTS.get(slot, ()):
+                getattr(work, name)(item)
 
 
 TILE = 512
 
 
-def beside_gate(work, step):
-    script = (("start_both", 0), ("start_both", 1)), (), (("forward", 0),), (("forward", 1),)
-    for turn, names in enumerate(script):
-        if names:
+def beside_gate(work, step, place):
+    script = {(0, 0): (("start_both", 0), ("start_both", 1)), (1, 1): (("forward", 0),), (3, 0): (("forward", 1),)}
+    for (turn, where), names in script.items():
+        if where == place:
 
             @pl.when(step == turn)
             def _(names=names, turn=turn):
@@ -743,9 +758,11 @@
         step = pl.program_id(0)
         work = Gather(0, LAST, (), refs[:1], refs[1], refs[2], None) if many else None
         if work:
-            beside_gate(work, step)
+            beside_gate(work, step, 0)
         gate = nn(x_ref[...], w_ref[:, :TILE])
         gate_ref[...] = gate.astype(BF16)
+        if work:
+            beside_gate(work, step, 1)
         up = nn(x_ref[...], w_ref[:, TILE:])
         up_ref[...] = up.astype(BF16)
         hidden_ref[...] = (gate * jax.nn.sigmoid(gate) * up).astype(BF16)
@@ -1457,8 +1474,7 @@
             gather = None
         mix = both_small[:, 24, :mix_size].reshape(-1)
         gains = jnp.broadcast_to(both_small[:, 25:27].reshape(2, 1, 2 * WIN)[:, :, :wide], (2, 8, wide))
-        qkv = nn(normed_one, qkv_weight).astype(BF16)
-        heads_out, saved, later = attention_forward(mix, qkv, toep, gains, jj, gather)
+        heads_out, saved, qkv, later = attention_forward(mix, normed_one, qkv_weight, toep, gains, jj, gather)
         if fused:
             out_weight, gu_weight, down_weight = later
         else:

time: 698 us -> 688 us (0.986)
  matrix products: 81.2 us -> 66.5 us
    dot_general x2 -> x1, matrix products: 18.6 us -> 4.71 us  [nn(): lax.dot_general(a, b, (((1,), (0,)), ((), ())), preferred_element_type=F32)]
    pallas_call x1, Pallas kernels: 83.9 us -> 91.5 us  [attention_forward(): pl.pallas_call(kernel, grid=(2, trees, 2), in_specs=common_specs(first) +...]
  transfers between devices with their start and end apart: 9 -> 9, of which waited for: 6 -> 6; matrix products, arithmetic and copies ran while one was open for 11% -> 9% of each run, Pallas kernels for 28% -> 28%
where the time goes in v6:
time: 688 us; the launch traced here: 683 us
  Pallas kernels  456 us (66%)
  matrix products  66.5 us (10%)
  starting transfers between devices  62.9 us (9%)
  other arithmetic  32.8 us (5%)
  local copies, waits for them, and re-layouts  30.1 us (4%)
  waiting for transfers between devices  17.6 us (3%)
  between operations  17.2 us (2%)
    pallas_call x1, Pallas kernels, finish_gradients(): pl.pallas_call(finish_kernel, in_specs=[vmem] * 2 + [anywhere] + [vmem] *...  137 us
    pallas_call x1, Pallas kernels, attention_backward(): pl.pallas_call(kernel, grid=(2, trees, 2), in_specs=common_specs() + [pl....  106 us
    pallas_call x1, Pallas kernels, attention_forward(): pl.pallas_call(kernel, grid=(2, trees, 2), in_specs=common_specs(first) +...  91.5 us
    ppermute x7, starting transfers between devices, over_core(): return lax.ppermute(value, 'core', [(0, 1), (1, 0)])  62.9 us
    pallas_call x1, Pallas kernels, opening(): pl.pallas_call(opening_kernel, in_specs=[vmem] * 3 + [anywhere] * 3, out_...  50.8 us
    dot_general x6, matrix products, nt(): lax.dot_general(a, b, (((1,), (1,)), ((), ())), preferred_element_type=F32)  44.7 us
    pallas_call x1, Pallas kernels, gated_forward(): pl.pallas_call(kernel, grid=(units // TILE,), in_specs=[pl.BlockSpec((row...  35.7 us
    pallas_call x1, Pallas kernels, gated_backward(): pl.pallas_call(kernel, grid=(units // TILE,), in_specs=[whole, pl.BlockSp...  34.6 us
  transfers between devices with their start and end apart: 9, of which 6 were waited for; matrix products, arithmetic and copies ran while one was open for 9% of the time, Pallas kernels for 28%

profile of v6, /device:TPU:0, one launch (start us, length us, event | category | flops | bytes accessed | tf_op | source)
XLA Modules:
  0.0 682.8 jit_solution(6727082020581394899)
XLA Ops:
  7.2 0.8 fusion.23
  9.3 0.8 reshape.109
  10.8 1.3 broadcast_in_dim.51.gain_ref.gain
  12.9 50.8 %shard_map.262 = (bf16[1536,2304]{1,0:T(8,128)(2,1)}, bf16[1152,1536]{1,0:T(8,128)(2,1)}, bf16[2,2,2,1536,256]{4,3,2,1,0:T(8,128)(2,1)}, f32[2,32,256]{2,1,0:T(8,128)}) custom-call(bf16[576,1536]{1,0:T(8,128)(2,1)} %tokens.1, f32[1,1536]{1,0:T(1,128)} %broadcast_in_dim.51.gain_ref.gain, f32[32,256]{1,0:T(8,128)} %fusion.15.small_ref, ...), custom_call_target="tpu_custom_call" | custom-call | tf_op jit(solution)/shard_map/pallas_call | solution.py:884
  66.4 1.3 stack.68.refs_5_.refs_4_
  68.3 91.5 %shard_map.263 = (bf16[1152,768]{1,0:T(8,128)(2,1)}, f32[2,2,2,2,576,256]{5,4,3,2,1,0:T(8,128)}, bf16[2,2,2,2,576,1536]{5,4,3,2,1,0:T(8,128)(2,1)}, bf16[2,2,2,2...) custom-call(f32[16]{0:T(128)} %reshape_squeeze.3.refs_0_, ...), custom_call_target="tpu_custom_call" | custom-call | flops 89999998976 | bytes 120000000 | tf_op jit(solution)/shard_map/pallas_call | solution.py:361
  159.8 3.6 convolution_convert_fusion.3
  163.5 48.4 %collective-permute-start.1 = (bf16[576,1536]{1,0:T(8,128)(2,1)S(1)}, bf16[576,1536]{1,0:T(8,128)(2,1)S(1)}, u32[]{:S(2)}, u32[]{:S(2)}) collective-permute-start(bf16[576,1536]{1,0:T(8,128)(2,1)S(1)} %convolution_convert_fusion.3), channel_id=1, source_target_pairs={{0,4},{4,0},{1,5},{5,1},{2,6},{6,2},{3,7},{7,3},{8,12},{12,8},{9,1... | collective-permute-start | bytes 5308424 | tf_op jit(solution)/shard_map/ppermute | solution.py:1404
  211.9 3.3 collective-permute-done.1
  215.2 1.9 multiply_reduce_fusion.3
  218.5 3.3 collective-permute-done.2
  221.9 2.0 pad_maximum_fusion.x_ref
  223.9 35.7 %shard_map.264 = (bf16[1152,2048]{1,0:T(8,128)(2,1)}, bf16[1152,2048]{1,0:T(8,128)(2,1)}, bf16[1152,2048]{1,0:T(8,128)(2,1)}, bf16[1536,2048]{1,0:T(8,128)(2,1)}) custom-call(bf16[1152,1536]{1,0:T(8,128)(2,1)} %pad_maximum_fusion.x_ref, bf16[1536,4096]{1,0:T(8,128)(2,1)} %get-tuple-element.59.w_ref, ...), custom_call_target="tpu_custom_call", output_to_operand_aliasing={{3}: (2, {})} | custom-call | tf_op jit(solution)/shard_map/pallas_call | solution.py:780
  259.6 7.5 %convolution_convert_fusion.2 = bf16[576,1536]{1,0:T(8,128)(2,1)S(1)} fusion(bf16[1536,2048]{1,0:T(8,128)(2,1)} %get-tuple-element.62.down_ref, bf16[1152,2048]{1,0:T(8,128)(2,1)} %get-tuple-element.61), kind=kOutput, calls=%fused_computation.20 | convolution fusion | flops 3624763392 | bytes 10420224 | tf_op jit(solution)/shard_map/dot_general | solution.py:40
  267.1 12.2 %collective-permute-start.3 = (bf16[576,1536]{1,0:T(8,128)(2,1)S(1)}, bf16[576,1536]{1,0:T(8,128)(2,1)S(1)}, u32[]{:S(2)}, u32[]{:S(2)}) collective-permute-start(bf16[576,1536]{1,0:T(8,128)(2,1)S(1)} %convolution_convert_fusion.2), channel_id=1, source_target_pairs={{0,4},{4,0},{1,5},{5,1},{2,6},{6,2},{3,7},{7,3},{8,12},{12,8},{9,1... | collective-permute-start | bytes 5308424 | tf_op jit(solution)/shard_map/ppermute | solution.py:1404
  279.3 3.3 collective-permute-done.3
  282.7 6.1 fusion.21
  289.1 3.3 collective-permute-done.4
  292.5 2.0 pad_maximum_fusion.1.d_ref
  294.5 10.3 %convolution_convert_fusion = bf16[1536,2048]{1,0:T(8,128)(2,1)} fusion(bf16[1152,2048]{1,0:T(8,128)(2,1)S(1)} %copy-done.15, bf16[576,1536]{1,0:T(8,128)(2,1)S(1)} %collective-permute-done.4, bf16[576,1536]{1,0:T(8,128)(2,1)S(1)} %get-tuple-element.156), kind=kOutput, calls=%fused_computation | convolution fusion | flops 7257980928 | bytes 14548992 | tf_op jit(solution)/shard_map/dot_general | solution.py:44
  304.9 34.6 %shard_map.265 = (bf16[1152,4096]{1,0:T(8,128)(2,1)}, bf16[1536,4096]{1,0:T(8,128)(2,1)}) custom-call(bf16[1152,1536]{1,0:T(8,128)(2,1)} %pad_maximum_fusion.1.d_ref, bf16[1536,2048]{1,0:T(8,128)(2,1)} %get-tuple-element.62.down_ref, bf16[1152,2048]{1,0:T(8,128)(2,1)} %get-tuple-element.64.gate_ref, bf16[1152,2048]{1,0:T(8,128)(2,1)} %get-tuple-element.65.up_ref, ...), custom_call_target="tpu_custom_call" | custom-call | flops 22000001024 | bytes 40000000 | tf_op jit(solution)/shard_map/pallas_call | solution.py:807
  339.5 12.0 %fusion.4 = bf16[576,1536]{1,0:T(8,128)(2,1)S(1)} fusion(bf16[1536,4096]{1,0:T(8,128)(2,1)} %get-tuple-element.59.w_ref, bf16[1152,4096]{1,0:T(8,128)(2,1)} %get-tuple-element.68), kind=kOutput, calls=%fused_computation.19 | convolution fusion | flops 7248642048 | bytes 19070976 | tf_op jit(solution)/shard_map/dot_general | solution.py:40
  352.1 3.4 collective-permute-done.5
  355.6 13.6 %multiply_reduce_fusion.2 = (f32[1536]{0:T(1024)}, f32[576]{0:T(1024)S(1)}, f32[576,1536]{1,0:T(8,128)S(1)}) fusion(f32[576,1536]{1,0:T(8,128)S(1)} %get-tuple-element.155, f32[576]{0:T(1024)S(1)} %get-tuple-element.140, bf16[576,1536]{1,0:T(8,128)(2,1)} %collective-permute-done.5, f32[1536]{0:T(1024)S(1)} %copy-done.11, ...), kind=kOutput, calls=%fused_computation.11 | convolution fusion | flops 7254833152 | bytes 26165760 | tf_op jit(solution)/shard_map/dot_general | solution.py:40
  369.2 5.9 fusion.22
  376.1 1.4 select_maximum_fusion.1
  378.2 0.8 collective-permute-done.6
  379.0 6.7 convolution_convert_fusion.1.out
  385.7 1.9 pad_maximum_fusion.2
  387.9 4.7 fusion.28.refs_5_
  392.6 106.0 %shard_map.266 = (bf16[1152,2304]{1,0:T(8,128)(2,1)}, f32[2,8,384]{2,1,0:T(8,128)}, f32[2,2,2,8,256]{4,3,2,1,0:T(8,128)}, f32[2,2,2,2,8,256]{5,4,3,2,1,0:T(8,128)}, bf16[1536,1024]{1,0:T(8,128)(2,1)}) custom-call(f32[16]{0:T(128)} %reshape_squeeze.3.refs_0_, bf16[1152,2304]{1,0:T(8,128)(2,1)} %get-tuple-element.69.refs_1_, ...), custom_call_target="tpu_custom_call" | custom-call | flops 1000000000 | bytes 1000000 | tf_op jit(solution)/shard_map/pallas_call | solution.py:400
  498.7 0.9 slice.152
  500.6 0.9 slice_reduce_fusion
  502.1 5.5 convert_element_type.87
  508.3 137.0 %shard_map.267 = (f32[8,1536]{1,0:T(8,128)}, f32[576,1536]{1,0:T(8,128)}, bf16[1536,1024]{1,0:T(8,128)(2,1)}, bf16[1536,1024]{1,0:T(8,128)(2,1)}, bf16[1536,1152]{1,0:T(8,128)(2,1)}, /*index=5*/bf16[1536,384]{1,0:T(8,128)(2,1)}) custom-call(f32[8,1536]{1,0:T(8,128)} %pad_maximum_fusion.3.small, bf16[384,4096]{1,0:T(8,128)(2,1)} %reduce-scatter.5.cloned.1.call-done.gu, ...), custom_call_target="tpu_custom_call" | custom-call | tf_op jit(solution)/shard_map/pallas_call | solution.py:1346
  645.3 0.8 slice.163
  648.0 1.5 fusion.25
  649.5 1.3 fusion.26
  650.8 5.3 fusion.24
  656.1 3.4 convert_element_type.85
  659.5 3.5 convert_element_type.86
  663.0 1.6 convert_element_type.84
  664.5 1.1 reshape.119
  666.3 1.3 reshape.121
  667.6 1.3 reshape.120
  668.9 1.3 dynamic-slice_reduce_fusion
  670.2 1.3 dynamic-slice_reduce_fusion.1
  672.8 1.8 copy.65
  (118 shorter events, 15.3 us)
Async XLA Ops:
  7.2 385.5 %reduce-scatter.3.cloned.1.call-start = ((), (), s32[]{:S(2)}) async-start(), calls=%async_computation.2 | async-start | bytes 7864320 | tf_op jit(solution)/shard_map/reduce_scatter | solution.py:1434
  8.0 151.8 %copy-start.9 = (s32[576]{0:T(1024)}, s32[576]{0:T(1024)S(1)}, u32[]{:S(2)}) copy-start(s32[576]{0:T(1024)S(1)} %get-tuple-element.111) | copy-start | bytes 6916
  8.0 274.7 %copy-start.12 = (f32[576]{0:T(1024)}, f32[576]{0:T(1024)S(1)}, u32[]{:S(2)}) copy-start(f32[576]{0:T(1024)S(1)} %get-tuple-element.110) | copy-start | bytes 6916
  8.0 57.8 %collective-permute-start = (s32[576]{0:T(1024)S(1)}, s32[576]{0:T(1024)S(1)}, u32[]{:S(2)}, u32[]{:S(2)}) collective-permute-start(s32[576]{0:T(1024)S(1)} %get-tuple-element.111), channel_id=1, source_target_pairs={{0,4},{4,0},{1,5},{5,1},{2,6},{6,2},{3,7},{7,3},{8,12},{12,8},{9,1... | collective-permute-start | bytes 6920 | tf_op jit(solution)/shard_map/ppermute | solution.py:1404
  159.8 55.4 %copy-start = (bf16[576,1536]{1,0:T(8,128)(2,1)S(1)}, bf16[576,1536]{1,0:T(8,128)(2,1)}, u32[]{:S(2)}) copy-start(bf16[576,1536]{1,0:T(8,128)(2,1)} %tokens.1) | copy-start | bytes 5308420
  159.8 55.4 %copy-start.16 = (bf16[1536,768]{1,0:T(8,128)(2,1)S(1)}, bf16[1536,768]{1,0:T(8,128)(2,1)}, u32[]{:S(2)}) copy-start(bf16[1536,768]{1,0:T(8,128)(2,1)} %get-tuple-element.58) | copy-start | bytes 7077892
  159.8 55.4 %copy-start.18 = (bf16[1152,768]{1,0:T(8,128)(2,1)S(1)}, bf16[1152,768]{1,0:T(8,128)(2,1)}, u32[]{:S(2)}) copy-start(bf16[1152,768]{1,0:T(8,128)(2,1)} %get-tuple-element.57) | copy-start | bytes 5308420
  163.5 54.2 %copy-start.11 = (f32[1536]{0:T(1024)S(1)}, f32[1536]{0:T(1024)}, u32[]{:S(2)}) copy-start(f32[1536]{0:T(1024)} %param.26) | copy-start | bytes 18436
  163.5 51.7 %collective-permute-start.1 = (bf16[576,1536]{1,0:T(8,128)(2,1)S(1)}, bf16[576,1536]{1,0:T(8,128)(2,1)S(1)}, u32[]{:S(2)}, u32[]{:S(2)}) collective-permute-start(bf16[576,1536]{1,0:T(8,128)(2,1)S(1)} %convolution_convert_fusion.3), channel_id=1, source_target_pairs={{0,4},{4,0},{1,5},{5,1},{2,6},{6,2},{3,7},{7,3},{8,12},{12,8},{9,1... | collective-permute-start | bytes 5308424 | tf_op jit(solution)/shard_map/ppermute | solution.py:1404
  218.1 3.8 collective-permute-start.2
  259.6 23.1 %copy-start.1 = (bf16[1536,2048]{1,0:T(8,128)(2,1)S(1)}, bf16[1536,2048]{1,0:T(8,128)(2,1)}, u32[]{:S(2)}) copy-start(bf16[1536,2048]{1,0:T(8,128)(2,1)} %get-tuple-element.62.down_ref) | copy-start | bytes 18874372
  259.6 23.1 %copy-start.6 = (bf16[576,1536]{1,0:T(8,128)(2,1)S(1)}, bf16[576,1536]{1,0:T(8,128)(2,1)}, u32[]{:S(2)}) copy-start(bf16[576,1536]{1,0:T(8,128)(2,1)} %param.16) | copy-start | bytes 5308420
  259.6 23.1 %copy-start.15 = (bf16[1152,2048]{1,0:T(8,128)(2,1)S(1)}, bf16[1152,2048]{1,0:T(8,128)(2,1)}, u32[]{:S(2)}) copy-start(bf16[1152,2048]{1,0:T(8,128)(2,1)} %get-tuple-element.61) | copy-start | bytes 14155780
  267.1 15.5 %collective-permute-start.3 = (bf16[576,1536]{1,0:T(8,128)(2,1)S(1)}, bf16[576,1536]{1,0:T(8,128)(2,1)S(1)}, u32[]{:S(2)}, u32[]{:S(2)}) collective-permute-start(bf16[576,1536]{1,0:T(8,128)(2,1)S(1)} %convolution_convert_fusion.2), channel_id=1, source_target_pairs={{0,4},{4,0},{1,5},{5,1},{2,6},{6,2},{3,7},{7,3},{8,12},{12,8},{9,1... | collective-permute-start | bytes 5308424 | tf_op jit(solution)/shard_map/ppermute | solution.py:1404
  288.8 3.7 collective-permute-start.4
  304.8 203.4 %reduce-scatter.5.cloned.1.call-start = ((), (), s32[]{:S(2)}) async-start(), calls=%async_computation.3 | async-start | bytes 15728640 | tf_op jit(solution)/shard_map/reduce_scatter | solution.py:1434
  351.6 17.6 %copy-start.2 = (f32[576,1536]{1,0:T(8,128)S(1)}, f32[576,1536]{1,0:T(8,128)}, u32[]{:S(2)}) copy-start(f32[576,1536]{1,0:T(8,128)} %get-tuple-element.157) | copy-start | bytes 10616836
  351.6 17.6 %copy-start.7 = (bf16[576,1536]{1,0:T(8,128)(2,1)S(1)}, bf16[576,1536]{1,0:T(8,128)(2,1)}, u32[]{:S(2)}) copy-start(bf16[576,1536]{1,0:T(8,128)(2,1)} %param.16) | copy-start | bytes 5308420
  351.6 17.6 %copy-start.13 = (f32[576]{0:T(1024)S(1)}, f32[576]{0:T(1024)}, u32[]{:S(2)}) copy-start(f32[576]{0:T(1024)} %copy-done.12) | copy-start | bytes 6916
  351.6 17.6 %copy-start.14 = (f32[576]{0:T(1024)S(1)}, f32[576]{0:T(1024)}, u32[]{:S(2)}) copy-start(f32[576]{0:T(1024)} %get-tuple-element.139) | copy-start | bytes 6916
  351.6 4.0 collective-permute-start.5
  369.2 6.3 copy-start.10
  375.0 4.0 collective-permute-start.6
  385.7 2.2 copy-start.17
  650.8 5.3 copy-start.5
  656.1 3.4 copy-start.4
  659.5 3.5 copy-start.8
  663.0 9.8 %copy-start.3 = (f32[576,1536]{1,0:T(8,128)S(1)}, f32[576,1536]{1,0:T(8,128)}, u32[]{:S(2)}) copy-start(f32[576,1536]{1,0:T(8,128)} %get-tuple-element.178) | copy-start | bytes 10616836
Sparse Core Ops, SparseCore 0:
  304.9 67.7 reduce-scatter.2
  375.9 131.1 reduce-scatter.4

commit v7 on v6

--- a/solution.py
+++ b/solution.py
@@ -690,13 +690,13 @@
     1: (("relay_z", 0), ("start_z", 2), ("pass_own", 0)),
     2: (("start_plane", 0),),
     3: (("relay_z", 1), ("start_z", 3), ("pass_own", 1)),
-    4: (("start_plane", 1), ("forward", 0)),
+    4: (("forward", 0), ("start_plane", 1)),
     5: (("relay_z", 2), ("start_z", 4), ("pass_own", 2)),
-    6: (("start_plane", 2), ("forward", 1)),
+    6: (("forward", 1), ("start_plane", 2)),
     7: (("relay_z", 3), ("pass_own", 3)),
-    8: (("start_plane", 3), ("forward", 2), ("start_z", 5)),
+    8: (("forward", 2), ("start_plane", 3), ("start_z", 5)),
     9: (("relay_z", 4), ("start_z", 6)),
-    10: (("start_plane", 4), ("forward", 3)),
+    10: (("forward", 3), ("start_plane", 4)),
     11: (("relay_only", 5),),
     12: (("forward", 4),),
     13: (("relay_only", 6),),

time: 688 us -> 688 us (level)
  Pallas kernels: 456 us -> 466 us
  starting transfers between devices: 62.9 us -> 54.6 us
    pallas_call x1, Pallas kernels: 91.5 us -> 102 us  [attention_forward(): pl.pallas_call(kernel, grid=(2, trees, 2), in_specs=common_specs(first) +...]
    ppermute x7, starting transfers between devices: 62.9 us -> 54.5 us  [over_core(): return lax.ppermute(value, 'core', [(0, 1), (1, 0)])]
where the time goes in v7:
time: 688 us; the launch traced here: 685 us
  Pallas kernels  466 us (68%)
  matrix products  66.3 us (10%)
  starting transfers between devices  54.6 us (8%)
  other arithmetic  32.8 us (5%)
  local copies, waits for them, and re-layouts  30.1 us (4%)
  waiting for transfers between devices  17.6 us (3%)
  between operations  17.2 us (2%)
    pallas_call x1, Pallas kernels, finish_gradients(): pl.pallas_call(finish_kernel, in_specs=[vmem] * 2 + [anywhere] + [vmem] *...  137 us
    pallas_call x1, Pallas kernels, attention_backward(): pl.pallas_call(kernel, grid=(2, trees, 2), in_specs=common_specs() + [pl....  107 us
    pallas_call x1, Pallas kernels, attention_forward(): pl.pallas_call(kernel, grid=(2, trees, 2), in_specs=common_specs(first) +...  102 us
    ppermute x7, starting transfers between devices, over_core(): return lax.ppermute(value, 'core', [(0, 1), (1, 0)])  54.5 us
    pallas_call x1, Pallas kernels, opening(): pl.pallas_call(opening_kernel, in_specs=[vmem] * 3 + [anywhere] * 3, out_...  50.8 us
    dot_general x6, matrix products, nt(): lax.dot_general(a, b, (((1,), (1,)), ((), ())), preferred_element_type=F32)  44.6 us
    pallas_call x1, Pallas kernels, gated_forward(): pl.pallas_call(kernel, grid=(units // TILE,), in_specs=[pl.BlockSpec((row...  34.9 us
    pallas_call x1, Pallas kernels, gated_backward(): pl.pallas_call(kernel, grid=(units // TILE,), in_specs=[whole, pl.BlockSp...  34.1 us
  transfers between devices with their start and end apart: 9, of which 6 were waited for; matrix products, arithmetic and copies ran while one was open for 9% of the time, Pallas kernels for 28%

profile of v7, /device:TPU:0, one launch (start us, length us, event | category | flops | bytes accessed | tf_op | source)
XLA Modules:
  0.0 684.8 jit_solution(4111236086784770591)
XLA Ops:
  7.2 0.8 fusion.23
  9.3 0.8 reshape.109
  10.8 1.3 broadcast_in_dim.51.gain_ref.gain
  12.9 50.8 %shard_map.262 = (bf16[1536,2304]{1,0:T(8,128)(2,1)}, bf16[1152,1536]{1,0:T(8,128)(2,1)}, bf16[2,2,2,1536,256]{4,3,2,1,0:T(8,128)(2,1)}, f32[2,32,256]{2,1,0:T(8,128)}) custom-call(bf16[576,1536]{1,0:T(8,128)(2,1)} %tokens.1, f32[1,1536]{1,0:T(1,128)} %broadcast_in_dim.51.gain_ref.gain, f32[32,256]{1,0:T(8,128)} %fusion.15.small_ref, ...), custom_call_target="tpu_custom_call" | custom-call | tf_op jit(solution)/shard_map/pallas_call | solution.py:884
  66.4 1.3 stack.68.refs_5_.refs_4_
  68.3 102.3 %shard_map.263 = (bf16[1152,768]{1,0:T(8,128)(2,1)}, f32[2,2,2,2,576,256]{5,4,3,2,1,0:T(8,128)}, bf16[2,2,2,2,576,1536]{5,4,3,2,1,0:T(8,128)(2,1)}, bf16[2,2,2,2...) custom-call(f32[16]{0:T(128)} %reshape_squeeze.3.refs_0_, ...), custom_call_target="tpu_custom_call" | custom-call | flops 89999998976 | bytes 120000000 | tf_op jit(solution)/shard_map/pallas_call | solution.py:361
  170.7 3.6 convolution_convert_fusion.3
  174.3 40.3 %collective-permute-start.1 = (bf16[576,1536]{1,0:T(8,128)(2,1)S(1)}, bf16[576,1536]{1,0:T(8,128)(2,1)S(1)}, u32[]{:S(2)}, u32[]{:S(2)}) collective-permute-start(bf16[576,1536]{1,0:T(8,128)(2,1)S(1)} %convolution_convert_fusion.3), channel_id=1, source_target_pairs={{0,4},{4,0},{1,5},{5,1},{2,6},{6,2},{3,7},{7,3},{8,12},{12,8},{9,1... | collective-permute-start | bytes 5308424 | tf_op jit(solution)/shard_map/ppermute | solution.py:1404
  214.7 3.3 collective-permute-done.1
  218.0 1.9 multiply_reduce_fusion.3
  221.3 3.3 collective-permute-done.2
  224.6 2.0 pad_maximum_fusion.x_ref
  226.6 34.9 %shard_map.264 = (bf16[1152,2048]{1,0:T(8,128)(2,1)}, bf16[1152,2048]{1,0:T(8,128)(2,1)}, bf16[1152,2048]{1,0:T(8,128)(2,1)}, bf16[1536,2048]{1,0:T(8,128)(2,1)}) custom-call(bf16[1152,1536]{1,0:T(8,128)(2,1)} %pad_maximum_fusion.x_ref, bf16[1536,4096]{1,0:T(8,128)(2,1)} %get-tuple-element.59.w_ref, ...), custom_call_target="tpu_custom_call", output_to_operand_aliasing={{3}: (2, {})} | custom-call | tf_op jit(solution)/shard_map/pallas_call | solution.py:780
  261.6 7.5 %convolution_convert_fusion.2 = bf16[576,1536]{1,0:T(8,128)(2,1)S(1)} fusion(bf16[1536,2048]{1,0:T(8,128)(2,1)} %get-tuple-element.62.down_ref, bf16[1152,2048]{1,0:T(8,128)(2,1)} %get-tuple-element.61), kind=kOutput, calls=%fused_computation.20 | convolution fusion | flops 3624763392 | bytes 10420224 | tf_op jit(solution)/shard_map/dot_general | solution.py:40
  269.1 12.0 %collective-permute-start.3 = (bf16[576,1536]{1,0:T(8,128)(2,1)S(1)}, bf16[576,1536]{1,0:T(8,128)(2,1)S(1)}, u32[]{:S(2)}, u32[]{:S(2)}) collective-permute-start(bf16[576,1536]{1,0:T(8,128)(2,1)S(1)} %convolution_convert_fusion.2), channel_id=1, source_target_pairs={{0,4},{4,0},{1,5},{5,1},{2,6},{6,2},{3,7},{7,3},{8,12},{12,8},{9,1... | collective-permute-start | bytes 5308424 | tf_op jit(solution)/shard_map/ppermute | solution.py:1404
  281.1 3.3 collective-permute-done.3
  284.4 6.1 fusion.21
  290.9 3.3 collective-permute-done.4
  294.2 2.0 pad_maximum_fusion.1.d_ref
  296.2 10.3 %convolution_convert_fusion = bf16[1536,2048]{1,0:T(8,128)(2,1)} fusion(bf16[1152,2048]{1,0:T(8,128)(2,1)S(1)} %copy-done.15, bf16[576,1536]{1,0:T(8,128)(2,1)S(1)} %collective-permute-done.4, bf16[576,1536]{1,0:T(8,128)(2,1)S(1)} %get-tuple-element.156), kind=kOutput, calls=%fused_computation | convolution fusion | flops 7257980928 | bytes 14548992 | tf_op jit(solution)/shard_map/dot_general | solution.py:44
  306.6 34.1 %shard_map.265 = (bf16[1152,4096]{1,0:T(8,128)(2,1)}, bf16[1536,4096]{1,0:T(8,128)(2,1)}) custom-call(bf16[1152,1536]{1,0:T(8,128)(2,1)} %pad_maximum_fusion.1.d_ref, bf16[1536,2048]{1,0:T(8,128)(2,1)} %get-tuple-element.62.down_ref, bf16[1152,2048]{1,0:T(8,128)(2,1)} %get-tuple-element.64.gate_ref, bf16[1152,2048]{1,0:T(8,128)(2,1)} %get-tuple-element.65.up_ref, ...), custom_call_target="tpu_custom_call" | custom-call | flops 22000001024 | bytes 40000000 | tf_op jit(solution)/shard_map/pallas_call | solution.py:807
  340.7 11.9 %fusion.4 = bf16[576,1536]{1,0:T(8,128)(2,1)S(1)} fusion(bf16[1536,4096]{1,0:T(8,128)(2,1)} %get-tuple-element.59.w_ref, bf16[1152,4096]{1,0:T(8,128)(2,1)} %get-tuple-element.68), kind=kOutput, calls=%fused_computation.19 | convolution fusion | flops 7248642048 | bytes 19070976 | tf_op jit(solution)/shard_map/dot_general | solution.py:40
  353.2 3.4 collective-permute-done.5
  356.7 13.6 %multiply_reduce_fusion.2 = (f32[1536]{0:T(1024)}, f32[576]{0:T(1024)S(1)}, f32[576,1536]{1,0:T(8,128)S(1)}) fusion(f32[576,1536]{1,0:T(8,128)S(1)} %get-tuple-element.155, f32[576]{0:T(1024)S(1)} %get-tuple-element.140, bf16[576,1536]{1,0:T(8,128)(2,1)} %collective-permute-done.5, f32[1536]{0:T(1024)S(1)} %copy-done.11, ...), kind=kOutput, calls=%fused_computation.11 | convolution fusion | flops 7254833152 | bytes 26165760 | tf_op jit(solution)/shard_map/dot_general | solution.py:40
  370.3 5.9 fusion.22
  377.1 1.4 select_maximum_fusion.1
  379.2 0.9 collective-permute-done.6
  380.1 6.7 convolution_convert_fusion.1.out
  386.8 1.9 pad_maximum_fusion.2
  389.0 4.7 fusion.28.refs_5_
  393.7 106.7 %shard_map.266 = (bf16[1152,2304]{1,0:T(8,128)(2,1)}, f32[2,8,384]{2,1,0:T(8,128)}, f32[2,2,2,8,256]{4,3,2,1,0:T(8,128)}, f32[2,2,2,2,8,256]{5,4,3,2,1,0:T(8,128)}, bf16[1536,1024]{1,0:T(8,128)(2,1)}) custom-call(f32[16]{0:T(128)} %reshape_squeeze.3.refs_0_, bf16[1152,2304]{1,0:T(8,128)(2,1)} %get-tuple-element.69.refs_1_, ...), custom_call_target="tpu_custom_call" | custom-call | flops 1000000000 | bytes 1000000 | tf_op jit(solution)/shard_map/pallas_call | solution.py:400
  500.4 0.9 slice.152
  502.3 0.9 slice_reduce_fusion
  503.8 5.4 convert_element_type.87
  509.9 137.4 %shard_map.267 = (f32[8,1536]{1,0:T(8,128)}, f32[576,1536]{1,0:T(8,128)}, bf16[1536,1024]{1,0:T(8,128)(2,1)}, bf16[1536,1024]{1,0:T(8,128)(2,1)}, bf16[1536,1152]{1,0:T(8,128)(2,1)}, /*index=5*/bf16[1536,384]{1,0:T(8,128)(2,1)}) custom-call(f32[8,1536]{1,0:T(8,128)} %pad_maximum_fusion.3.small, bf16[384,4096]{1,0:T(8,128)(2,1)} %reduce-scatter.5.cloned.1.call-done.gu, ...), custom_call_target="tpu_custom_call" | custom-call | tf_op jit(solution)/shard_map/pallas_call | solution.py:1346
  647.3 0.8 slice.163
  650.0 1.5 fusion.25
  651.5 1.3 fusion.26
  652.8 5.3 fusion.24
  658.1 3.4 convert_element_type.85
  661.5 3.5 convert_element_type.86
  665.0 1.6 convert_element_type.84
  666.6 1.1 reshape.119
  668.3 1.3 reshape.121
  669.6 1.3 reshape.120
  670.9 1.3 dynamic-slice_reduce_fusion
  672.2 1.3 dynamic-slice_reduce_fusion.1
  674.8 1.8 copy.65
  (118 shorter events, 15.2 us)
Async XLA Ops:
  7.2 386.6 %reduce-scatter.3.cloned.1.call-start = ((), (), s32[]{:S(2)}) async-start(), calls=%async_computation.2 | async-start | bytes 7864320 | tf_op jit(solution)/shard_map/reduce_scatter | solution.py:1434
  8.0 162.6 %copy-start.9 = (s32[576]{0:T(1024)}, s32[576]{0:T(1024)S(1)}, u32[]{:S(2)}) copy-start(s32[576]{0:T(1024)S(1)} %get-tuple-element.111) | copy-start | bytes 6916
  8.0 276.4 %copy-start.12 = (f32[576]{0:T(1024)}, f32[576]{0:T(1024)S(1)}, u32[]{:S(2)}) copy-start(f32[576]{0:T(1024)S(1)} %get-tuple-element.110) | copy-start | bytes 6916
  8.0 57.8 %collective-permute-start = (s32[576]{0:T(1024)S(1)}, s32[576]{0:T(1024)S(1)}, u32[]{:S(2)}, u32[]{:S(2)}) collective-permute-start(s32[576]{0:T(1024)S(1)} %get-tuple-element.111), channel_id=1, source_target_pairs={{0,4},{4,0},{1,5},{5,1},{2,6},{6,2},{3,7},{7,3},{8,12},{12,8},{9,1... | collective-permute-start | bytes 6920 | tf_op jit(solution)/shard_map/ppermute | solution.py:1404
  170.6 47.4 %copy-start = (bf16[576,1536]{1,0:T(8,128)(2,1)S(1)}, bf16[576,1536]{1,0:T(8,128)(2,1)}, u32[]{:S(2)}) copy-start(bf16[576,1536]{1,0:T(8,128)(2,1)} %tokens.1) | copy-start | bytes 5308420
  170.6 47.4 %copy-start.16 = (bf16[1536,768]{1,0:T(8,128)(2,1)S(1)}, bf16[1536,768]{1,0:T(8,128)(2,1)}, u32[]{:S(2)}) copy-start(bf16[1536,768]{1,0:T(8,128)(2,1)} %get-tuple-element.58) | copy-start | bytes 7077892
  170.6 47.3 %copy-start.18 = (bf16[1152,768]{1,0:T(8,128)(2,1)S(1)}, bf16[1152,768]{1,0:T(8,128)(2,1)}, u32[]{:S(2)}) copy-start(bf16[1152,768]{1,0:T(8,128)(2,1)} %get-tuple-element.57) | copy-start | bytes 5308420
  174.3 46.2 %copy-start.11 = (f32[1536]{0:T(1024)S(1)}, f32[1536]{0:T(1024)}, u32[]{:S(2)}) copy-start(f32[1536]{0:T(1024)} %param.26) | copy-start | bytes 18436
  174.3 43.7 %collective-permute-start.1 = (bf16[576,1536]{1,0:T(8,128)(2,1)S(1)}, bf16[576,1536]{1,0:T(8,128)(2,1)S(1)}, u32[]{:S(2)}, u32[]{:S(2)}) collective-permute-start(bf16[576,1536]{1,0:T(8,128)(2,1)S(1)} %convolution_convert_fusion.3), channel_id=1, source_target_pairs={{0,4},{4,0},{1,5},{5,1},{2,6},{6,2},{3,7},{7,3},{8,12},{12,8},{9,1... | collective-permute-start | bytes 5308424 | tf_op jit(solution)/shard_map/ppermute | solution.py:1404
  220.9 3.8 collective-permute-start.2
  261.6 22.8 %copy-start.1 = (bf16[1536,2048]{1,0:T(8,128)(2,1)S(1)}, bf16[1536,2048]{1,0:T(8,128)(2,1)}, u32[]{:S(2)}) copy-start(bf16[1536,2048]{1,0:T(8,128)(2,1)} %get-tuple-element.62.down_ref) | copy-start | bytes 18874372
  261.6 22.8 %copy-start.6 = (bf16[576,1536]{1,0:T(8,128)(2,1)S(1)}, bf16[576,1536]{1,0:T(8,128)(2,1)}, u32[]{:S(2)}) copy-start(bf16[576,1536]{1,0:T(8,128)(2,1)} %param.16) | copy-start | bytes 5308420
  261.6 22.8 %copy-start.15 = (bf16[1152,2048]{1,0:T(8,128)(2,1)S(1)}, bf16[1152,2048]{1,0:T(8,128)(2,1)}, u32[]{:S(2)}) copy-start(bf16[1152,2048]{1,0:T(8,128)(2,1)} %get-tuple-element.61) | copy-start | bytes 14155780
  269.1 15.3 %collective-permute-start.3 = (bf16[576,1536]{1,0:T(8,128)(2,1)S(1)}, bf16[576,1536]{1,0:T(8,128)(2,1)S(1)}, u32[]{:S(2)}, u32[]{:S(2)}) collective-permute-start(bf16[576,1536]{1,0:T(8,128)(2,1)S(1)} %convolution_convert_fusion.2), channel_id=1, source_target_pairs={{0,4},{4,0},{1,5},{5,1},{2,6},{6,2},{3,7},{7,3},{8,12},{12,8},{9,1... | collective-permute-start | bytes 5308424 | tf_op jit(solution)/shard_map/ppermute | solution.py:1404
  290.5 3.7 collective-permute-start.4
  306.6 203.4 %reduce-scatter.5.cloned.1.call-start = ((), (), s32[]{:S(2)}) async-start(), calls=%async_computation.3 | async-start | bytes 15728640 | tf_op jit(solution)/shard_map/reduce_scatter | solution.py:1434
  352.6 17.7 %copy-start.2 = (f32[576,1536]{1,0:T(8,128)S(1)}, f32[576,1536]{1,0:T(8,128)}, u32[]{:S(2)}) copy-start(f32[576,1536]{1,0:T(8,128)} %get-tuple-element.157) | copy-start | bytes 10616836
  352.6 17.6 %copy-start.7 = (bf16[576,1536]{1,0:T(8,128)(2,1)S(1)}, bf16[576,1536]{1,0:T(8,128)(2,1)}, u32[]{:S(2)}) copy-start(bf16[576,1536]{1,0:T(8,128)(2,1)} %param.16) | copy-start | bytes 5308420
  352.6 17.6 %copy-start.13 = (f32[576]{0:T(1024)S(1)}, f32[576]{0:T(1024)}, u32[]{:S(2)}) copy-start(f32[576]{0:T(1024)} %copy-done.12) | copy-start | bytes 6916
  352.7 17.6 %copy-start.14 = (f32[576]{0:T(1024)S(1)}, f32[576]{0:T(1024)}, u32[]{:S(2)}) copy-start(f32[576]{0:T(1024)} %get-tuple-element.139) | copy-start | bytes 6916
  352.7 4.0 collective-permute-start.5
  370.3 6.3 copy-start.10
  376.2 3.9 collective-permute-start.6
  386.8 2.2 copy-start.17
  652.8 5.3 copy-start.5
  658.1 3.4 copy-start.4
  661.5 3.5 copy-start.8
  665.0 9.8 %copy-start.3 = (f32[576,1536]{1,0:T(8,128)S(1)}, f32[576,1536]{1,0:T(8,128)}, u32[]{:S(2)}) copy-start(f32[576,1536]{1,0:T(8,128)} %get-tuple-element.178) | copy-start | bytes 10616836
Sparse Core Ops, SparseCore 0:
  306.7 68.4 reduce-scatter.2
  378.3 131.2 reduce-scatter.4

commit v8 on v6

--- a/solution.py
+++ b/solution.py
@@ -697,8 +697,8 @@
     8: (("start_plane", 3), ("forward", 2), ("start_z", 5)),
     9: (("relay_z", 4), ("start_z", 6)),
     10: (("start_plane", 4), ("forward", 3)),
-    11: (("relay_only", 5),),
-    12: (("forward", 4),),
+    11: (("forward", 4),),
+    12: (("relay_only", 5),),
     13: (("relay_only", 6),),
 }
 

time: 688 us -> 693 us (level)
  no operation moved by 1% of the time
where the time goes in v8:
time: 693 us; the launch traced here: 689 us
  Pallas kernels  462 us (67%)
  matrix products  66.5 us (10%)
  starting transfers between devices  62.6 us (9%)
  other arithmetic  32.9 us (5%)
  local copies, waits for them, and re-layouts  30.1 us (4%)
  waiting for transfers between devices  17.6 us (3%)
  between operations  17.2 us (2%)
    pallas_call x1, Pallas kernels, finish_gradients(): pl.pallas_call(finish_kernel, in_specs=[vmem] * 2 + [anywhere] + [vmem] *...  140 us
    pallas_call x1, Pallas kernels, attention_backward(): pl.pallas_call(kernel, grid=(2, trees, 2), in_specs=common_specs() + [pl....  106 us
    pallas_call x1, Pallas kernels, attention_forward(): pl.pallas_call(kernel, grid=(2, trees, 2), in_specs=common_specs(first) +...  95.2 us
    ppermute x7, starting transfers between devices, over_core(): return lax.ppermute(value, 'core', [(0, 1), (1, 0)])  62.6 us
    pallas_call x1, Pallas kernels, opening(): pl.pallas_call(opening_kernel, in_specs=[vmem] * 3 + [anywhere] * 3, out_...  50.8 us
    dot_general x6, matrix products, nt(): lax.dot_general(a, b, (((1,), (1,)), ((), ())), preferred_element_type=F32)  44.7 us
    pallas_call x1, Pallas kernels, gated_forward(): pl.pallas_call(kernel, grid=(units // TILE,), in_specs=[pl.BlockSpec((row...  34.9 us
    pallas_call x1, Pallas kernels, gated_backward(): pl.pallas_call(kernel, grid=(units // TILE,), in_specs=[whole, pl.BlockSp...  34.5 us
  transfers between devices with their start and end apart: 9, of which 6 were waited for; matrix products, arithmetic and copies ran while one was open for 9% of the time, Pallas kernels for 28%

profile of v8, /device:TPU:0, one launch (start us, length us, event | category | flops | bytes accessed | tf_op | source)
XLA Modules:
  0.0 688.6 jit_solution(8682189387798581240)
XLA Ops:
  7.2 0.8 fusion.23
  9.3 0.8 reshape.109
  10.8 1.3 broadcast_in_dim.51.gain_ref.gain
  12.9 50.8 %shard_map.262 = (bf16[1536,2304]{1,0:T(8,128)(2,1)}, bf16[1152,1536]{1,0:T(8,128)(2,1)}, bf16[2,2,2,1536,256]{4,3,2,1,0:T(8,128)(2,1)}, f32[2,32,256]{2,1,0:T(8,128)}) custom-call(bf16[576,1536]{1,0:T(8,128)(2,1)} %tokens.1, f32[1,1536]{1,0:T(1,128)} %broadcast_in_dim.51.gain_ref.gain, f32[32,256]{1,0:T(8,128)} %fusion.15.small_ref, ...), custom_call_target="tpu_custom_call" | custom-call | tf_op jit(solution)/shard_map/pallas_call | solution.py:884
  66.4 1.3 stack.68.refs_5_.refs_4_
  68.3 95.2 %shard_map.263 = (bf16[1152,768]{1,0:T(8,128)(2,1)}, f32[2,2,2,2,576,256]{5,4,3,2,1,0:T(8,128)}, bf16[2,2,2,2,576,1536]{5,4,3,2,1,0:T(8,128)(2,1)}, bf16[2,2,2,2...) custom-call(f32[16]{0:T(128)} %reshape_squeeze.3.refs_0_, ...), custom_call_target="tpu_custom_call" | custom-call | flops 89999998976 | bytes 120000000 | tf_op jit(solution)/shard_map/pallas_call | solution.py:361
  163.5 3.6 convolution_convert_fusion.3
  167.2 48.4 %collective-permute-start.1 = (bf16[576,1536]{1,0:T(8,128)(2,1)S(1)}, bf16[576,1536]{1,0:T(8,128)(2,1)S(1)}, u32[]{:S(2)}, u32[]{:S(2)}) collective-permute-start(bf16[576,1536]{1,0:T(8,128)(2,1)S(1)} %convolution_convert_fusion.3), channel_id=1, source_target_pairs={{0,4},{4,0},{1,5},{5,1},{2,6},{6,2},{3,7},{7,3},{8,12},{12,8},{9,1... | collective-permute-start | bytes 5308424 | tf_op jit(solution)/shard_map/ppermute | solution.py:1404
  215.6 3.3 collective-permute-done.1
  218.9 1.9 multiply_reduce_fusion.3
  222.2 3.3 collective-permute-done.2
  225.6 2.0 pad_maximum_fusion.x_ref
  227.6 34.9 %shard_map.264 = (bf16[1152,2048]{1,0:T(8,128)(2,1)}, bf16[1152,2048]{1,0:T(8,128)(2,1)}, bf16[1152,2048]{1,0:T(8,128)(2,1)}, bf16[1536,2048]{1,0:T(8,128)(2,1)}) custom-call(bf16[1152,1536]{1,0:T(8,128)(2,1)} %pad_maximum_fusion.x_ref, bf16[1536,4096]{1,0:T(8,128)(2,1)} %get-tuple-element.59.w_ref, ...), custom_call_target="tpu_custom_call", output_to_operand_aliasing={{3}: (2, {})} | custom-call | tf_op jit(solution)/shard_map/pallas_call | solution.py:780
  262.5 7.5 %convolution_convert_fusion.2 = bf16[576,1536]{1,0:T(8,128)(2,1)S(1)} fusion(bf16[1536,2048]{1,0:T(8,128)(2,1)} %get-tuple-element.62.down_ref, bf16[1152,2048]{1,0:T(8,128)(2,1)} %get-tuple-element.61), kind=kOutput, calls=%fused_computation.20 | convolution fusion | flops 3624763392 | bytes 10420224 | tf_op jit(solution)/shard_map/dot_general | solution.py:40
  270.0 12.0 %collective-permute-start.3 = (bf16[576,1536]{1,0:T(8,128)(2,1)S(1)}, bf16[576,1536]{1,0:T(8,128)(2,1)S(1)}, u32[]{:S(2)}, u32[]{:S(2)}) collective-permute-start(bf16[576,1536]{1,0:T(8,128)(2,1)S(1)} %convolution_convert_fusion.2), channel_id=1, source_target_pairs={{0,4},{4,0},{1,5},{5,1},{2,6},{6,2},{3,7},{7,3},{8,12},{12,8},{9,1... | collective-permute-start | bytes 5308424 | tf_op jit(solution)/shard_map/ppermute | solution.py:1404
  282.0 3.3 collective-permute-done.3
  285.3 6.1 fusion.21
  291.8 3.3 collective-permute-done.4
  295.1 2.0 pad_maximum_fusion.1.d_ref
  297.1 10.3 %convolution_convert_fusion = bf16[1536,2048]{1,0:T(8,128)(2,1)} fusion(bf16[1152,2048]{1,0:T(8,128)(2,1)S(1)} %copy-done.15, bf16[576,1536]{1,0:T(8,128)(2,1)S(1)} %collective-permute-done.4, bf16[576,1536]{1,0:T(8,128)(2,1)S(1)} %get-tuple-element.156), kind=kOutput, calls=%fused_computation | convolution fusion | flops 7257980928 | bytes 14548992 | tf_op jit(solution)/shard_map/dot_general | solution.py:44
  307.5 34.5 %shard_map.265 = (bf16[1152,4096]{1,0:T(8,128)(2,1)}, bf16[1536,4096]{1,0:T(8,128)(2,1)}) custom-call(bf16[1152,1536]{1,0:T(8,128)(2,1)} %pad_maximum_fusion.1.d_ref, bf16[1536,2048]{1,0:T(8,128)(2,1)} %get-tuple-element.62.down_ref, bf16[1152,2048]{1,0:T(8,128)(2,1)} %get-tuple-element.64.gate_ref, bf16[1152,2048]{1,0:T(8,128)(2,1)} %get-tuple-element.65.up_ref, ...), custom_call_target="tpu_custom_call" | custom-call | flops 22000001024 | bytes 40000000 | tf_op jit(solution)/shard_map/pallas_call | solution.py:807
  342.0 12.1 %fusion.4 = bf16[576,1536]{1,0:T(8,128)(2,1)S(1)} fusion(bf16[1536,4096]{1,0:T(8,128)(2,1)} %get-tuple-element.59.w_ref, bf16[1152,4096]{1,0:T(8,128)(2,1)} %get-tuple-element.68), kind=kOutput, calls=%fused_computation.19 | convolution fusion | flops 7248642048 | bytes 19070976 | tf_op jit(solution)/shard_map/dot_general | solution.py:40
  354.6 3.4 collective-permute-done.5
  358.0 13.6 %multiply_reduce_fusion.2 = (f32[1536]{0:T(1024)}, f32[576]{0:T(1024)S(1)}, f32[576,1536]{1,0:T(8,128)S(1)}) fusion(f32[576,1536]{1,0:T(8,128)S(1)} %get-tuple-element.155, f32[576]{0:T(1024)S(1)} %get-tuple-element.140, bf16[576,1536]{1,0:T(8,128)(2,1)} %collective-permute-done.5, f32[1536]{0:T(1024)S(1)} %copy-done.11, ...), kind=kOutput, calls=%fused_computation.11 | convolution fusion | flops 7254833152 | bytes 26165760 | tf_op jit(solution)/shard_map/dot_general | solution.py:40
  371.6 5.9 fusion.22
  378.5 1.4 select_maximum_fusion.1
  380.6 0.8 collective-permute-done.6
  381.5 6.7 convolution_convert_fusion.1.out
  388.2 1.9 pad_maximum_fusion.2
  390.4 4.7 fusion.28.refs_5_
  395.1 106.3 %shard_map.266 = (bf16[1152,2304]{1,0:T(8,128)(2,1)}, f32[2,8,384]{2,1,0:T(8,128)}, f32[2,2,2,8,256]{4,3,2,1,0:T(8,128)}, f32[2,2,2,2,8,256]{5,4,3,2,1,0:T(8,128)}, bf16[1536,1024]{1,0:T(8,128)(2,1)}) custom-call(f32[16]{0:T(128)} %reshape_squeeze.3.refs_0_, bf16[1152,2304]{1,0:T(8,128)(2,1)} %get-tuple-element.69.refs_1_, ...), custom_call_target="tpu_custom_call" | custom-call | flops 1000000000 | bytes 1000000 | tf_op jit(solution)/shard_map/pallas_call | solution.py:400
  501.4 0.9 slice.152
  503.3 0.9 slice_reduce_fusion
  504.8 5.5 convert_element_type.87
  511.0 140.1 %shard_map.267 = (f32[8,1536]{1,0:T(8,128)}, f32[576,1536]{1,0:T(8,128)}, bf16[1536,1024]{1,0:T(8,128)(2,1)}, bf16[1536,1024]{1,0:T(8,128)(2,1)}, bf16[1536,1152]{1,0:T(8,128)(2,1)}, /*index=5*/bf16[1536,384]{1,0:T(8,128)(2,1)}) custom-call(f32[8,1536]{1,0:T(8,128)} %pad_maximum_fusion.3.small, bf16[384,4096]{1,0:T(8,128)(2,1)} %reduce-scatter.5.cloned.1.call-done.gu, ...), custom_call_target="tpu_custom_call" | custom-call | tf_op jit(solution)/shard_map/pallas_call | solution.py:1346
  651.1 0.8 slice.163
  653.8 1.5 fusion.25
  655.3 1.3 fusion.26
  656.6 5.3 fusion.24
  661.9 3.4 convert_element_type.85
  665.3 3.5 convert_element_type.86
  668.8 1.6 convert_element_type.84
  670.4 1.1 reshape.119
  672.1 1.3 reshape.121
  673.4 1.3 reshape.120
  674.7 1.3 dynamic-slice_reduce_fusion
  676.0 1.3 dynamic-slice_reduce_fusion.1
  678.6 1.8 copy.65
  (118 shorter events, 15.2 us)
Async XLA Ops:
  7.2 387.9 %reduce-scatter.3.cloned.1.call-start = ((), (), s32[]{:S(2)}) async-start(), calls=%async_computation.2 | async-start | bytes 7864320 | tf_op jit(solution)/shard_map/reduce_scatter | solution.py:1434
  8.0 155.4 %copy-start.9 = (s32[576]{0:T(1024)}, s32[576]{0:T(1024)S(1)}, u32[]{:S(2)}) copy-start(s32[576]{0:T(1024)S(1)} %get-tuple-element.111) | copy-start | bytes 6916
  8.0 277.3 %copy-start.12 = (f32[576]{0:T(1024)}, f32[576]{0:T(1024)S(1)}, u32[]{:S(2)}) copy-start(f32[576]{0:T(1024)S(1)} %get-tuple-element.110) | copy-start | bytes 6916
  8.0 57.8 %collective-permute-start = (s32[576]{0:T(1024)S(1)}, s32[576]{0:T(1024)S(1)}, u32[]{:S(2)}, u32[]{:S(2)}) collective-permute-start(s32[576]{0:T(1024)S(1)} %get-tuple-element.111), channel_id=1, source_target_pairs={{0,4},{4,0},{1,5},{5,1},{2,6},{6,2},{3,7},{7,3},{8,12},{12,8},{9,1... | collective-permute-start | bytes 6920 | tf_op jit(solution)/shard_map/ppermute | solution.py:1404
  163.5 55.5 %copy-start = (bf16[576,1536]{1,0:T(8,128)(2,1)S(1)}, bf16[576,1536]{1,0:T(8,128)(2,1)}, u32[]{:S(2)}) copy-start(bf16[576,1536]{1,0:T(8,128)(2,1)} %tokens.1) | copy-start | bytes 5308420
  163.5 55.5 %copy-start.16 = (bf16[1536,768]{1,0:T(8,128)(2,1)S(1)}, bf16[1536,768]{1,0:T(8,128)(2,1)}, u32[]{:S(2)}) copy-start(bf16[1536,768]{1,0:T(8,128)(2,1)} %get-tuple-element.58) | copy-start | bytes 7077892
  163.5 55.5 %copy-start.18 = (bf16[1152,768]{1,0:T(8,128)(2,1)S(1)}, bf16[1152,768]{1,0:T(8,128)(2,1)}, u32[]{:S(2)}) copy-start(bf16[1152,768]{1,0:T(8,128)(2,1)} %get-tuple-element.57) | copy-start | bytes 5308420
  167.1 54.3 %copy-start.11 = (f32[1536]{0:T(1024)S(1)}, f32[1536]{0:T(1024)}, u32[]{:S(2)}) copy-start(f32[1536]{0:T(1024)} %param.26) | copy-start | bytes 18436
  167.2 51.8 %collective-permute-start.1 = (bf16[576,1536]{1,0:T(8,128)(2,1)S(1)}, bf16[576,1536]{1,0:T(8,128)(2,1)S(1)}, u32[]{:S(2)}, u32[]{:S(2)}) collective-permute-start(bf16[576,1536]{1,0:T(8,128)(2,1)S(1)} %convolution_convert_fusion.3), channel_id=1, source_target_pairs={{0,4},{4,0},{1,5},{5,1},{2,6},{6,2},{3,7},{7,3},{8,12},{12,8},{9,1... | collective-permute-start | bytes 5308424 | tf_op jit(solution)/shard_map/ppermute | solution.py:1404
  221.8 3.8 collective-permute-start.2
  262.5 22.8 %copy-start.1 = (bf16[1536,2048]{1,0:T(8,128)(2,1)S(1)}, bf16[1536,2048]{1,0:T(8,128)(2,1)}, u32[]{:S(2)}) copy-start(bf16[1536,2048]{1,0:T(8,128)(2,1)} %get-tuple-element.62.down_ref) | copy-start | bytes 18874372
  262.5 22.8 %copy-start.6 = (bf16[576,1536]{1,0:T(8,128)(2,1)S(1)}, bf16[576,1536]{1,0:T(8,128)(2,1)}, u32[]{:S(2)}) copy-start(bf16[576,1536]{1,0:T(8,128)(2,1)} %param.16) | copy-start | bytes 5308420
  262.5 22.8 %copy-start.15 = (bf16[1152,2048]{1,0:T(8,128)(2,1)S(1)}, bf16[1152,2048]{1,0:T(8,128)(2,1)}, u32[]{:S(2)}) copy-start(bf16[1152,2048]{1,0:T(8,128)(2,1)} %get-tuple-element.61) | copy-start | bytes 14155780
  270.0 15.3 %collective-permute-start.3 = (bf16[576,1536]{1,0:T(8,128)(2,1)S(1)}, bf16[576,1536]{1,0:T(8,128)(2,1)S(1)}, u32[]{:S(2)}, u32[]{:S(2)}) collective-permute-start(bf16[576,1536]{1,0:T(8,128)(2,1)S(1)} %convolution_convert_fusion.2), channel_id=1, source_target_pairs={{0,4},{4,0},{1,5},{5,1},{2,6},{6,2},{3,7},{7,3},{8,12},{12,8},{9,1... | collective-permute-start | bytes 5308424 | tf_op jit(solution)/shard_map/ppermute | solution.py:1404
  291.4 3.7 collective-permute-start.4
  307.5 203.5 %reduce-scatter.5.cloned.1.call-start = ((), (), s32[]{:S(2)}) async-start(), calls=%async_computation.3 | async-start | bytes 15728640 | tf_op jit(solution)/shard_map/reduce_scatter | solution.py:1434
  354.1 17.5 %copy-start.2 = (f32[576,1536]{1,0:T(8,128)S(1)}, f32[576,1536]{1,0:T(8,128)}, u32[]{:S(2)}) copy-start(f32[576,1536]{1,0:T(8,128)} %get-tuple-element.157) | copy-start | bytes 10616836
  354.1 17.5 %copy-start.7 = (bf16[576,1536]{1,0:T(8,128)(2,1)S(1)}, bf16[576,1536]{1,0:T(8,128)(2,1)}, u32[]{:S(2)}) copy-start(bf16[576,1536]{1,0:T(8,128)(2,1)} %param.16) | copy-start | bytes 5308420
  354.1 17.5 %copy-start.13 = (f32[576]{0:T(1024)S(1)}, f32[576]{0:T(1024)}, u32[]{:S(2)}) copy-start(f32[576]{0:T(1024)} %copy-done.12) | copy-start | bytes 6916
  354.1 17.5 %copy-start.14 = (f32[576]{0:T(1024)S(1)}, f32[576]{0:T(1024)}, u32[]{:S(2)}) copy-start(f32[576]{0:T(1024)} %get-tuple-element.139) | copy-start | bytes 6916
  354.1 3.9 collective-permute-start.5
  371.6 6.3 copy-start.10
  377.5 3.9 collective-permute-start.6
  388.2 2.2 copy-start.17
  656.6 5.3 copy-start.5
  661.9 3.4 copy-start.4
  665.3 3.5 copy-start.8
  668.8 9.8 %copy-start.3 = (f32[576,1536]{1,0:T(8,128)S(1)}, f32[576,1536]{1,0:T(8,128)}, u32[]{:S(2)}) copy-start(f32[576,1536]{1,0:T(8,128)} %get-tuple-element.178) | copy-start | bytes 10616836
Sparse Core Ops, SparseCore 0:
  307.6 67.9 reduce-scatter.2
  378.7 131.2 reduce-scatter.4
